TPU v7x, 32 devices: a whole 2x2x4 slice. The times are simulated.
32 devices in a mesh: dp: 8 (over z, core), tensor: 4 (over y, x).
Axes of the slice: x: 2, y: 2, z: 4, core: 2. Of those that a mesh axis runs over, the one named last changes fastest.
Arguments:
- tokens: bfloat16 [36928, 1024], P(('dp', 'tensor')), may hold values from -6 to 6
- first_gain: float32 [1024], replicated, may hold values from 0.5 to 1.5
- first_shift: float32 [1024], replicated, may hold values from -1.5 to 1.5
- joint_weight: bfloat16 [1024, 3, 1024], P('dp', None, 'tensor'), may hold values from -0.1875 to 0.1875
- joint_bias: bfloat16 [2, 16, 64], P(None, 'tensor', 'dp'), may hold values from -3 to 3
- output_weight: bfloat16 [1024, 1024], P('tensor', 'dp'), may hold values from -1 to 1
- output_bias: float32 [1024], replicated, may hold values from -1.5 to 1.5
- second_gain: float32 [1024], replicated, may hold values from 0.5 to 1.5
- second_shift: float32 [1024], replicated, may hold values from -1.5 to 1.5
- expand_weight: bfloat16 [1024, 4096], P('dp', 'tensor'), may hold values from -0.1875 to 0.1875
- expand_bias: bfloat16 [64, 64], P('tensor', 'dp'), may hold values from -3 to 3
- shrink_weight: bfloat16 [4096, 1024], P('tensor', 'dp'), may hold values from -0.1875 to 0.1875
- shrink_bias: float32 [1024], replicated, may hold values from -1.5 to 1.5
- cotangent: bfloat16 [36928, 1024], P(('dp', 'tensor')), may hold values from -6 to 6
- image_count: int32 [8], P('dp'), may hold values from 1 to 8, 56 in all
- threshold: float32 [16], P('tensor'), may hold values from 2 to 20
Outputs:
- block_out: bfloat16 [36928, 1024], P(('dp', 'tensor'))
- tokens_grad: bfloat16 [36928, 1024], P(('dp', 'tensor'))
- first_gain_grad: float32 [1024], P('dp')
- first_shift_grad: float32 [1024], P('dp')
- joint_grad: float32 [1024, 3, 1024], P('dp', None, 'tensor')
- joint_bias_grad: float32 [2, 16, 64], P(None, 'tensor', 'dp')
- output_grad: float32 [1024, 1024], P('tensor', 'dp')
- output_bias_grad: float32 [1024], P('dp')
- second_gain_grad: float32 [1024], P('dp')
- second_shift_grad: float32 [1024], P('dp')
- expand_grad: float32 [1024, 4096], P('dp', 'tensor')
- expand_bias_grad: float32 [64, 64], P('tensor', 'dp')
- shrink_grad: float32 [4096, 1024], P('tensor', 'dp')
- shrink_bias_grad: float32 [1024], P('dp')
- clipped_joint: bfloat16 [1024, 2, 1024], P('dp', None, 'tensor')
- clipped_bias: bfloat16 [16, 64], P('tensor', 'dp')
- factors: float32 [16], P('tensor')
Inputs may be any that keep to these rules, and one draw needn't show every extreme that they name: `image_count`: every index of dp holds 1 to 8 images, in its first slots; the counts sum to 56 and some index holds exactly 8.
All inputs are finite; a program needn't handle non-finite values. No bound on the sum of `image_count` on one device may be relied on, other than what follows from the above.
Results may differ from a plain program's by a relative error of at most 0.023.
Values may be sent and summed in bfloat16 or wider, within the bound.
No kernel may reach another device: no remote copies, remote signals or barrier semaphores. Data moves between devices by JAX's collectives and lax.ppermute only.
A program may use at most 320 MiB of HBM per device.

v0:
```python
from functools import partial

import jax
import jax.numpy as jnp
from jax import lax
from jax.sharding import PartitionSpec as P

D = 1024
HEADS = 16
HEAD_DIM = 64
SEQ = 577


def norm_forward(values, gain, shift):
    center = values - jnp.mean(values, axis=-1, keepdims=True)
    inverse = lax.rsqrt(jnp.mean(center * center, axis=-1, keepdims=True) + 1e-05)
    unit = center * inverse
    return (unit * gain + shift, unit, inverse)


def norm_backward(grad, unit, inverse, gain):
    scaled = grad * gain
    inner = (
        scaled
        - jnp.mean(scaled, axis=-1, keepdims=True)
        - unit * jnp.mean(scaled * unit, axis=-1, keepdims=True)
    )
    return (inner * inverse, jnp.sum(grad * unit, axis=0), jnp.sum(grad, axis=0))


def attend(scale, packed):
    queries = packed[:, 0]
    keys = packed[:, 1]
    values = packed[:, 2]
    scores = scale * jnp.einsum("qhd,khd->hqk", queries, keys, preferred_element_type=jnp.float32)
    peak = jnp.max(scores, axis=(1, 2))
    rowmax = jnp.max(scores, axis=-1, keepdims=True)
    expo = jnp.exp(scores - rowmax)
    total = jnp.sum(expo, axis=-1, keepdims=True)
    probs = expo / total
    mixed = jnp.einsum(
        "hqk,khd->qhd", probs.astype(jnp.bfloat16), values, preferred_element_type=jnp.float32
    )
    return (mixed.astype(jnp.bfloat16), rowmax + jnp.log(total), peak)


def attend_back(scale, item):
    packed, logsum, dmixed = item
    queries = packed[:, 0]
    keys = packed[:, 1]
    values = packed[:, 2]
    scores = scale * jnp.einsum("qhd,khd->hqk", queries, keys, preferred_element_type=jnp.float32)
    probs = jnp.exp(scores - logsum)
    dvalues = jnp.einsum(
        "hqk,qhd->khd", probs.astype(jnp.bfloat16), dmixed, preferred_element_type=jnp.float32
    )
    dprobs = jnp.einsum("qhd,khd->hqk", dmixed, values, preferred_element_type=jnp.float32)
    dscores = (probs * (dprobs - jnp.sum(probs * dprobs, axis=-1, keepdims=True))).astype(
        jnp.bfloat16
    )
    dqueries = scale * jnp.einsum("hqk,khd->qhd", dscores, keys, preferred_element_type=jnp.float32)
    dkeys = scale * jnp.einsum("hqk,qhd->khd", dscores, queries, preferred_element_type=jnp.float32)
    return jnp.stack([dqueries, dkeys, dvalues], axis=1).astype(jnp.bfloat16)


def per_device(
    tokens,
    first_gain,
    first_shift,
    joint_weight,
    joint_bias,
    output_weight,
    output_bias,
    second_gain,
    second_shift,
    expand_weight,
    expand_bias,
    shrink_weight,
    shrink_bias,
    cotangent,
    image_count,
    threshold,
):
    local_rows = tokens.shape[0]
    tensor_index = lax.axis_index("tensor")
    scale = HEAD_DIM ** (-0.5)
    joint_full, output_full, expand_full, shrink_full, jbias_full, ebias_full = (
        lax.all_gather(joint_weight, "dp", axis=0, tiled=True),
        lax.all_gather(output_weight, "dp", axis=1, tiled=True),
        lax.all_gather(expand_weight, "dp", axis=0, tiled=True),
        lax.all_gather(shrink_weight, "dp", axis=1, tiled=True),
        lax.all_gather(joint_bias, "dp", axis=2, tiled=True),
        lax.all_gather(expand_bias, "dp", axis=1, tiled=True),
    )
    heads_local = jbias_full.shape[1]
    count = image_count[0]
    row_ids = tensor_index * local_rows + jnp.arange(local_rows, dtype=jnp.int32)
    row_live = (row_ids // SEQ < count).astype(jnp.float32)[:, None]
    inputs = tokens.astype(jnp.float32)
    normed, unit_one, inverse_one = norm_forward(inputs, first_gain, first_shift)
    dout = cotangent.astype(jnp.float32) * row_live
    dresult = dout.astype(jnp.bfloat16)
    joint_wide, output_wide, expand_wide, shrink_wide, jbias_wide, ebias_wide = (
        lax.all_gather(joint_full, "tensor", axis=2, tiled=True),
        lax.all_gather(output_full, "tensor", axis=0, tiled=True),
        lax.all_gather(expand_full, "tensor", axis=1, tiled=True),
        lax.all_gather(shrink_full, "tensor", axis=0, tiled=True),
        lax.all_gather(jbias_full, "tensor", axis=1, tiled=True),
        lax.all_gather(ebias_full, "tensor", axis=0, tiled=True),
    )
    own_images = local_rows // SEQ
    image_ids = tensor_index * own_images + jnp.arange(own_images, dtype=jnp.int32)
    image_live = image_ids < count
    normed_rows = normed.astype(jnp.bfloat16)
    bias_query = jbias_wide[0].astype(jnp.float32).reshape(D)
    bias_value = jbias_wide[1].astype(jnp.float32).reshape(D)
    bias_rows = jnp.stack([bias_query, jnp.zeros_like(bias_query), bias_value])
    packed = (
        jnp.einsum("rd,dcj->rcj", normed_rows, joint_wide, preferred_element_type=jnp.float32)
        + bias_rows
    ).astype(jnp.bfloat16)
    per_image = packed.reshape(own_images, SEQ, 3, HEADS, HEAD_DIM)
    mixed, logsum, peaks = lax.map(partial(attend, scale), per_image)
    mixed_rows = mixed.reshape(local_rows, D)
    peak_all = jnp.max(jnp.where(image_live[:, None], peaks, -1e30), axis=0)
    middle = (
        inputs + jnp.dot(mixed_rows, output_wide, preferred_element_type=jnp.float32) + output_bias
    )
    second, unit_two, inverse_two = norm_forward(middle, second_gain, second_shift)
    second_rows = second.astype(jnp.bfloat16)
    hidden = jnp.dot(
        second_rows, expand_wide, preferred_element_type=jnp.float32
    ) + ebias_wide.astype(jnp.float32).reshape(-1)
    sigma = jax.nn.sigmoid(1.702 * hidden)
    active = (hidden * sigma).astype(jnp.bfloat16)
    result = jnp.dot(active, shrink_wide, preferred_element_type=jnp.float32) + shrink_bias
    block_out = (row_live * (middle + result)).astype(jnp.bfloat16)
    shrink_grad = jnp.einsum("rf,rd->fd", active, dresult, preferred_element_type=jnp.float32)
    dactive = jnp.einsum("rd,fd->rf", dresult, shrink_wide, preferred_element_type=jnp.float32)
    dhidden = (dactive * (sigma + 1.702 * hidden * sigma * (1.0 - sigma))).astype(jnp.bfloat16)
    expand_bias_grad = jnp.sum(dhidden, axis=0, dtype=jnp.float32)
    expand_grad = jnp.einsum("rd,rf->df", second_rows, dhidden, preferred_element_type=jnp.float32)
    dsecond = jnp.einsum("rf,df->rd", dhidden, expand_wide, preferred_element_type=jnp.float32)
    dmiddle_part, second_gain_grad, second_shift_grad = norm_backward(
        dsecond, unit_two, inverse_two, second_gain
    )
    dmiddle = dout + dmiddle_part
    dbranch = dmiddle.astype(jnp.bfloat16)
    output_grad = jnp.einsum("rj,rd->jd", mixed_rows, dbranch, preferred_element_type=jnp.float32)
    dmixed = jnp.einsum(
        "rd,jd->rj", dbranch, output_wide, preferred_element_type=jnp.float32
    ).astype(jnp.bfloat16)
    dmixed = dmixed.reshape(own_images, SEQ, HEADS, HEAD_DIM)
    dpacked = lax.map(partial(attend_back, scale), (per_image, logsum, dmixed))
    dpacked_rows = dpacked.reshape(local_rows, 3, D)
    joint_grad = jnp.einsum(
        "rd,rcj->dcj", normed_rows, dpacked_rows, preferred_element_type=jnp.float32
    )
    bias_sums = jnp.sum(dpacked_rows, axis=0, dtype=jnp.float32)
    joint_bias_grad = jnp.stack([bias_sums[0], bias_sums[2]]).reshape(2, HEADS, HEAD_DIM)
    dnormed = jnp.einsum(
        "rcj,dcj->rd", dpacked_rows, joint_wide, preferred_element_type=jnp.float32
    )
    joint_grad, output_grad, expand_grad, shrink_grad, joint_bias_grad, expand_bias_grad = (
        lax.psum_scatter(
            joint_grad.astype(jnp.bfloat16), "tensor", scatter_dimension=2, tiled=True
        ).astype(jnp.float32),
        lax.psum_scatter(
            output_grad.astype(jnp.bfloat16), "tensor", scatter_dimension=0, tiled=True
        ).astype(jnp.float32),
        lax.psum_scatter(
            expand_grad.astype(jnp.bfloat16), "tensor", scatter_dimension=1, tiled=True
        ).astype(jnp.float32),
        lax.psum_scatter(
            shrink_grad.astype(jnp.bfloat16), "tensor", scatter_dimension=0, tiled=True
        ).astype(jnp.float32),
        lax.psum_scatter(
            joint_bias_grad.astype(jnp.bfloat16), "tensor", scatter_dimension=1, tiled=True
        ).astype(jnp.float32),
        lax.psum_scatter(
            expand_bias_grad.reshape(-1, HEAD_DIM).astype(jnp.bfloat16),
            "tensor",
            scatter_dimension=0,
            tiled=True,
        ).astype(jnp.float32),
    )
    dinput_part, first_gain_grad, first_shift_grad = norm_backward(
        dnormed, unit_one, inverse_one, first_gain
    )
    tokens_grad = (dmiddle + dinput_part).astype(jnp.bfloat16)
    top_all = lax.pmax(peak_all, ("dp", "tensor"))
    top = lax.dynamic_slice_in_dim(top_all, tensor_index * heads_local, heads_local, 0)
    factors = jnp.sqrt(threshold / jnp.maximum(top, threshold))
    columns = jnp.repeat(factors, HEAD_DIM)
    clipped_joint = (joint_weight[:, 0:2, :].astype(jnp.float32) * columns).astype(jnp.bfloat16)
    clipped_bias = (joint_bias[0].astype(jnp.float32) * factors[:, None]).astype(jnp.bfloat16)
    output_bias_grad = jnp.sum(dbranch, axis=0, dtype=jnp.float32)
    shrink_bias_grad = jnp.sum(dresult, axis=0, dtype=jnp.float32)
    vectors = jnp.stack(
        [
            first_gain_grad,
            first_shift_grad,
            output_bias_grad,
            second_gain_grad,
            second_shift_grad,
            shrink_bias_grad,
        ]
    )
    vectors = lax.psum(vectors, "tensor")
    (
        joint_grad,
        output_grad,
        expand_grad,
        shrink_grad,
        joint_bias_grad,
        expand_bias_grad,
        vectors,
    ) = (
        lax.psum_scatter(
            joint_grad.astype(jnp.bfloat16), "dp", scatter_dimension=0, tiled=True
        ).astype(jnp.float32),
        lax.psum_scatter(
            output_grad.astype(jnp.bfloat16), "dp", scatter_dimension=1, tiled=True
        ).astype(jnp.float32),
        lax.psum_scatter(
            expand_grad.astype(jnp.bfloat16), "dp", scatter_dimension=0, tiled=True
        ).astype(jnp.float32),
        lax.psum_scatter(
            shrink_grad.astype(jnp.bfloat16), "dp", scatter_dimension=1, tiled=True
        ).astype(jnp.float32),
        lax.psum_scatter(
            joint_bias_grad.astype(jnp.bfloat16), "dp", scatter_dimension=2, tiled=True
        ).astype(jnp.float32),
        lax.psum_scatter(
            expand_bias_grad.astype(jnp.bfloat16), "dp", scatter_dimension=1, tiled=True
        ).astype(jnp.float32),
        lax.psum_scatter(
            vectors.astype(jnp.bfloat16), "dp", scatter_dimension=1, tiled=True
        ).astype(jnp.float32),
    )
    return (
        block_out,
        tokens_grad,
        vectors[0],
        vectors[1],
        joint_grad,
        joint_bias_grad,
        output_grad,
        vectors[2],
        vectors[3],
        vectors[4],
        expand_grad,
        expand_bias_grad,
        shrink_grad,
        vectors[5],
        clipped_joint,
        clipped_bias,
        factors,
    )


def solution(mesh):
    placed = (
        P(("dp", "tensor"), None),
        P(),
        P(),
        P("dp", None, "tensor"),
        P(None, "tensor", "dp"),
        P("tensor", "dp"),
        P(),
        P(),
        P(),
        P("dp", "tensor"),
        P("tensor", "dp"),
        P("tensor", "dp"),
        P(),
        P(("dp", "tensor"), None),
        P("dp"),
        P("tensor"),
    )
    return jax.shard_map(
        per_device,
        mesh=mesh,
        in_specs=placed,
        out_specs=(
            P(("dp", "tensor"), None),
            P(("dp", "tensor"), None),
            P("dp"),
            P("dp"),
            P("dp", None, "tensor"),
            P(None, "tensor", "dp"),
            P("tensor", "dp"),
            P("dp"),
            P("dp"),
            P("dp"),
            P("dp", "tensor"),
            P("tensor", "dp"),
            P("tensor", "dp"),
            P("dp"),
            P("dp", None, "tensor"),
            P("tensor", "dp"),
            P("tensor"),
        ),
        check_vma=False,
    )
```

profile of v0, /device:TPU:0, one launch (start us, length us, event | category | flops | bytes accessed | tf_op | source)
XLA Modules:
  0.0 1089.4 jit_solution(5886886146818288967)
XLA Ops:
  9.5 28.0 %all-gather.8.cloned.1.call-done = bf16[1024,3,256]{2,0,1:T(8,128)(2,1)} async-done(((bf16[128,3,256]{2,0,1:T(8,128)(2,1)}), bf16[1024,3,256]{2,0,1:T(8,128)(2,1)}) %all-gather.8.cloned.1.call-update) | async-done | bytes 1572880 | tf_op jit(solution)/shard_map/all_gather | solution.py:88
  37.5 15.3 %all_gather.40 = bf16[256,1024]{1,0:T(8,128)(2,1)} all-gather(bf16[256,128]{1,0:T(8,128)(2,1)} %param.25), channel_id=1, replica_groups=mesh['dp'=8,'tensor'=4] {'dp'}, dimensions={1}, use_global_device_ids=true | all-gather | bytes 589824 | tf_op jit(solution)/shard_map/all_gather | solution.py:89
  52.9 16.1 %all-gather.14.cloned.1.call-done = bf16[1024,1024]{1,0:T(8,128)(2,1)} async-done(((bf16[128,1024]{1,0:T(8,128)(2,1)}), bf16[1024,1024]{1,0:T(8,128)(2,1)}) %all-gather.14.cloned.1.call-update) | async-done | bytes 2097168 | tf_op jit(solution)/shard_map/all_gather | solution.py:90
  69.9 12.8 %all_gather.44 = bf16[16,64]{0,1:T(8,128)(2,1)S(1)} all-gather(bf16[16,8]{0,1:T(8,128)(2,1)S(1)} %copy-done.39), channel_id=1, replica_groups=mesh['dp'=8,'tensor'=4] {'dp'}, dimensions={1}, use_global_device_ids=true | all-gather | bytes 2304 | tf_op jit(solution)/shard_map/all_gather | solution.py:93
  82.7 8.1 all_gather.45
  91.6 14.0 %all_gather.38 = bf16[2,4,64]{1,0,2:T(2,128)(2,1)S(1)} all-gather(bf16[2,4,8]{1,0,2:T(2,128)(2,1)S(1)} %copy.79), channel_id=1, replica_groups=mesh['dp'=8,'tensor'=4] {'dp'}, dimensions={2}, use_global_device_ids=true | all-gather | bytes 1152 | tf_op jit(solution)/shard_map/all_gather | solution.py:92
  105.7 8.0 all_gather.39
  115.9 55.4 %all-gather.10.cloned.1.call-done = bf16[1024,3,1024]{2,0,1:T(8,128)(2,1)} async-done(((bf16[1024,3,256]{2,0,1:T(8,128)(2,1)}), bf16[1024,3,1024]{2,0,1:T(8,128)(2,1)}) %all-gather.10.cloned.1.call-update) | async-done | bytes 6291472 | tf_op jit(solution)/shard_map/all_gather | solution.py:104
  171.3 13.0 %add_convert_fusion = bf16[1154,3,1024]{2,0,1:T(8,128)(2,1)} fusion(bf16[1024,3,1024]{2,0,1:T(8,128)(2,1)} %all-gather.10.cloned.1.call-done, f32[3,1024]{1,0:T(4,128)S(1)} %pad_maximum_fusion, bf16[1154,1024]{1,0:T(8,128)(2,1)S(1)} %copy-done.3, f32[1024]{0:T(1024)S(1)} %copy-done.44, f32[1024]{0:T(1024)S(1)} %copy-done.37, f32[1154]{0:T(1024)S(1)} %add_rsqrt_fusion.1, ...), kind=kOutput, calls=%fused_computation.49 | convolution fusion | flops 7274520576 | bytes 15774736 | tf_op jit(solution)/shard_map/rd,dcj->rcj/dot_general | solution.py:119
  184.3 20.3 %reshape.250 = bf16[2,577,3,16,64]{4,3,1,0,2:T(8,128)(2,1)} reshape(bf16[1154,3,1024]{2,0,1:T(8,128)(2,1)} %add_convert_fusion) | data formatting | bytes 14180352 | tf_op jit(solution)/shard_map/reshape | solution.py:122
  204.7 18.6 %copy.82 = bf16[2,577,3,16,64]{1,4,3,2,0:T(8,128)(2,1)} copy(bf16[2,577,3,16,64]{4,3,1,0,2:T(8,128)(2,1)} %reshape.250) | data formatting | bytes 14180352 | tf_op jit(solution)/shard_map/while | solution.py:123
  223.3 71.7 %while.24 = (s32[]{:T(128)}, bf16[2,577,16,64]{1,3,2,0:T(8,128)(2,1)S(1)}, f32[2,16,577,1]{2,1,3,0:T(8,128)S(1)}, f32[2,16]{1,0:T(2,128)S(1)}, bf16[2,577,3,16,64]{1,4,3,2,0:T(8,128)(2,1)}, /*index=5*/s32[]{:T(128)}, s32[]{:T(128)}) while((s32[]{:T(128)}, bf16[2,577,16,64]{1,3,2,0:T(8,128)(2,1)S(1)}, f32[2,16,577,1]{2,1,3,0:T(8,128)S(1)}, ...), condition=%wide.region_6.7_spmd, body=%wide.region_2.6_spmd.sunk | while | flops 1417527296 | bytes 76571296 | solution.py:123
  225.9 10.0 multiply_reduce_fusion.10
  236.0 11.8 %multiply_reduce_fusion.11 = (f32[16]{0:T(128)S(1)}, f32[16,577]{1,0:T(8,128)S(1)}) fusion(f32[16,577,577]{1,2,0:T(8,128)} %get-tuple-element.292, f32[16,577]{1,0:T(8,128)S(1)} %get-tuple-element.293), kind=kLoop, calls=%fused_computation.3.clone.1 | loop fusion | flops 21298208 | bytes 21381376 | tf_op jit(solution)/shard_map/while/body/eval_jaxpr/reduce_max | solution.py:36
  247.8 12.0 %fusion.92 = bf16[2,577,16,64]{1,3,2,0:T(8,128)(2,1)S(1)} fusion(bf16[2,577,16,64]{1,3,2,0:T(8,128)(2,1)S(1)} %get-tuple-element.311, s32[]{:T(128)S(6)} %copy.125, f32[16,577,577]{1,2,0:T(8,128)} %get-tuple-element.292, f32[16,577]{1,0:T(8,128)S(1)} %get-tuple-element.294, f32[16,577]{1,0:T(8,128)S(1)} %get-tuple-element.293, ...), kind=kOutput, calls=%fused_computation.9.clone.1 | convolution fusion | flops 703736896 | bytes 24010820 | tf_op jit(solution)/shard_map/while/body/eval_jaxpr/hqk,khd->qhd/dot_general | solution.py:41
  262.4 10.0 multiply_reduce_fusion.10
  272.4 11.8 %multiply_reduce_fusion.11 = (f32[16]{0:T(128)S(1)}, f32[16,577]{1,0:T(8,128)S(1)}) fusion(f32[16,577,577]{1,2,0:T(8,128)} %get-tuple-element.292, f32[16,577]{1,0:T(8,128)S(1)} %get-tuple-element.293), kind=kLoop, calls=%fused_computation.3.clone.1 | loop fusion | flops 21298208 | bytes 21381376 | tf_op jit(solution)/shard_map/while/body/eval_jaxpr/reduce_max | solution.py:36
  284.3 10.6 fusion.92
  296.5 6.1 copy.83
  302.6 7.0 reshape.224
  309.7 6.2 fusion.63
  318.8 23.7 %multiply_convert_fusion.3 = (bf16[1154,4096]{1,0:T(8,128)(2,1)}, f32[1154,4096]{1,0:T(8,128)}) fusion(f32[4096]{0:T(1024)S(1)} %copy-done.28, bf16[1024,4096]{1,0:T(8,128)(2,1)} %all-gather.16.cloned.1.call-done, f32[1154,1024]{1,0:T(8,128)} %copy-done.6, f32[1024]{0:T(1024)S(1)} %copy-done.46, f32[1024]{0:T(1024)S(1)} %copy-done.33, ...), kind=kOutput, calls=%fused_computation.45 | convolution fusion | flops 9719449600 | bytes 41509904 | tf_op jit(solution)/shard_map/dot_general | solution.py:131
  342.4 44.8 %all-gather.20.cloned.1.call-done = bf16[4096,1024]{1,0:T(8,128)(2,1)} async-done(((bf16[1024,1024]{1,0:T(8,128)(2,1)}), bf16[4096,1024]{1,0:T(8,128)(2,1)}) %all-gather.20.cloned.1.call-update) | async-done | bytes 8388624 | tf_op jit(solution)/shard_map/all_gather | solution.py:107
  387.2 22.4 %fusion.64 = (bf16[4096]{0:T(1024)(128)(2,1)}, bf16[1154,4096]{1,0:T(8,128)(2,1)}) fusion(f32[1154,4096]{1,0:T(8,128)} %get-tuple-element.222, bf16[4096,1024]{1,0:T(8,128)(2,1)} %all-gather.20.cloned.1.call-done, bf16[1154,1024]{1,0:T(8,128)(2,1)S(1)} %copy-done.12, f32[1154]{0:T(1024)S(1)} %copy-done.20), kind=kOutput, calls=%fused_computation.132 | convolution fusion | flops 9735989248 | bytes 39125512 | tf_op jit(solution)/shard_map/rd,fd->rf/dot_general | solution.py:139
  409.6 19.6 %multiply_reduce_fusion.3 = (f32[1024]{0:T(1024)}, f32[1154]{0:T(1024)S(1)}, f32[1154]{0:T(1024)S(1)}, f32[1024]{0:T(1024)}, f32[1154,1024]{1,0:T(8,128)S(1)}) fusion(f32[1154,1024]{1,0:T(8,128)} %copy-done.6, f32[1154]{0:T(1024)S(1)} %add_rsqrt_fusion, f32[1154]{0:T(1024)S(1)} %broadcast_multiply_fusion.4, f32[1024]{0:T(1024)S(1)} %copy-done.33, ...), kind=kOutput, calls=%fused_computation.74 | convolution fusion | flops 9691084800 | bytes 27326496 | tf_op jit(solution)/shard_map/rf,df->rd/dot_general | solution.py:143
  429.2 3.2 convert_reduce_fusion.2
  434.5 4.0 convolution_convert_fusion.4
  439.0 5.7 convolution_convert_fusion.2
  444.8 5.1 reshape.233
  449.8 7.1 copy.87
  456.9 151.4 %while.25 = (s32[]{:T(128)}, bf16[2,577,3,16,64]{1,4,3,2,0:T(8,128)(2,1)}, bf16[2,577,3,16,64]{1,4,3,2,0:T(8,128)(2,1)}, f32[2,16,577,1]{2,1,3,0:T(8,128)S(1)}, bf16[2,577,16,64]{1,3,2,0:T(8,128)(2,1)}, /*index=5*/s32[]{:T(128)}) while((s32[]{:T(128)}, bf16[2,577,3,16,64]{1,4,3,2,0:T(8,128)(2,1)}, bf16[2,577,3,16,64]{1,4,3,2,0:T(8,128)(2,1)}, ...), condition=%wide.region_13.14_spmd, body=%wide.region_11.13_spmd.sunk | while | flops 3486695424 | bytes 264860736 | solution.py:154
  461.4 10.1 fusion.97
  471.5 12.5 %fusion.98 = bf16[1,577,1,16,64]{1,4,3,2,0:T(8,128)(2,1)S(1)} fusion(f32[16,577,577]{1,2,0:T(8,128)} %fusion.97, f32[16,577]{1,0:T(8,128)S(1)} %dynamic-slice_bitcast_fusion.8, bf16[2,577,16,64]{1,3,2,0:T(8,128)(2,1)} %get-tuple-element.340, s32[]{:T(128)S(6)} %copy.135), kind=kOutput, calls=%fused_computation.30.clone.1 | convolution fusion | flops 698410048 | bytes 26449988 | tf_op jit(solution)/shard_map/while/body/eval_jaxpr/hqk,qhd->khd/dot_general | solution.py:54
  483.9 15.8 %multiply_reduce_fusion.12 = (f32[16,577]{1,0:T(8,128)S(1)}, f32[16,577,577]{1,2,0:T(8,128)}) fusion(f32[16,577,577]{1,2,0:T(8,128)} %fusion.97, f32[16,577]{1,0:T(8,128)S(1)} %dynamic-slice_bitcast_fusion.8, bf16[577,3,16,64]{0,3,2,1:T(8,128)(2,1)} %copy-done.1, bf16[2,577,16,64]{1,3,2,0:T(8,128)(2,1)} %get-tuple-element.340, s32[]{:T(128)S(6)} %copy.135), kind=kOutput, calls=%fused_computation.17.clone.1 | convolution fusion | flops 703136768 | bytes 47923396 | tf_op jit(solution)/shard_map/while/body/eval_jaxpr/qhd,khd->hqk/dot_general | solution.py:57
  499.8 16.0 %multiply_convert_fusion.7 = bf16[16,577,577]{1,2,0:T(8,128)(2,1)S(1)} fusion(f32[16,577,577]{1,2,0:T(8,128)} %get-tuple-element.301, f32[16,577,577]{1,2,0:T(8,128)} %fusion.97, f32[16,577]{1,0:T(8,128)S(1)} %get-tuple-element.302, f32[16,577]{1,0:T(8,128)S(1)} %dynamic-slice_bitcast_fusion.8), kind=kLoop, calls=%fused_computation.16.clone.1 | loop fusion | flops 26634320 | bytes 53342496 | tf_op jit(solution)/shard_map/while/body/eval_jaxpr/convert_element_type | solution.py:58
  515.8 4.4 copy-done
  522.5 8.0 fusion.99
  537.1 10.0 fusion.97
  547.1 12.3 %fusion.98 = bf16[1,577,1,16,64]{1,4,3,2,0:T(8,128)(2,1)S(1)} fusion(f32[16,577,577]{1,2,0:T(8,128)} %fusion.97, f32[16,577]{1,0:T(8,128)S(1)} %dynamic-slice_bitcast_fusion.8, bf16[2,577,16,64]{1,3,2,0:T(8,128)(2,1)} %get-tuple-element.340, s32[]{:T(128)S(6)} %copy.135), kind=kOutput, calls=%fused_computation.30.clone.1 | convolution fusion | flops 698410048 | bytes 26449988 | tf_op jit(solution)/shard_map/while/body/eval_jaxpr/hqk,qhd->khd/dot_general | solution.py:54
  559.4 15.8 %multiply_reduce_fusion.12 = (f32[16,577]{1,0:T(8,128)S(1)}, f32[16,577,577]{1,2,0:T(8,128)}) fusion(f32[16,577,577]{1,2,0:T(8,128)} %fusion.97, f32[16,577]{1,0:T(8,128)S(1)} %dynamic-slice_bitcast_fusion.8, bf16[577,3,16,64]{0,3,2,1:T(8,128)(2,1)} %copy-done.1, bf16[2,577,16,64]{1,3,2,0:T(8,128)(2,1)} %get-tuple-element.340, s32[]{:T(128)S(6)} %copy.135), kind=kOutput, calls=%fused_computation.17.clone.1 | convolution fusion | flops 703136768 | bytes 47923396 | tf_op jit(solution)/shard_map/while/body/eval_jaxpr/qhd,khd->hqk/dot_general | solution.py:57
  575.3 16.0 %multiply_convert_fusion.7 = bf16[16,577,577]{1,2,0:T(8,128)(2,1)S(1)} fusion(f32[16,577,577]{1,2,0:T(8,128)} %get-tuple-element.301, f32[16,577,577]{1,2,0:T(8,128)} %fusion.97, f32[16,577]{1,0:T(8,128)S(1)} %get-tuple-element.302, f32[16,577]{1,0:T(8,128)S(1)} %dynamic-slice_bitcast_fusion.8), kind=kLoop, calls=%fused_computation.16.clone.1 | loop fusion | flops 26634320 | bytes 53342496 | tf_op jit(solution)/shard_map/while/body/eval_jaxpr/convert_element_type | solution.py:58
  591.3 4.4 copy-done
  598.0 8.0 fusion.99
  608.4 15.6 %copy.88 = bf16[2,577,3,16,64]{1,0,4,3,2:T(2,128)(2,1)} copy(bf16[2,577,3,16,64]{1,4,3,2,0:T(8,128)(2,1)} %get-tuple-element.75) | data formatting | bytes 14180352 | tf_op jit(solution)/shard_map/while | solution.py:154
  624.1 16.7 %reshape.226 = bf16[1154,3,1024]{0,2,1:T(8,128)(2,1)} reshape(bf16[2,577,3,16,64]{1,0,4,3,2:T(2,128)(2,1)} %copy.88) | data formatting | bytes 14180352 | tf_op jit(solution)/shard_map/reshape | solution.py:155
  640.8 15.1 %convolution_convert_fusion.3 = bf16[1024,3,1024]{2,0,1:T(8,128)(2,1)} fusion(bf16[1154,3,1024]{0,2,1:T(8,128)(2,1)} %reshape.226, bf16[1154,1024]{1,0:T(8,128)(2,1)S(1)} %copy-done.5, f32[1024]{0:T(1024)S(1)} %copy-done.45, f32[1024]{0:T(1024)S(1)} %copy-done.38, f32[1154]{0:T(1024)S(1)} %copy-done.23, f32[1154]{0:T(1024)S(1)} %copy-done.17), kind=kOutput, calls=%fused_computation.87 | convolution fusion | flops 7270576128 | bytes 15762448 | tf_op jit(solution)/shard_map/rd,rcj->dcj/dot_general | solution.py:156
  656.6 16.7 %convolution_convert_fusion.1 = bf16[4096,1024]{1,0:T(8,128)(2,1)} fusion(bf16[1154,4096]{1,0:T(8,128)(2,1)} %get-tuple-element.221, bf16[1154,1024]{1,0:T(8,128)(2,1)} %param.33, f32[1154]{0:T(1024)S(1)} %copy-done.21), kind=kOutput, calls=%fused_computation.51 | convolution fusion | flops 9688193024 | bytes 20210184 | tf_op jit(solution)/shard_map/rf,rd->fd/dot_general | solution.py:138
  674.1 18.9 %convolution_convert_fusion = bf16[1024,4096]{1,0:T(8,128)(2,1)} fusion(bf16[1154,4096]{1,0:T(8,128)(2,1)} %get-tuple-element.226, f32[1154,1024]{1,0:T(8,128)} %copy-done.6, f32[1024]{0:T(1024)S(1)} %copy-done.47, f32[1024]{0:T(1024)S(1)} %copy-done.34, f32[1154]{0:T(1024)S(1)} %copy-done.25, f32[1154]{0:T(1024)S(1)} %copy-done.19), kind=kOutput, calls=%fused_computation.50 | convolution fusion | flops 9690556416 | bytes 22586384 | tf_op jit(solution)/shard_map/rd,rf->df/dot_general | solution.py:142
  693.1 16.2 %fusion.43 = (f32[1024]{0:T(1024)S(1)}, f32[1154]{0:T(1024)S(1)}, f32[1154]{0:T(1024)S(1)}, f32[1024]{0:T(1024)S(1)}, f32[1154,1024,1]{1,0,2:T(8,128)}) fusion(bf16[1154,1024]{1,0:T(8,128)(2,1)S(1)} %copy-done.5, f32[1154]{0:T(1024)S(1)} %copy-done.23, f32[1154]{0:T(1024)S(1)} %copy-done.17, f32[1024]{0:T(1024)S(1)} %copy-done.38, ...), kind=kOutput, calls=%fused_computation.68 | convolution fusion | flops 7272153088 | bytes 20502560 | tf_op jit(solution)/shard_map/rcj,dcj->rd/dot_general | solution.py:161
  709.3 16.4 %psum.7 = bf16[6,1024]{1,0:T(8,128)(2,1)S(1)} all-reduce(f32[6,1024]{1,0:T(8,128)S(1)} %stack.46), channel_id=1, replica_groups=mesh['dp'=8,'tensor'=4] {'tensor'}, use_global_device_ids=true, to_apply=%region_22.23 | all-reduce | flops 6144 | bytes 36864 | tf_op jit(solution)/shard_map/psum | solution.py:209
  729.5 87.6 %reduce-scatter.29.cloned.1.call-done = bf16[1024,1024]{1,0:T(8,128)(2,1)} async-done(((bf16[4096,1024]{1,0:T(8,128)(2,1)}), bf16[1024,1024]{1,0:T(8,128)(2,1)}) %reduce-scatter.29.cloned.1.call-update) | async-done | bytes 2097168 | tf_op jit(solution)/shard_map/reduce_scatter | solution.py:174
  817.1 4.2 copy.111
  824.7 39.9 %pmax.7 = f32[16]{0:T(128)S(1)} all-reduce(f32[16]{0:T(128)S(1)} %select_reduce_fusion), channel_id=1, replica_groups=mesh['dp'=8,'tensor'=4] {'dp','tensor'}, use_global_device_ids=true, to_apply=%region_39.40 | all-reduce | flops 16 | bytes 128 | tf_op jit(solution)/shard_map/pmax | solution.py:191
  866.3 4.5 reduce.2
  870.9 17.1 %all-reduce.5 = (bf16[2,16,64]{2,1,0:T(8,128)(2,1)S(1)}, bf16[64,64]{1,0:T(8,128)(2,1)S(1)}) all-reduce(bf16[2,16,64]{2,1,0:T(8,128)(2,1)S(1)} %pad_maximum_fusion.1, bf16[64,64]{1,0:T(8,128)(2,1)S(1)} %convert_element_type.201), channel_id=5, replica_groups=mesh['dp'=8,'tensor'=4] {'tensor'}, use_global_device_ids=true, to_apply=%region_27.28.clone | all-reduce | flops 6144 | bytes 24576
  888.0 13.9 %all-reduce.4 = (bf16[2,4,64]{2,1,0:T(4,128)(2,1)S(1)}, bf16[16,64]{1,0:T(8,128)(2,1)S(1)}) all-reduce(bf16[2,4,64]{2,1,0:T(4,128)(2,1)S(1)} %constant_dynamic-slice_fusion.1, bf16[16,64]{1,0:T(8,128)(2,1)S(1)} %constant_dynamic-slice_fusion), channel_id=6, replica_groups=mesh['dp'=8,'tensor'=4] {'dp'}, use_global_device_ids=true, to_apply=%region_28.29.clone | all-reduce | flops 1536 | bytes 6144
  903.4 4.8 reduce-scatter.25.cloned.1.call-done
  908.2 5.7 fusion.42
  914.0 16.8 %multiply_convert_fusion.4 = bf16[1154,1024]{1,0:T(8,128)(2,1)} fusion(f32[1154,1024]{1,0:T(8,128)} %copy-done.6, bf16[1154,4096]{1,0:T(8,128)(2,1)} %get-tuple-element.221, bf16[4096,1024]{1,0:T(8,128)(2,1)} %all-gather.20.cloned.1.call-done, f32[1024]{0:T(1024)S(1)} %copy-done.48, f32[1154]{0:T(1024)S(1)} %copy-done.21), kind=kOutput, calls=%fused_computation.80 | convolution fusion | flops 9685180416 | bytes 24941064 | tf_op jit(solution)/shard_map/dot_general | solution.py:136
  930.8 10.5 reduce-scatter.31.cloned.1.call-done
  942.7 30.6 %reduce-scatter.33.cloned.1.call-done = bf16[128,256]{1,0:T(8,128)(2,1)} async-done(((bf16[1024,256]{1,0:T(8,128)(2,1)}), bf16[128,256]{1,0:T(8,128)(2,1)}) %reduce-scatter.33.cloned.1.call-update) | async-done | bytes 65552
  974.9 33.1 %reduce-scatter.21.cloned.1.call-done = bf16[128,3,256]{2,0,1:T(8,128)(2,1)} async-done(((bf16[1024,3,256]{2,0,1:T(8,128)(2,1)}), bf16[128,3,256]{2,0,1:T(8,128)(2,1)}) %reduce-scatter.21.cloned.1.call-update) | async-done | bytes 196624 | tf_op jit(solution)/shard_map/reduce_scatter | solution.py:219
  1009.7 34.2 %reduce-scatter.35.cloned.1.call-done = bf16[128,1024]{1,0:T(8,128)(2,1)} async-done(((bf16[1024,1024]{1,0:T(8,128)(2,1)}), bf16[128,1024]{1,0:T(8,128)(2,1)}) %reduce-scatter.35.cloned.1.call-update) | async-done | bytes 262160
  1045.9 34.8 %reduce-scatter.27.cloned.1.call-done = bf16[128,1024]{1,0:T(8,128)(2,1)} async-done(((bf16[1024,1024]{1,0:T(8,128)(2,1)}), bf16[128,1024]{1,0:T(8,128)(2,1)}) %reduce-scatter.27.cloned.1.call-update) | async-done | bytes 262160 | tf_op jit(solution)/shard_map/reduce_scatter | solution.py:225
  (211 shorter events, 53.6 us)
Async XLA Ops:
  7.2 62.6 %copy-start.30 = (bf16[2,4,8]{2,1,0:T(4,128)(2,1)S(1)}, bf16[2,4,8]{2,1,0:T(4,128)(2,1)}, u32[]{:S(2)}) copy-start(bf16[2,4,8]{2,1,0:T(4,128)(2,1)} %param.24) | copy-start | bytes 388
  7.2 62.7 %copy-start.39 = (bf16[16,8]{0,1:T(8,128)(2,1)S(1)}, bf16[16,8]{0,1:T(8,128)(2,1)}, u32[]{:S(2)}) copy-start(bf16[16,8]{0,1:T(8,128)(2,1)} %param.30) | copy-start | bytes 772
  7.2 107.4 %copy-start.3 = (bf16[1154,1024]{1,0:T(8,128)(2,1)S(1)}, bf16[1154,1024]{1,0:T(8,128)(2,1)}, u32[]{:S(2)}) copy-start(bf16[1154,1024]{1,0:T(8,128)(2,1)} %param.20) | copy-start | bytes 7090180
  7.2 30.2 %all-gather.8.cloned.1.call-start = ((), (), s32[]{:S(2)}) async-start(), calls=%async_computation.9 | async-start | bytes 1769472 | tf_op jit(solution)/shard_map/all_gather | solution.py:88
  8.0 61.0 %all-gather.14.cloned.1.call-start = ((), (), s32[]{:S(2)}) async-start(), calls=%async_computation.12 | async-start | bytes 2359296 | tf_op jit(solution)/shard_map/all_gather | solution.py:90
  8.7 107.2 %all-gather.18.cloned.1.call-start = ((), (), s32[]{:S(2)}) async-start(), calls=%async_computation.14 | async-start | bytes 2359296 | tf_op jit(solution)/shard_map/all_gather | solution.py:91
  9.4 161.8 %all-gather.10.cloned.1.call-start = ((), (), s32[]{:S(2)}) async-start(), calls=%async_computation.10 | async-start | bytes 7864320 | tf_op jit(solution)/shard_map/all_gather | solution.py:104
  37.5 272.2 %all-gather.12.cloned.1.call-start = ((), (), s32[]{:S(2)}) async-start(), calls=%async_computation.11 | async-start | bytes 2621440 | tf_op jit(solution)/shard_map/all_gather | solution.py:105
  52.8 118.5 %copy-start.37 = (f32[1024]{0:T(1024)S(1)}, f32[1024]{0:T(1024)}, u32[]{:S(2)}) copy-start(f32[1024]{0:T(1024)} %param.21) | copy-start | bytes 12292
  52.8 118.5 %copy-start.44 = (f32[1024]{0:T(1024)S(1)}, f32[1024]{0:T(1024)}, u32[]{:S(2)}) copy-start(f32[1024]{0:T(1024)} %param.22) | copy-start | bytes 12292
  52.8 265.9 %all-gather.16.cloned.1.call-start = ((), (), s32[]{:S(2)}) async-start(), calls=%async_computation.13 | async-start | bytes 10485760 | tf_op jit(solution)/shard_map/all_gather | solution.py:106
  69.0 318.2 %all-gather.20.cloned.1.call-start = ((), (), s32[]{:S(2)}) async-start(), calls=%async_computation.15 | async-start | bytes 10485760 | tf_op jit(solution)/shard_map/all_gather | solution.py:107
  115.0 69.3 %copy-start.16 = (f32[1154]{0:T(1024)}, f32[1154]{0:T(1024)S(1)}, u32[]{:S(2)}) copy-start(f32[1154]{0:T(1024)S(1)} %broadcast_multiply_fusion.5) | copy-start | bytes 13852
  115.8 68.5 %copy-start.22 = (f32[1154]{0:T(1024)}, f32[1154]{0:T(1024)S(1)}, u32[]{:S(2)}) copy-start(f32[1154]{0:T(1024)S(1)} %add_rsqrt_fusion.1) | copy-start | bytes 13852
  115.9 610.9 %reduce-scatter.23.cloned.1.call-start = ((), (), s32[]{:S(2)}) async-start(), calls=%async_computation.18 | async-start | bytes 2621440 | tf_op jit(solution)/shard_map/reduce_scatter | solution.py:168
  204.7 18.6 %copy-start.9 = (bf16[2,577,16,64]{1,3,2,0:T(8,128)(2,1)S(1)}, bf16[2,577,16,64]{1,3,2,0:T(8,128)(2,1)}, u32[]{:S(2)}) copy-start(bf16[2,577,16,64]{1,3,2,0:T(8,128)(2,1)} %custom-call) | copy-start | bytes 7090180
  296.5 13.1 %copy-start.14 = (f32[2,16,577,1]{2,1,3,0:T(8,128)}, f32[2,16,577,1]{2,1,3,0:T(8,128)S(1)}, u32[]{:S(2)}) copy-start(f32[2,16,577,1]{2,1,3,0:T(8,128)S(1)} %get-tuple-element.327) | copy-start | bytes 221572
  296.5 13.1 %copy-start.40 = (f32[2,16]{1,0:T(2,128)}, f32[2,16]{1,0:T(2,128)S(1)}, u32[]{:S(2)}) copy-start(f32[2,16]{1,0:T(2,128)S(1)} %get-tuple-element.76) | copy-start | bytes 388
  296.5 13.2 %copy-start.4 = (bf16[1154,1024]{1,0:T(8,128)(2,1)S(1)}, bf16[1154,1024]{1,0:T(8,128)(2,1)}, u32[]{:S(2)}) copy-start(bf16[1154,1024]{1,0:T(8,128)(2,1)} %param.20) | copy-start | bytes 7090180
  296.5 13.2 %copy-start.43 = (f32[1024]{0:T(1024)S(1)}, f32[1024]{0:T(1024)}, u32[]{:S(2)}) copy-start(f32[1024]{0:T(1024)} %param.26) | copy-start | bytes 12292
  315.9 2.2 copy-start.6
  315.9 2.9 copy-start.28
  315.9 2.9 copy-start.33
  315.9 2.9 copy-start.46
  315.9 113.3 %copy-start.18 = (f32[1154]{0:T(1024)}, f32[1154]{0:T(1024)S(1)}, u32[]{:S(2)}) copy-start(f32[1154]{0:T(1024)S(1)} %broadcast_multiply_fusion.4) | copy-start | bytes 13852
  318.7 110.5 %copy-start.24 = (f32[1154]{0:T(1024)}, f32[1154]{0:T(1024)S(1)}, u32[]{:S(2)}) copy-start(f32[1154]{0:T(1024)S(1)} %add_rsqrt_fusion) | copy-start | bytes 13852
  318.7 68.5 %copy-start.12 = (bf16[1154,1024]{1,0:T(8,128)(2,1)S(1)}, bf16[1154,1024]{1,0:T(8,128)(2,1)}, u32[]{:S(2)}) copy-start(bf16[1154,1024]{1,0:T(8,128)(2,1)} %param.33) | copy-start | bytes 7090180
  318.7 68.5 %copy-start.20 = (f32[1154]{0:T(1024)S(1)}, f32[1154]{0:T(1024)}, u32[]{:S(2)}) copy-start(f32[1154]{0:T(1024)} %fusion.54) | copy-start | bytes 13852
  409.6 19.6 %copy-start.7 = (f32[1154,1024]{1,0:T(8,128)S(1)}, f32[1154,1024]{1,0:T(8,128)}, u32[]{:S(2)}) copy-start(f32[1154,1024]{1,0:T(8,128)} %copy-done.6) | copy-start | bytes 14180356
  429.2 5.3 copy-start.11
  432.4 2.1 copy-start.8
  438.6 290.4 %reduce-scatter.19.cloned.1.call-start = ((), (), s32[]{:S(2)}) async-start(), calls=%async_computation.16 | async-start | bytes 7864320 | tf_op jit(solution)/shard_map/reduce_scatter | solution.py:165
  449.8 7.1 copy-start.15
  459.5 1.9 copy-start.1
  499.8 20.4 %copy-start.2 = (bf16[577,3,16,64]{0,3,2,1:T(8,128)(2,1)S(1)}, bf16[577,3,16,64]{0,3,2,1:T(8,128)(2,1)}, u32[]{:S(2)}) copy-start(bf16[577,3,16,64]{0,3,2,1:T(8,128)(2,1)} %copy-done.1) | copy-start | bytes 10635268 | tf_op jit(solution)/shard_map/while
  515.8 4.4 copy-start
  535.1 1.9 copy-start.1
  575.3 20.4 %copy-start.2 = (bf16[577,3,16,64]{0,3,2,1:T(8,128)(2,1)S(1)}, bf16[577,3,16,64]{0,3,2,1:T(8,128)(2,1)}, u32[]{:S(2)}) copy-start(bf16[577,3,16,64]{0,3,2,1:T(8,128)(2,1)} %copy-done.1) | copy-start | bytes 10635268 | tf_op jit(solution)/shard_map/while
  591.3 4.4 copy-start
  624.0 16.7 %copy-start.5 = (bf16[1154,1024]{1,0:T(8,128)(2,1)S(1)}, bf16[1154,1024]{1,0:T(8,128)(2,1)}, u32[]{:S(2)}) copy-start(bf16[1154,1024]{1,0:T(8,128)(2,1)} %param.20) | copy-start | bytes 7090180
  624.0 16.7 %copy-start.17 = (f32[1154]{0:T(1024)S(1)}, f32[1154]{0:T(1024)}, u32[]{:S(2)}) copy-start(f32[1154]{0:T(1024)} %copy-done.16) | copy-start | bytes 13852
  624.0 16.7 %copy-start.23 = (f32[1154]{0:T(1024)S(1)}, f32[1154]{0:T(1024)}, u32[]{:S(2)}) copy-start(f32[1154]{0:T(1024)} %copy-done.22) | copy-start | bytes 13852
  624.0 16.7 %copy-start.38 = (f32[1024]{0:T(1024)S(1)}, f32[1024]{0:T(1024)}, u32[]{:S(2)}) copy-start(f32[1024]{0:T(1024)} %param.21) | copy-start | bytes 12292
  624.1 16.7 %copy-start.45 = (f32[1024]{0:T(1024)S(1)}, f32[1024]{0:T(1024)}, u32[]{:S(2)}) copy-start(f32[1024]{0:T(1024)} %param.22) | copy-start | bytes 12292
  655.9 161.2 %reduce-scatter.29.cloned.1.call-start = ((), (), s32[]{:S(2)}) async-start(), calls=%async_computation.21 | async-start | bytes 10485760 | tf_op jit(solution)/shard_map/reduce_scatter | solution.py:174
  673.4 234.8 %reduce-scatter.25.cloned.1.call-start = ((), (), s32[]{:S(2)}) async-start(), calls=%async_computation.19 | async-start | bytes 10485760 | tf_op jit(solution)/shard_map/reduce_scatter | solution.py:171
  693.0 16.3 %copy-start.26 = (f32[1024]{0:T(1024)S(1)}, f32[1024]{0:T(1024)}, u32[]{:S(2)}) copy-start(f32[1024]{0:T(1024)} %get-tuple-element.204) | copy-start | bytes 12292
  693.0 16.2 %copy-start.27 = (f32[1024]{0:T(1024)S(1)}, f32[1024]{0:T(1024)}, u32[]{:S(2)}) copy-start(f32[1024]{0:T(1024)} %get-tuple-element.210) | copy-start | bytes 12292
  693.0 16.2 %copy-start.35 = (f32[1024]{0:T(1024)S(1)}, f32[1024]{0:T(1024)}, u32[]{:S(2)}) copy-start(f32[1024]{0:T(1024)} %get-tuple-element.170) | copy-start | bytes 12292
  693.0 16.2 %copy-start.36 = (f32[1024]{0:T(1024)S(1)}, f32[1024]{0:T(1024)}, u32[]{:S(2)}) copy-start(f32[1024]{0:T(1024)} %get-tuple-element.176) | copy-start | bytes 12292
  693.0 248.3 %reduce-scatter.31.cloned.1.call-start = ((), (), s32[]{:S(2)}) async-start(), calls=%async_computation.22 | async-start | bytes 294912
  726.6 94.8 %copy-start.13 = (bf16[128,3,256]{2,0,1:T(8,128)(2,1)S(1)}, bf16[128,3,256]{2,0,1:T(8,128)(2,1)}, u32[]{:S(2)}) copy-start(bf16[128,3,256]{2,0,1:T(8,128)(2,1)} %param.23) | copy-start | bytes 589828
  726.6 94.8 %copy-start.50 = (u32[32]{0:T(128)S(1)}, u32[32]{0:T(128)}, u32[]{:S(2)}) copy-start(u32[32]{0:T(128)} %constant.99) | copy-start | bytes 388
  726.6 95.4 %copy-start.49 = (u32[32]{0:T(128)S(1)}, u32[32]{0:T(128)}, u32[]{:S(2)}) copy-start(u32[32]{0:T(128)} %constant.95) | copy-start | bytes 388
  726.6 97.3 %copy-start.41 = (f32[2,16]{1,0:T(2,128)S(1)}, f32[2,16]{1,0:T(2,128)}, u32[]{:S(2)}) copy-start(f32[2,16]{1,0:T(2,128)} %copy-done.40) | copy-start | bytes 388
  726.7 137.9 %copy-start.42 = (f32[4]{0:T(128)S(1)}, f32[4]{0:T(128)}, u32[]{:S(2)}) copy-start(f32[4]{0:T(128)} %param.35) | copy-start | bytes 52
  726.7 138.1 %copy-start.31 = (bf16[2,4,8]{2,1,0:T(4,128)(2,1)S(1)}, bf16[2,4,8]{2,1,0:T(4,128)(2,1)}, u32[]{:S(2)}) copy-start(bf16[2,4,8]{2,1,0:T(4,128)(2,1)} %param.24) | copy-start | bytes 388
  726.7 246.6 %reduce-scatter.33.cloned.1.call-start = ((), (), s32[]{:S(2)}) async-start(), calls=%async_computation.23 | async-start | bytes 589824
  728.9 137.4 %copy-start.29 = (bf16[4096]{0:T(1024)(128)(2,1)S(1)}, bf16[4096]{0:T(1024)(128)(2,1)}, u32[]{:S(2)}) copy-start(bf16[4096]{0:T(1024)(128)(2,1)} %get-tuple-element.225) | copy-start | bytes 24580
  728.9 279.1 %reduce-scatter.21.cloned.1.call-start = ((), (), s32[]{:S(2)}) async-start(), calls=%async_computation.17 | async-start | bytes 1769472 | tf_op jit(solution)/shard_map/reduce_scatter | solution.py:219
  729.5 314.4 %reduce-scatter.35.cloned.1.call-start = ((), (), s32[]{:S(2)}) async-start(), calls=%async_computation.24 | async-start | bytes 2359296
  821.3 259.3 %reduce-scatter.27.cloned.1.call-start = ((), (), s32[]{:S(2)}) async-start(), calls=%async_computation.20 | async-start | bytes 2359296 | tf_op jit(solution)/shard_map/reduce_scatter | solution.py:225
  864.7 43.6 %copy-start.32 = (f32[4]{0:T(128)}, f32[4]{0:T(128)S(1)}, u32[]{:S(2)}) copy-start(f32[4]{0:T(128)S(1)} %fusion.57) | copy-start | bytes 52
  908.2 5.8 copy-start.48
  (6 other events, 5.1 us)
Sparse Core Ops, SparseCore 0:
  9.7 27.7 all-gather.7
  39.0 29.8 all-gather.13
  70.6 29.9 all-gather.17
  102.3 68.9 all-gather.9
  173.0 35.3 all-gather.11
  210.0 87.5 all-gather.15
  299.5 87.5 all-gather.19
  438.7 35.1 reduce-scatter.22
  656.0 71.3 reduce-scatter.18
  730.6 86.4 reduce-scatter.28
  820.2 87.9 reduce-scatter.24
  911.0 30.3 reduce-scatter.30
  944.2 29.0 reduce-scatter.32
  975.6 32.3 reduce-scatter.20
  1010.2 33.6 reduce-scatter.34
  1046.2 34.4 reduce-scatter.26
where the time goes:
time: 1100 us; the launch traced here: 1090 us
  waiting for transfers between devices  383 us (35%)
  matrix products  318 us (29%)
  blocking collectives  146 us (13%)
  local copies, waits for them, and re-layouts  140 us (13%)
  other arithmetic  83.5 us (8%)
  between operations  17.7 us (2%)
    reduce_scatter x1, waiting for transfers between devices, per_device(): lax.psum_scatter(shrink_grad.astype(jnp.bfloat16), 'tensor', scatter_dime...  87.6 us
    unnamed x19, waiting for transfers between devices  78.1 us
    all_gather x1, waiting for transfers between devices, per_device(): lax.all_gather(joint_full, 'tensor', axis=2, tiled=True)  55.4 us
    all_gather x1, waiting for transfers between devices, per_device(): lax.all_gather(shrink_full, 'tensor', axis=0, tiled=True)  44.8 us
    pmax x1, blocking collectives, per_device(): top_all = lax.pmax(peak_all, ('dp', 'tensor'))  39.9 us
    reduce_scatter x1, waiting for transfers between devices, per_device(): lax.psum_scatter(expand_grad.astype(jnp.bfloat16), 'dp', scatter_dimensio...  34.8 us
    reduce_scatter x1, waiting for transfers between devices, per_device(): lax.psum_scatter(joint_grad.astype(jnp.bfloat16), 'dp', scatter_dimension...  33.1 us
    convert_element_type x2, other arithmetic, attend_back(): (probs * (dprobs - jnp.sum(probs * dprobs, axis=-1, keepdims=True))).asty...  32 us
  transfers between devices with their start and end apart: 16, of which 11 were waited for; matrix products, arithmetic and copies ran while one was open for 43% of the time, Pallas kernels for 0%

commit v1 on v0

v1 whole, which is shorter than its diff:
```python
from functools import partial

import jax
import jax.numpy as jnp
from jax import lax
from jax.experimental import pallas as pl
from jax.experimental.pallas import tpu as pltpu
from jax.sharding import PartitionSpec as P

D = 1024
FF = 4096
HEADS = 16
HEAD_DIM = 64
SEQ = 577
SP = 592
LP = 640
LOG2E = 1.4426950408889634
NEG = -1e30
BF = jnp.bfloat16
F32 = jnp.float32
AXES = ("dp", "tensor")
VMEM_LIMIT = 60 * 2**20


def dotf(a, b, ca, cb):
    return lax.dot_general(a, b, (((ca,), (cb,)), ((), ())), preferred_element_type=F32)


def params():
    return pltpu.CompilerParams(vmem_limit_bytes=VMEM_LIMIT)


def cost(flops, nbytes, trans=0):
    return pl.CostEstimate(flops=int(flops), bytes_accessed=int(nbytes), transcendentals=int(trans))


def whole(shape):
    zeros = (0,) * len(shape)
    return pl.BlockSpec(shape, lambda *_: zeros)


class Layout:
    def __init__(self, ndp, nt):
        self.ndp, self.nt, self.nz = ndp, nt, ndp // 2
        self.size = ndp * nt
        self.rows = D // ndp
        self.cols = FF // nt
        self.tbits = nt.bit_length() - 1
        self.zbits = self.nz.bit_length() - 1
        self.core = nt
        self.cw = D // nt

    def mask(self, bit):
        kind, b = bit
        return (1 << b) if kind == "t" else (self.nt * 2) << b

    def order(self, half):
        z = [("z", b) for b in reversed(range(self.zbits))]
        t = [("t", b) for b in range(self.tbits)]
        if half == 1:
            t = t[::-1]
        out = []
        while z or t:
            if z and len(z) >= len(t):
                out.append(z.pop(0))
            else:
                out.append(t.pop(0))
        return out


def swap(x, mask, size):
    return lax.ppermute(x, AXES, [(i, i ^ mask) for i in range(size)])


def gather_half(lay, piece, half):
    held = [(piece[None], [(0, 0, 0)])]
    for bit in lay.order(half):
        if len(held) == 4:
            held = [(jnp.concatenate([b for b, _ in held]), [o for _, os in held for o in os])]
        kind, b = bit
        more = []
        for buf, offs in held:
            got = swap(buf, lay.mask(bit), lay.size)
            if kind == "z":
                new = [(z ^ (1 << b), t, c) for z, t, c in offs]
            else:
                new = [(z, t ^ (1 << b), c) for z, t, c in offs]
            more.append((got, new))
        held = held + more
    more = []
    for buf, offs in held:
        more.append((swap(buf, lay.core, lay.size), [(z, t, 1) for z, t, _ in offs]))
    return held + more


def gather_group(lay, piece_a, piece_b):
    return gather_half(lay, piece_a, 0), gather_half(lay, piece_b, 1)


def group_refs(group):
    return [buf for half in group for buf, _ in half]


def piece_list(group):
    out = []
    n = 0
    for h, half in enumerate(group):
        for _, offs in half:
            for i, (z, t, c) in enumerate(offs):
                out.append((h, n, i, z, t, c))
            n += 1
    return out


def start_pieces(lay, pieces, bufs, me, spans, dst, sem):
    for h, n, i, z, t, c in pieces:
        row = ((z ^ me[0]) * 2 + (c ^ me[1])) * lay.rows
        row = pl.multiple_of(row, lay.rows)
        ref, base = dst(t, t ^ me[2])
        for first, width, at in spans[h]:
            if isinstance(base, int):
                where = pl.ds(base + at, width)
            else:
                where = pl.ds(pl.multiple_of(base + at, 128), width)
            pltpu.make_async_copy(
                bufs[n].at[i, pl.ds(0, lay.rows), pl.ds(first, width)],
                ref.at[pl.ds(row, lay.rows), where],
                sem(t),
            ).start()


def wait_all(ref, sem):
    pltpu.make_async_copy(ref, ref, sem).wait()


ANY = pl.BlockSpec(memory_space=pl.ANY)


def project(lay, me, group, normed, bias_rows):
    rows = normed.shape[0]
    bufs = group_refs(group)
    pieces = piece_list(group)
    cw = lay.cw
    half = lay.cols // 2
    spans = ([(0, 2 * cw, 0)], [(0, cw, 2 * cw)])

    def kernel(me_ref, *refs):
        src = refs[: len(bufs)]
        x_ref, b_ref, o_ref, w, sem = refs[len(bufs) :]
        o = pl.program_id(0)
        idx = (me_ref[0], me_ref[1], me_ref[2])

        @pl.when(o == 0)
        def _():
            start_pieces(lay, pieces, src, idx, spans, lambda to, t: (w.at[to], 0), lambda to: sem.at[to])

        wait_all(w.at[o], sem.at[o])
        y = jnp.dot(x_ref[...], w[o], preferred_element_type=F32) + b_ref[...]
        o_ref[:, :cw] = (y[:, :cw] * HEAD_DIM**-0.5).astype(BF)
        o_ref[:, cw:] = y[:, cw:].astype(BF)

    return pl.pallas_call(
        kernel,
        grid_spec=pltpu.PrefetchScalarGridSpec(
            num_scalar_prefetch=1,
            grid=(lay.nt,),
            in_specs=[ANY] * len(bufs)
            + [
                pl.BlockSpec((rows, D), lambda o, m: (0, 0)),
                pl.BlockSpec((1, 3 * cw), lambda o, m: (0, o ^ m[2])),
            ],
            out_specs=pl.BlockSpec((rows, 3 * cw), lambda o, m: (0, o ^ m[2])),
            scratch_shapes=[
                pltpu.VMEM((lay.nt, D, 3 * cw), BF),
                pltpu.SemaphoreType.DMA((lay.nt,)),
            ],
        ),
        out_shape=jax.ShapeDtypeStruct((rows, 3 * D), BF),
        compiler_params=params(),
        cost_estimate=cost(2 * rows * D * 3 * D, 16e6),
        name="project",
    )(me, *bufs, normed, bias_rows)


def flip(x):
    pad = jnp.zeros((LP - x.shape[0], x.shape[1]), x.dtype)
    return jnp.concatenate([x, pad], axis=0).T


def key_rows():
    row = lax.broadcasted_iota(jnp.int32, (16, LP), 0)
    lane = lax.broadcasted_iota(jnp.int32, (16, LP), 1)
    return jnp.where(row < 3, 1.0, jnp.where((row == 3) & (lane >= SEQ), NEG, 0.0)).astype(BF)


def split_rows(v):
    row = lax.broadcasted_iota(jnp.int32, (16, LP), 0)
    hi = v.astype(BF).astype(F32)
    mid = (v - hi).astype(BF).astype(F32)
    lo = v - hi - mid
    rest = jnp.where(row == 2, lo, jnp.where(row == 3, 1.0, 0.0))
    return jnp.where(row == 0, hi, jnp.where(row == 1, mid, rest)).astype(BF)


def split_query(q):
    v = q.astype(F32) * LOG2E
    hi = v.astype(BF)
    return hi, (v - hi.astype(F32)).astype(BF)


def attend_kernel(hl, p_ref, o_ref, lse_ref, top_ref):
    cw = hl * HEAD_DIM
    xt = flip(p_ref[...])
    aux = key_rows()
    none = split_rows(jnp.zeros((1, LP), F32))
    first = lax.broadcasted_iota(jnp.int32, (16, LP), 0) == 0
    ones = jnp.where(first, 1.0, 0.0).astype(BF)
    valid = lax.broadcasted_iota(jnp.int32, (1, LP), 1) < SEQ
    outs = []
    for h in range(hl):
        q = xt[h * HEAD_DIM : (h + 1) * HEAD_DIM]
        k = xt[cw + h * HEAD_DIM : cw + (h + 1) * HEAD_DIM]
        v = xt[2 * cw + h * HEAD_DIM : 2 * cw + (h + 1) * HEAD_DIM]
        hi, lo = split_query(q)
        s = dotf(jnp.concatenate([k, k, aux], 0), jnp.concatenate([hi, lo, none], 0), 0, 0)
        m = jnp.max(s, axis=0, keepdims=True)
        p = jnp.exp2(s - m).astype(BF)
        o = dotf(jnp.concatenate([v, ones], 0), p, 1, 0)
        total = o[HEAD_DIM : HEAD_DIM + 1]
        outs.append((o[:HEAD_DIM] / total).astype(BF))
        lse_ref[0, 0, h : h + 1, :] = m + jnp.log2(total)
        top_ref[0, 0, h : h + 1, :] = jnp.where(valid, m, NEG)
    o_ref[...] = jnp.concatenate(outs, 0).T[:SP]


def attend(lay, packed):
    rows = packed.shape[0]
    own = rows // SP
    cw = lay.cw
    hl = cw // HEAD_DIM
    stat = pl.BlockSpec((1, 1, hl, LP), lambda i, t: (i, t, 0, 0))
    stat_shape = jax.ShapeDtypeStruct((own, lay.nt, hl, LP), F32)
    return pl.pallas_call(
        partial(attend_kernel, hl),
        grid=(own, lay.nt),
        in_specs=[pl.BlockSpec((SP, 3 * cw), lambda i, t: (i, t))],
        out_specs=[pl.BlockSpec((SP, cw), lambda i, t: (i, t)), stat, stat],
        out_shape=[jax.ShapeDtypeStruct((rows, D), BF), stat_shape, stat_shape],
        compiler_params=params(),
        cost_estimate=cost(22e9, 10e6),
        name="attend",
    )(packed)


def attend_back_kernel(hl, p_ref, o_ref, g_ref, lse_ref, d_ref, sum_ref):
    cw = hl * HEAD_DIM
    xt = flip(p_ref[...])
    ot = flip(o_ref[...])
    gt = flip(g_ref[...])
    aux = key_rows()
    ones = jnp.where(lax.broadcasted_iota(jnp.int32, (16, LP), 0) < 3, 1.0, 0.0).astype(BF)
    dq, dk, dv = [], [], []
    for h in range(hl):
        at = slice(h * HEAD_DIM, (h + 1) * HEAD_DIM)
        q = xt[at]
        k = xt[cw + h * HEAD_DIM : cw + (h + 1) * HEAD_DIM]
        v = xt[2 * cw + h * HEAD_DIM : 2 * cw + (h + 1) * HEAD_DIM]
        g = gt[at]
        hi, lo = split_query(q)
        delta = jnp.sum(ot[at].astype(F32) * g.astype(F32), axis=0, keepdims=True)
        minus = split_rows(-lse_ref[0, 0, h : h + 1, :])
        s = dotf(jnp.concatenate([k, k, aux], 0), jnp.concatenate([hi, lo, minus], 0), 0, 0)
        p = jnp.exp2(s)
        d = dotf(jnp.concatenate([v, ones], 0), jnp.concatenate([g, split_rows(-delta)], 0), 0, 0)
        ds = (p * d).astype(BF)
        dv.append(dotf(g, p.astype(BF), 1, 1).astype(BF))
        dq.append((HEAD_DIM**-0.5 * dotf(k, ds, 1, 0)).astype(BF))
        dk.append(dotf(q, ds, 1, 1).astype(BF))
    out = jnp.concatenate(dq + dk + dv, 0).T[:SP]
    d_ref[...] = out
    sum_ref[0, 0, :, :] = jnp.sum(out.astype(F32), axis=0, keepdims=True)


def attend_back(lay, packed, mixed, dmixed, lse):
    rows = packed.shape[0]
    own = rows // SP
    cw = lay.cw
    hl = cw // HEAD_DIM
    return pl.pallas_call(
        partial(attend_back_kernel, hl),
        grid=(own, lay.nt),
        in_specs=[
            pl.BlockSpec((SP, 3 * cw), lambda i, t: (i, t)),
            pl.BlockSpec((SP, cw), lambda i, t: (i, t)),
            pl.BlockSpec((SP, cw), lambda i, t: (i, t)),
            pl.BlockSpec((1, 1, hl, LP), lambda i, t: (i, t, 0, 0)),
        ],
        out_specs=[
            pl.BlockSpec((SP, 3 * cw), lambda i, t: (i, t)),
            pl.BlockSpec((1, 1, 1, 3 * cw), lambda i, t: (i, t, 0, 0)),
        ],
        out_shape=[
            jax.ShapeDtypeStruct(packed.shape, BF),
            jax.ShapeDtypeStruct((own, lay.nt, 1, 3 * cw), F32),
        ],
        compiler_params=params(),
        cost_estimate=cost(35e9, 20e6),
        name="attend_back",
    )(packed, mixed, dmixed, lse)


def unit_of(values):
    center = values - jnp.mean(values, axis=-1, keepdims=True)
    inverse = lax.rsqrt(jnp.mean(center * center, axis=-1, keepdims=True) + 1e-05)
    return center * inverse, inverse


def norm_back(grad, unit, inverse, gain):
    scaled = grad * gain
    inner = (
        scaled
        - jnp.mean(scaled, axis=-1, keepdims=True)
        - unit * jnp.mean(scaled * unit, axis=-1, keepdims=True)
    )
    return inner * inverse


def add_rows(ref, first, rows):
    step = pl.program_id(0)

    @pl.when(step == 0)
    def _():
        for r, row in enumerate(rows):
            ref[r : r + 1, :] = row

    @pl.when(step > 0)
    def _():
        for r, row in enumerate(rows):
            ref[r : r + 1, :] += row


def column_sum(x):
    return jnp.sum(x, axis=0, keepdims=True)


def out_project(lay, me, group, mixed, inputs, bias, gain, shift):
    rows = mixed.shape[0]
    bufs = group_refs(group)
    pieces = piece_list(group)
    cw = lay.cw
    spans = ([], [(cw, cw, 0)])

    def kernel(me_ref, *refs):
        src = refs[: len(bufs)]
        m_ref, x_ref, b_ref, g_ref, s_ref, mid_ref, sec_ref, w, sem = refs[len(bufs) :]
        idx = (me_ref[0], me_ref[1], me_ref[2])

        @pl.when(pl.program_id(0) == 0)
        def _():
            start_pieces(lay, pieces, src, idx, spans, lambda to, t: (w, t * cw), lambda to: sem)
            wait_all(w, sem)

        middle = x_ref[...].astype(F32) + dotf(m_ref[...], w[...], 1, 1) + b_ref[...]
        mid_ref[...] = middle
        unit, _ = unit_of(middle)
        sec_ref[...] = (unit * g_ref[...] + s_ref[...]).astype(BF)

    block = pl.BlockSpec((SP, D), lambda i, m: (i, 0))
    row = pl.BlockSpec((1, D), lambda i, m: (0, 0))
    return pl.pallas_call(
        kernel,
        grid_spec=pltpu.PrefetchScalarGridSpec(
            num_scalar_prefetch=1,
            grid=(rows // SP,),
            in_specs=[ANY] * len(bufs) + [block, block, row, row, row],
            out_specs=[block, block],
            scratch_shapes=[pltpu.VMEM((D, D), BF), pltpu.SemaphoreType.DMA],
        ),
        out_shape=[jax.ShapeDtypeStruct((rows, D), F32), jax.ShapeDtypeStruct((rows, D), BF)],
        compiler_params=params(),
        cost_estimate=cost(2 * rows * D * D, 14e6),
        name="out_project",
    )(me, *bufs, mixed, inputs, bias, gain, shift)


def feed(lay, me, expand, shrink, second, dresult, bias):
    rows = second.shape[0]
    bufs_e, bufs_s = group_refs(expand), group_refs(shrink)
    pieces_e, pieces_s = piece_list(expand), piece_list(shrink)
    ne, ns = len(bufs_e), len(bufs_s)
    cols = lay.cols
    half = cols // 2
    spans = ([(0, half, 0)], [(0, half, half)])
    step_rows = SP

    def kernel(me_ref, *refs):
        src_e, src_s = refs[:ne], refs[ne : ne + ns]
        x_ref, g_ref, b_ref, a_ref, d_ref, c_ref, we, ws, sem_e, sem_s = refs[ne + ns :]
        o = pl.program_id(0)
        idx = (me_ref[0], me_ref[1], me_ref[2])

        @pl.when(o == 0)
        def _():
            start_pieces(lay, pieces_e, src_e, idx, spans, lambda to, t: (we.at[to], 0), lambda to: sem_e.at[to])
            start_pieces(lay, pieces_s, src_s, idx, spans, lambda to, t: (ws.at[to], 0), lambda to: sem_s.at[to])

        wait_all(we.at[o], sem_e.at[o])
        wait_all(ws.at[o], sem_s.at[o])
        for j in range(cols // 512):
            cs = slice(j * 512, (j + 1) * 512)
            total = None
            for r in range(rows // step_rows):
                rs = slice(r * step_rows, (r + 1) * step_rows)
                hidden = jnp.dot(x_ref[rs, :], we[o, :, cs], preferred_element_type=F32) + b_ref[:, cs]
                dact = jnp.dot(g_ref[rs, :], ws[o, :, cs], preferred_element_type=F32)
                sigma = jax.nn.sigmoid(1.702 * hidden)
                active = hidden * sigma
                a_ref[rs, cs] = active.astype(BF)
                dh = (dact * (sigma + 1.702 * active * (1.0 - sigma))).astype(BF)
                d_ref[rs, cs] = dh
                part = column_sum(dh.astype(F32))
                total = part if total is None else total + part
            c_ref[:, cs] = total

    return pl.pallas_call(
        kernel,
        grid_spec=pltpu.PrefetchScalarGridSpec(
            num_scalar_prefetch=1,
            grid=(lay.nt,),
            in_specs=[ANY] * (ne + ns)
            + [
                pl.BlockSpec((rows, D), lambda o, m: (0, 0)),
                pl.BlockSpec((rows, D), lambda o, m: (0, 0)),
                pl.BlockSpec((1, cols), lambda o, m: (0, o ^ m[2])),
            ],
            out_specs=[
                pl.BlockSpec((rows, cols), lambda o, m: (0, o ^ m[2])),
                pl.BlockSpec((rows, cols), lambda o, m: (0, o ^ m[2])),
                pl.BlockSpec((1, cols), lambda o, m: (0, o ^ m[2])),
            ],
            scratch_shapes=[
                pltpu.VMEM((lay.nt, D, cols), BF),
                pltpu.VMEM((lay.nt, D, cols), BF),
                pltpu.SemaphoreType.DMA((lay.nt,)),
                pltpu.SemaphoreType.DMA((lay.nt,)),
            ],
        ),
        out_shape=[
            jax.ShapeDtypeStruct((rows, FF), BF),
            jax.ShapeDtypeStruct((rows, FF), BF),
            jax.ShapeDtypeStruct((1, FF), F32),
        ],
        compiler_params=params(),
        cost_estimate=cost(4 * rows * D * FF, 40e6),
        name="feed",
    )(me, *bufs_e, *bufs_s, second, dresult, bias)


def feed_out(lay, me, shrink, active, middle, bias):
    rows = active.shape[0]
    bufs = group_refs(shrink)
    pieces = piece_list(shrink)
    cols = lay.cols
    half = cols // 2
    spans = ([(0, half, 0)], [(0, half, half)])
    own = rows // SP

    def kernel(me_ref, *refs):
        src = refs[: len(bufs)]
        a_ref, mid_ref, b_ref, o_ref, w, sem = refs[len(bufs) :]
        idx = (me_ref[0], me_ref[1], me_ref[2])

        @pl.when(pl.program_id(0) == 0)
        def _():
            start_pieces(lay, pieces, src, idx, spans, lambda to, t: (w, t * cols), lambda to: sem)
            wait_all(w, sem)

        live = me_ref[2] * own + pl.program_id(0) < me_ref[3]
        out = mid_ref[...] + dotf(a_ref[...], w[...], 1, 1) + b_ref[...]
        o_ref[...] = jnp.where(live, out, 0.0).astype(BF)

    return pl.pallas_call(
        kernel,
        grid_spec=pltpu.PrefetchScalarGridSpec(
            num_scalar_prefetch=1,
            grid=(own,),
            in_specs=[ANY] * len(bufs)
            + [
                pl.BlockSpec((SP, FF), lambda i, m: (i, 0)),
                pl.BlockSpec((SP, D), lambda i, m: (i, 0)),
                pl.BlockSpec((1, D), lambda i, m: (0, 0)),
            ],
            out_specs=pl.BlockSpec((SP, D), lambda i, m: (i, 0)),
            scratch_shapes=[pltpu.VMEM((D, FF), BF), pltpu.SemaphoreType.DMA],
        ),
        out_shape=jax.ShapeDtypeStruct((rows, D), BF),
        compiler_params=params(),
        cost_estimate=cost(2 * rows * D * FF, 25e6),
        name="feed_out",
    )(me, *bufs, active, middle, bias)


def feed_back(lay, me, expand, joint, dhidden, middle, dresult, gain):
    rows = dhidden.shape[0]
    bufs_e, bufs_o = group_refs(expand), group_refs(joint)
    pieces_e, pieces_o = piece_list(expand), piece_list(joint)
    ne, no = len(bufs_e), len(bufs_o)
    cols, cw = lay.cols, lay.cw
    half = cols // 2
    spans = ([(0, half, 0)], [(0, half, half)])
    spans_o = ([], [(cw, cw, 0)])

    def kernel(me_ref, *refs):
        src_e, src_o = refs[:ne], refs[ne : ne + no]
        h_ref, mid_ref, g_ref, n_ref, dm_ref, db_ref, dx_ref, v_ref, we, wo, sem_e, sem_o = refs[ne + no :]
        idx = (me_ref[0], me_ref[1], me_ref[2])

        @pl.when(pl.program_id(0) == 0)
        def _():
            start_pieces(lay, pieces_e, src_e, idx, spans, lambda to, t: (we, t * cols), lambda to: sem_e)
            start_pieces(lay, pieces_o, src_o, idx, spans_o, lambda to, t: (wo, t * cw), lambda to: sem_o)
            wait_all(we, sem_e)
            wait_all(wo, sem_o)

        dsecond = dotf(h_ref[...], we[...], 1, 1)
        unit, inverse = unit_of(mid_ref[...])
        dmiddle = g_ref[...].astype(F32) + norm_back(dsecond, unit, inverse, n_ref[...])
        dm_ref[...] = dmiddle
        dbranch = dmiddle.astype(BF)
        db_ref[...] = dbranch
        dx_ref[...] = jnp.dot(dbranch, wo[...], preferred_element_type=F32).astype(BF)
        add_rows(v_ref, 0, [column_sum(dsecond * unit), column_sum(dsecond), column_sum(dbranch.astype(F32)), column_sum(g_ref[...].astype(F32))])

    block = pl.BlockSpec((SP, D), lambda i, m: (i, 0))
    return pl.pallas_call(
        kernel,
        grid_spec=pltpu.PrefetchScalarGridSpec(
            num_scalar_prefetch=1,
            grid=(rows // SP,),
            in_specs=[ANY] * (ne + no)
            + [
                pl.BlockSpec((SP, FF), lambda i, m: (i, 0)),
                block,
                block,
                pl.BlockSpec((1, D), lambda i, m: (0, 0)),
            ],
            out_specs=[block, block, block, pl.BlockSpec((4, D), lambda i, m: (0, 0))],
            scratch_shapes=[
                pltpu.VMEM((D, FF), BF),
                pltpu.VMEM((D, D), BF),
                pltpu.SemaphoreType.DMA,
                pltpu.SemaphoreType.DMA,
            ],
        ),
        out_shape=[
            jax.ShapeDtypeStruct((rows, D), F32),
            jax.ShapeDtypeStruct((rows, D), BF),
            jax.ShapeDtypeStruct((rows, D), BF),
            jax.ShapeDtypeStruct((4, D), F32),
        ],
        compiler_params=params(),
        cost_estimate=cost(2 * rows * D * (FF + D), 35e6),
        name="feed_back",
    )(me, *bufs_e, *bufs_o, dhidden, middle, dresult, gain)


def project_back(lay, me, group, dpacked, inputs, dmiddle, gain):
    rows = dpacked.shape[0]
    bufs = group_refs(group)
    pieces = piece_list(group)
    cw = lay.cw
    spans = ([(0, 2 * cw, 0)], [(0, cw, 2 * cw)])

    def kernel(me_ref, *refs):
        src = refs[: len(bufs)]
        p_ref, x_ref, dm_ref, n_ref, o_ref, v_ref, w, sem = refs[len(bufs) :]
        idx = (me_ref[0], me_ref[1], me_ref[2])

        @pl.when(pl.program_id(0) == 0)
        def _():
            start_pieces(lay, pieces, src, idx, spans, lambda to, t: (w, t * 3 * cw), lambda to: sem)
            wait_all(w, sem)

        dnormed = dotf(p_ref[...], w[...], 1, 1)
        unit, inverse = unit_of(x_ref[...].astype(F32))
        o_ref[...] = (dm_ref[...] + norm_back(dnormed, unit, inverse, n_ref[...])).astype(BF)
        add_rows(v_ref, 0, [column_sum(dnormed * unit), column_sum(dnormed)])

    block = pl.BlockSpec((SP, D), lambda i, m: (i, 0))
    return pl.pallas_call(
        kernel,
        grid_spec=pltpu.PrefetchScalarGridSpec(
            num_scalar_prefetch=1,
            grid=(rows // SP,),
            in_specs=[ANY] * len(bufs)
            + [
                pl.BlockSpec((SP, 3 * D), lambda i, m: (i, 0)),
                block,
                block,
                pl.BlockSpec((1, D), lambda i, m: (0, 0)),
            ],
            out_specs=[block, pl.BlockSpec((2, D), lambda i, m: (0, 0))],
            scratch_shapes=[pltpu.VMEM((D, 3 * D), BF), pltpu.SemaphoreType.DMA],
        ),
        out_shape=[jax.ShapeDtypeStruct((rows, D), BF), jax.ShapeDtypeStruct((2, D), F32)],
        compiler_params=params(),
        cost_estimate=cost(2 * rows * D * 3 * D, 25e6),
        name="project_back",
    )(me, *bufs, dpacked, inputs, dmiddle, gain)


def insert_bit(s, b, value):
    return ((s >> b) << (b + 1)) | (value << b) | (s & ((1 << b) - 1))


def weight_grad(lay, me, lhss, halves, toffs, steps, sibling, received=None, name="grad"):
    rows = lhss[0].shape[0]
    z, dr = lay.nz, lay.rows
    half = lay.cols // 2
    nl = len(lhss)
    parts = [(h, *part) for h in range(2) for part in halves[h]]
    nr = 0 if received is None else 2

    def kernel(me_ref, *refs):
        lhs_refs = refs[:nl]
        rhs_refs = refs[nl : nl + len(parts)]
        got = refs[nl + len(parts) : nl + len(parts) + nr]
        outs = refs[nl + len(parts) + nr : nl + len(parts) + nr + 2]
        sel = refs[nl + len(parts) + nr + 2 :]
        s = pl.program_id(0)

        @pl.when(s == 0)
        def _():
            side = me_ref[1] ^ 1 if sibling else me_ref[1]
            for ref, scratch in zip(lhs_refs, sel):
                for zo in range(z):
                    at = pl.multiple_of((zo ^ me_ref[0]) * (2 * dr), 128)
                    block = ref[:, pl.ds(at, 2 * dr)]
                    scratch[:, zo * dr : (zo + 1) * dr] = jnp.where(side == 0, block[:, :dr], block[:, dr:])

        at = [0, 0]
        for (h, li, _, width, _), ref in zip(parts, rhs_refs):
            y = dotf(sel[li][...], ref[...], 0, 0).reshape(z, dr, width)
            cs = pl.ds(at[h], width)
            at[h] += width
            if nr:
                y = y + got[h][0, :, :, cs].astype(F32)
            outs[h][0, :, :, cs] = y.astype(BF)

    def rhs_spec(h, width, index):
        return pl.BlockSpec((rows, width), lambda s, m: (0, index(toffs[h](s) ^ m[2])))

    def got_spec(h):
        return pl.BlockSpec((1, z, dr, half), lambda s, m: (toffs[h](s), 0, 0, 0))

    piece = pl.BlockSpec((1, z, dr, half), lambda s, m: (s, 0, 0, 0))
    return pl.pallas_call(
        kernel,
        grid_spec=pltpu.PrefetchScalarGridSpec(
            num_scalar_prefetch=1,
            grid=(steps,),
            in_specs=[pl.BlockSpec((rows, D), lambda s, m: (0, 0))] * nl
            + [rhs_spec(h, width, index) for h, _, _, width, index in parts]
            + [got_spec(h) for h in range(nr)],
            out_specs=[piece, piece],
            scratch_shapes=[pltpu.VMEM((rows, z * dr), BF)] * nl,
        ),
        out_shape=[jax.ShapeDtypeStruct((steps, z, dr, half), BF)] * 2,
        compiler_params=params(),
        cost_estimate=cost(2 * rows * z * dr * steps * 2 * half, 15e6),
        name=name,
    )(me, *lhss, *[part[2] for part in parts], *(received or []))


def half_axes(lay, half):
    first = lay.order(half)[-1]
    t = [("t", b) for b in reversed(range(lay.tbits)) if ("t", b) != first]
    z = [("z", b) for b in reversed(range(lay.zbits))]
    return t + z


def scatter_half(lay, half, send, keep):
    order = lay.order(half)[::-1]
    axes = half_axes(lay, half)
    shape = (2,) * len(axes) + send.shape[2:]
    got = swap(send, lay.mask(order[0]), lay.size).reshape(shape)
    keep = keep.reshape(shape)
    for bit in order[1:]:
        axis = axes.index(bit)
        pick = lambda x, i: lax.index_in_dim(x, i, axis, keepdims=False)
        send = (pick(keep, 1).astype(F32) + pick(got, 1).astype(F32)).astype(BF)
        keep = (pick(keep, 0).astype(F32) + pick(got, 0).astype(F32)).astype(BF)
        axes = axes[:axis] + axes[axis + 1 :]
        got = swap(send, lay.mask(bit), lay.size)
    return keep.astype(F32) + got.astype(F32)


def reduce_group(lay, me, lhss, halves, name):
    every = lambda s: s
    both = weight_grad(lay, me, lhss, halves, (every, every), lay.nt, True, name=name + "_other")
    received = [swap(x, lay.core, lay.size) for x in both]
    bits = [lay.order(h)[-1][1] for h in range(2)]
    out = []
    for value in (1, 0):
        toffs = tuple(partial(lambda b, s: insert_bit(s, b, value), b) for b in bits)
        out.append(
            weight_grad(
                lay, me, lhss, halves, toffs, lay.nt // 2, False, received, name=name + ("_keep", "_send")[value]
            )
        )
    send, keep = out
    return [scatter_half(lay, h, send[h], keep[h]) for h in range(2)]


def all_sum(lay, x, combine=jnp.add):
    for bit in lay.order(0):
        x = combine(x, swap(x, lay.mask(bit), lay.size))
    return combine(x, swap(x, lay.core, lay.size))


def pad_rows(x):
    own = x.shape[0] // SEQ
    return jnp.pad(x.reshape(own, SEQ, D), ((0, 0), (0, SP - SEQ), (0, 0))).reshape(own * SP, D)


def unpad_rows(x):
    own = x.shape[0] // SP
    return x.reshape(own, SP, D)[:, :SEQ].reshape(own * SEQ, D)


def per_device(
    lay,
    tokens,
    first_gain,
    first_shift,
    joint_weight,
    joint_bias,
    output_weight,
    output_bias,
    second_gain,
    second_shift,
    expand_weight,
    expand_bias,
    shrink_weight,
    shrink_bias,
    cotangent,
    image_count,
    threshold,
):
    own = tokens.shape[0] // SEQ
    nt, cw, dr = lay.nt, lay.cw, lay.rows
    half = lay.cols // 2
    hl = cw // HEAD_DIM
    tensor = lax.axis_index("tensor").astype(jnp.int32)
    dp = lax.axis_index("dp").astype(jnp.int32)
    count = image_count[0]
    me = jnp.stack([dp // 2, dp % 2, tensor, count])

    joint_a = joint_weight[:, :2].reshape(dr, 2 * cw)
    small = jnp.concatenate([joint_bias.reshape(-1), expand_bias.reshape(-1)])
    n_small = small.shape[0]
    extra = jnp.pad(small[None], ((0, 15), (0, half - n_small)))
    joint_b = jnp.concatenate(
        [jnp.concatenate([joint_weight[:, 2], output_weight.T], axis=1), extra], axis=0
    )
    joint = gather_group(lay, joint_a, joint_b)
    shrink_t = shrink_weight.T
    expand = gather_group(lay, expand_weight[:, :half], expand_weight[:, half:])
    shrink = gather_group(lay, shrink_t[:, :half], shrink_t[:, half:])

    found = jnp.concatenate([buf[:, dr, :n_small] for buf, _ in joint[1]])
    offsets = [(z * 2 + c) * nt + t for _, offs in joint[1] for z, t, c in offs]
    order = jnp.asarray(offsets, jnp.int32) ^ (dp * nt + tensor)
    pick = (jnp.arange(lay.size, dtype=jnp.int32)[:, None] == order[None, :]).astype(BF)
    biases = jnp.dot(pick, found, preferred_element_type=F32)
    nb = joint_bias.size
    jb = biases[:, :nb].reshape(lay.ndp, nt, 2, hl, HEAD_DIM // lay.ndp)
    jb = jb.transpose(1, 2, 3, 0, 4).reshape(nt, 2, cw)
    bias_rows = jnp.concatenate([jb[:, 0], jnp.zeros_like(jb[:, 0]), jb[:, 1]], axis=1).reshape(1, 3 * D)
    eb = biases[:, nb:].reshape(lay.ndp, nt, FF // HEAD_DIM // nt, HEAD_DIM // lay.ndp)
    expand_row = eb.transpose(1, 2, 0, 3).reshape(1, FF)

    image_ids = tensor * own + jnp.arange(own, dtype=jnp.int32)
    image_live = image_ids < count
    inputs = pad_rows(tokens)
    live_rows = jnp.repeat(image_live, SEQ)[:, None]
    dresult = pad_rows(jnp.where(live_rows, cotangent, jnp.zeros_like(cotangent)))
    unit, _ = unit_of(inputs.astype(F32))
    normed = (unit * first_gain + first_shift).astype(BF)

    packed = project(lay, me, joint, normed, bias_rows)
    mixed, lse, tops = attend(lay, packed)
    row = lambda v: v.reshape(1, D)
    middle, second = out_project(
        lay, me, joint, mixed, inputs, row(output_bias), row(second_gain), row(second_shift)
    )
    active, dhidden, expand_sum = feed(lay, me, expand, shrink, second, dresult, expand_row)

    col = lambda h: (lambda t: t * 2 + h)
    shrink_pieces = reduce_group(
        lay, me, [dresult], [[(0, active, half, col(h))] for h in range(2)], "shrink_grad"
    )
    expand_pieces = reduce_group(
        lay, me, [second], [[(0, dhidden, half, col(h))] for h in range(2)], "expand_grad"
    )
    dmiddle, dbranch, dmixed, sums_two = feed_back(
        lay, me, expand, joint, dhidden, middle, dresult, row(second_gain)
    )
    dpacked, packed_sums = attend_back(lay, packed, mixed, dmixed, lse)
    part = lambda c: (lambda t: t * 3 + c)
    joint_pieces = reduce_group(
        lay,
        me,
        [normed, dbranch],
        [
            [(0, dpacked, cw, part(0)), (0, dpacked, cw, part(1))],
            [(0, dpacked, cw, part(2)), (1, mixed, cw, lambda t: t)],
        ],
        "joint_grad",
    )
    token_rows, sums_one = project_back(lay, me, joint, dpacked, inputs, dmiddle, row(first_gain))
    result = feed_out(lay, me, shrink, active, middle, row(shrink_bias))
    block_out = unpad_rows(result)
    tokens_grad = unpad_rows(token_rows)

    early = jnp.concatenate([sums_two.reshape(-1, 128), expand_sum.reshape(-1, 128)])
    early = all_sum(lay, early)
    head_sums = jnp.sum(packed_sums, axis=0).reshape(nt, 3, cw)
    late = jnp.concatenate(
        [sums_one.reshape(-1, 128), head_sums[:, 0].reshape(-1, 128), head_sums[:, 2].reshape(-1, 128)]
    )
    late = all_sum(lay, late)
    sums_two = early[: 4 * D // 128].reshape(4, D)
    expand_sum = early[4 * D // 128 :].reshape(FF)
    sums_one = late[: 2 * D // 128].reshape(2, D)
    bias_sum = late[2 * D // 128 :].reshape(2, D)
    mine = lambda v: lax.dynamic_slice_in_dim(v, dp * dr, dr, v.ndim - 1)
    sums_one, sums_two = mine(sums_one), mine(sums_two)
    share = HEAD_DIM // lay.ndp
    units = FF // HEAD_DIM // nt
    expand_bias_grad = lax.dynamic_slice(
        expand_sum.reshape(FF // HEAD_DIM, HEAD_DIM), (tensor * units, dp * share), (units, share)
    )
    joint_bias_grad = lax.dynamic_slice(
        bias_sum.reshape(2, HEADS, HEAD_DIM), (0, tensor * hl, dp * share), (2, hl, share)
    )

    tops = jnp.max(tops, axis=-1).reshape(own, HEADS) / LOG2E
    peak = jnp.max(jnp.where(image_live[:, None], tops, NEG), axis=0)
    peak = all_sum(lay, jnp.broadcast_to(peak[:, None], (HEADS, 128)), jnp.maximum)[:, 0]
    top = lax.dynamic_slice_in_dim(peak, tensor * hl, hl, 0)
    factors = jnp.sqrt(threshold / jnp.maximum(top, threshold))
    columns = jnp.repeat(factors, HEAD_DIM)
    clipped_joint = (joint_weight[:, 0:2, :].astype(F32) * columns).astype(BF)
    clipped_bias = (joint_bias[0].astype(F32) * factors[:, None]).astype(BF)

    ja, jb = joint_pieces
    joint_grad = jnp.concatenate([ja, jb[:, :cw]], axis=1).reshape(dr, 3, cw)
    output_grad = jb[:, cw:].T
    expand_grad = jnp.concatenate(expand_pieces, axis=1)
    shrink_grad = jnp.concatenate(shrink_pieces, axis=1).T
    return (
        block_out,
        tokens_grad,
        sums_one[0],
        sums_one[1],
        joint_grad,
        joint_bias_grad,
        output_grad,
        sums_two[2],
        sums_two[0],
        sums_two[1],
        expand_grad,
        expand_bias_grad,
        shrink_grad,
        sums_two[3],
        clipped_joint,
        clipped_bias,
        factors,
    )


def solution(mesh):
    placed = (
        P(("dp", "tensor"), None),
        P(),
        P(),
        P("dp", None, "tensor"),
        P(None, "tensor", "dp"),
        P("tensor", "dp"),
        P(),
        P(),
        P(),
        P("dp", "tensor"),
        P("tensor", "dp"),
        P("tensor", "dp"),
        P(),
        P(("dp", "tensor"), None),
        P("dp"),
        P("tensor"),
    )
    lay = Layout(mesh.shape["dp"], mesh.shape["tensor"])
    return jax.shard_map(
        partial(per_device, lay),
        mesh=mesh,
        in_specs=placed,
        out_specs=(
            P(("dp", "tensor"), None),
            P(("dp", "tensor"), None),
            P("dp"),
            P("dp"),
            P("dp", None, "tensor"),
            P(None, "tensor", "dp"),
            P("tensor", "dp"),
            P("dp"),
            P("dp"),
            P("dp"),
            P("dp", "tensor"),
            P("tensor", "dp"),
            P("tensor", "dp"),
            P("dp"),
            P("dp", None, "tensor"),
            P("tensor", "dp"),
            P("tensor"),
        ),
        check_vma=False,
    )
```

time: 1100 us -> 674 us (0.61)
  matrix products: 318 us -> 0.78 us
  Pallas kernels: 0 us -> 279 us
  waiting for transfers between devices: 383 us -> 172 us
  blocking collectives: 146 us -> 0 us
  starting transfers between devices: 1.04 us -> 90.2 us
  local copies, waits for them, and re-layouts: 140 us -> 77.5 us
  other arithmetic: 83.5 us -> 41.7 us
  between operations: 17.7 us -> 2.84 us
    dot_general x26 -> x1, matrix products: 318 us -> 0.78 us  [per_device(): biases = jnp.dot(pick, found, preferred_element_type=F32)]
    pallas_call x0 -> x17, Pallas kernels: none -> 279 us  [the longest x9 85.8 us: weight_grad(): pl.pallas_call(kernel, grid_spec=pltpu.PrefetchScalarGridSpec(num_scalar_...]
    ppermute x0 -> x105, waiting for transfers between devices: none -> 172 us  [swap(): return lax.ppermute(x, AXES, [(i, i ^ mask) for i in range(size)])]
    reduce_scatter x6 -> x0, waiting for transfers between devices: 160 us -> none  [the longest x1 87.6 us: per_device(): lax.psum_scatter(shrink_grad.astype(jnp.bfloat16), 'tensor', scatter_dime...]
    all_gather x7 -> x0, waiting for transfers between devices: 144 us -> none  [the longest x1 55.4 us: per_device(): lax.all_gather(joint_full, 'tensor', axis=2, tiled=True)]
    ppermute x0 -> x105, starting transfers between devices: none -> 90.2 us  [swap(): return lax.ppermute(x, AXES, [(i, i ^ mask) for i in range(size)])]
    unnamed x19 -> x0, waiting for transfers between devices: 78.1 us -> none
    while x16 -> x0, local copies, waits for them, and re-layouts: 60.1 us -> none  [the longest x2 24.7 us: per_device(): mixed, logsum, peaks = lax.map(partial(attend, scale), per_image)]
  transfers between devices with their start and end apart: 16 -> 105, of which waited for: 11 -> 37; matrix products, arithmetic and copies ran while one was open for 43% -> 17% of each run, Pallas kernels for 0% -> 42%
where the time goes in v1:
time: 674 us; the launch traced here: 664 us
  Pallas kernels  279 us (41%)
  waiting for transfers between devices  172 us (26%)
  starting transfers between devices  90.2 us (13%)
  local copies, waits for them, and re-layouts  77.5 us (11%)
  other arithmetic  41.7 us (6%)
    ppermute x105, waiting for transfers between devices, swap(): return lax.ppermute(x, AXES, [(i, i ^ mask) for i in range(size)])  172 us
    ppermute x105, starting transfers between devices, swap(): return lax.ppermute(x, AXES, [(i, i ^ mask) for i in range(size)])  90.2 us
    pallas_call x9, Pallas kernels, weight_grad(): pl.pallas_call(kernel, grid_spec=pltpu.PrefetchScalarGridSpec(num_scalar_...  85.8 us
    pallas_call x1, Pallas kernels, attend_back(): pl.pallas_call(partial(attend_back_kernel, hl), grid=(own, lay.nt), in_sp...  41 us
    pallas_call x1, Pallas kernels, feed(): pl.pallas_call(kernel, grid_spec=pltpu.PrefetchScalarGridSpec(num_scalar_...  35.6 us
    unnamed x128, local copies, waits for them, and re-layouts  33.9 us
    pallas_call x1, Pallas kernels, feed_back(): pl.pallas_call(kernel, grid_spec=pltpu.PrefetchScalarGridSpec(num_scalar_...  27.4 us
    pallas_call x1, Pallas kernels, attend(): pl.pallas_call(partial(attend_kernel, hl), grid=(own, lay.nt), in_specs=[...  25.1 us
  transfers between devices with their start and end apart: 105, of which 37 were waited for; matrix products, arithmetic and copies ran while one was open for 17% of the time, Pallas kernels for 42%

profile of v1, /device:TPU:0, one launch (start us, length us, event | category | flops | bytes accessed | tf_op | source)
XLA Modules:
  0.0 663.5 jit_solution(18386725949724427571)
XLA Ops:
  2.5 3.0 collective-permute-start.41
  5.5 2.6 collective-permute-start.40
  17.8 2.7 collective-permute-start
  20.9 2.2 collective-permute-start.30
  24.9 2.3 collective-permute-done
  28.8 2.7 collective-permute-done.30
  31.5 2.9 collective-permute-start.50
  34.4 8.9 %collective-permute-done.20 = bf16[1,128,512]{2,1,0:T(8,128)(2,1)S(1)} collective-permute-done((bf16[1,128,512]{2,1,0:T(8,128)(2,1)S(1)}, bf16[1,128,512]{2,1,0:T(8,128)(2,1)S(1)}, u32[]{:S(2)}, u32[]{:S(2)}) %collective-permute-start.20) | collective-permute-done | bytes 131104 | tf_op jit(solution)/shard_map/ppermute | solution.py:72
  46.2 3.2 collective-permute-done.12
  52.2 2.6 collective-permute-start.43
  56.5 2.6 collective-permute-start.23
  60.0 7.6 %collective-permute-done.43.refs_1_.refs_17_ = bf16[4,128,512]{2,1,0:T(8,128)(2,1)S(1)} collective-permute-done((bf16[4,128,512]{2,1,0:T(8,128)(2,1)S(1)}, bf16[4,128,512]{2,1,0:T(8,128)(2,1)S(1)}, u32[]{:S(2)}, u32[]{:S(2)}) %collective-permute-start.43) | collective-permute-done | bytes 524320 | tf_op jit(solution)/shard_map/ppermute | solution.py:72
  73.0 5.9 collective-permute-done.23.refs_1_
  85.9 17.0 %collective-permute-done.33.refs_9_ = bf16[4,128,512]{2,1,0:T(8,128)(2,1)} collective-permute-done((bf16[4,128,512]{2,1,0:T(8,128)(2,1)}, bf16[4,128,512]{2,1,0:T(8,128)(2,1)}, u32[]{:S(2)}, u32[]{:S(2)}) %collective-permute-start.33) | collective-permute-done | bytes 524320 | tf_op jit(solution)/shard_map/ppermute | solution.py:72
  107.2 2.1 reshape.437
  111.2 19.4 %collective-permute-done.54.refs_10_.refs_26_ = bf16[4,144,512]{2,1,0:T(8,128)(2,1)} collective-permute-done((bf16[4,144,512]{2,1,0:T(8,128)(2,1)S(1)}, bf16[4,144,512]{2,1,0:T(8,128)(2,1)}, u32[]{:S(2)}, u32[]{:S(2)}) %collective-permute-start.54) | collective-permute-done | bytes 589856 | tf_op jit(solution)/shard_map/ppermute | solution.py:72
  130.6 12.3 %collective-permute-done.55.refs_11_.refs_27_ = bf16[4,144,512]{2,1,0:T(8,128)(2,1)} collective-permute-done((bf16[4,144,512]{2,1,0:T(8,128)(2,1)}, bf16[4,144,512]{2,1,0:T(8,128)(2,1)}, u32[]{:S(2)}, u32[]{:S(2)}) %collective-permute-start.55) | collective-permute-done | bytes 589856 | tf_op jit(solution)/shard_map/ppermute | solution.py:72
  143.7 3.6 reshape.445
  157.4 9.1 %collective-permute-done.13.refs_25_.refs_9_ = bf16[4,128,512]{2,1,0:T(8,128)(2,1)} collective-permute-done((bf16[4,128,512]{2,1,0:T(8,128)(2,1)}, bf16[4,128,512]{2,1,0:T(8,128)(2,1)}, u32[]{:S(2)}, u32[]{:S(2)}) %collective-permute-start.13) | collective-permute-done | bytes 524320 | tf_op jit(solution)/shard_map/ppermute | solution.py:72
  168.3 3.0 add_convert_fusion.refs_16_.refs_0_
  177.6 3.9 collective-permute-done.45.refs_3_.refs_19_
  185.1 7.3 %collective-permute-done.25.refs_3_ = bf16[4,128,512]{2,1,0:T(8,128)(2,1)} collective-permute-done((bf16[4,128,512]{2,1,0:T(8,128)(2,1)}, bf16[4,128,512]{2,1,0:T(8,128)(2,1)}, u32[]{:S(2)}, u32[]{:S(2)}) %collective-permute-start.25) | collective-permute-done | bytes 524320 | tf_op jit(solution)/shard_map/ppermute | solution.py:72
  195.8 15.0 %project.1.p_ref = bf16[1184,3072]{1,0:T(8,128)(2,1)} custom-call(s32[4]{0:T(128)} %pad_add_fusion.me_ref, bf16[4,128,512]{2,1,0:T(8,128)(2,1)} %copy-done.16, bf16[4,128,512]{2,1,0:T(8,128)(2,1)} %copy-done.20, bf16[4,128,512]{2,1,0:T(8,128)(2,1)} %copy-done.18, bf16[4,128,512]{2,1,0:T(8,128)(2,1)} %collective-permute-done.45.refs_3_.refs_19_, ...), custom_call_target="tpu_custom_call" | custom-call | flops 7449083904 | bytes 16000000 | tf_op jit(solution)/shard_map/project/pallas_call | solution.py:162
  212.4 25.1 %attend.1 = (bf16[1184,1024]{1,0:T(8,128)(2,1)}, f32[2,4,4,640]{3,2,1,0:T(4,128)}, f32[2,4,4,640]{3,2,1,0:T(4,128)}) custom-call(bf16[1184,3072]{1,0:T(8,128)(2,1)} %project.1.p_ref), custom_call_target="tpu_custom_call" | custom-call | flops 22000001024 | bytes 10000000 | tf_op jit(solution)/shard_map/attend/pallas_call | solution.py:243
  239.9 9.6 %out_project.1 = (f32[1184,1024]{1,0:T(8,128)}, bf16[1184,1024]{1,0:T(8,128)(2,1)}) custom-call(s32[4]{0:T(128)} %pad_add_fusion.me_ref, bf16[4,128,512]{2,1,0:T(8,128)(2,1)} %copy-done.16, bf16[4,128,512]{2,1,0:T(8,128)(2,1)} %copy-done.20, bf16[4,128,512]{2,1,0:T(8,128)(2,1)} %copy-done.18, bf16[4,128,512]{2,1,0:T(8,128)(2,1)} %collective-permute-done.45.refs_3_.refs_19_, ...), custom_call_target="tpu_custom_call" | custom-call | flops 2483027968 | bytes 14000000 | tf_op jit(solution)/shard_map/out_project/pallas_call | solution.py:370
  249.6 3.1 collective-permute-start.100
  252.7 35.6 %feed.1 = (bf16[1184,4096]{1,0:T(8,128)(2,1)}, bf16[1184,4096]{1,0:T(8,128)(2,1)}, f32[1,4096]{1,0:T(1,128)}) custom-call(s32[4]{0:T(128)} %pad_add_fusion.me_ref, bf16[4,128,512]{2,1,0:T(8,128)(2,1)} %copy-done.22, bf16[4,128,512]{2,1,0:T(8,128)(2,1)} %copy-done.39, bf16[4,128,512]{2,1,0:T(8,128)(2,1)} %copy-done.38, ...), custom_call_target="tpu_custom_call" | custom-call | flops 19864223744 | bytes 40000000 | tf_op jit(solution)/shard_map/feed/pallas_call | solution.py:425
  288.3 27.4 %feed_back.1 = (f32[1184,1024]{1,0:T(8,128)}, bf16[1184,1024]{1,0:T(8,128)(2,1)}, bf16[1184,1024]{1,0:T(8,128)(2,1)}, f32[4,1024]{1,0:T(4,128)}) custom-call(s32[4]{0:T(128)} %pad_add_fusion.me_ref, bf16[4,128,512]{2,1,0:T(8,128)(2,1)} %copy-done.22, bf16[4,128,512]{2,1,0:T(8,128)(2,1)} %copy-done.39, bf16[4,128,512]{2,1,0:T(8,128)(2,1)} %copy-done.38, ...), custom_call_target="tpu_custom_call" | custom-call | flops 12415139840 | bytes 35000000 | tf_op jit(solution)/shard_map/feed_back/pallas_call | solution.py:535
  315.7 41.0 %attend_back.1 = (bf16[1184,3072]{1,0:T(8,128)(2,1)}, f32[2,4,1,768]{3,2,1,0:T(1,128)}) custom-call(bf16[1184,3072]{1,0:T(8,128)(2,1)} %project.1.p_ref, bf16[1184,1024]{1,0:T(8,128)(2,1)} %get-tuple-element.51.refs_16_.o_ref.refs_5_, bf16[1184,1024]{1,0:T(8,128)(2,1)} %get-tuple-element.56.g_ref, f32[2,4,4,640]{3,2,1,0:T(4,128)} %get-tuple-element.57.lse_ref), custom_call_target="tpu_custom_call" | custom-call | flops 35000000512 | bytes 20000000 | tf_op jit(solution)/shard_map/attend_back/pallas_call | solution.py:289
  357.5 19.0 %project_back.1 = (bf16[1184,1024]{1,0:T(8,128)(2,1)}, f32[2,1024]{1,0:T(2,128)}) custom-call(s32[4]{0:T(128)} %pad_add_fusion.me_ref, bf16[4,128,512]{2,1,0:T(8,128)(2,1)} %copy-done.16, bf16[4,128,512]{2,1,0:T(8,128)(2,1)} %copy-done.20, bf16[4,128,512]{2,1,0:T(8,128)(2,1)} %copy-done.18, bf16[4,128,512]{2,1,0:T(8,128)(2,1)} %collective-permute-done.45.refs_3_.refs_19_, ...), custom_call_target="tpu_custom_call" | custom-call | flops 7449083904 | bytes 25000000 | tf_op jit(solution)/shard_map/project_back/pallas_call | solution.py:590
  377.4 2.9 collective-permute-start.75
  380.3 12.2 %joint_grad_other.1 = (bf16[4,4,128,512]{3,2,1,0:T(8,128)(2,1)}, bf16[4,4,128,512]{3,2,1,0:T(8,128)(2,1)}) custom-call(s32[4]{0:T(128)} %pad_add_fusion.me_ref, bf16[1184,1024]{1,0:T(8,128)(2,1)} %add_convert_fusion.refs_16_.refs_0_, bf16[1184,1024]{1,0:T(8,128)(2,1)} %get-tuple-element.63.refs_1_, ...), custom_call_target="tpu_custom_call" | custom-call | flops 4966055936 | bytes 15000000 | tf_op jit(solution)/shard_map/joint_grad_other/pallas_call | solution.py:657
  393.4 20.0 %feed_out.1 = bf16[1184,1024]{1,0:T(8,128)(2,1)} custom-call(s32[4]{0:T(128)} %pad_add_fusion.me_ref, bf16[4,128,512]{2,1,0:T(8,128)(2,1)} %pad_maximum_fusion.1.refs_16_.refs_0_, bf16[4,128,512]{2,1,0:T(8,128)(2,1)} %copy-done.36, bf16[4,128,512]{2,1,0:T(8,128)(2,1)} %collective-permute-done.4.refs_18_.refs_2_, bf16[4,128,512]{2,1,0:T(8,128)(2,1)} %copy-done.42, ...), custom_call_target="tpu_custom_call" | custom-call | flops 9932111872 | bytes 25000000 | tf_op jit(solution)/shard_map/feed_out/pallas_call | solution.py:482
  415.2 10.9 %shrink_grad_other.1 = (bf16[4,4,128,512]{3,2,1,0:T(8,128)(2,1)}, bf16[4,4,128,512]{3,2,1,0:T(8,128)(2,1)}) custom-call(s32[4]{0:T(128)} %pad_add_fusion.me_ref, bf16[1184,1024]{1,0:T(8,128)(2,1)} %bitcast.334, bf16[1184,4096]{1,0:T(8,128)(2,1)} %get-tuple-element.53.refs_16_.refs_1_.refs_2_, bf16[1184,4096]{1,0:T(8,128)(2,1)} %get-tuple-element.53.refs_16_.refs_1_.refs_2_), custom_call_target="tpu_custom_call" | custom-call | flops 4966055936 | bytes 15000000 | tf_op jit(solution)/shard_map/shrink_grad_other/pallas_call | solution.py:657
  427.9 10.9 %expand_grad_other.1 = (bf16[4,4,128,512]{3,2,1,0:T(8,128)(2,1)}, bf16[4,4,128,512]{3,2,1,0:T(8,128)(2,1)}) custom-call(s32[4]{0:T(128)} %pad_add_fusion.me_ref, bf16[1184,1024]{1,0:T(8,128)(2,1)} %get-tuple-element.52.refs_32_.refs_0_, bf16[1184,4096]{1,0:T(8,128)(2,1)} %get-tuple-element.55.refs_32_.refs_1_.refs_2_, ...), custom_call_target="tpu_custom_call" | custom-call | flops 4966055936 | bytes 15000000 | tf_op jit(solution)/shard_map/expand_grad_other/pallas_call | solution.py:657
  448.1 2.6 collective-permute-done.61
  450.7 3.0 collective-permute-done.104
  454.1 3.4 collective-permute-done.62
  458.1 3.2 collective-permute-done.63
  466.7 3.5 collective-permute-done.77
  471.3 2.9 collective-permute-done.78
  477.4 9.5 %joint_grad_send.1 = (bf16[2,4,128,512]{3,2,1,0:T(8,128)(2,1)}, bf16[2,4,128,512]{3,2,1,0:T(8,128)(2,1)}) custom-call(s32[4]{0:T(128)} %pad_add_fusion.me_ref, bf16[1184,1024]{1,0:T(8,128)(2,1)} %add_convert_fusion.refs_16_.refs_0_, bf16[1184,1024]{1,0:T(8,128)(2,1)} %get-tuple-element.63.refs_1_, ...), custom_call_target="tpu_custom_call" | custom-call | flops 2483027968 | bytes 15000000 | tf_op jit(solution)/shard_map/joint_grad_send/pallas_call | solution.py:657
  487.3 9.3 %joint_grad_keep.1 = (bf16[2,4,128,512]{3,2,1,0:T(8,128)(2,1)}, bf16[2,4,128,512]{3,2,1,0:T(8,128)(2,1)}) custom-call(s32[4]{0:T(128)} %pad_add_fusion.me_ref, bf16[1184,1024]{1,0:T(8,128)(2,1)} %add_convert_fusion.refs_16_.refs_0_, bf16[1184,1024]{1,0:T(8,128)(2,1)} %get-tuple-element.63.refs_1_, ...), custom_call_target="tpu_custom_call" | custom-call | flops 2483027968 | bytes 15000000 | tf_op jit(solution)/shard_map/joint_grad_keep/pallas_call | solution.py:657
  498.0 8.2 %shrink_grad_keep.1 = (bf16[2,4,128,512]{3,2,1,0:T(8,128)(2,1)}, bf16[2,4,128,512]{3,2,1,0:T(8,128)(2,1)}) custom-call(s32[4]{0:T(128)} %pad_add_fusion.me_ref, bf16[1184,1024]{1,0:T(8,128)(2,1)} %bitcast.335, bf16[1184,4096]{1,0:T(8,128)(2,1)} %get-tuple-element.53.refs_16_.refs_1_.refs_2_, bf16[1184,4096]{1,0:T(8,128)(2,1)} %get-tuple-element.53.refs_16_.refs_1_.refs_2_, ...), custom_call_target="tpu_custom_call" | custom-call | flops 2483027968 | bytes 15000000 | tf_op jit(solution)/shard_map/shrink_grad_keep/pallas_call | solution.py:657
  510.3 8.1 %shrink_grad_send.1 = (bf16[2,4,128,512]{3,2,1,0:T(8,128)(2,1)}, bf16[2,4,128,512]{3,2,1,0:T(8,128)(2,1)}) custom-call(s32[4]{0:T(128)} %pad_add_fusion.me_ref, bf16[1184,1024]{1,0:T(8,128)(2,1)} %bitcast.336, bf16[1184,4096]{1,0:T(8,128)(2,1)} %get-tuple-element.53.refs_16_.refs_1_.refs_2_, bf16[1184,4096]{1,0:T(8,128)(2,1)} %get-tuple-element.53.refs_16_.refs_1_.refs_2_, ...), custom_call_target="tpu_custom_call" | custom-call | flops 2483027968 | bytes 15000000 | tf_op jit(solution)/shard_map/shrink_grad_send/pallas_call | solution.py:657
  529.0 8.2 %expand_grad_send.1 = (bf16[2,4,128,512]{3,2,1,0:T(8,128)(2,1)}, bf16[2,4,128,512]{3,2,1,0:T(8,128)(2,1)}) custom-call(s32[4]{0:T(128)} %pad_add_fusion.me_ref, bf16[1184,1024]{1,0:T(8,128)(2,1)} %get-tuple-element.52.refs_32_.refs_0_, bf16[1184,4096]{1,0:T(8,128)(2,1)} %get-tuple-element.55.refs_32_.refs_1_.refs_2_, ...), custom_call_target="tpu_custom_call" | custom-call | flops 2483027968 | bytes 15000000 | tf_op jit(solution)/shard_map/expand_grad_send/pallas_call | solution.py:657
  537.8 8.4 %expand_grad_keep.1 = (bf16[2,4,128,512]{3,2,1,0:T(8,128)(2,1)}, bf16[2,4,128,512]{3,2,1,0:T(8,128)(2,1)}) custom-call(s32[4]{0:T(128)} %pad_add_fusion.me_ref, bf16[1184,1024]{1,0:T(8,128)(2,1)} %get-tuple-element.52.refs_32_.refs_0_, bf16[1184,4096]{1,0:T(8,128)(2,1)} %get-tuple-element.55.refs_32_.refs_1_.refs_2_, ...), custom_call_target="tpu_custom_call" | custom-call | flops 2483027968 | bytes 15000000 | tf_op jit(solution)/shard_map/expand_grad_keep/pallas_call | solution.py:657
  547.0 2.2 fusion.64
  553.4 2.1 fusion.2
  555.8 2.2 fusion.66
  565.8 2.1 fusion.60
  571.2 2.8 collective-permute-done.82
  574.4 2.1 fusion.4
  580.9 2.3 fusion.62
  585.2 2.1 fusion.7
  606.4 8.8 %collective-permute-done.83 = bf16[2,2,128,512]{3,2,1,0:T(8,128)(2,1)} collective-permute-done((bf16[2,2,128,512]{3,2,1,0:T(8,128)(2,1)}, bf16[2,2,128,512]{3,2,1,0:T(8,128)(2,1)}, u32[]{:S(2)}, u32[]{:S(2)}) %collective-permute-start.83) | collective-permute-done | bytes 524320 | tf_op jit(solution)/shard_map/ppermute | solution.py:72
  618.1 6.4 collective-permute-done.87
  627.7 2.9 collective-permute-start.74
  631.0 2.8 collective-permute-start.99
  634.0 12.8 %collective-permute-done.70 = bf16[128,512]{0,1:T(8,128)(2,1)S(1)} collective-permute-done((bf16[128,512]{0,1:T(8,128)(2,1)S(1)}, bf16[128,512]{0,1:T(8,128)(2,1)S(1)}, u32[]{:S(2)}, u32[]{:S(2)}) %collective-permute-start.70) | collective-permute-done | bytes 131104 | tf_op jit(solution)/shard_map/ppermute | solution.py:72
  646.9 4.2 collective-permute-done.74
  651.1 2.8 collective-permute-done.95
  653.9 2.8 collective-permute-done.99
  657.4 2.1 collective-permute-done.85
  (435 shorter events, 167.0 us)
Async XLA Ops:
  23.2 20.1 %collective-permute-start.51 = (bf16[1,144,512]{2,1,0:T(8,128)(2,1)S(1)}, bf16[1,144,512]{2,1,0:T(8,128)(2,1)S(1)}, u32[]{:S(2)}, u32[]{:S(2)}) collective-permute-start(bf16[1,144,512]{2,1,0:T(8,128)(2,1)S(1)} %fusion.40), channel_id=1, source_target_pairs={{0,2},{1,3},{2,0},{3,1},{4,6},{5,7},{6,4},{7,5},{8,10},{9,11},{10,... | collective-permute-start | bytes 442376 | tf_op jit(solution)/shard_map/ppermute | solution.py:72
  27.2 29.3 %collective-permute-start.46 = (bf16[4,128,512]{2,1,0:T(8,128)(2,1)S(1)}, bf16[4,128,512]{2,1,0:T(8,128)(2,1)S(1)}, u32[]{:S(2)}, u32[]{:S(2)}) collective-permute-start(bf16[4,128,512]{2,1,0:T(8,128)(2,1)S(1)} %constant_dynamic-update-slice_fusion.refs_0_.refs_16_), channel_id=1, source_target_pairs={{0,4},{1,5},{2,6},{3,7},{4,0},{5,1},{6,2},{7,3},{8,12},{9,13},{10,... | collective-permute-start | bytes 1572872 | tf_op jit(solution)/shard_map/ppermute | solution.py:72
  27.2 31.9 %collective-permute-start.44 = (bf16[4,128,512]{2,1,0:T(8,128)(2,1)S(1)}, bf16[4,128,512]{2,1,0:T(8,128)(2,1)S(1)}, u32[]{:S(2)}, u32[]{:S(2)}) collective-permute-start(bf16[4,128,512]{2,1,0:T(8,128)(2,1)S(1)} %constant_dynamic-update-slice_fusion.refs_0_.refs_16_), channel_id=1, source_target_pairs={{0,2},{1,3},{2,0},{3,1},{4,6},{5,7},{6,4},{7,5},{8,10},{9,11},{10,... | collective-permute-start | bytes 1572872 | tf_op jit(solution)/shard_map/ppermute | solution.py:72
  52.2 15.4 %collective-permute-start.43 = (bf16[4,128,512]{2,1,0:T(8,128)(2,1)S(1)}, bf16[4,128,512]{2,1,0:T(8,128)(2,1)S(1)}, u32[]{:S(2)}, u32[]{:S(2)}) collective-permute-start(bf16[4,128,512]{2,1,0:T(8,128)(2,1)S(1)} %constant_dynamic-update-slice_fusion.refs_0_.refs_16_), channel_id=1, source_target_pairs={{0,8},{1,9},{2,10},{3,11},{4,12},{5,13},{6,14},{7,15},{8,0},{9,1},... | collective-permute-start | bytes 1572872 | tf_op jit(solution)/shard_map/ppermute | solution.py:72
  54.9 17.4 %collective-permute-start.26 = (bf16[4,128,512]{2,1,0:T(8,128)(2,1)S(1)}, bf16[4,128,512]{2,1,0:T(8,128)(2,1)S(1)}, u32[]{:S(2)}, u32[]{:S(2)}) collective-permute-start(bf16[4,128,512]{2,1,0:T(8,128)(2,1)S(1)} %pad_maximum_fusion.3.refs_0_), channel_id=1, source_target_pairs={{0,4},{1,5},{2,6},{3,7},{4,0},{5,1},{6,2},{7,3},{8,12},{9,13},{10,... | collective-permute-start | bytes 1572872 | tf_op jit(solution)/shard_map/ppermute | solution.py:72
  56.4 16.5 %collective-permute-start.24 = (bf16[4,128,512]{2,1,0:T(8,128)(2,1)S(1)}, bf16[4,128,512]{2,1,0:T(8,128)(2,1)S(1)}, u32[]{:S(2)}, u32[]{:S(2)}) collective-permute-start(bf16[4,128,512]{2,1,0:T(8,128)(2,1)S(1)} %pad_maximum_fusion.3.refs_0_), channel_id=1, source_target_pairs={{0,2},{1,3},{2,0},{3,1},{4,6},{5,7},{6,4},{7,5},{8,10},{9,11},{10,... | collective-permute-start | bytes 1572872 | tf_op jit(solution)/shard_map/ppermute | solution.py:72
  56.5 22.4 %collective-permute-start.23 = (bf16[4,128,512]{2,1,0:T(8,128)(2,1)S(1)}, bf16[4,128,512]{2,1,0:T(8,128)(2,1)S(1)}, u32[]{:S(2)}, u32[]{:S(2)}) collective-permute-start(bf16[4,128,512]{2,1,0:T(8,128)(2,1)S(1)} %pad_maximum_fusion.3.refs_0_), channel_id=1, source_target_pairs={{0,8},{1,9},{2,10},{3,11},{4,12},{5,13},{6,14},{7,15},{8,0},{9,1},... | collective-permute-start | bytes 1572872 | tf_op jit(solution)/shard_map/ppermute | solution.py:72
  59.9 19.0 %collective-permute-start.36 = (bf16[4,128,512]{2,1,0:T(8,128)(2,1)}, bf16[4,128,512]{2,1,0:T(8,128)(2,1)S(1)}, u32[]{:S(2)}, u32[]{:S(2)}) collective-permute-start(bf16[4,128,512]{2,1,0:T(8,128)(2,1)} %pad_maximum_fusion.4.refs_8_), channel_id=1, source_target_pairs={{0,4},{1,5},{2,6},{3,7},{4,0},{5,1},{6,2},{7,3},{8,12},{9,13},{10,... | collective-permute-start | bytes 1572872 | tf_op jit(solution)/shard_map/ppermute | solution.py:72
  68.5 36.5 %collective-permute-start.53 = (bf16[4,144,512]{2,1,0:T(8,128)(2,1)S(1)}, bf16[4,144,512]{2,1,0:T(8,128)(2,1)}, u32[]{:S(2)}, u32[]{:S(2)}) collective-permute-start(bf16[4,144,512]{2,1,0:T(8,128)(2,1)S(1)} %pad_maximum_fusion.refs_8_.refs_24_), channel_id=1, source_target_pairs={{0,8},{1,9},{2,10},{3,11},{4,12},{5,13},{6,14},{7,15},{8,0},{9,1},... | collective-permute-start | bytes 1769480 | tf_op jit(solution)/shard_map/ppermute | solution.py:72
  72.9 29.9 %collective-permute-start.33 = (bf16[4,128,512]{2,1,0:T(8,128)(2,1)}, bf16[4,128,512]{2,1,0:T(8,128)(2,1)}, u32[]{:S(2)}, u32[]{:S(2)}) collective-permute-start(bf16[4,128,512]{2,1,0:T(8,128)(2,1)} %pad_maximum_fusion.4.refs_8_), channel_id=1, source_target_pairs={{0,8},{1,9},{2,10},{3,11},{4,12},{5,13},{6,14},{7,15},{8,0},{9,1},... | collective-permute-start | bytes 1572872 | tf_op jit(solution)/shard_map/ppermute | solution.py:72
  78.9 24.0 %collective-permute-start.6 = (bf16[4,128,512]{2,1,0:T(8,128)(2,1)}, bf16[4,128,512]{2,1,0:T(8,128)(2,1)}, u32[]{:S(2)}, u32[]{:S(2)}) collective-permute-start(bf16[4,128,512]{2,1,0:T(8,128)(2,1)} %pad_maximum_fusion.1.refs_16_.refs_0_), channel_id=1, source_target_pairs={{0,4},{1,5},{2,6},{3,7},{4,0},{5,1},{6,2},{7,3},{8,12},{9,13},{10,... | collective-permute-start | bytes 1572872 | tf_op jit(solution)/shard_map/ppermute | solution.py:72
  79.7 23.8 %collective-permute-start.4 = (bf16[4,128,512]{2,1,0:T(8,128)(2,1)}, bf16[4,128,512]{2,1,0:T(8,128)(2,1)}, u32[]{:S(2)}, u32[]{:S(2)}) collective-permute-start(bf16[4,128,512]{2,1,0:T(8,128)(2,1)} %pad_maximum_fusion.1.refs_16_.refs_0_), channel_id=1, source_target_pairs={{0,2},{1,3},{2,0},{3,1},{4,6},{5,7},{6,4},{7,5},{8,10},{9,11},{10,... | collective-permute-start | bytes 1572872 | tf_op jit(solution)/shard_map/ppermute | solution.py:72
  84.4 26.3 %collective-permute-start.3 = (bf16[4,128,512]{2,1,0:T(8,128)(2,1)}, bf16[4,128,512]{2,1,0:T(8,128)(2,1)S(1)}, u32[]{:S(2)}, u32[]{:S(2)}) collective-permute-start(bf16[4,128,512]{2,1,0:T(8,128)(2,1)} %pad_maximum_fusion.1.refs_16_.refs_0_), channel_id=1, source_target_pairs={{0,8},{1,9},{2,10},{3,11},{4,12},{5,13},{6,14},{7,15},{8,0},{9,1},... | collective-permute-start | bytes 1572872 | tf_op jit(solution)/shard_map/ppermute | solution.py:72
  102.9 48.7 %collective-permute-start.14 = (bf16[4,128,512]{2,1,0:T(8,128)(2,1)}, bf16[4,128,512]{2,1,0:T(8,128)(2,1)}, u32[]{:S(2)}, u32[]{:S(2)}) collective-permute-start(bf16[4,128,512]{2,1,0:T(8,128)(2,1)} %pad_maximum_fusion.2.refs_24_.refs_8_), channel_id=1, source_target_pairs={{0,1},{1,0},{2,3},{3,2},{4,5},{5,4},{6,7},{7,6},{8,9},{9,8},{10,11... | collective-permute-start | bytes 1572872 | tf_op jit(solution)/shard_map/ppermute | solution.py:72
  103.5 27.0 %collective-permute-start.54 = (bf16[4,144,512]{2,1,0:T(8,128)(2,1)S(1)}, bf16[4,144,512]{2,1,0:T(8,128)(2,1)}, u32[]{:S(2)}, u32[]{:S(2)}) collective-permute-start(bf16[4,144,512]{2,1,0:T(8,128)(2,1)S(1)} %pad_maximum_fusion.refs_8_.refs_24_), channel_id=1, source_target_pairs={{0,1},{1,0},{2,3},{3,2},{4,5},{5,4},{6,7},{7,6},{8,9},{9,8},{10,11... | collective-permute-start | bytes 1769480 | tf_op jit(solution)/shard_map/ppermute | solution.py:72
  104.9 37.9 %collective-permute-start.55 = (bf16[4,144,512]{2,1,0:T(8,128)(2,1)}, bf16[4,144,512]{2,1,0:T(8,128)(2,1)}, u32[]{:S(2)}, u32[]{:S(2)}) collective-permute-start(bf16[4,144,512]{2,1,0:T(8,128)(2,1)} %collective-permute-done.53.refs_9_.refs_25_), channel_id=1, source_target_pairs={{0,1},{1,0},{2,3},{3,2},{4,5},{5,4},{6,7},{7,6},{8,9},{9,8},{10,11... | collective-permute-start | bytes 1769480 | tf_op jit(solution)/shard_map/ppermute | solution.py:72
  110.7 55.8 %collective-permute-start.56 = (bf16[4,144,512]{2,1,0:T(8,128)(2,1)S(1)}, bf16[4,144,512]{2,1,0:T(8,128)(2,1)}, u32[]{:S(2)}, u32[]{:S(2)}) collective-permute-start(bf16[4,144,512]{2,1,0:T(8,128)(2,1)S(1)} %pad_maximum_fusion.refs_8_.refs_24_), channel_id=1, source_target_pairs={{0,4},{1,5},{2,6},{3,7},{4,0},{5,1},{6,2},{7,3},{8,12},{9,13},{10,... | collective-permute-start | bytes 1769480 | tf_op jit(solution)/shard_map/ppermute | solution.py:72
  110.7 57.1 %collective-permute-start.57 = (bf16[4,144,512]{2,1,0:T(8,128)(2,1)}, bf16[4,144,512]{2,1,0:T(8,128)(2,1)}, u32[]{:S(2)}, u32[]{:S(2)}) collective-permute-start(bf16[4,144,512]{2,1,0:T(8,128)(2,1)} %collective-permute-done.53.refs_9_.refs_25_), channel_id=1, source_target_pairs={{0,4},{1,5},{2,6},{3,7},{4,0},{5,1},{6,2},{7,3},{8,12},{9,13},{10,... | collective-permute-start | bytes 1769480 | tf_op jit(solution)/shard_map/ppermute | solution.py:72
  130.6 37.0 %collective-permute-start.58 = (bf16[4,144,512]{2,1,0:T(8,128)(2,1)}, bf16[4,144,512]{2,1,0:T(8,128)(2,1)}, u32[]{:S(2)}, u32[]{:S(2)}) collective-permute-start(bf16[4,144,512]{2,1,0:T(8,128)(2,1)} %collective-permute-done.54.refs_10_.refs_26_), channel_id=1, source_target_pairs={{0,4},{1,5},{2,6},{3,7},{4,0},{5,1},{6,2},{7,3},{8,12},{9,13},{10,... | collective-permute-start | bytes 1769480 | tf_op jit(solution)/shard_map/ppermute | solution.py:72
  142.8 25.3 %collective-permute-start.59 = (bf16[4,144,512]{2,1,0:T(8,128)(2,1)}, bf16[4,144,512]{2,1,0:T(8,128)(2,1)}, u32[]{:S(2)}, u32[]{:S(2)}) collective-permute-start(bf16[4,144,512]{2,1,0:T(8,128)(2,1)} %collective-permute-done.55.refs_11_.refs_27_), channel_id=1, source_target_pairs={{0,4},{1,5},{2,6},{3,7},{4,0},{5,1},{6,2},{7,3},{8,12},{9,13},{10,... | collective-permute-start | bytes 1769480 | tf_op jit(solution)/shard_map/ppermute | solution.py:72
  176.6 15.8 %collective-permute-start.25 = (bf16[4,128,512]{2,1,0:T(8,128)(2,1)}, bf16[4,128,512]{2,1,0:T(8,128)(2,1)}, u32[]{:S(2)}, u32[]{:S(2)}) collective-permute-start(bf16[4,128,512]{2,1,0:T(8,128)(2,1)} %copy-done.39), channel_id=1, source_target_pairs={{0,2},{1,3},{2,0},{3,1},{4,6},{5,7},{6,4},{7,5},{8,10},{9,11},{10,... | collective-permute-start | bytes 1572872 | tf_op jit(solution)/shard_map/ppermute | solution.py:72
  177.6 15.9 %collective-permute-start.37 = (bf16[4,128,512]{2,1,0:T(8,128)(2,1)}, bf16[4,128,512]{2,1,0:T(8,128)(2,1)S(1)}, u32[]{:S(2)}, u32[]{:S(2)}) collective-permute-start(bf16[4,128,512]{2,1,0:T(8,128)(2,1)} %collective-permute-done.33.refs_9_), channel_id=1, source_target_pairs={{0,4},{1,5},{2,6},{3,7},{4,0},{5,1},{6,2},{7,3},{8,12},{9,13},{10,... | collective-permute-start | bytes 1572872 | tf_op jit(solution)/shard_map/ppermute | solution.py:72
  192.4 19.0 %collective-permute-start.7 = (bf16[4,128,512]{2,1,0:T(8,128)(2,1)}, bf16[4,128,512]{2,1,0:T(8,128)(2,1)S(1)}, u32[]{:S(2)}, u32[]{:S(2)}) collective-permute-start(bf16[4,128,512]{2,1,0:T(8,128)(2,1)} %copy-done.36), channel_id=1, source_target_pairs={{0,4},{1,5},{2,6},{3,7},{4,0},{5,1},{6,2},{7,3},{8,12},{9,13},{10,... | collective-permute-start | bytes 1572872 | tf_op jit(solution)/shard_map/ppermute | solution.py:72
  192.4 19.1 %collective-permute-start.5 = (bf16[4,128,512]{2,1,0:T(8,128)(2,1)}, bf16[4,128,512]{2,1,0:T(8,128)(2,1)S(1)}, u32[]{:S(2)}, u32[]{:S(2)}) collective-permute-start(bf16[4,128,512]{2,1,0:T(8,128)(2,1)} %copy-done.36), channel_id=1, source_target_pairs={{0,2},{1,3},{2,0},{3,1},{4,6},{5,7},{6,4},{7,5},{8,10},{9,11},{10,... | collective-permute-start | bytes 1572872 | tf_op jit(solution)/shard_map/ppermute | solution.py:72
  193.5 17.4 %collective-permute-start.8 = (bf16[4,128,512]{2,1,0:T(8,128)(2,1)}, bf16[4,128,512]{2,1,0:T(8,128)(2,1)S(1)}, u32[]{:S(2)}, u32[]{:S(2)}) collective-permute-start(bf16[4,128,512]{2,1,0:T(8,128)(2,1)} %collective-permute-done.4.refs_18_.refs_2_), channel_id=1, source_target_pairs={{0,4},{1,5},{2,6},{3,7},{4,0},{5,1},{6,2},{7,3},{8,12},{9,13},{10,... | collective-permute-start | bytes 1572872 | tf_op jit(solution)/shard_map/ppermute | solution.py:72
  195.0 16.9 %collective-permute-start.18 = (bf16[4,128,512]{2,1,0:T(8,128)(2,1)}, bf16[4,128,512]{2,1,0:T(8,128)(2,1)S(1)}, u32[]{:S(2)}, u32[]{:S(2)}) collective-permute-start(bf16[4,128,512]{2,1,0:T(8,128)(2,1)} %collective-permute-done.14.refs_26_.refs_10_), channel_id=1, source_target_pairs={{0,4},{1,5},{2,6},{3,7},{4,0},{5,1},{6,2},{7,3},{8,12},{9,13},{10,... | collective-permute-start | bytes 1572872 | tf_op jit(solution)/shard_map/ppermute | solution.py:72
  195.0 17.0 %collective-permute-start.15 = (bf16[4,128,512]{2,1,0:T(8,128)(2,1)}, bf16[4,128,512]{2,1,0:T(8,128)(2,1)}, u32[]{:S(2)}, u32[]{:S(2)}) collective-permute-start(bf16[4,128,512]{2,1,0:T(8,128)(2,1)} %collective-permute-done.13.refs_25_.refs_9_), channel_id=1, source_target_pairs={{0,1},{1,0},{2,3},{3,2},{4,5},{5,4},{6,7},{7,6},{8,9},{9,8},{10,11... | collective-permute-start | bytes 1572872 | tf_op jit(solution)/shard_map/ppermute | solution.py:72
  210.8 38.7 %collective-permute-start.17 = (bf16[4,128,512]{2,1,0:T(8,128)(2,1)}, bf16[4,128,512]{2,1,0:T(8,128)(2,1)}, u32[]{:S(2)}, u32[]{:S(2)}) collective-permute-start(bf16[4,128,512]{2,1,0:T(8,128)(2,1)} %collective-permute-done.13.refs_25_.refs_9_), channel_id=1, source_target_pairs={{0,4},{1,5},{2,6},{3,7},{4,0},{5,1},{6,2},{7,3},{8,12},{9,13},{10,... | collective-permute-start | bytes 1572872 | tf_op jit(solution)/shard_map/ppermute | solution.py:72
  211.4 41.3 %collective-permute-start.29 = (bf16[4,128,512]{2,1,0:T(8,128)(2,1)}, bf16[4,128,512]{2,1,0:T(8,128)(2,1)}, u32[]{:S(2)}, u32[]{:S(2)}) collective-permute-start(bf16[4,128,512]{2,1,0:T(8,128)(2,1)} %collective-permute-done.25.refs_3_), channel_id=1, source_target_pairs={{0,4},{1,5},{2,6},{3,7},{4,0},{5,1},{6,2},{7,3},{8,12},{9,13},{10,... | collective-permute-start | bytes 1572872 | tf_op jit(solution)/shard_map/ppermute | solution.py:72
  211.5 41.2 %collective-permute-start.39 = (bf16[4,128,512]{2,1,0:T(8,128)(2,1)}, bf16[4,128,512]{2,1,0:T(8,128)(2,1)}, u32[]{:S(2)}, u32[]{:S(2)}) collective-permute-start(bf16[4,128,512]{2,1,0:T(8,128)(2,1)} %collective-permute-done.35.refs_11_), channel_id=1, source_target_pairs={{0,4},{1,5},{2,6},{3,7},{4,0},{5,1},{6,2},{7,3},{8,12},{9,13},{10,... | collective-permute-start | bytes 1572872 | tf_op jit(solution)/shard_map/ppermute | solution.py:72
  211.9 40.7 %collective-permute-start.9 = (bf16[4,128,512]{2,1,0:T(8,128)(2,1)S(1)}, bf16[4,128,512]{2,1,0:T(8,128)(2,1)}, u32[]{:S(2)}, u32[]{:S(2)}) collective-permute-start(bf16[4,128,512]{2,1,0:T(8,128)(2,1)S(1)} %collective-permute-done.5.refs_19_.refs_3_), channel_id=1, source_target_pairs={{0,4},{1,5},{2,6},{3,7},{4,0},{5,1},{6,2},{7,3},{8,12},{9,13},{10,... | collective-permute-start | bytes 1572872 | tf_op jit(solution)/shard_map/ppermute | solution.py:72
  212.0 40.7 %collective-permute-start.19 = (bf16[4,128,512]{2,1,0:T(8,128)(2,1)}, bf16[4,128,512]{2,1,0:T(8,128)(2,1)}, u32[]{:S(2)}, u32[]{:S(2)}) collective-permute-start(bf16[4,128,512]{2,1,0:T(8,128)(2,1)} %collective-permute-done.15.refs_27_.refs_11_), channel_id=1, source_target_pairs={{0,4},{1,5},{2,6},{3,7},{4,0},{5,1},{6,2},{7,3},{8,12},{9,13},{10,... | collective-permute-start | bytes 1572872 | tf_op jit(solution)/shard_map/ppermute | solution.py:72
  249.6 143.0 %collective-permute-start.100 = (f32[16,128]{0,1:T(8,128)S(1)}, f32[16,128]{0,1:T(8,128)S(1)}, u32[]{:S(2)}, u32[]{:S(2)}) collective-permute-start(f32[16,128]{0,1:T(8,128)S(1)} %broadcast_in_dim.85), channel_id=1, source_target_pairs={{0,16},{1,17},{2,18},{3,19},{4,20},{5,21},{6,22},{7,23},{8,24},{9,... | collective-permute-start | bytes 24584 | tf_op jit(solution)/shard_map/ppermute | solution.py:72
  377.3 69.1 %collective-permute-start.60 = (f32[32,128]{1,0:T(8,128)S(1)}, f32[32,128]{1,0:T(8,128)S(1)}, u32[]{:S(2)}, u32[]{:S(2)}) collective-permute-start(f32[32,128]{1,0:T(8,128)S(1)} %constant_dynamic-update-slice_fusion.4), channel_id=1, source_target_pairs={{0,16},{1,17},{2,18},{3,19},{4,20},{5,21},{6,22},{7,23},{8,24},{9,... | collective-permute-start | bytes 49160 | tf_op jit(solution)/shard_map/ppermute | solution.py:72
  377.4 70.7 %collective-permute-start.75 = (f32[64,128]{1,0:T(8,128)S(1)}, f32[64,128]{1,0:T(8,128)S(1)}, u32[]{:S(2)}, u32[]{:S(2)}) collective-permute-start(f32[64,128]{1,0:T(8,128)S(1)} %pad_maximum_fusion.7), channel_id=1, source_target_pairs={{0,16},{1,17},{2,18},{3,19},{4,20},{5,21},{6,22},{7,23},{8,24},{9,... | collective-permute-start | bytes 98312 | tf_op jit(solution)/shard_map/ppermute | solution.py:72
  392.5 83.1 %collective-permute-start.65 = (bf16[4,4,128,512]{3,2,1,0:T(8,128)(2,1)}, bf16[4,4,128,512]{3,2,1,0:T(8,128)(2,1)}, u32[]{:S(2)}, u32[]{:S(2)}) collective-permute-start(bf16[4,4,128,512]{3,2,1,0:T(8,128)(2,1)} %get-tuple-element.64), channel_id=1, source_target_pairs={{0,4},{1,5},{2,6},{3,7},{4,0},{5,1},{6,2},{7,3},{8,12},{9,13},{10,... | collective-permute-start | bytes 6291464 | tf_op jit(solution)/shard_map/ppermute | solution.py:72
  392.6 20.9 %collective-permute-start.101 = (f32[16,128]{0,1:T(8,128)S(1)}, f32[16,128]{0,1:T(8,128)S(1)}, u32[]{:S(2)}, u32[]{:S(2)}) collective-permute-start(f32[16,128]{0,1:T(8,128)S(1)} %broadcast_maximum_fusion), channel_id=1, source_target_pairs={{0,1},{1,0},{2,3},{3,2},{4,5},{5,4},{6,7},{7,6},{8,9},{9,8},{10,11... | collective-permute-start | bytes 24584 | tf_op jit(solution)/shard_map/ppermute | solution.py:72
  426.2 20.7 %collective-permute-start.103 = (f32[16,128]{0,1:T(8,128)S(1)}, f32[16,128]{0,1:T(8,128)S(1)}, u32[]{:S(2)}, u32[]{:S(2)}) collective-permute-start(f32[16,128]{0,1:T(8,128)S(1)} %max.20), channel_id=1, source_target_pairs={{0,2},{1,3},{2,0},{3,1},{4,6},{5,7},{6,4},{7,5},{8,10},{9,11},{10,... | collective-permute-start | bytes 24584 | tf_op jit(solution)/shard_map/ppermute | solution.py:72
  446.4 31.0 %collective-permute-start.66 = (bf16[4,4,128,512]{3,2,1,0:T(8,128)(2,1)}, bf16[4,4,128,512]{3,2,1,0:T(8,128)(2,1)}, u32[]{:S(2)}, u32[]{:S(2)}) collective-permute-start(bf16[4,4,128,512]{3,2,1,0:T(8,128)(2,1)} %get-tuple-element.65), channel_id=1, source_target_pairs={{0,4},{1,5},{2,6},{3,7},{4,0},{5,1},{6,2},{7,3},{8,12},{9,13},{10,... | collective-permute-start | bytes 6291464 | tf_op jit(solution)/shard_map/ppermute | solution.py:72
  446.4 50.2 %collective-permute-start.90 = (bf16[4,4,128,512]{3,2,1,0:T(8,128)(2,1)}, bf16[4,4,128,512]{3,2,1,0:T(8,128)(2,1)S(1)}, u32[]{:S(2)}, u32[]{:S(2)}) collective-permute-start(bf16[4,4,128,512]{3,2,1,0:T(8,128)(2,1)} %get-tuple-element.78), channel_id=1, source_target_pairs={{0,4},{1,5},{2,6},{3,7},{4,0},{5,1},{6,2},{7,3},{8,12},{9,13},{10,... | collective-permute-start | bytes 6291464 | tf_op jit(solution)/shard_map/ppermute | solution.py:72
  450.7 47.2 %collective-permute-start.91 = (bf16[4,4,128,512]{3,2,1,0:T(8,128)(2,1)}, bf16[4,4,128,512]{3,2,1,0:T(8,128)(2,1)}, u32[]{:S(2)}, u32[]{:S(2)}) collective-permute-start(bf16[4,4,128,512]{3,2,1,0:T(8,128)(2,1)} %get-tuple-element.79), channel_id=1, source_target_pairs={{0,4},{1,5},{2,6},{3,7},{4,0},{5,1},{6,2},{7,3},{8,12},{9,13},{10,... | collective-permute-start | bytes 6291464 | tf_op jit(solution)/shard_map/ppermute | solution.py:72
  475.4 52.6 %collective-permute-start.80 = (bf16[4,4,128,512]{3,2,1,0:T(8,128)(2,1)}, bf16[4,4,128,512]{3,2,1,0:T(8,128)(2,1)}, u32[]{:S(2)}, u32[]{:S(2)}) collective-permute-start(bf16[4,4,128,512]{3,2,1,0:T(8,128)(2,1)} %get-tuple-element.72), channel_id=1, source_target_pairs={{0,4},{1,5},{2,6},{3,7},{4,0},{5,1},{6,2},{7,3},{8,12},{9,13},{10,... | collective-permute-start | bytes 6291464 | tf_op jit(solution)/shard_map/ppermute | solution.py:72
  475.6 53.4 %collective-permute-start.81 = (bf16[4,4,128,512]{3,2,1,0:T(8,128)(2,1)}, bf16[4,4,128,512]{3,2,1,0:T(8,128)(2,1)}, u32[]{:S(2)}, u32[]{:S(2)}) collective-permute-start(bf16[4,4,128,512]{3,2,1,0:T(8,128)(2,1)} %get-tuple-element.73), channel_id=1, source_target_pairs={{0,4},{1,5},{2,6},{3,7},{4,0},{5,1},{6,2},{7,3},{8,12},{9,13},{10,... | collective-permute-start | bytes 6291464 | tf_op jit(solution)/shard_map/ppermute | solution.py:72
  486.9 59.4 %collective-permute-start.67 = (bf16[2,4,128,512]{3,2,1,0:T(8,128)(2,1)}, bf16[2,4,128,512]{3,2,1,0:T(8,128)(2,1)}, u32[]{:S(2)}, u32[]{:S(2)}) collective-permute-start(bf16[2,4,128,512]{3,2,1,0:T(8,128)(2,1)} %get-tuple-element.67), channel_id=1, source_target_pairs={{0,2},{1,3},{2,0},{3,1},{4,6},{5,7},{6,4},{7,5},{8,10},{9,11},{10,... | collective-permute-start | bytes 3145736 | tf_op jit(solution)/shard_map/ppermute | solution.py:72
  496.6 58.9 %collective-permute-start.71 = (bf16[2,4,128,512]{3,2,1,0:T(8,128)(2,1)}, bf16[2,4,128,512]{3,2,1,0:T(8,128)(2,1)}, u32[]{:S(2)}, u32[]{:S(2)}) collective-permute-start(bf16[2,4,128,512]{3,2,1,0:T(8,128)(2,1)} %get-tuple-element.69), channel_id=1, source_target_pairs={{0,1},{1,0},{2,3},{3,2},{4,5},{5,4},{6,7},{7,6},{8,9},{9,8},{10,11... | collective-permute-start | bytes 3145736 | tf_op jit(solution)/shard_map/ppermute | solution.py:72
  526.2 37.9 %collective-permute-start.92 = (bf16[2,4,128,512]{3,2,1,0:T(8,128)(2,1)}, bf16[2,4,128,512]{3,2,1,0:T(8,128)(2,1)}, u32[]{:S(2)}, u32[]{:S(2)}) collective-permute-start(bf16[2,4,128,512]{3,2,1,0:T(8,128)(2,1)} %get-tuple-element.81), channel_id=1, source_target_pairs={{0,2},{1,3},{2,0},{3,1},{4,6},{5,7},{6,4},{7,5},{8,10},{9,11},{10,... | collective-permute-start | bytes 3145736 | tf_op jit(solution)/shard_map/ppermute | solution.py:72
  528.0 52.9 %collective-permute-start.96 = (bf16[2,4,128,512]{3,2,1,0:T(8,128)(2,1)}, bf16[2,4,128,512]{3,2,1,0:T(8,128)(2,1)}, u32[]{:S(2)}, u32[]{:S(2)}) collective-permute-start(bf16[2,4,128,512]{3,2,1,0:T(8,128)(2,1)} %get-tuple-element.83), channel_id=1, source_target_pairs={{0,1},{1,0},{2,3},{3,2},{4,5},{5,4},{6,7},{7,6},{8,9},{9,8},{10,11... | collective-permute-start | bytes 3145736 | tf_op jit(solution)/shard_map/ppermute | solution.py:72
  537.2 36.8 %collective-permute-start.82 = (bf16[2,4,128,512]{3,2,1,0:T(8,128)(2,1)}, bf16[2,4,128,512]{3,2,1,0:T(8,128)(2,1)}, u32[]{:S(2)}, u32[]{:S(2)}) collective-permute-start(bf16[2,4,128,512]{3,2,1,0:T(8,128)(2,1)} %get-tuple-element.75), channel_id=1, source_target_pairs={{0,2},{1,3},{2,0},{3,1},{4,6},{5,7},{6,4},{7,5},{8,10},{9,11},{10,... | collective-permute-start | bytes 3145736 | tf_op jit(solution)/shard_map/ppermute | solution.py:72
  546.2 31.4 %collective-permute-start.86 = (bf16[2,4,128,512]{3,2,1,0:T(8,128)(2,1)}, bf16[2,4,128,512]{3,2,1,0:T(8,128)(2,1)}, u32[]{:S(2)}, u32[]{:S(2)}) collective-permute-start(bf16[2,4,128,512]{3,2,1,0:T(8,128)(2,1)} %get-tuple-element.77), channel_id=1, source_target_pairs={{0,1},{1,0},{2,3},{3,2},{4,5},{5,4},{6,7},{7,6},{8,9},{9,8},{10,11... | collective-permute-start | bytes 3145736 | tf_op jit(solution)/shard_map/ppermute | solution.py:72
  555.5 38.6 %collective-permute-start.68 = (bf16[2,2,128,512]{2,3,1,0:T(8,128)(2,1)}, bf16[2,2,128,512]{2,3,1,0:T(8,128)(2,1)}, u32[]{:S(2)}, u32[]{:S(2)}) collective-permute-start(bf16[2,2,128,512]{2,3,1,0:T(8,128)(2,1)} %fusion.2), channel_id=1, source_target_pairs={{0,8},{1,9},{2,10},{3,11},{4,12},{5,13},{6,14},{7,15},{8,0},{9,1},... | collective-permute-start | bytes 1572872 | tf_op jit(solution)/shard_map/ppermute | solution.py:72
  564.1 32.9 %collective-permute-start.72 = (bf16[2,2,128,512]{2,3,1,0:T(8,128)(2,1)}, bf16[2,2,128,512]{2,3,1,0:T(8,128)(2,1)}, u32[]{:S(2)}, u32[]{:S(2)}) collective-permute-start(bf16[2,2,128,512]{2,3,1,0:T(8,128)(2,1)} %fusion.3), channel_id=1, source_target_pairs={{0,8},{1,9},{2,10},{3,11},{4,12},{5,13},{6,14},{7,15},{8,0},{9,1},... | collective-permute-start | bytes 1572872 | tf_op jit(solution)/shard_map/ppermute | solution.py:72
  574.0 25.5 %collective-permute-start.93 = (bf16[2,2,128,512]{2,3,1,0:T(8,128)(2,1)}, bf16[2,2,128,512]{2,3,1,0:T(8,128)(2,1)}, u32[]{:S(2)}, u32[]{:S(2)}) collective-permute-start(bf16[2,2,128,512]{2,3,1,0:T(8,128)(2,1)} %fusion.6), channel_id=1, source_target_pairs={{0,8},{1,9},{2,10},{3,11},{4,12},{5,13},{6,14},{7,15},{8,0},{9,1},... | collective-permute-start | bytes 1572872 | tf_op jit(solution)/shard_map/ppermute | solution.py:72
  587.3 16.7 %collective-permute-start.97 = (bf16[2,2,128,512]{2,3,1,0:T(8,128)(2,1)}, bf16[2,2,128,512]{2,3,1,0:T(8,128)(2,1)}, u32[]{:S(2)}, u32[]{:S(2)}) collective-permute-start(bf16[2,2,128,512]{2,3,1,0:T(8,128)(2,1)} %fusion.7), channel_id=1, source_target_pairs={{0,8},{1,9},{2,10},{3,11},{4,12},{5,13},{6,14},{7,15},{8,0},{9,1},... | collective-permute-start | bytes 1572872 | tf_op jit(solution)/shard_map/ppermute | solution.py:72
  589.0 26.2 %collective-permute-start.83 = (bf16[2,2,128,512]{3,2,1,0:T(8,128)(2,1)}, bf16[2,2,128,512]{3,2,1,0:T(8,128)(2,1)}, u32[]{:S(2)}, u32[]{:S(2)}) collective-permute-start(bf16[2,2,128,512]{3,2,1,0:T(8,128)(2,1)} %fusion.4), channel_id=1, source_target_pairs={{0,8},{1,9},{2,10},{3,11},{4,12},{5,13},{6,14},{7,15},{8,0},{9,1},... | collective-permute-start | bytes 1572872 | tf_op jit(solution)/shard_map/ppermute | solution.py:72
  594.1 30.4 %collective-permute-start.87 = (bf16[2,2,128,512]{3,2,1,0:T(8,128)(2,1)}, bf16[2,2,128,512]{3,2,1,0:T(8,128)(2,1)S(1)}, u32[]{:S(2)}, u32[]{:S(2)}) collective-permute-start(bf16[2,2,128,512]{3,2,1,0:T(8,128)(2,1)} %fusion.5), channel_id=1, source_target_pairs={{0,8},{1,9},{2,10},{3,11},{4,12},{5,13},{6,14},{7,15},{8,0},{9,1},... | collective-permute-start | bytes 1572872 | tf_op jit(solution)/shard_map/ppermute | solution.py:72
  597.1 28.8 %collective-permute-start.69 = (bf16[2,128,512]{1,2,0:T(8,128)(2,1)S(1)}, bf16[2,128,512]{1,2,0:T(8,128)(2,1)S(1)}, u32[]{:S(2)}, u32[]{:S(2)}) collective-permute-start(bf16[2,128,512]{1,2,0:T(8,128)(2,1)S(1)} %get-tuple-element.255), channel_id=1, source_target_pairs={{0,1},{1,0},{2,3},{3,2},{4,5},{5,4},{6,7},{7,6},{8,9},{9,8},{10,11... | collective-permute-start | bytes 786440 | tf_op jit(solution)/shard_map/ppermute | solution.py:72
  599.6 27.9 %collective-permute-start.73 = (bf16[2,128,512]{1,2,0:T(8,128)(2,1)S(1)}, bf16[2,128,512]{1,2,0:T(8,128)(2,1)S(1)}, u32[]{:S(2)}, u32[]{:S(2)}) collective-permute-start(bf16[2,128,512]{1,2,0:T(8,128)(2,1)S(1)} %get-tuple-element.261), channel_id=1, source_target_pairs={{0,2},{1,3},{2,0},{3,1},{4,6},{5,7},{6,4},{7,5},{8,10},{9,11},{10,... | collective-permute-start | bytes 786440 | tf_op jit(solution)/shard_map/ppermute | solution.py:72
  604.0 23.7 %collective-permute-start.94 = (bf16[2,128,512]{1,2,0:T(8,128)(2,1)S(1)}, bf16[2,128,512]{1,2,0:T(8,128)(2,1)S(1)}, u32[]{:S(2)}, u32[]{:S(2)}) collective-permute-start(bf16[2,128,512]{1,2,0:T(8,128)(2,1)S(1)} %get-tuple-element.239), channel_id=1, source_target_pairs={{0,1},{1,0},{2,3},{3,2},{4,5},{5,4},{6,7},{7,6},{8,9},{9,8},{10,11... | collective-permute-start | bytes 786440 | tf_op jit(solution)/shard_map/ppermute | solution.py:72
  615.2 15.4 %collective-permute-start.98 = (bf16[2,128,512]{1,2,0:T(8,128)(2,1)S(1)}, bf16[2,128,512]{1,2,0:T(8,128)(2,1)S(1)}, u32[]{:S(2)}, u32[]{:S(2)}) collective-permute-start(bf16[2,128,512]{1,2,0:T(8,128)(2,1)S(1)} %get-tuple-element.245), channel_id=1, source_target_pairs={{0,2},{1,3},{2,0},{3,1},{4,6},{5,7},{6,4},{7,5},{8,10},{9,11},{10,... | collective-permute-start | bytes 786440 | tf_op jit(solution)/shard_map/ppermute | solution.py:72
  627.5 19.4 %collective-permute-start.70 = (bf16[128,512]{0,1:T(8,128)(2,1)S(1)}, bf16[128,512]{0,1:T(8,128)(2,1)S(1)}, u32[]{:S(2)}, u32[]{:S(2)}) collective-permute-start(bf16[128,512]{0,1:T(8,128)(2,1)S(1)} %fusion.42), channel_id=1, source_target_pairs={{0,16},{1,17},{2,18},{3,19},{4,20},{5,21},{6,22},{7,23},{8,24},{9,... | collective-permute-start | bytes 393224 | tf_op jit(solution)/shard_map/ppermute | solution.py:72
  627.7 23.4 %collective-permute-start.74 = (bf16[128,512]{0,1:T(8,128)(2,1)S(1)}, bf16[128,512]{0,1:T(8,128)(2,1)S(1)}, u32[]{:S(2)}, u32[]{:S(2)}) collective-permute-start(bf16[128,512]{0,1:T(8,128)(2,1)S(1)} %fusion.44), channel_id=1, source_target_pairs={{0,16},{1,17},{2,18},{3,19},{4,20},{5,21},{6,22},{7,23},{8,24},{9,... | collective-permute-start | bytes 393224 | tf_op jit(solution)/shard_map/ppermute | solution.py:72
  630.6 23.2 %collective-permute-start.95 = (bf16[128,512]{0,1:T(8,128)(2,1)S(1)}, bf16[128,512]{0,1:T(8,128)(2,1)S(1)}, u32[]{:S(2)}, u32[]{:S(2)}) collective-permute-start(bf16[128,512]{0,1:T(8,128)(2,1)S(1)} %fusion.50), channel_id=1, source_target_pairs={{0,16},{1,17},{2,18},{3,19},{4,20},{5,21},{6,22},{7,23},{8,24},{9,... | collective-permute-start | bytes 393224 | tf_op jit(solution)/shard_map/ppermute | solution.py:72
  631.0 25.7 %collective-permute-start.99 = (bf16[128,512]{0,1:T(8,128)(2,1)S(1)}, bf16[128,512]{0,1:T(8,128)(2,1)S(1)}, u32[]{:S(2)}, u32[]{:S(2)}) collective-permute-start(bf16[128,512]{0,1:T(8,128)(2,1)S(1)} %fusion.52), channel_id=1, source_target_pairs={{0,16},{1,17},{2,18},{3,19},{4,20},{5,21},{6,22},{7,23},{8,24},{9,... | collective-permute-start | bytes 393224 | tf_op jit(solution)/shard_map/ppermute | solution.py:72
  633.8 25.7 %collective-permute-start.85 = (bf16[128,512]{1,0:T(8,128)(2,1)S(1)}, bf16[128,512]{1,0:T(8,128)(2,1)S(1)}, u32[]{:S(2)}, u32[]{:S(2)}) collective-permute-start(bf16[128,512]{1,0:T(8,128)(2,1)S(1)} %fusion.46), channel_id=1, source_target_pairs={{0,16},{1,17},{2,18},{3,19},{4,20},{5,21},{6,22},{7,23},{8,24},{9,... | collective-permute-start | bytes 393224 | tf_op jit(solution)/shard_map/ppermute | solution.py:72
  (87 other events, 1204.2 us)

commit v2 on v0

v2 whole, which is shorter than its diff:
```python
from functools import partial

import jax
import jax.numpy as jnp
from jax import lax
from jax.experimental import pallas as pl
from jax.experimental.pallas import tpu as pltpu
from jax.sharding import PartitionSpec as P

D = 1024
FF = 4096
HEADS = 16
HEAD_DIM = 64
SEQ = 577
SP = 592
LP = 640
LOG2E = 1.4426950408889634
NEG = -1e30
BF = jnp.bfloat16
F32 = jnp.float32
AXES = ("dp", "tensor")
VMEM_LIMIT = 60 * 2**20


def dotf(a, b, ca, cb):
    return lax.dot_general(a, b, (((ca,), (cb,)), ((), ())), preferred_element_type=F32)


def whole(shape):
    zeros = (0,) * len(shape)
    return pl.BlockSpec(shape, lambda *_: zeros)


ANY = pl.BlockSpec(memory_space=pl.ANY)


class Runner:
    def __init__(self, me):
        self.me = me
        self.token = jnp.zeros((8, 128), F32)

    def __call__(self, name, us, kernel, grid, ins, outs, scratch=(), through=()):
        n_in, n_out = len(ins), len(outs)
        through = [self.token] + list(through)
        n = len(through)

        def body(me_ref, *refs):
            first = refs[:n_in]
            second = refs[n_in + n : n_in + n + n_out]
            kernel(me_ref, *first, *second, *refs[n_in + 2 * n + n_out :])

        got = pl.pallas_call(
            body,
            grid_spec=pltpu.PrefetchScalarGridSpec(
                num_scalar_prefetch=1,
                grid=grid,
                in_specs=[spec for _, spec in ins] + [ANY] * n,
                out_specs=[spec for _, spec in outs] + [ANY] * n,
                scratch_shapes=list(scratch),
            ),
            out_shape=[shape for shape, _ in outs] + [jax.ShapeDtypeStruct(a.shape, a.dtype) for a in through],
            input_output_aliases={1 + n_in + i: n_out + i for i in range(n)},
            compiler_params=pltpu.CompilerParams(vmem_limit_bytes=VMEM_LIMIT),
            cost_estimate=pl.CostEstimate(flops=int(2e11), bytes_accessed=int(2e8), transcendentals=0),
            name=name,
        )(self.me, *[a for a, _ in ins], *through)
        self.token = got[n_out]
        return got[:n_out], got[n_out + 1 :]


class Layout:
    def __init__(self, ndp, nt):
        self.ndp, self.nt, self.nz = ndp, nt, ndp // 2
        self.size = ndp * nt
        self.rows = D // ndp
        self.cols = FF // nt
        self.tbits = nt.bit_length() - 1
        self.zbits = self.nz.bit_length() - 1
        self.core = nt
        self.cw = D // nt


def stage_mask(lay, bit):
    kind, b = bit
    return (1 << b) if kind == "t" else (lay.nt * 2) << b


def swap(x, mask, size):
    return lax.ppermute(x, AXES, [(i, i ^ mask) for i in range(size)])


class Gather:
    def __init__(self, lay, piece):
        self.lay = lay
        self.held = piece[None]

    def along(self):
        step = 2 * self.lay.nt
        self.got = [self.held] + [swap(self.held, z * step, self.lay.size) for z in range(1, self.lay.nz)]

    def spread(self):
        self.held = jnp.concatenate(self.got)
        self.got = [self.held] + [swap(self.held, t, self.lay.size) for t in range(1, self.lay.nt)]
        self.other = [swap(self.held, self.lay.core, self.lay.size)]

    def share(self):
        lay = self.lay
        self.bufs = self.got + self.other + [swap(b, lay.core, lay.size) for b in self.got[1:]]
        self.pieces = [(c * lay.nt + t, z, z, t, c) for c in range(2) for t in range(lay.nt) for z in range(lay.nz)]


class Chain:
    def __init__(self, lay, piece, reverse):
        self.lay = lay
        z = [("z", b) for b in reversed(range(lay.zbits))]
        t = [("t", b) for b in range(lay.tbits)]
        t = t[::-1] if reverse else t
        self.stages = []
        while z or t:
            self.stages.append(z.pop(0) if z and len(z) >= len(t) else t.pop(0))
        self.held, self.offs = piece[None], [(0, 0)]

    def send(self):
        self.got = swap(self.held, stage_mask(self.lay, self.stages[0]), self.lay.size)

    def land(self):
        kind, b = self.stages.pop(0)
        dz, dt = ((1 << b), 0) if kind == "z" else (0, (1 << b))
        self.offs = self.offs + [(z ^ dz, t ^ dt) for z, t in self.offs]
        self.held = jnp.concatenate([self.held, self.got])

    def share(self):
        self.bufs = [self.held, swap(self.held, self.lay.core, self.lay.size)]
        self.pieces = [(c, i, z, t, c) for c in range(2) for i, (z, t) in enumerate(self.offs)]


class Shards:
    def __init__(self, lay, piece):
        self.bufs = [lax.all_gather(piece, AXES)]


def gate(run, *lists):
    flat = [x for some in lists for x in some]
    _, flat = run("gate", 0.5, lambda *refs: None, (1,), [], [], (), flat)
    flat = list(flat)
    return [[flat.pop(0) for _ in some] for some in lists]


def start_pieces(lay, group, bufs, me_ref, spans, sem, keep=None):
    me = (me_ref[0], me_ref[1], me_ref[2])
    if isinstance(group, Shards):
        pieces = [(0, dp * lay.nt + t, dp * lay.rows, t ^ me[2], t) for t in range(lay.nt) for dp in range(lay.ndp)]
    else:
        pieces = []
        for b, i, z, t, c in group.pieces:
            if keep is None or keep(t):
                row = pl.multiple_of(((z ^ me[0]) * 2 + (c ^ me[1])) * lay.rows, lay.rows)
                pieces.append((b, i, row, t, t ^ me[2]))
    for b, i, row, to, t in pieces:
        for first, width, place in spans:
            ref, at = place(to, t)
            if not isinstance(at, int):
                at = pl.multiple_of(at, 128)
            pltpu.make_async_copy(
                bufs[b].at[i, pl.ds(0, lay.rows), pl.ds(first, width)],
                ref.at[pl.ds(row, lay.rows), pl.ds(at, width)],
                sem(to),
            ).start()


def wait_all(ref, sem):
    pltpu.make_async_copy(ref, ref, sem).wait()


def flip(x):
    pad = jnp.zeros((LP - x.shape[0], x.shape[1]), x.dtype)
    return jnp.concatenate([x, pad], axis=0).T


def key_rows():
    row = lax.broadcasted_iota(jnp.int32, (16, LP), 0)
    lane = lax.broadcasted_iota(jnp.int32, (16, LP), 1)
    return jnp.where(row < 3, 1.0, jnp.where((row == 3) & (lane >= SEQ), NEG, 0.0)).astype(BF)


def split_rows(v):
    row = lax.broadcasted_iota(jnp.int32, (16, LP), 0)
    hi = v.astype(BF).astype(F32)
    mid = (v - hi).astype(BF).astype(F32)
    lo = v - hi - mid
    rest = jnp.where(row == 2, lo, jnp.where(row == 3, 1.0, 0.0))
    return jnp.where(row == 0, hi, jnp.where(row == 1, mid, rest)).astype(BF)


def split_query(q):
    v = q.astype(F32) * LOG2E
    hi = v.astype(BF)
    return hi, (v - hi.astype(F32)).astype(BF)


def attend_kernel(hl, p_ref, o_ref, lse_ref, top_ref):
    cw = hl * HEAD_DIM
    xt = flip(p_ref[...])
    aux = key_rows()
    none = split_rows(jnp.zeros((1, LP), F32))
    first = lax.broadcasted_iota(jnp.int32, (16, LP), 0) == 0
    ones = jnp.where(first, 1.0, 0.0).astype(BF)
    valid = lax.broadcasted_iota(jnp.int32, (1, LP), 1) < SEQ
    outs = []
    for h in range(hl):
        q = xt[h * HEAD_DIM : (h + 1) * HEAD_DIM]
        k = xt[cw + h * HEAD_DIM : cw + (h + 1) * HEAD_DIM]
        v = xt[2 * cw + h * HEAD_DIM : 2 * cw + (h + 1) * HEAD_DIM]
        hi, lo = split_query(q)
        s = dotf(jnp.concatenate([k, k, aux], 0), jnp.concatenate([hi, lo, none], 0), 0, 0)
        m = jnp.max(s, axis=0, keepdims=True)
        p = jnp.exp2(s - m).astype(BF)
        o = dotf(jnp.concatenate([v, ones], 0), p, 1, 0)
        total = o[HEAD_DIM : HEAD_DIM + 1]
        outs.append((o[:HEAD_DIM] / total).astype(BF))
        lse_ref[0, 0, h : h + 1, :] = m + jnp.log2(total)
        top_ref[0, 0, h : h + 1, :] = jnp.where(valid, m, NEG)
    o_ref[...] = jnp.concatenate(outs, 0).T[:SP]


def attend_back_kernel(hl, p_ref, o_ref, g_ref, lse_ref, d_ref, sum_ref):
    cw = hl * HEAD_DIM
    xt = flip(p_ref[...])
    ot = flip(o_ref[...])
    gt = flip(g_ref[...])
    aux = key_rows()
    ones = jnp.where(lax.broadcasted_iota(jnp.int32, (16, LP), 0) < 3, 1.0, 0.0).astype(BF)
    dq, dk, dv = [], [], []
    for h in range(hl):
        at = slice(h * HEAD_DIM, (h + 1) * HEAD_DIM)
        q = xt[at]
        k = xt[cw + h * HEAD_DIM : cw + (h + 1) * HEAD_DIM]
        v = xt[2 * cw + h * HEAD_DIM : 2 * cw + (h + 1) * HEAD_DIM]
        g = gt[at]
        hi, lo = split_query(q)
        delta = jnp.sum(ot[at].astype(F32) * g.astype(F32), axis=0, keepdims=True)
        minus = split_rows(-lse_ref[0, 0, h : h + 1, :])
        s = dotf(jnp.concatenate([k, k, aux], 0), jnp.concatenate([hi, lo, minus], 0), 0, 0)
        p = jnp.exp2(s)
        d = dotf(jnp.concatenate([v, ones], 0), jnp.concatenate([g, split_rows(-delta)], 0), 0, 0)
        ds = (p * d).astype(BF)
        dv.append(dotf(g, p.astype(BF), 1, 1).astype(BF))
        dq.append((HEAD_DIM**-0.5 * dotf(k, ds, 1, 0)).astype(BF))
        dk.append(dotf(q, ds, 1, 1).astype(BF))
    out = jnp.concatenate(dq + dk + dv, 0).T[:SP]
    d_ref[...] = out
    sum_ref[0, 0, :, :] = jnp.sum(out.astype(F32), axis=0, keepdims=True)


def unit_of(values):
    center = values - jnp.mean(values, axis=-1, keepdims=True)
    inverse = lax.rsqrt(jnp.mean(center * center, axis=-1, keepdims=True) + 1e-05)
    return center * inverse, inverse


def norm_back(grad, unit, inverse, gain):
    scaled = grad * gain
    inner = (
        scaled
        - jnp.mean(scaled, axis=-1, keepdims=True)
        - unit * jnp.mean(scaled * unit, axis=-1, keepdims=True)
    )
    return inner * inverse


def add_rows(ref, rows):
    step = pl.program_id(0)

    @pl.when(step == 0)
    def _():
        for r, row in enumerate(rows):
            ref[r : r + 1, :] = row

    @pl.when(step > 0)
    def _():
        for r, row in enumerate(rows):
            ref[r : r + 1, :] += row


def column_sum(x):
    return jnp.sum(x, axis=0, keepdims=True)


def row_block(width):
    return pl.BlockSpec((SP, width), lambda i, m: (i, 0))


def one_row(width):
    return pl.BlockSpec((1, width), lambda i, m: (0, 0))


def put_pieces(lay, me_ref, y, other, own, first=0):
    dr, width = lay.rows, y.shape[1]
    cs = pl.ds(first, width)
    y = y.astype(BF)
    for c in range(2):

        @pl.when(me_ref[1] == c)
        def _(c=c):
            for z in range(lay.nz):
                at = z ^ me_ref[0]
                a, b = (2 * z + c) * dr, (2 * z + 1 - c) * dr
                own[0, at, :, cs] = y[a : a + dr]
                other[0, at, :, cs] = y[b : b + dr]


def piece_out(lay, width):
    return (
        jax.ShapeDtypeStruct((lay.nt, lay.nz, lay.rows, width), BF),
        pl.BlockSpec((1, lay.nz, lay.rows, width), lambda o, *rest: (o, 0, 0, 0)),
    )


def start_joint(lay, joint, bufs, me_ref, place, sem, keep=None):
    for h, chain in enumerate(joint):
        width = chain.held.shape[-1]
        at = 0 if h == 0 else 3 * lay.cw - width
        spans = [(0, width, lambda to, t: (place(to), at))]
        start_pieces(lay, chain, bufs[2 * h : 2 * h + 2], me_ref, spans, sem, keep)


def attend_all(lay, run, joint, normed, bias_rows):
    rows = normed.shape[0]
    own, cw = rows // SP, lay.cw
    hl = cw // HEAD_DIM
    wide = 3 * cw

    def kernel(me_ref, *refs):
        bufs = refs[:4]
        x_ref, b_ref, p_ref, o_ref, lse_ref, top_ref, w, sem = refs[4:]
        o, i = pl.program_id(0), pl.program_id(1)

        @pl.when((o == 0) & (i == 0))
        def _():
            start_joint(lay, joint, bufs, me_ref, lambda to: w.at[to], lambda to: sem.at[to])

        @pl.when(i == 0)
        def _():
            wait_all(w.at[o], sem.at[o])

        y = jnp.dot(x_ref[...], w[o], preferred_element_type=F32) + b_ref[...]
        p_ref[:, :cw] = (y[:, :cw] * HEAD_DIM**-0.5).astype(BF)
        p_ref[:, cw:] = y[:, cw:].astype(BF)
        attend_kernel(hl, p_ref, o_ref, lse_ref, top_ref)

    stat = pl.BlockSpec((1, 1, hl, LP), lambda o, i, m: (i, o ^ m[2], 0, 0))
    stat_shape = jax.ShapeDtypeStruct((own, lay.nt, hl, LP), F32)
    out, _ = run(
        "attend", 36, kernel, (lay.nt, own),
        [(b, ANY) for chain in joint for b in chain.bufs]
        + [
            (normed, pl.BlockSpec((SP, D), lambda o, i, m: (i, 0))),
            (bias_rows, pl.BlockSpec((1, wide), lambda o, i, m: (0, o ^ m[2]))),
        ],
        [
            (jax.ShapeDtypeStruct((rows, lay.nt * wide), BF), pl.BlockSpec((SP, wide), lambda o, i, m: (i, o ^ m[2]))),
            (jax.ShapeDtypeStruct((rows, D), BF), pl.BlockSpec((SP, cw), lambda o, i, m: (i, o ^ m[2]))),
            (stat_shape, stat),
            (stat_shape, stat),
        ],
        [pltpu.VMEM((lay.nt, D, wide), BF), pltpu.SemaphoreType.DMA((lay.nt,))],
    )
    return out


def out_project(lay, run, group, mixed, inputs, bias, gain, shift):
    rows = inputs.shape[0]
    cw = lay.cw
    nb = len(group.bufs)

    def kernel(me_ref, *refs):
        bufs = refs[:nb]
        m_ref, x_ref, b_ref, g_ref, s_ref, mid_ref, sec_ref, w, sem = refs[nb:]

        @pl.when(pl.program_id(0) == 0)
        def _():
            spans = [(0, cw, lambda to, t: (w, t * cw))]
            start_pieces(lay, group, bufs, me_ref, spans, lambda to: sem)
            wait_all(w, sem)

        middle = x_ref[...].astype(F32) + dotf(m_ref[...], w[...], 1, 1) + b_ref[...]
        mid_ref[...] = middle.astype(BF)
        unit, _ = unit_of(middle)
        sec_ref[...] = (unit * g_ref[...] + s_ref[...]).astype(BF)

    out, _ = run(
        "out_project", 10, kernel, (rows // SP,),
        [(b, ANY) for b in group.bufs]
        + [(mixed, row_block(D)), (inputs, row_block(D))]
        + [(v, one_row(D)) for v in (bias, gain, shift)],
        [
            (jax.ShapeDtypeStruct((rows, D), BF), row_block(D)),
            (jax.ShapeDtypeStruct((rows, D), BF), row_block(D)),
        ],
        [pltpu.VMEM((D, D), BF), pltpu.SemaphoreType.DMA],
    )
    return out


def feed(lay, run, group, second, dresult, bias, dsecond=None, through=()):
    rows = second.shape[0]
    half = lay.cols // 2
    more = dsecond is not None
    nb = len(group.bufs)

    def kernel(me_ref, *refs):
        bufs = refs[:nb]
        x_ref, g_ref, b_ref, *refs = refs[nb:]
        if more:
            before, *refs = refs
        a_ref, s_ref, sec_ref, other, mine, we, ws, d_s, acc, sem_e, sem_s, sem = refs
        o = pl.program_id(0)

        @pl.when(o == 0)
        def _():
            spans = [(0, half, lambda to, t: (we.at[to], 0))]
            start_pieces(lay, group, bufs, me_ref, spans, lambda to: sem_e.at[to])
            spans = [(half, half, lambda to, t: (ws.at[to], 0))]
            start_pieces(lay, group, bufs, me_ref, spans, lambda to: sem_s.at[to])
            if more:
                pltpu.make_async_copy(before, acc, sem).start()
                pltpu.make_async_copy(before, acc, sem).wait()
            else:
                acc[...] = jnp.zeros_like(acc)

        wait_all(we.at[o], sem_e.at[o])
        wait_all(ws.at[o], sem_s.at[o])
        total = None
        for r in range(rows // SP):
            rs = slice(r * SP, (r + 1) * SP)
            hidden = jnp.dot(x_ref[rs, :], we[o], preferred_element_type=F32) + b_ref[...]
            dact = jnp.dot(g_ref[rs, :], ws[o], preferred_element_type=F32)
            sigma = 0.5 + 0.5 * jnp.tanh(0.851 * hidden)
            active = hidden * sigma
            a_ref[rs, :] = active.astype(BF)
            dh = (dact * (sigma + 1.702 * active * (1.0 - sigma))).astype(BF)
            d_s[rs, :] = dh
            part = column_sum(dh.astype(F32))
            total = part if total is None else total + part
            acc[rs, :] += dotf(dh, we[o], 1, 1)
        s_ref[...] = total
        put_pieces(lay, me_ref, dotf(x_ref[...], d_s[...], 0, 0), other, mine)
        put_pieces(lay, me_ref, dotf(g_ref[...], a_ref[...], 0, 0), other, mine, half)

        @pl.when(o == lay.nt - 1)
        def _():
            sec_ref[...] = acc[...].astype(sec_ref.dtype)

    line = pl.BlockSpec((1, half), lambda o, m: (0, o ^ m[2]))
    full = pl.BlockSpec((rows, D), lambda o, m: (0, 0))
    weights = pltpu.VMEM((lay.nt, D, half), BF)
    sems = pltpu.SemaphoreType.DMA((lay.nt,))
    return run(
        "feed", 33, kernel, (lay.nt,),
        [(b, ANY) for b in group.bufs]
        + [(second, full), (dresult, full), (bias, line)] + ([(dsecond, ANY)] if more else []),
        [
            (jax.ShapeDtypeStruct((rows, lay.nt * half), BF), pl.BlockSpec((rows, half), lambda o, m: (0, o ^ m[2]))),
            (jax.ShapeDtypeStruct((1, lay.nt * half), F32), line),
            (jax.ShapeDtypeStruct((rows, D), BF if more else F32), full),
        ]
        + [piece_out(lay, 2 * half)] * 2,
        [
            weights,
            weights,
            pltpu.VMEM((rows, half), BF),
            pltpu.VMEM((rows, D), F32),
            sems,
            sems,
            pltpu.SemaphoreType.DMA,
        ],
        through,
    )


def feed_out(lay, run, groups, active, middle, bias, more=()):
    rows = middle.shape[0]
    own = rows // SP
    half = lay.cols // 2
    wide = lay.nt * half

    n0, n1 = [len(group.bufs) for group in groups]

    def kernel(me_ref, *refs):
        bufs = (refs[:n0], refs[n0 : n0 + n1])
        a0_ref, a1_ref, mid_ref, b_ref, o_ref, w, sem = refs[n0 + n1 :]

        @pl.when(pl.program_id(0) == 0)
        def _():
            for g, group in enumerate(groups):
                spans = [(half, half, lambda to, t, g=g: (w.at[g], t * half))]
                start_pieces(lay, group, bufs[g], me_ref, spans, lambda to: sem)
            wait_all(w, sem)

        live = me_ref[2] * own + pl.program_id(0) < me_ref[3]
        out = mid_ref[...].astype(F32) + dotf(a0_ref[...], w[0], 1, 1) + dotf(a1_ref[...], w[1], 1, 1) + b_ref[...]
        o_ref[...] = jnp.where(live, out, 0.0).astype(BF)

    (result,), more = run(
        "feed_out", 20, kernel, (own,),
        [(b, ANY) for g in groups for b in g.bufs]
        + [(a, row_block(wide)) for a in active]
        + [(middle, row_block(D)), (bias, one_row(D))],
        [(jax.ShapeDtypeStruct((rows, D), BF), row_block(D))],
        [pltpu.VMEM((2, D, wide), BF), pltpu.SemaphoreType.DMA],
        more,
    )
    return result, more


def feed_back(lay, run, group, dsecond, middle, dresult, mixed, gain):
    rows = middle.shape[0]
    cw, nt = lay.cw, lay.nt
    steps = rows // SP

    nb = len(group.bufs)

    def kernel(me_ref, *refs):
        bufs = refs[:nb]
        d_ref, mid_ref, g_ref, m_ref, n_ref, dm_ref, dx_ref, v_ref, other, own, w, acc, sem = refs[nb:]
        i = pl.program_id(0)

        @pl.when(i == 0)
        def _():
            spans = [(0, cw, lambda to, t: (w, t * cw))]
            start_pieces(lay, group, bufs, me_ref, spans, lambda to: sem)
            wait_all(w, sem)

        dsecond = d_ref[...].astype(F32)
        unit, inverse = unit_of(mid_ref[...].astype(F32))
        dout = g_ref[...].astype(F32)
        dmiddle = dout + norm_back(dsecond, unit, inverse, n_ref[...])
        dbranch = dmiddle.astype(BF)
        dm_ref[...] = dbranch
        dx_ref[...] = jnp.dot(dbranch, w[...], preferred_element_type=F32).astype(BF)
        sums = [dsecond * unit, dsecond, dbranch.astype(F32), dout]
        add_rows(v_ref, [column_sum(v) for v in sums])
        y = dotf(dbranch, m_ref[...], 0, 0)

        @pl.when(i == 0)
        def _():
            acc[...] = y

        @pl.when(i > 0)
        def _():
            acc[...] += y

        @pl.when(i == steps - 1)
        def _():
            for t in range(nt):
                to = t ^ me_ref[2]
                put_pieces(
                    lay, me_ref, acc[:, t * cw : (t + 1) * cw], other.at[pl.ds(to, 1)], own.at[pl.ds(to, 1)]
                )

    piece = jax.ShapeDtypeStruct((nt, lay.nz, lay.rows, cw), BF)
    out, _ = run(
        "feed_back", 10, kernel, (steps,),
        [(b, ANY) for b in group.bufs]
        + [(v, row_block(D)) for v in (dsecond, middle, dresult, mixed)]
        + [(gain, one_row(D))],
        [
            (jax.ShapeDtypeStruct((rows, D), BF), row_block(D)),
            (jax.ShapeDtypeStruct((rows, D), BF), row_block(D)),
            (jax.ShapeDtypeStruct((4, D), F32), whole((4, D))),
            (piece, whole(piece.shape)),
            (piece, whole(piece.shape)),
        ],
        [pltpu.VMEM((D, D), BF), pltpu.VMEM((D, D), F32), pltpu.SemaphoreType.DMA],
    )
    return out


def attend_back(lay, run, to, joint, packed, mixed, dmixed, lse, normed, output, last=None):
    rows = packed.shape[0]
    own, cw = rows // SP, lay.cw
    hl = cw // HEAD_DIM
    w3 = 3 * cw
    np = 0 if last is None else len(last[0])

    def kernel(me_ref, *refs):
        bufs = refs[:4]
        p_ref, m_ref, g_ref, lse_ref, x_ref, go_other, go_own, *refs = refs[4:]
        if last is not None:
            parts = refs[:np]
            in_ref, dm_ref, gain_ref, *refs = refs[np:]
            sum_ref, out_ref, v_ref, other, mine, w, dp, total, sem = refs
        else:
            sum_ref, out_ref, other, mine, w, dp, total, sem = refs
        i = pl.program_id(0)

        @pl.when(i == 0)
        def _():
            start_joint(lay, joint, bufs, me_ref, lambda _: w, lambda _: sem, lambda t: t == to)

        attend_back_kernel(hl, p_ref, m_ref, g_ref, lse_ref, dp, sum_ref)

        @pl.when(i == 0)
        def _():
            wait_all(w, sem)

        dnormed = dotf(dp[...], w[...], 1, 1)
        y = dotf(x_ref[...], dp[...], 0, 0)
        if last is None:
            out_ref[...] = dnormed.astype(BF)
        else:
            for part in parts:
                dnormed += part[...].astype(F32)
            unit, inverse = unit_of(in_ref[...].astype(F32))
            dinput = norm_back(dnormed, unit, inverse, gain_ref[...])
            out_ref[...] = (dm_ref[...].astype(F32) + dinput).astype(BF)
            add_rows(v_ref, [column_sum(dnormed * unit), column_sum(dnormed)])

        @pl.when(i == 0)
        def _():
            total[...] = y

        @pl.when(i > 0)
        def _():
            total[...] += y

        @pl.when(i == own - 1)
        def _():
            put_pieces(lay, me_ref, total[...], other, mine)
            other[:, :, :, w3:] = go_other[...]
            mine[:, :, :, w3:] = go_own[...]

    spec = lambda width: pl.BlockSpec((SP, width), lambda i, m: (i, to ^ m[2]))
    part = pl.BlockSpec((1, lay.nz, lay.rows, cw), lambda i, m: (to, 0, 0, 0))
    piece = jax.ShapeDtypeStruct((1, lay.nz, lay.rows, w3 + cw), BF)
    out, _ = run(
        "attend_back", 38, kernel, (own,),
        [(b, ANY) for chain in joint for b in chain.bufs]
        + [
            (packed, spec(w3)),
            (mixed, spec(cw)),
            (dmixed, spec(cw)),
            (lse, pl.BlockSpec((1, 1, hl, LP), lambda i, m: (i, to ^ m[2], 0, 0))),
            (normed, row_block(D)),
            (output[0], part),
            (output[1], part),
        ]
        + ([(x, row_block(D)) for x in (*last[0], last[1], last[2])] + [(last[3], one_row(D))] if last else []),
        [
            (jax.ShapeDtypeStruct((own, 1, 1, w3), F32), pl.BlockSpec((1, 1, 1, w3), lambda i, m: (i, 0, 0, 0))),
            (jax.ShapeDtypeStruct((rows, D), BF), row_block(D)),
        ]
        + ([(jax.ShapeDtypeStruct((2, D), F32), whole((2, D)))] if last else [])
        + [(piece, whole(piece.shape))] * 2,
        [pltpu.VMEM((D, w3), BF), pltpu.VMEM((SP, w3), BF), pltpu.VMEM((D, w3), F32), pltpu.SemaphoreType.DMA],
    )
    return out


def insert_bit(s, b, value):
    return ((s >> b) << (b + 1)) | (value << b) | (s & ((1 << b) - 1))


def along(lay, run, arrays, more=()):
    z, dr, width = arrays[0].shape
    n = len(arrays)
    w = 256 if width % 256 == 0 else 128

    def kernel(me_ref, *refs):
        for k in range(z):
            total = refs[0][k].astype(F32)
            for ref in refs[1:n]:
                total += ref[k].astype(F32)
            refs[n + k][...] = total.astype(BF)

    block = pl.BlockSpec((z, dr, w), lambda s, m: (0, 0, s))
    out = (jax.ShapeDtypeStruct((dr, width), BF), pl.BlockSpec((dr, w), lambda s, m: (0, s)))
    sums, more = run("add_plane", 4, kernel, (width // w,), [(x, block) for x in arrays], [out] * z, (), more)
    return [swap(x, k * 2 * lay.nt, lay.size) if k else x for k, x in enumerate(sums)], more


def total_of(ends):
    total = ends[0].astype(F32)
    for x in ends[1:]:
        total = total + x.astype(F32)
    return total


class Butterfly:
    def __init__(self, lay, reverse, other, own):
        self.lay = lay
        bits = list(range(lay.tbits))
        self.bits = bits[::-1] if reverse else bits
        self.left = bits[::-1]
        self.keep = own
        self.got = swap(other, lay.core, lay.size)

    def fold(self, run):
        bit = self.bits.pop(0)
        low = len(self.left) - 1 - self.left.index(bit)
        self.left.remove(bit)
        n, z, dr, width = self.keep.shape
        block = (1, z // 2, dr, width)
        ins, outs = [], []
        for value in (1, 0):
            spec = pl.BlockSpec(block, lambda s, j, m, value=value: (insert_bit(s, low, value), j, 0, 0))
            ins += [(self.keep, spec), (self.got, spec)]
            shape = jax.ShapeDtypeStruct((n // 2, z, dr, width), BF)
            outs.append((shape, pl.BlockSpec(block, lambda s, j, m: (s, j, 0, 0))))

        def kernel(me_ref, *refs):
            for i in range(2):
                refs[4 + i][...] = refs[2 * i][...] + refs[2 * i + 1][...]

        (send, self.keep), _ = run("add", 4, kernel, (n // 2, 2), ins, outs)
        self.got = swap(send, 1 << bit, self.lay.size)

    def along(self, run, more=()):
        self.ends, more = along(self.lay, run, [self.keep[0], self.got[0]], more)
        return more


class Direct:
    def __init__(self, lay):
        self.lay = lay
        self.parts = []

    def start(self, to, other, own):
        self.waiting = (to, own[0], swap(other[0], self.lay.core, self.lay.size))

    def spread(self, run):
        to, own, got = self.waiting
        z, dr, width = own.shape

        def kernel(me_ref, a_ref, b_ref, o_ref):
            o_ref[...] = a_ref[...] + b_ref[...]

        block = pl.BlockSpec((1, dr, width), lambda s, m: (s, 0, 0))
        (x,), _ = run("add_core", 2, kernel, (z,), [(own, block), (got, block)], [(jax.ShapeDtypeStruct(own.shape, BF), block)])
        self.parts.append(swap(x, to, self.lay.size))

    def along(self, run, more=()):
        self.ends, more = along(self.lay, run, list(self.waiting[1:]) + self.parts, more)
        return more


class Sum:
    def __init__(self, lay, x, combine=jnp.add):
        self.lay, self.x, self.combine = lay, x, combine
        self.masks = [1 << b for b in range((lay.size - 1).bit_length())]
        self.send()

    def send(self):
        self.got = swap(self.x, self.masks.pop(0), self.lay.size)

    def land(self, passed=None):
        if passed:
            self.got = passed[0]
        self.x = self.combine(self.x, self.got)
        if self.masks:
            self.send()
        else:
            self.got = None


def pad_rows(x):
    own = x.shape[0] // SEQ
    return jnp.pad(x.reshape(own, SEQ, D), ((0, 0), (0, SP - SEQ), (0, 0))).reshape(own * SP, D)


def unpad_rows(x):
    own = x.shape[0] // SP
    return x.reshape(own, SP, D)[:, :SEQ].reshape(own * SEQ, D)


def per_device(
    lay,
    tokens,
    first_gain,
    first_shift,
    joint_weight,
    joint_bias,
    output_weight,
    output_bias,
    second_gain,
    second_shift,
    expand_weight,
    expand_bias,
    shrink_weight,
    shrink_bias,
    cotangent,
    image_count,
    threshold,
):
    own = tokens.shape[0] // SEQ
    nt, cw, dr = lay.nt, lay.cw, lay.rows
    half = lay.cols // 2
    hl = cw // HEAD_DIM
    tensor = lax.axis_index("tensor").astype(jnp.int32)
    dp = lax.axis_index("dp").astype(jnp.int32)
    count = image_count[0]
    run = Runner(jnp.stack([dp // 2, dp % 2, tensor, count]))

    shrink_t = shrink_weight.T
    split = 3 * cw // 2 if cw % 256 == 0 else 2 * cw
    flat = joint_weight.reshape(dr, 3 * cw)
    joint = [Chain(lay, flat[:, :split], False), Chain(lay, flat[:, split:], True)]
    small = jnp.concatenate([joint_bias.reshape(-1), expand_bias.reshape(-1)])
    n_small = small.shape[0]
    piece = jnp.concatenate([output_weight.T, jnp.pad(small[None], ((0, 15), (0, cw - n_small)))])
    ((piece,),) = gate(run, [piece])
    output = Shards(lay, piece)
    halves = [
        jnp.concatenate([w[:, g * half : (g + 1) * half] for w in (expand_weight, shrink_t)], axis=1)
        for g in range(2)
    ]
    feeds = [Gather(lay, halves[0])]

    biases = output.bufs[0][:, dr].astype(F32)
    nb = joint_bias.size
    jb = biases[:, :nb].reshape(lay.ndp, nt, 2, hl, HEAD_DIM // lay.ndp)
    jb = jb.transpose(2, 1, 3, 0, 4).reshape(2, nt, 1, cw)
    bias_rows = jnp.concatenate([jb[0], jnp.zeros_like(jb[0]), jb[1]], axis=1).reshape(1, 3 * D)
    eb = biases[:, nb:n_small].reshape(lay.ndp, nt, FF // HEAD_DIM // nt, HEAD_DIM // lay.ndp)
    eb = eb.transpose(1, 2, 0, 3).reshape(nt, 2, half)
    expand_rows = [eb[:, g].reshape(1, nt * half) for g in range(2)]

    image_ids = tensor * own + jnp.arange(own, dtype=jnp.int32)
    image_live = image_ids < count
    inputs = pad_rows(tokens)
    live_rows = jnp.repeat(image_live, SEQ)[:, None]
    dresult = pad_rows(jnp.where(live_rows, cotangent, jnp.zeros_like(cotangent)))
    unit, _ = unit_of(inputs.astype(F32))
    normed = (unit * first_gain + first_shift).astype(BF)
    row = lambda v: v.reshape(1, D)

    for chain in joint:
        chain.send()
    while len(joint[0].stages) > 2:
        for chain in joint:
            chain.land()
            chain.send()
    (joint[0].got, joint[1].got), (feeds[0].held,) = gate(run, [chain.got for chain in joint], [feeds[0].held])
    for chain in joint:
        chain.land()
        chain.send()
    feeds[0].along()
    (joint[0].got, joint[1].got), feeds[0].got[1:], (inputs, dresult, normed), (halves[1],) = gate(
        run, [chain.got for chain in joint], feeds[0].got[1:], [inputs, dresult, normed], [halves[1]]
    )
    for chain in joint:
        chain.land()
        chain.share()
    feeds.append(Shards(lay, halves[1]))
    feeds[0].spread()
    packed, mixed, lse, tops = attend_all(lay, run, joint, normed, bias_rows)
    (feeds[0].got[1:],) = gate(run, feeds[0].got[1:])
    feeds[0].share()
    middle, second = out_project(
        lay, run, output, mixed, inputs, row(output_bias), row(second_gain), row(second_shift)
    )

    (active0, expand_sum0, dsecond, *pieces), _ = feed(lay, run, feeds[0], second, dresult, expand_rows[0])
    grads = [Butterfly(lay, True, *pieces)]
    active1, expand_sum1, dsecond, *pieces = feed(
        lay, run, feeds[1], second, dresult, expand_rows[1], dsecond
    )[0]
    grads.append(Butterfly(lay, False, *pieces))
    grads[0].fold(run)
    dmiddle, dmixed, sums_two, *out_pieces = feed_back(
        lay, run, output, dsecond, middle, dresult, mixed, row(second_gain)
    )
    grads[1].fold(run)

    packed_sums, dnormed = [], []
    total = Direct(lay)

    def back(to, last=None):
        part, out, *more = attend_back(
            lay, run, to, joint, packed, mixed, dmixed, lse, normed, out_pieces, last
        )
        packed_sums.append(part)
        total.start(to, *more[-2:])
        return out, more[0]

    for n, to in enumerate(range(nt - 1, 0, -1)):
        dnormed.append(back(to)[0])
        if n < 2:
            grads[n].fold(run)
        elif n == 2 and not grads[0].bits:
            grads[0].along(run)
        total.spread(run)
    token_rows, sums_one = back(0, (dnormed, inputs, dmiddle, row(first_gain)))

    tops = jnp.max(tops, axis=-1).reshape(own, HEADS) / LOG2E
    peak = jnp.max(jnp.where(image_live[:, None], tops, NEG), axis=0)
    peak = jnp.broadcast_to(peak[:, None], (HEADS, 128))
    expand_sum = jnp.stack([expand_sum0.reshape(nt, half), expand_sum1.reshape(nt, half)], axis=1)
    heads = jnp.concatenate([jnp.sum(x, axis=0) for x in packed_sums[::-1]]).reshape(nt, 3, cw)
    heads = heads[jnp.arange(nt) ^ tensor]
    vectors = [sums_two, expand_sum, sums_one, heads[:, 0], heads[:, 2]]
    sums = jnp.concatenate([peak] + [v.reshape(-1, 128) for v in vectors])
    is_peak = lax.broadcasted_iota(jnp.int32, sums.shape, 0) < HEADS
    small = Sum(lay, sums, lambda a, b: jnp.where(is_peak, jnp.maximum(a, b), a + b))
    while grads[1].bits:
        for sc in grads:
            sc.fold(run)
    if nt != 4:
        grads[0].along(run)
    small.land(grads[1].along(run, [small.got]))
    small.land(total.along(run, [small.got]))
    result, passed = feed_out(lay, run, feeds, [active0, active1], middle, row(shrink_bias), [small.got])
    small.land(passed)
    while small.got is not None:
        small.land()

    block_out = unpad_rows(result)
    tokens_grad = unpad_rows(token_rows)
    sums = small.x
    peak = sums[:HEADS, 0]
    at = [HEADS, HEADS + 4 * D // 128, HEADS + (4 * D + FF) // 128, HEADS + (6 * D + FF) // 128]
    sums_two = sums[at[0] : at[1]].reshape(4, D)
    expand_sum = sums[at[1] : at[2]].reshape(FF)
    sums_one = sums[at[2] : at[3]].reshape(2, D)
    bias_sum = sums[at[3] :].reshape(2, D)
    mine = lambda v: lax.dynamic_slice_in_dim(v, dp * dr, dr, v.ndim - 1)
    sums_one, sums_two = mine(sums_one), mine(sums_two)
    share = HEAD_DIM // lay.ndp
    units = FF // HEAD_DIM // nt
    expand_bias_grad = lax.dynamic_slice(
        expand_sum.reshape(FF // HEAD_DIM, HEAD_DIM), (tensor * units, dp * share), (units, share)
    )
    joint_bias_grad = lax.dynamic_slice(
        bias_sum.reshape(2, HEADS, HEAD_DIM), (0, tensor * hl, dp * share), (2, hl, share)
    )

    top = lax.dynamic_slice_in_dim(peak, tensor * hl, hl, 0)
    factors = jnp.sqrt(threshold / jnp.maximum(top, threshold))
    columns = jnp.repeat(factors, HEAD_DIM)
    clipped_joint = (joint_weight[:, 0:2, :].astype(F32) * columns).astype(BF)
    clipped_bias = (joint_bias[0].astype(F32) * factors[:, None]).astype(BF)

    feed_a, feed_b, total = [total_of(g.ends) for g in (*grads, total)]
    joint_grad = total[:, : 3 * cw].reshape(dr, 3, cw)
    output_grad = total[:, 3 * cw :].T
    expand_grad = jnp.concatenate([feed_a[:, :half], feed_b[:, :half]], axis=1)
    shrink_grad = jnp.concatenate([feed_a[:, half:], feed_b[:, half:]], axis=1).T
    return (
        block_out,
        tokens_grad,
        sums_one[0],
        sums_one[1],
        joint_grad,
        joint_bias_grad,
        output_grad,
        sums_two[2],
        sums_two[0],
        sums_two[1],
        expand_grad,
        expand_bias_grad,
        shrink_grad,
        sums_two[3],
        clipped_joint,
        clipped_bias,
        factors,
    )


def solution(mesh):
    placed = (
        P(("dp", "tensor"), None),
        P(),
        P(),
        P("dp", None, "tensor"),
        P(None, "tensor", "dp"),
        P("tensor", "dp"),
        P(),
        P(),
        P(),
        P("dp", "tensor"),
        P("tensor", "dp"),
        P("tensor", "dp"),
        P(),
        P(("dp", "tensor"), None),
        P("dp"),
        P("tensor"),
    )
    lay = Layout(mesh.shape["dp"], mesh.shape["tensor"])
    return jax.shard_map(
        partial(per_device, lay),
        mesh=mesh,
        in_specs=placed,
        out_specs=(
            P(("dp", "tensor"), None),
            P(("dp", "tensor"), None),
            P("dp"),
            P("dp"),
            P("dp", None, "tensor"),
            P(None, "tensor", "dp"),
            P("tensor", "dp"),
            P("dp"),
            P("dp"),
            P("dp"),
            P("dp", "tensor"),
            P("tensor", "dp"),
            P("tensor", "dp"),
            P("dp"),
            P("dp", None, "tensor"),
            P("tensor", "dp"),
            P("tensor"),
        ),
        check_vma=False,
    )
```

time: 1100 us -> 570 us (0.52)
  matrix products: 318 us -> 0 us
  Pallas kernels: 0 us -> 301 us
  waiting for transfers between devices: 383 us -> 102 us
  blocking collectives: 146 us -> 0 us
  local copies, waits for them, and re-layouts: 140 us -> 59.5 us
  other arithmetic: 83.5 us -> 29.8 us
  starting transfers between devices: 1.04 us -> 52.8 us
    dot_general x26 -> x0, matrix products: 318 us -> none  [the longest x2 31.7 us: attend_back(): jnp.einsum('qhd,khd->hqk', dmixed, values, preferred_element_type=jnp.flo...]
    pallas_call x0 -> x24, Pallas kernels: none -> 301 us  [__call__(): pl.pallas_call(body, grid_spec=pltpu.PrefetchScalarGridSpec(num_scalar_pr...]
    reduce_scatter x6 -> x0, waiting for transfers between devices: 160 us -> none  [the longest x1 87.6 us: per_device(): lax.psum_scatter(shrink_grad.astype(jnp.bfloat16), 'tensor', scatter_dime...]
    all_gather x7 -> x2, waiting for transfers between devices: 144 us -> 0.02 us  [__init__(): self.bufs = [lax.all_gather(piece, AXES)]]
    ppermute x0 -> x47, waiting for transfers between devices: none -> 102 us  [swap(): return lax.ppermute(x, AXES, [(i, i ^ mask) for i in range(size)])]
    unnamed x19 -> x2, waiting for transfers between devices: 78.1 us -> 0.03 us
    while x16 -> x0, local copies, waits for them, and re-layouts: 60.1 us -> none  [the longest x2 24.7 us: per_device(): mixed, logsum, peaks = lax.map(partial(attend, scale), per_image)]
    all_gather x5 -> x0, blocking collectives: 58.2 us -> none  [the longest x1 15.3 us: per_device(): lax.all_gather(output_weight, 'dp', axis=1, tiled=True)]
  transfers between devices with their start and end apart: 16 -> 49, of which waited for: 11 -> 18; matrix products, arithmetic and copies ran while one was open for 43% -> 13% of each run, Pallas kernels for 0% -> 49%
where the time goes in v2:
time: 570 us; the launch traced here: 561 us
  Pallas kernels  301 us (53%)
  waiting for transfers between devices  102 us (18%)
  local copies, waits for them, and re-layouts  59.5 us (10%)
  starting transfers between devices  52.8 us (9%)
  other arithmetic  29.8 us (5%)
  between operations  16 us (3%)
    pallas_call x24, Pallas kernels, __call__(): pl.pallas_call(body, grid_spec=pltpu.PrefetchScalarGridSpec(num_scalar_pr...  301 us
    ppermute x47, waiting for transfers between devices, swap(): return lax.ppermute(x, AXES, [(i, i ^ mask) for i in range(size)])  102 us
    ppermute x47, starting transfers between devices, swap(): return lax.ppermute(x, AXES, [(i, i ^ mask) for i in range(size)])  52.7 us
    unnamed x155, local copies, waits for them, and re-layouts  27.9 us
  transfers between devices with their start and end apart: 49, of which 18 were waited for; matrix products, arithmetic and copies ran while one was open for 13% of the time, Pallas kernels for 49%

profile of v2, /device:TPU:0, one launch (start us, length us, event | category | flops | bytes accessed | tf_op | source)
XLA Modules:
  0.0 561.4 jit_solution(7163548131801671236)
XLA Ops:
  9.1 4.0 collective-permute-start.3
  19.8 2.1 reshape.204
  23.3 1.7 pad.12
  25.7 4.2 add_convert_fusion.refs_8_
  29.8 1.7 broadcast_select_fusion
  32.6 1.9 collective-permute-start.4
  35.5 1.6 collective-permute-start.1
  39.1 1.8 pad_maximum_fusion.4
  40.9 1.6 collective-permute-start.5
  42.5 1.8 pad_maximum_fusion.3
  46.3 2.1 reshape.206
  48.4 1.7 pad.13
  52.4 2.9 collective-permute-done.5.refs_2_
  55.3 7.1 %collective-permute-done.2.refs_1_ = bf16[4,128,384]{2,1,0:T(8,128)(2,1)S(1)} collective-permute-done((bf16[4,128,384]{2,1,0:T(8,128)(2,1)}, bf16[4,128,384]{2,1,0:T(8,128)(2,1)S(1)}, u32[]{:S(2)}, u32[]{:S(2)}) %collective-permute-start.2) | collective-permute-done | bytes 393248 | tf_op jit(solution)/shard_map/ppermute | solution.py:89
  67.8 1.6 collective-permute-start.6
  71.7 1.5 constant_dynamic-update-slice_fusion.7
  73.9 3.5 collective-permute-start.10
  80.6 5.3 collective-permute-done.10.refs_5_
  85.9 4.0 collective-permute-done.8.refs_3_
  89.9 9.6 %collective-permute-done.9.refs_4_ = bf16[1,128,1024]{2,1,0:T(8,128)(2,1)S(1)} collective-permute-done((bf16[1,128,1024]{2,1,0:T(8,128)(2,1)S(1)}, bf16[1,128,1024]{2,1,0:T(8,128)(2,1)S(1)}, u32[]{:S(2)}, u32[]{:S(2)}) %collective-permute-start.9) | collective-permute-done | bytes 262176 | tf_op jit(solution)/shard_map/ppermute | solution.py:89
  101.5 2.2 constant_dynamic-update-slice_fusion.9.refs_2_
  103.7 2.1 constant_dynamic-update-slice_fusion.4.refs_0_
  111.2 2.1 collective-permute-start.15
  117.8 36.3 %attend.1 = (bf16[1184,3072]{1,0:T(8,128)(2,1)}, bf16[1184,1024]{1,0:T(8,128)(2,1)}, f32[2,4,4,640]{3,2,1,0:T(4,128)}, f32[2,4,4,640]{3,2,1,0:T(4,128)}, f32[8,128]{1,0:T(8,128)}) custom-call(s32[4]{0:T(128)} %pad_add_fusion.me_ref, bf16[16,128,384]{2,1,0:T(8,128)(2,1)} %constant_dynamic-update-slice_fusion.4.refs_0_, ...), custom_call_target="tpu_custom_call", output_to_operand_aliasing={{4}: (7, {})} | custom-call | flops 199999995904 | bytes 200000000 | tf_op jit(solution)/shard_map/attend/pallas_call | solution.py:52
  154.2 13.3 %collective-permute-done.15.refs_3_ = bf16[4,128,1024]{2,1,0:T(8,128)(2,1)} collective-permute-done((bf16[4,128,1024]{2,1,0:T(8,128)(2,1)}, bf16[4,128,1024]{2,1,0:T(8,128)(2,1)}, u32[]{:S(2)}, u32[]{:S(2)}) %collective-permute-start.15) | collective-permute-done | bytes 1048608 | tf_op jit(solution)/shard_map/ppermute | solution.py:89
  168.8 9.5 %out_project.1 = (bf16[1184,1024]{1,0:T(8,128)(2,1)}, bf16[1184,1024]{1,0:T(8,128)(2,1)}, f32[8,128]{1,0:T(8,128)}) custom-call(s32[4]{0:T(128)} %pad_add_fusion.me_ref, bf16[32,144,256]{2,1,0:T(8,128)(2,1)} %bitcast.100, bf16[1184,1024]{1,0:T(8,128)(2,1)} %get-tuple-element.139.refs_1_.refs_4_.refs_5_, ...), custom_call_target="tpu_custom_call", output_to_operand_aliasing={{2}: (7, {})} | custom-call | flops 199999995904 | bytes 200000000 | tf_op jit(solution)/shard_map/out_project/pallas_call | solution.py:52
  180.4 39.7 %feed.2 = (bf16[1184,2048]{1,0:T(8,128)(2,1)}, f32[1,2048]{1,0:T(1,128)}, f32[1184,1024]{1,0:T(8,128)}, bf16[4,4,128,1024]{3,2,1,0:T(8,128)(2,1)}, bf16[4,4,128,1024]{3,2,1,0:T(8,128)(2,1)}, /*index=5*/f32[8,128]{1,0:T(8,128)}) custom-call(s32[4]{0:T(128)} %pad_add_fusion.me_ref, ...), custom_call_target="tpu_custom_call", output_to_operand_aliasing={{5}: (12, {})} | custom-call | flops 199999995904 | bytes 200000000 | tf_op jit(solution)/shard_map/feed/pallas_call | solution.py:52
  220.7 41.1 %feed.3 = (bf16[1184,2048]{1,0:T(8,128)(2,1)}, f32[1,2048]{1,0:T(1,128)}, bf16[1184,1024]{1,0:T(8,128)(2,1)}, bf16[4,4,128,1024]{3,2,1,0:T(8,128)(2,1)}, bf16[4,...) custom-call(s32[4]{0:T(128)} %pad_add_fusion.me_ref, ...), custom_call_target="tpu_custom_call", output_to_operand_aliasing={{5}: (6, {})} | custom-call | flops 199999995904 | bytes 200000000 | tf_op jit(solution)/shard_map/feed/pallas_call | solution.py:52
  261.9 6.4 %add.168 = (bf16[2,4,128,1024]{3,2,1,0:T(8,128)(2,1)}, bf16[2,4,128,1024]{3,2,1,0:T(8,128)(2,1)}, f32[8,128]{1,0:T(8,128)}) custom-call(s32[4]{0:T(128)} %pad_add_fusion.me_ref, bf16[4,4,128,1024]{3,2,1,0:T(8,128)(2,1)} %get-tuple-element.152.refs_0_.refs_2_, ...), custom_call_target="tpu_custom_call", output_to_operand_aliasing={{2}: (5, {})} | custom-call | flops 199999995904 | bytes 200000000 | tf_op jit(solution)/shard_map/add/pallas_call | solution.py:52
  269.3 18.6 %feed_back.1 = (bf16[1184,1024]{1,0:T(8,128)(2,1)}, bf16[1184,1024]{1,0:T(8,128)(2,1)}, f32[4,1024]{1,0:T(4,128)}, bf16[4,4,128,256]{3,2,1,0:T(8,128)(2,1)}, bf1...) custom-call(s32[4]{0:T(128)} %pad_add_fusion.me_ref, ...), custom_call_target="tpu_custom_call", output_to_operand_aliasing={{5}: (7, {})} | custom-call | flops 199999995904 | bytes 200000000 | tf_op jit(solution)/shard_map/feed_back/pallas_call | solution.py:52
  290.0 6.4 %add.169 = (bf16[2,4,128,1024]{3,2,1,0:T(8,128)(2,1)}, bf16[2,4,128,1024]{3,2,1,0:T(8,128)(2,1)}, f32[8,128]{1,0:T(8,128)}) custom-call(s32[4]{0:T(128)} %pad_add_fusion.me_ref, bf16[4,4,128,1024]{3,2,1,0:T(8,128)(2,1)} %get-tuple-element.160.refs_0_.refs_2_, ...), custom_call_target="tpu_custom_call", output_to_operand_aliasing={{2}: (5, {})} | custom-call | flops 199999995904 | bytes 200000000 | tf_op jit(solution)/shard_map/add/pallas_call | solution.py:52
  296.4 19.8 %attend_back.4 = (f32[2,1,1,768]{3,2,1,0:T(1,128)}, bf16[1184,1024]{1,0:T(8,128)(2,1)}, bf16[1,4,128,1024]{3,2,1,0:T(8,128)(2,1)}, bf16[1,4,128,1024]{3,2,1,0:T(8,128)(2,1)}, f32[8,128]{1,0:T(8,128)}) custom-call(s32[4]{0:T(128)} %pad_add_fusion.me_ref, ...), custom_call_target="tpu_custom_call", output_to_operand_aliasing={{4}: (12, {})} | custom-call | flops 199999995904 | bytes 200000000 | tf_op jit(solution)/shard_map/attend_back/pallas_call | solution.py:52
  317.8 4.1 add.170
  323.3 4.2 add_core.3
  327.5 20.3 %attend_back.5 = (f32[2,1,1,768]{3,2,1,0:T(1,128)}, bf16[1184,1024]{1,0:T(8,128)(2,1)}, bf16[1,4,128,1024]{3,2,1,0:T(8,128)(2,1)}, bf16[1,4,128,1024]{3,2,1,0:T(8,128)(2,1)}, f32[8,128]{1,0:T(8,128)}) custom-call(s32[4]{0:T(128)} %pad_add_fusion.me_ref, ...), custom_call_target="tpu_custom_call", output_to_operand_aliasing={{4}: (12, {})} | custom-call | flops 199999995904 | bytes 200000000 | tf_op jit(solution)/shard_map/attend_back/pallas_call | solution.py:52
  349.2 16.1 %collective-permute-done.25.refs_1_.refs_3_ = bf16[2,4,128,1024]{3,2,1,0:T(8,128)(2,1)} collective-permute-done((bf16[2,4,128,1024]{3,2,1,0:T(8,128)(2,1)}, bf16[2,4,128,1024]{3,2,1,0:T(8,128)(2,1)}, u32[]{:S(2)}, u32[]{:S(2)}) %collective-permute-start.25) | collective-permute-done | bytes 2097184 | tf_op jit(solution)/shard_map/ppermute | solution.py:89
  365.3 3.9 add.171
  370.2 4.2 add_core.4
  374.4 20.0 %attend_back.6 = (f32[2,1,1,768]{3,2,1,0:T(1,128)}, bf16[1184,1024]{1,0:T(8,128)(2,1)}, bf16[1,4,128,1024]{3,2,1,0:T(8,128)(2,1)}, bf16[1,4,128,1024]{3,2,1,0:T(8,128)(2,1)}, f32[8,128]{1,0:T(8,128)}) custom-call(s32[4]{0:T(128)} %pad_add_fusion.me_ref, ...), custom_call_target="tpu_custom_call", output_to_operand_aliasing={{4}: (12, {})} | custom-call | flops 199999995904 | bytes 200000000 | tf_op jit(solution)/shard_map/attend_back/pallas_call | solution.py:52
  394.5 4.3 add_plane.3
  399.4 4.2 add_core.5
  403.7 25.5 %attend_back.7 = (f32[2,1,1,768]{3,2,1,0:T(1,128)}, bf16[1184,1024]{1,0:T(8,128)(2,1)}, f32[2,1024]{1,0:T(2,128)}, bf16[1,4,128,1024]{3,2,1,0:T(8,128)(2,1)}, bf...) custom-call(s32[4]{0:T(128)} %pad_add_fusion.me_ref, ...), custom_call_target="tpu_custom_call", output_to_operand_aliasing={{5}: (18, {})} | custom-call | flops 199999995904 | bytes 200000000 | tf_op jit(solution)/shard_map/attend_back/pallas_call | solution.py:52
  432.1 3.0 collective-permute-start.42
  437.1 4.4 add_plane.4
  441.6 2.0 collective-permute-start.29
  443.5 3.2 collective-permute-done.41
  446.7 1.6 collective-permute-start.30
  448.3 5.5 collective-permute-done.42
  455.9 1.7 collective-permute-done.44
  457.6 4.7 collective-permute-start.45
  463.5 10.6 %collective-permute-done.45 = bf16[128,1024]{1,0:T(8,128)(2,1)S(1)} collective-permute-done((bf16[128,1024]{1,0:T(8,128)(2,1)}, bf16[128,1024]{1,0:T(8,128)(2,1)S(1)}, u32[]{:S(2)}, u32[]{:S(2)}) %collective-permute-start.45) | collective-permute-done | bytes 262176 | tf_op jit(solution)/shard_map/ppermute | solution.py:89
  476.2 1.9 reshape.222
  478.8 3.9 collective-permute-done.46
  485.0 4.8 collective-permute-done.30.refs_3_
  491.5 5.1 add_plane.5
  499.4 20.1 %feed_out.1 = (bf16[1184,1024]{1,0:T(8,128)(2,1)}, f32[8,128]{1,0:T(8,128)}, f32[112,128]{1,0:T(8,128)}) custom-call(s32[4]{0:T(128)} %pad_add_fusion.me_ref, bf16[4,128,1024]{2,1,0:T(8,128)(2,1)} %constant_dynamic-update-slice_fusion.refs_0_, bf16[4,128,1024]{2,1,0:T(8,128)(2,1)} %get-tuple-element.135.refs_1_, ...), custom_call_target="tpu_custom_call", output_to_operand_aliasing={{1}: (14, {}), {2}: (15, {})} | custom-call | flops 199999995904 | bytes 200000000 | tf_op jit(solution)/shard_map/feed_out/pallas_call | solution.py:52
  520.5 1.7 collective-permute-start.36
  522.3 2.5 collective-permute-done.36
  524.8 2.7 collective-permute-start.37
  529.7 1.6 collective-permute-start.39
  531.3 2.4 collective-permute-start.40
  533.7 1.9 slice.161
  535.6 1.9 reshape.220
  542.0 9.2 %collective-permute-done.39 = bf16[128,1024]{1,0:T(8,128)(2,1)S(1)} collective-permute-done((bf16[128,1024]{1,0:T(8,128)(2,1)}, bf16[128,1024]{1,0:T(8,128)(2,1)S(1)}, u32[]{:S(2)}, u32[]{:S(2)}) %collective-permute-start.39) | collective-permute-done | bytes 262176 | tf_op jit(solution)/shard_map/ppermute | solution.py:89
  (328 shorter events, 83.0 us)
Async XLA Ops:
  7.2 106.2 %all-gather.5.cloned.1.call-start = ((), (), s32[]{:S(2)}) async-start(), calls=%async_computation | async-start | bytes 2433024 | tf_op jit(solution)/shard_map/all_gather | solution.py:139
  9.1 22.6 %collective-permute-start.3 = (bf16[1,128,384]{2,1,0:T(8,128)(2,1)}, bf16[1,128,384]{2,1,0:T(8,128)(2,1)}, u32[]{:S(2)}, u32[]{:S(2)}) collective-permute-start(bf16[1,128,384]{2,1,0:T(8,128)(2,1)} %bitcast.6), channel_id=1, source_target_pairs={{0,16},{1,17},{2,18},{3,19},{4,20},{5,21},{6,22},{7,23},{8,24},{9,... | collective-permute-start | bytes 294920 | tf_op jit(solution)/shard_map/ppermute | solution.py:89
  13.9 20.7 %collective-permute-start = (bf16[1,128,384]{2,1,0:T(8,128)(2,1)}, bf16[1,128,384]{2,1,0:T(8,128)(2,1)}, u32[]{:S(2)}, u32[]{:S(2)}) collective-permute-start(bf16[1,128,384]{2,1,0:T(8,128)(2,1)} %bitcast.5), channel_id=1, source_target_pairs={{0,16},{1,17},{2,18},{3,19},{4,20},{5,21},{6,22},{7,23},{8,24},{9,... | collective-permute-start | bytes 294920 | tf_op jit(solution)/shard_map/ppermute | solution.py:89
  19.7 201.0 %all-gather.7.cloned.1.call-start = ((), (), s32[]{:S(2)}) async-start(), calls=%async_computation.1 | async-start | bytes 8650752 | tf_op jit(solution)/shard_map/all_gather | solution.py:139
  32.6 6.4 %collective-permute-start.4 = (bf16[2,128,384]{2,1,0:T(8,128)(2,1)S(1)}, bf16[2,128,384]{2,1,0:T(8,128)(2,1)S(1)}, u32[]{:S(2)}, u32[]{:S(2)}) collective-permute-start(bf16[2,128,384]{2,1,0:T(8,128)(2,1)S(1)} %pad_maximum_fusion.7), channel_id=1, source_target_pairs={{0,2},{1,3},{2,0},{3,1},{4,6},{5,7},{6,4},{7,5},{8,10},{9,11},{10,... | collective-permute-start | bytes 589832 | tf_op jit(solution)/shard_map/ppermute | solution.py:89
  35.5 7.0 %collective-permute-start.1 = (bf16[2,128,384]{2,1,0:T(8,128)(2,1)S(1)}, bf16[2,128,384]{2,1,0:T(8,128)(2,1)S(1)}, u32[]{:S(2)}, u32[]{:S(2)}) collective-permute-start(bf16[2,128,384]{2,1,0:T(8,128)(2,1)S(1)} %pad_maximum_fusion.6), channel_id=1, source_target_pairs={{0,1},{1,0},{2,3},{3,2},{4,5},{5,4},{6,7},{7,6},{8,9},{9,8},{10,11... | collective-permute-start | bytes 589832 | tf_op jit(solution)/shard_map/ppermute | solution.py:89
  40.9 14.4 %collective-permute-start.5 = (bf16[4,128,384]{2,1,0:T(8,128)(2,1)}, bf16[4,128,384]{2,1,0:T(8,128)(2,1)S(1)}, u32[]{:S(2)}, u32[]{:S(2)}) collective-permute-start(bf16[4,128,384]{2,1,0:T(8,128)(2,1)} %pad_maximum_fusion.4), channel_id=1, source_target_pairs={{0,8},{1,9},{2,10},{3,11},{4,12},{5,13},{6,14},{7,15},{8,0},{9,1},... | collective-permute-start | bytes 1179656 | tf_op jit(solution)/shard_map/ppermute | solution.py:89
  44.3 18.1 %collective-permute-start.2 = (bf16[4,128,384]{2,1,0:T(8,128)(2,1)}, bf16[4,128,384]{2,1,0:T(8,128)(2,1)S(1)}, u32[]{:S(2)}, u32[]{:S(2)}) collective-permute-start(bf16[4,128,384]{2,1,0:T(8,128)(2,1)} %pad_maximum_fusion.3), channel_id=1, source_target_pairs={{0,8},{1,9},{2,10},{3,11},{4,12},{5,13},{6,14},{7,15},{8,0},{9,1},... | collective-permute-start | bytes 1179656 | tf_op jit(solution)/shard_map/ppermute | solution.py:89
  65.4 34.1 %collective-permute-start.7 = (bf16[8,128,384]{2,1,0:T(8,128)(2,1)S(1)}, bf16[8,128,384]{2,1,0:T(8,128)(2,1)S(1)}, u32[]{:S(2)}, u32[]{:S(2)}) collective-permute-start(bf16[8,128,384]{2,1,0:T(8,128)(2,1)S(1)} %pad_maximum_fusion.1), channel_id=1, source_target_pairs={{0,1},{1,0},{2,3},{3,2},{4,5},{5,4},{6,7},{7,6},{8,9},{9,8},{10,11... | collective-permute-start | bytes 2359304 | tf_op jit(solution)/shard_map/ppermute | solution.py:89
  67.8 31.7 %collective-permute-start.6 = (bf16[8,128,384]{2,1,0:T(8,128)(2,1)S(1)}, bf16[8,128,384]{2,1,0:T(8,128)(2,1)S(1)}, u32[]{:S(2)}, u32[]{:S(2)}) collective-permute-start(bf16[8,128,384]{2,1,0:T(8,128)(2,1)S(1)} %pad_maximum_fusion), channel_id=1, source_target_pairs={{0,2},{1,3},{2,0},{3,1},{4,6},{5,7},{6,4},{7,5},{8,10},{9,11},{10,... | collective-permute-start | bytes 2359304 | tf_op jit(solution)/shard_map/ppermute | solution.py:89
  73.9 12.0 %collective-permute-start.10 = (bf16[1,128,1024]{2,1,0:T(8,128)(2,1)S(1)}, bf16[1,128,1024]{2,1,0:T(8,128)(2,1)S(1)}, u32[]{:S(2)}, u32[]{:S(2)}) collective-permute-start(bf16[1,128,1024]{2,1,0:T(8,128)(2,1)S(1)} %copy-done.11), channel_id=1, source_target_pairs={{0,24},{1,25},{2,26},{3,27},{4,28},{5,29},{6,30},{7,31},{8,16},{9,... | collective-permute-start | bytes 786440 | tf_op jit(solution)/shard_map/ppermute | solution.py:89
  77.4 12.5 %collective-permute-start.8 = (bf16[1,128,1024]{2,1,0:T(8,128)(2,1)S(1)}, bf16[1,128,1024]{2,1,0:T(8,128)(2,1)S(1)}, u32[]{:S(2)}, u32[]{:S(2)}) collective-permute-start(bf16[1,128,1024]{2,1,0:T(8,128)(2,1)S(1)} %copy-done.11), channel_id=1, source_target_pairs={{0,8},{1,9},{2,10},{3,11},{4,12},{5,13},{6,14},{7,15},{8,0},{9,1},... | collective-permute-start | bytes 786440 | tf_op jit(solution)/shard_map/ppermute | solution.py:89
  77.4 22.1 %collective-permute-start.9 = (bf16[1,128,1024]{2,1,0:T(8,128)(2,1)S(1)}, bf16[1,128,1024]{2,1,0:T(8,128)(2,1)S(1)}, u32[]{:S(2)}, u32[]{:S(2)}) collective-permute-start(bf16[1,128,1024]{2,1,0:T(8,128)(2,1)S(1)} %copy-done.11), channel_id=1, source_target_pairs={{0,16},{1,17},{2,18},{3,19},{4,20},{5,21},{6,22},{7,23},{8,24},{9,... | collective-permute-start | bytes 786440 | tf_op jit(solution)/shard_map/ppermute | solution.py:89
  103.7 12.5 %collective-permute-start.12 = (bf16[16,128,384]{2,1,0:T(8,128)(2,1)}, bf16[16,128,384]{2,1,0:T(8,128)(2,1)S(1)}, u32[]{:S(2)}, u32[]{:S(2)}) collective-permute-start(bf16[16,128,384]{2,1,0:T(8,128)(2,1)} %constant_dynamic-update-slice_fusion.9.refs_2_), channel_id=1, source_target_pairs={{0,4},{1,5},{2,6},{3,7},{4,0},{5,1},{6,2},{7,3},{8,12},{9,13},{10,... | collective-permute-start | bytes 4718600 | tf_op jit(solution)/shard_map/ppermute | solution.py:89
  105.8 10.4 %collective-permute-start.11 = (bf16[16,128,384]{2,1,0:T(8,128)(2,1)}, bf16[16,128,384]{2,1,0:T(8,128)(2,1)S(1)}, u32[]{:S(2)}, u32[]{:S(2)}) collective-permute-start(bf16[16,128,384]{2,1,0:T(8,128)(2,1)} %constant_dynamic-update-slice_fusion.4.refs_0_), channel_id=1, source_target_pairs={{0,4},{1,5},{2,6},{3,7},{4,0},{5,1},{6,2},{7,3},{8,12},{9,13},{10,... | collective-permute-start | bytes 4718600 | tf_op jit(solution)/shard_map/ppermute | solution.py:89
  109.9 44.3 %collective-permute-start.13 = (bf16[4,128,1024]{2,1,0:T(8,128)(2,1)}, bf16[4,128,1024]{2,1,0:T(8,128)(2,1)}, u32[]{:S(2)}, u32[]{:S(2)}) collective-permute-start(bf16[4,128,1024]{2,1,0:T(8,128)(2,1)} %constant_dynamic-update-slice_fusion.refs_0_), channel_id=1, source_target_pairs={{0,1},{1,0},{2,3},{3,2},{4,5},{5,4},{6,7},{7,6},{8,9},{9,8},{10,11... | collective-permute-start | bytes 3145736 | tf_op jit(solution)/shard_map/ppermute | solution.py:89
  110.6 43.6 %collective-permute-start.14 = (bf16[4,128,1024]{2,1,0:T(8,128)(2,1)}, bf16[4,128,1024]{2,1,0:T(8,128)(2,1)}, u32[]{:S(2)}, u32[]{:S(2)}) collective-permute-start(bf16[4,128,1024]{2,1,0:T(8,128)(2,1)} %constant_dynamic-update-slice_fusion.refs_0_), channel_id=1, source_target_pairs={{0,2},{1,3},{2,0},{3,1},{4,6},{5,7},{6,4},{7,5},{8,10},{9,11},{10,... | collective-permute-start | bytes 3145736 | tf_op jit(solution)/shard_map/ppermute | solution.py:89
  111.2 56.2 %collective-permute-start.15 = (bf16[4,128,1024]{2,1,0:T(8,128)(2,1)}, bf16[4,128,1024]{2,1,0:T(8,128)(2,1)}, u32[]{:S(2)}, u32[]{:S(2)}) collective-permute-start(bf16[4,128,1024]{2,1,0:T(8,128)(2,1)} %constant_dynamic-update-slice_fusion.refs_0_), channel_id=1, source_target_pairs={{0,3},{1,2},{2,1},{3,0},{4,7},{5,6},{6,5},{7,4},{8,11},{9,10},{10,... | collective-permute-start | bytes 3145736 | tf_op jit(solution)/shard_map/ppermute | solution.py:89
  116.1 64.3 %collective-permute-start.16 = (bf16[4,128,1024]{2,1,0:T(8,128)(2,1)}, bf16[4,128,1024]{2,1,0:T(8,128)(2,1)}, u32[]{:S(2)}, u32[]{:S(2)}) collective-permute-start(bf16[4,128,1024]{2,1,0:T(8,128)(2,1)} %constant_dynamic-update-slice_fusion.refs_0_), channel_id=1, source_target_pairs={{0,4},{1,5},{2,6},{3,7},{4,0},{5,1},{6,2},{7,3},{8,12},{9,13},{10,... | collective-permute-start | bytes 3145736 | tf_op jit(solution)/shard_map/ppermute | solution.py:89
  168.1 12.3 %collective-permute-start.17 = (bf16[4,128,1024]{2,1,0:T(8,128)(2,1)}, bf16[4,128,1024]{2,1,0:T(8,128)(2,1)}, u32[]{:S(2)}, u32[]{:S(2)}) collective-permute-start(bf16[4,128,1024]{2,1,0:T(8,128)(2,1)} %get-tuple-element.135.refs_1_), channel_id=1, source_target_pairs={{0,4},{1,5},{2,6},{3,7},{4,0},{5,1},{6,2},{7,3},{8,12},{9,13},{10,... | collective-permute-start | bytes 3145736 | tf_op jit(solution)/shard_map/ppermute | solution.py:89
  168.2 12.2 %collective-permute-start.18 = (bf16[4,128,1024]{2,1,0:T(8,128)(2,1)}, bf16[4,128,1024]{2,1,0:T(8,128)(2,1)}, u32[]{:S(2)}, u32[]{:S(2)}) collective-permute-start(bf16[4,128,1024]{2,1,0:T(8,128)(2,1)} %get-tuple-element.136.refs_2_), channel_id=1, source_target_pairs={{0,4},{1,5},{2,6},{3,7},{4,0},{5,1},{6,2},{7,3},{8,12},{9,13},{10,... | collective-permute-start | bytes 3145736 | tf_op jit(solution)/shard_map/ppermute | solution.py:89
  168.7 11.8 %collective-permute-start.19 = (bf16[4,128,1024]{2,1,0:T(8,128)(2,1)}, bf16[4,128,1024]{2,1,0:T(8,128)(2,1)}, u32[]{:S(2)}, u32[]{:S(2)}) collective-permute-start(bf16[4,128,1024]{2,1,0:T(8,128)(2,1)} %get-tuple-element.137.refs_3_), channel_id=1, source_target_pairs={{0,4},{1,5},{2,6},{3,7},{4,0},{5,1},{6,2},{7,3},{8,12},{9,13},{10,... | collective-permute-start | bytes 3145736 | tf_op jit(solution)/shard_map/ppermute | solution.py:89
  220.1 41.8 %collective-permute-start.20 = (bf16[4,4,128,1024]{3,2,1,0:T(8,128)(2,1)}, bf16[4,4,128,1024]{3,2,1,0:T(8,128)(2,1)}, u32[]{:S(2)}, u32[]{:S(2)}) collective-permute-start(bf16[4,4,128,1024]{3,2,1,0:T(8,128)(2,1)} %get-tuple-element.153), channel_id=1, source_target_pairs={{0,4},{1,5},{2,6},{3,7},{4,0},{5,1},{6,2},{7,3},{8,12},{9,13},{10,... | collective-permute-start | bytes 12582920 | tf_op jit(solution)/shard_map/ppermute | solution.py:89
  261.8 28.2 %collective-permute-start.21 = (bf16[4,4,128,1024]{3,2,1,0:T(8,128)(2,1)}, bf16[4,4,128,1024]{3,2,1,0:T(8,128)(2,1)}, u32[]{:S(2)}, u32[]{:S(2)}) collective-permute-start(bf16[4,4,128,1024]{3,2,1,0:T(8,128)(2,1)} %get-tuple-element.161), channel_id=1, source_target_pairs={{0,4},{1,5},{2,6},{3,7},{4,0},{5,1},{6,2},{7,3},{8,12},{9,13},{10,... | collective-permute-start | bytes 12582920 | tf_op jit(solution)/shard_map/ppermute | solution.py:89
  268.3 49.5 %collective-permute-start.23 = (bf16[2,4,128,1024]{3,2,1,0:T(8,128)(2,1)}, bf16[2,4,128,1024]{3,2,1,0:T(8,128)(2,1)}, u32[]{:S(2)}, u32[]{:S(2)}) collective-permute-start(bf16[2,4,128,1024]{3,2,1,0:T(8,128)(2,1)} %get-tuple-element.168), channel_id=1, source_target_pairs={{0,2},{1,3},{2,0},{3,1},{4,6},{5,7},{6,4},{7,5},{8,10},{9,11},{10,... | collective-permute-start | bytes 6291464 | tf_op jit(solution)/shard_map/ppermute | solution.py:89
  269.3 18.7 %copy-start.51 = (f32[1,2048]{1,0:T(1,128)S(1)}, f32[1,2048]{1,0:T(1,128)}, u32[]{:S(2)}) copy-start(f32[1,2048]{1,0:T(1,128)} %get-tuple-element.199) | copy-start | bytes 24580
  269.3 18.7 %copy-start.52 = (f32[1,2048]{1,0:T(1,128)S(1)}, f32[1,2048]{1,0:T(1,128)}, u32[]{:S(2)}) copy-start(f32[1,2048]{1,0:T(1,128)} %get-tuple-element.200) | copy-start | bytes 24580
  316.2 7.0 %collective-permute-start.22 = (bf16[4,128,1024]{2,1,0:T(8,128)(2,1)}, bf16[4,128,1024]{2,1,0:T(8,128)(2,1)}, u32[]{:S(2)}, u32[]{:S(2)}) collective-permute-start(bf16[4,128,1024]{2,1,0:T(8,128)(2,1)} %bitcast.104), channel_id=1, source_target_pairs={{0,4},{1,5},{2,6},{3,7},{4,0},{5,1},{6,2},{7,3},{8,12},{9,13},{10,... | collective-permute-start | bytes 3145736 | tf_op jit(solution)/shard_map/ppermute | solution.py:89
  316.5 48.8 %collective-permute-start.25 = (bf16[2,4,128,1024]{3,2,1,0:T(8,128)(2,1)}, bf16[2,4,128,1024]{3,2,1,0:T(8,128)(2,1)}, u32[]{:S(2)}, u32[]{:S(2)}) collective-permute-start(bf16[2,4,128,1024]{3,2,1,0:T(8,128)(2,1)} %get-tuple-element.176), channel_id=1, source_target_pairs={{0,1},{1,0},{2,3},{3,2},{4,5},{5,4},{6,7},{7,6},{8,9},{9,8},{10,11... | collective-permute-start | bytes 6291464 | tf_op jit(solution)/shard_map/ppermute | solution.py:89
  321.9 72.6 %collective-permute-start.27 = (bf16[1,4,128,1024]{3,2,1,0:T(8,128)(2,1)}, bf16[1,4,128,1024]{3,2,1,0:T(8,128)(2,1)}, u32[]{:S(2)}, u32[]{:S(2)}) collective-permute-start(bf16[1,4,128,1024]{3,2,1,0:T(8,128)(2,1)} %get-tuple-element.185), channel_id=1, source_target_pairs={{0,1},{1,0},{2,3},{3,2},{4,5},{5,4},{6,7},{7,6},{8,9},{9,8},{10,11... | collective-permute-start | bytes 3145736 | tf_op jit(solution)/shard_map/ppermute | solution.py:89
  347.8 22.4 %collective-permute-start.24 = (bf16[4,128,1024]{2,1,0:T(8,128)(2,1)}, bf16[4,128,1024]{2,1,0:T(8,128)(2,1)}, u32[]{:S(2)}, u32[]{:S(2)}) collective-permute-start(bf16[4,128,1024]{2,1,0:T(8,128)(2,1)} %bitcast.105), channel_id=1, source_target_pairs={{0,4},{1,5},{2,6},{3,7},{4,0},{5,1},{6,2},{7,3},{8,12},{9,13},{10,... | collective-permute-start | bytes 3145736 | tf_op jit(solution)/shard_map/ppermute | solution.py:89
  369.2 67.3 %collective-permute-start.32 = (bf16[1,4,128,1024]{3,2,1,0:T(8,128)(2,1)}, bf16[1,4,128,1024]{3,2,1,0:T(8,128)(2,1)}, u32[]{:S(2)}, u32[]{:S(2)}) collective-permute-start(bf16[1,4,128,1024]{3,2,1,0:T(8,128)(2,1)} %get-tuple-element.195), channel_id=1, source_target_pairs={{0,2},{1,3},{2,0},{3,1},{4,6},{5,7},{6,4},{7,5},{8,10},{9,11},{10,... | collective-permute-start | bytes 3145736 | tf_op jit(solution)/shard_map/ppermute | solution.py:89
  394.4 5.1 collective-permute-start.26
  403.7 27.0 %copy-start.46 = (f32[1,3,256]{2,1,0:T(4,128)S(1)}, f32[1,3,256]{2,1,0:T(4,128)}, u32[]{:S(2)}) copy-start(f32[1,3,256]{2,1,0:T(4,128)} %concatenate.86) | copy-start | bytes 9220
  403.7 27.0 %copy-start.47 = (f32[1,3,256]{2,1,0:T(4,128)S(1)}, f32[1,3,256]{2,1,0:T(4,128)}, u32[]{:S(2)}) copy-start(f32[1,3,256]{2,1,0:T(4,128)} %concatenate.85) | copy-start | bytes 9220
  403.7 27.0 %copy-start.48 = (f32[1,3,256]{2,1,0:T(4,128)S(1)}, f32[1,3,256]{2,1,0:T(4,128)}, u32[]{:S(2)}) copy-start(f32[1,3,256]{2,1,0:T(4,128)} %concatenate.84) | copy-start | bytes 9220
  403.7 27.7 %copy-start.39 = (f32[112,128]{1,0:T(8,128)S(1)}, f32[112,128]{1,0:T(8,128)}, u32[]{:S(2)}) copy-start(f32[112,128]{1,0:T(8,128)} %constant_dynamic-update-slice_fusion.17) | copy-start | bytes 172036
  431.5 5.0 collective-permute-start.33
  432.1 14.6 %collective-permute-start.41 = (bf16[128,1024]{1,0:T(8,128)(2,1)}, bf16[128,1024]{1,0:T(8,128)(2,1)}, u32[]{:S(2)}, u32[]{:S(2)}) collective-permute-start(bf16[128,1024]{1,0:T(8,128)(2,1)} %get-tuple-element.218), channel_id=1, source_target_pairs={{0,8},{1,9},{2,10},{3,11},{4,12},{5,13},{6,14},{7,15},{8,0},{9,1},... | collective-permute-start | bytes 786440 | tf_op jit(solution)/shard_map/ppermute | solution.py:89
  432.1 21.7 %collective-permute-start.42 = (bf16[128,1024]{1,0:T(8,128)(2,1)}, bf16[128,1024]{1,0:T(8,128)(2,1)}, u32[]{:S(2)}, u32[]{:S(2)}) collective-permute-start(bf16[128,1024]{1,0:T(8,128)(2,1)} %get-tuple-element.219), channel_id=1, source_target_pairs={{0,16},{1,17},{2,18},{3,19},{4,20},{5,21},{6,22},{7,23},{8,24},{9,... | collective-permute-start | bytes 786440 | tf_op jit(solution)/shard_map/ppermute | solution.py:89
  435.1 18.8 %collective-permute-start.43 = (bf16[128,1024]{1,0:T(8,128)(2,1)}, bf16[128,1024]{1,0:T(8,128)(2,1)}, u32[]{:S(2)}, u32[]{:S(2)}) collective-permute-start(bf16[128,1024]{1,0:T(8,128)(2,1)} %get-tuple-element.220), channel_id=1, source_target_pairs={{0,24},{1,25},{2,26},{3,27},{4,28},{5,29},{6,30},{7,31},{8,16},{9,... | collective-permute-start | bytes 786440 | tf_op jit(solution)/shard_map/ppermute | solution.py:89
  437.1 25.1 %copy-start.29 = (bf16[128,1024]{1,0:T(8,128)(2,1)S(1)}, bf16[128,1024]{1,0:T(8,128)(2,1)}, u32[]{:S(2)}) copy-start(bf16[128,1024]{1,0:T(8,128)(2,1)} %get-tuple-element.217) | copy-start | bytes 786436
  441.6 16.0 %collective-permute-start.44 = (bf16[128,1024]{1,0:T(8,128)(2,1)}, bf16[128,1024]{1,0:T(8,128)(2,1)S(1)}, u32[]{:S(2)}, u32[]{:S(2)}) collective-permute-start(bf16[128,1024]{1,0:T(8,128)(2,1)} %get-tuple-element.222), channel_id=1, source_target_pairs={{0,8},{1,9},{2,10},{3,11},{4,12},{5,13},{6,14},{7,15},{8,0},{9,1},... | collective-permute-start | bytes 786440 | tf_op jit(solution)/shard_map/ppermute | solution.py:89
  441.6 43.5 %collective-permute-start.29 = (bf16[4,128,1024]{2,1,0:T(8,128)(2,1)}, bf16[4,128,1024]{2,1,0:T(8,128)(2,1)}, u32[]{:S(2)}, u32[]{:S(2)}) collective-permute-start(bf16[4,128,1024]{2,1,0:T(8,128)(2,1)} %get-tuple-element.191), channel_id=1, source_target_pairs={{0,3},{1,2},{2,1},{3,0},{4,7},{5,6},{6,5},{7,4},{8,11},{9,10},{10,... | collective-permute-start | bytes 3145736 | tf_op jit(solution)/shard_map/ppermute | solution.py:89
  446.7 43.1 %collective-permute-start.30 = (bf16[4,128,1024]{2,1,0:T(8,128)(2,1)}, bf16[4,128,1024]{2,1,0:T(8,128)(2,1)}, u32[]{:S(2)}, u32[]{:S(2)}) collective-permute-start(bf16[4,128,1024]{2,1,0:T(8,128)(2,1)} %get-tuple-element.192), channel_id=1, source_target_pairs={{0,2},{1,3},{2,0},{3,1},{4,6},{5,7},{6,4},{7,5},{8,10},{9,11},{10,... | collective-permute-start | bytes 3145736 | tf_op jit(solution)/shard_map/ppermute | solution.py:89
  453.8 37.0 %collective-permute-start.28 = (bf16[4,128,1024]{2,1,0:T(8,128)(2,1)}, bf16[4,128,1024]{2,1,0:T(8,128)(2,1)}, u32[]{:S(2)}, u32[]{:S(2)}) collective-permute-start(bf16[4,128,1024]{2,1,0:T(8,128)(2,1)} %bitcast.32), channel_id=1, source_target_pairs={{0,4},{1,5},{2,6},{3,7},{4,0},{5,1},{6,2},{7,3},{8,12},{9,13},{10,... | collective-permute-start | bytes 3145736 | tf_op jit(solution)/shard_map/ppermute | solution.py:89
  453.8 37.0 %collective-permute-start.31 = (bf16[4,128,1024]{2,1,0:T(8,128)(2,1)}, bf16[4,128,1024]{2,1,0:T(8,128)(2,1)}, u32[]{:S(2)}, u32[]{:S(2)}) collective-permute-start(bf16[4,128,1024]{2,1,0:T(8,128)(2,1)} %get-tuple-element.193), channel_id=1, source_target_pairs={{0,1},{1,0},{2,3},{3,2},{4,5},{5,4},{6,7},{7,6},{8,9},{9,8},{10,11... | collective-permute-start | bytes 3145736 | tf_op jit(solution)/shard_map/ppermute | solution.py:89
  455.9 20.1 %copy-start.1 = (bf16[1184,1024]{1,0:T(8,128)(2,1)S(1)}, bf16[1184,1024]{1,0:T(8,128)(2,1)}, u32[]{:S(2)}) copy-start(bf16[1184,1024]{1,0:T(8,128)(2,1)} %get-tuple-element.211) | copy-start | bytes 7274500
  457.6 16.5 %collective-permute-start.45 = (bf16[128,1024]{1,0:T(8,128)(2,1)}, bf16[128,1024]{1,0:T(8,128)(2,1)S(1)}, u32[]{:S(2)}, u32[]{:S(2)}) collective-permute-start(bf16[128,1024]{1,0:T(8,128)(2,1)} %get-tuple-element.223), channel_id=1, source_target_pairs={{0,16},{1,17},{2,18},{3,19},{4,20},{5,21},{6,22},{7,23},{8,24},{9,... | collective-permute-start | bytes 786440 | tf_op jit(solution)/shard_map/ppermute | solution.py:89
  474.1 8.6 %collective-permute-start.46 = (bf16[128,1024]{1,0:T(8,128)(2,1)}, bf16[128,1024]{1,0:T(8,128)(2,1)S(1)}, u32[]{:S(2)}, u32[]{:S(2)}) collective-permute-start(bf16[128,1024]{1,0:T(8,128)(2,1)} %get-tuple-element.224), channel_id=1, source_target_pairs={{0,24},{1,25},{2,26},{3,27},{4,28},{5,29},{6,30},{7,31},{8,16},{9,... | collective-permute-start | bytes 786440 | tf_op jit(solution)/shard_map/ppermute | solution.py:89
  482.7 8.1 %collective-permute-start.34 = (f32[112,128]{1,0:T(8,128)S(1)}, f32[112,128]{1,0:T(8,128)S(1)}, u32[]{:S(2)}, u32[]{:S(2)}) collective-permute-start(f32[112,128]{1,0:T(8,128)S(1)} %add_select_fusion.4), channel_id=1, source_target_pairs={{0,2},{1,3},{2,0},{3,1},{4,6},{5,7},{6,4},{7,5},{8,10},{9,11},{10,... | collective-permute-start | bytes 172040 | tf_op jit(solution)/shard_map/ppermute | solution.py:89
  497.5 1.3 collective-permute-start.35
  499.4 20.1 %copy-start.35 = (f32[112,128]{1,0:T(8,128)S(1)}, f32[112,128]{1,0:T(8,128)}, u32[]{:S(2)}) copy-start(f32[112,128]{1,0:T(8,128)} %copy-done.34) | copy-start | bytes 172036
  499.4 20.1 %copy-start.50 = (pred[112]{0:T(512)(128)(4,1)S(1)}, pred[112]{0:T(512)(128)(4,1)}, u32[]{:S(2)}) copy-start(pred[112]{0:T(512)(128)(4,1)} %iota_compare_fusion.1) | copy-start | bytes 340
  499.4 22.8 %copy-start.14 = (f32[128,512]{1,0:T(8,128)S(1)}, f32[128,512]{1,0:T(8,128)}, u32[]{:S(2)}) copy-start(f32[128,512]{1,0:T(8,128)} %get-tuple-element.276) | copy-start | bytes 786436
  499.4 22.8 %copy-start.16 = (f32[128,512]{1,0:T(8,128)S(1)}, f32[128,512]{1,0:T(8,128)}, u32[]{:S(2)}) copy-start(f32[128,512]{1,0:T(8,128)} %get-tuple-element.278) | copy-start | bytes 786436
  499.4 28.1 %copy-start.13 = (f32[128,512]{1,0:T(8,128)S(1)}, f32[128,512]{1,0:T(8,128)}, u32[]{:S(2)}) copy-start(f32[128,512]{1,0:T(8,128)} %get-tuple-element.277) | copy-start | bytes 786436
  499.4 28.1 %copy-start.15 = (f32[128,512]{1,0:T(8,128)S(1)}, f32[128,512]{1,0:T(8,128)}, u32[]{:S(2)}) copy-start(f32[128,512]{1,0:T(8,128)} %get-tuple-element.279) | copy-start | bytes 786436
  520.5 4.2 collective-permute-start.36
  524.8 12.7 %collective-permute-start.37 = (f32[112,128]{1,0:T(8,128)S(1)}, f32[112,128]{1,0:T(8,128)S(1)}, u32[]{:S(2)}, u32[]{:S(2)}) collective-permute-start(f32[112,128]{1,0:T(8,128)S(1)} %add_select_fusion.1), channel_id=1, source_target_pairs={{0,16},{1,17},{2,18},{3,19},{4,20},{5,21},{6,22},{7,23},{8,24},{9,... | collective-permute-start | bytes 172040 | tf_op jit(solution)/shard_map/ppermute | solution.py:89
  529.3 12.7 %collective-permute-start.38 = (bf16[128,1024]{1,0:T(8,128)(2,1)}, bf16[128,1024]{1,0:T(8,128)(2,1)S(1)}, u32[]{:S(2)}, u32[]{:S(2)}) collective-permute-start(bf16[128,1024]{1,0:T(8,128)(2,1)} %get-tuple-element.214), channel_id=1, source_target_pairs={{0,8},{1,9},{2,10},{3,11},{4,12},{5,13},{6,14},{7,15},{8,0},{9,1},... | collective-permute-start | bytes 786440 | tf_op jit(solution)/shard_map/ppermute | solution.py:89
  529.7 21.6 %collective-permute-start.39 = (bf16[128,1024]{1,0:T(8,128)(2,1)}, bf16[128,1024]{1,0:T(8,128)(2,1)S(1)}, u32[]{:S(2)}, u32[]{:S(2)}) collective-permute-start(bf16[128,1024]{1,0:T(8,128)(2,1)} %get-tuple-element.215), channel_id=1, source_target_pairs={{0,16},{1,17},{2,18},{3,19},{4,20},{5,21},{6,22},{7,23},{8,24},{9,... | collective-permute-start | bytes 786440 | tf_op jit(solution)/shard_map/ppermute | solution.py:89
  531.3 20.0 %collective-permute-start.40 = (bf16[128,1024]{1,0:T(8,128)(2,1)}, bf16[128,1024]{1,0:T(8,128)(2,1)}, u32[]{:S(2)}, u32[]{:S(2)}) collective-permute-start(bf16[128,1024]{1,0:T(8,128)(2,1)} %get-tuple-element.216), channel_id=1, source_target_pairs={{0,24},{1,25},{2,26},{3,27},{4,28},{5,29},{6,30},{7,31},{8,16},{9,... | collective-permute-start | bytes 786440 | tf_op jit(solution)/shard_map/ppermute | solution.py:89
  535.6 15.6 %copy-start.30 = (bf16[128,1024]{1,0:T(8,128)(2,1)S(1)}, bf16[128,1024]{1,0:T(8,128)(2,1)}, u32[]{:S(2)}) copy-start(bf16[128,1024]{1,0:T(8,128)(2,1)} %get-tuple-element.213) | copy-start | bytes 786436
  (50 other events, 259.4 us)
Sparse Core Ops, SparseCore 0:
  19.8 65.4 all-gather.4
  113.5 84.6 all-gather.6

commit v3 on v2

--- a/solution.py
+++ b/solution.py
@@ -61,7 +61,7 @@
             out_shape=[shape for shape, _ in outs] + [jax.ShapeDtypeStruct(a.shape, a.dtype) for a in through],
             input_output_aliases={1 + n_in + i: n_out + i for i in range(n)},
             compiler_params=pltpu.CompilerParams(vmem_limit_bytes=VMEM_LIMIT),
-            cost_estimate=pl.CostEstimate(flops=int(2e11), bytes_accessed=int(2e8), transcendentals=0),
+            cost_estimate=pl.CostEstimate(flops=int(us * 1.1e9), bytes_accessed=int(us * 1e6), transcendentals=0),
             name=name,
         )(self.me, *[a for a, _ in ins], *through)
         self.token = got[n_out]
@@ -89,26 +89,6 @@
     return lax.ppermute(x, AXES, [(i, i ^ mask) for i in range(size)])
 
 
-class Gather:
-    def __init__(self, lay, piece):
-        self.lay = lay
-        self.held = piece[None]
-
-    def along(self):
-        step = 2 * self.lay.nt
-        self.got = [self.held] + [swap(self.held, z * step, self.lay.size) for z in range(1, self.lay.nz)]
-
-    def spread(self):
-        self.held = jnp.concatenate(self.got)
-        self.got = [self.held] + [swap(self.held, t, self.lay.size) for t in range(1, self.lay.nt)]
-        self.other = [swap(self.held, self.lay.core, self.lay.size)]
-
-    def share(self):
-        lay = self.lay
-        self.bufs = self.got + self.other + [swap(b, lay.core, lay.size) for b in self.got[1:]]
-        self.pieces = [(c * lay.nt + t, z, z, t, c) for c in range(2) for t in range(lay.nt) for z in range(lay.nz)]
-
-
 class Chain:
     def __init__(self, lay, piece, reverse):
         self.lay = lay
@@ -129,9 +109,21 @@
         self.offs = self.offs + [(z ^ dz, t ^ dt) for z, t in self.offs]
         self.held = jnp.concatenate([self.held, self.got])
 
+    def send_last(self):
+        self.send()
+        self.bufs = [self.held, None, swap(self.held, self.lay.core, self.lay.size), None]
+
     def share(self):
-        self.bufs = [self.held, swap(self.held, self.lay.core, self.lay.size)]
-        self.pieces = [(c, i, z, t, c) for c in range(2) for i, (z, t) in enumerate(self.offs)]
+        (kind, b), lay = self.stages.pop(0), self.lay
+        dz, dt = ((1 << b), 0) if kind == "z" else (0, (1 << b))
+        self.bufs[1], self.bufs[3] = self.got, swap(self.got, lay.core, lay.size)
+        more = [(z ^ dz, t ^ dt) for z, t in self.offs]
+        self.pieces = [
+            (2 * c + k, i, z, t, c)
+            for c in range(2)
+            for k, offs in enumerate((self.offs, more))
+            for i, (z, t) in enumerate(offs)
+        ]
 
 
 class Shards:
@@ -141,7 +133,7 @@
 
 def gate(run, *lists):
     flat = [x for some in lists for x in some]
-    _, flat = run("gate", 0.5, lambda *refs: None, (1,), [], [], (), flat)
+    _, flat = run("gate", 0, lambda *refs: None, (1,), [], [], (), flat)
     flat = list(flat)
     return [[flat.pop(0) for _ in some] for some in lists]
 
@@ -321,7 +313,7 @@
         width = chain.held.shape[-1]
         at = 0 if h == 0 else 3 * lay.cw - width
         spans = [(0, width, lambda to, t: (place(to), at))]
-        start_pieces(lay, chain, bufs[2 * h : 2 * h + 2], me_ref, spans, sem, keep)
+        start_pieces(lay, chain, bufs[4 * h : 4 * h + 4], me_ref, spans, sem, keep)
 
 
 def attend_all(lay, run, joint, normed, bias_rows):
@@ -331,8 +323,8 @@
     wide = 3 * cw
 
     def kernel(me_ref, *refs):
-        bufs = refs[:4]
-        x_ref, b_ref, p_ref, o_ref, lse_ref, top_ref, w, sem = refs[4:]
+        bufs = refs[:8]
+        x_ref, b_ref, p_ref, o_ref, lse_ref, top_ref, w, sem = refs[8:]
         o, i = pl.program_id(0), pl.program_id(1)
 
         @pl.when((o == 0) & (i == 0))
@@ -389,7 +381,7 @@
         sec_ref[...] = (unit * g_ref[...] + s_ref[...]).astype(BF)
 
     out, _ = run(
-        "out_project", 10, kernel, (rows // SP,),
+        "out_project", 9, kernel, (rows // SP,),
         [(b, ANY) for b in group.bufs]
         + [(mixed, row_block(D)), (inputs, row_block(D))]
         + [(v, one_row(D)) for v in (bias, gain, shift)],
@@ -402,15 +394,16 @@
     return out
 
 
-def feed(lay, run, group, second, dresult, bias, dsecond=None, through=()):
+def feed(lay, run, expand, shrink, second, dresult, bias, dsecond=None):
     rows = second.shape[0]
     half = lay.cols // 2
     more = dsecond is not None
-    nb = len(group.bufs)
+    (group_e, first_e), (group_s, first_s) = expand, shrink
+    ne, ns = len(group_e.bufs), len(group_s.bufs)
 
     def kernel(me_ref, *refs):
-        bufs = refs[:nb]
-        x_ref, g_ref, b_ref, *refs = refs[nb:]
+        bufs_e, bufs_s = refs[:ne], refs[ne : ne + ns]
+        x_ref, g_ref, b_ref, *refs = refs[ne + ns :]
         if more:
             before, *refs = refs
         a_ref, s_ref, sec_ref, other, mine, we, ws, d_s, acc, sem_e, sem_s, sem = refs
@@ -418,10 +411,10 @@
 
         @pl.when(o == 0)
         def _():
-            spans = [(0, half, lambda to, t: (we.at[to], 0))]
-            start_pieces(lay, group, bufs, me_ref, spans, lambda to: sem_e.at[to])
-            spans = [(half, half, lambda to, t: (ws.at[to], 0))]
-            start_pieces(lay, group, bufs, me_ref, spans, lambda to: sem_s.at[to])
+            spans = [(first_e, half, lambda to, t: (we.at[to], 0))]
+            start_pieces(lay, group_e, bufs_e, me_ref, spans, lambda to: sem_e.at[to])
+            spans = [(first_s, half, lambda to, t: (ws.at[to], 0))]
+            start_pieces(lay, group_s, bufs_s, me_ref, spans, lambda to: sem_s.at[to])
             if more:
                 pltpu.make_async_copy(before, acc, sem).start()
                 pltpu.make_async_copy(before, acc, sem).wait()
@@ -455,9 +448,9 @@
     full = pl.BlockSpec((rows, D), lambda o, m: (0, 0))
     weights = pltpu.VMEM((lay.nt, D, half), BF)
     sems = pltpu.SemaphoreType.DMA((lay.nt,))
-    return run(
-        "feed", 33, kernel, (lay.nt,),
-        [(b, ANY) for b in group.bufs]
+    out, _ = run(
+        "feed", 40, kernel, (lay.nt,),
+        [(b, ANY) for b in (*group_e.bufs, *group_s.bufs)]
         + [(second, full), (dresult, full), (bias, line)] + ([(dsecond, ANY)] if more else []),
         [
             (jax.ShapeDtypeStruct((rows, lay.nt * half), BF), pl.BlockSpec((rows, half), lambda o, m: (0, o ^ m[2]))),
@@ -474,40 +467,43 @@
             sems,
             pltpu.SemaphoreType.DMA,
         ],
-        through,
-    )
-
-
-def feed_out(lay, run, groups, active, middle, bias, more=()):
-    rows = middle.shape[0]
+    )
+    return out
+
+
+def feed_out(lay, run, shrink, active, base, bias=None, more=()):
+    rows = base.shape[0]
     own = rows // SP
     half = lay.cols // 2
     wide = lay.nt * half
-
-    n0, n1 = [len(group.bufs) for group in groups]
+    group, first = shrink
+    nb = len(group.bufs)
 
     def kernel(me_ref, *refs):
-        bufs = (refs[:n0], refs[n0 : n0 + n1])
-        a0_ref, a1_ref, mid_ref, b_ref, o_ref, w, sem = refs[n0 + n1 :]
+        bufs = refs[:nb]
+        a_ref, base_ref, *refs = refs[nb:]
+        o_ref, w, sem = refs[-3:]
 
         @pl.when(pl.program_id(0) == 0)
         def _():
-            for g, group in enumerate(groups):
-                spans = [(half, half, lambda to, t, g=g: (w.at[g], t * half))]
-                start_pieces(lay, group, bufs[g], me_ref, spans, lambda to: sem)
+            spans = [(first, half, lambda to, t: (w, t * half))]
+            start_pieces(lay, group, bufs, me_ref, spans, lambda to: sem)
             wait_all(w, sem)
 
-        live = me_ref[2] * own + pl.program_id(0) < me_ref[3]
-        out = mid_ref[...].astype(F32) + dotf(a0_ref[...], w[0], 1, 1) + dotf(a1_ref[...], w[1], 1, 1) + b_ref[...]
-        o_ref[...] = jnp.where(live, out, 0.0).astype(BF)
+        out = base_ref[...].astype(F32) + dotf(a_ref[...], w[...], 1, 1)
+        if bias is None:
+            o_ref[...] = out
+        else:
+            live = me_ref[2] * own + pl.program_id(0) < me_ref[3]
+            o_ref[...] = jnp.where(live, out + refs[0][...], 0.0).astype(BF)
 
     (result,), more = run(
-        "feed_out", 20, kernel, (own,),
-        [(b, ANY) for g in groups for b in g.bufs]
-        + [(a, row_block(wide)) for a in active]
-        + [(middle, row_block(D)), (bias, one_row(D))],
-        [(jax.ShapeDtypeStruct((rows, D), BF), row_block(D))],
-        [pltpu.VMEM((2, D, wide), BF), pltpu.SemaphoreType.DMA],
+        "feed_out", 12, kernel, (own,),
+        [(b, ANY) for b in group.bufs]
+        + [(active, row_block(wide)), (base, row_block(D))]
+        + ([] if bias is None else [(bias, one_row(D))]),
+        [(jax.ShapeDtypeStruct((rows, D), F32 if bias is None else BF), row_block(D))],
+        [pltpu.VMEM((D, wide), BF), pltpu.SemaphoreType.DMA],
         more,
     )
     return result, more
@@ -560,7 +556,7 @@
 
     piece = jax.ShapeDtypeStruct((nt, lay.nz, lay.rows, cw), BF)
     out, _ = run(
-        "feed_back", 10, kernel, (steps,),
+        "feed_back", 19, kernel, (steps,),
         [(b, ANY) for b in group.bufs]
         + [(v, row_block(D)) for v in (dsecond, middle, dresult, mixed)]
         + [(gain, one_row(D))],
@@ -576,7 +572,7 @@
     return out
 
 
-def attend_back(lay, run, to, joint, packed, mixed, dmixed, lse, normed, output, last=None):
+def attend_back(lay, run, to, joint, packed, mixed, dmixed, lse, normed, output, last=None, more=()):
     rows = packed.shape[0]
     own, cw = rows // SP, lay.cw
     hl = cw // HEAD_DIM
@@ -584,8 +580,8 @@
     np = 0 if last is None else len(last[0])
 
     def kernel(me_ref, *refs):
-        bufs = refs[:4]
-        p_ref, m_ref, g_ref, lse_ref, x_ref, go_other, go_own, *refs = refs[4:]
+        bufs = refs[:8]
+        p_ref, m_ref, g_ref, lse_ref, x_ref, go_other, go_own, *refs = refs[8:]
         if last is not None:
             parts = refs[:np]
             in_ref, dm_ref, gain_ref, *refs = refs[np:]
@@ -633,8 +629,8 @@
     spec = lambda width: pl.BlockSpec((SP, width), lambda i, m: (i, to ^ m[2]))
     part = pl.BlockSpec((1, lay.nz, lay.rows, cw), lambda i, m: (to, 0, 0, 0))
     piece = jax.ShapeDtypeStruct((1, lay.nz, lay.rows, w3 + cw), BF)
-    out, _ = run(
-        "attend_back", 38, kernel, (own,),
+    return run(
+        "attend_back", 20, kernel, (own,),
         [(b, ANY) for chain in joint for b in chain.bufs]
         + [
             (packed, spec(w3)),
@@ -653,8 +649,8 @@
         + ([(jax.ShapeDtypeStruct((2, D), F32), whole((2, D)))] if last else [])
         + [(piece, whole(piece.shape))] * 2,
         [pltpu.VMEM((D, w3), BF), pltpu.VMEM((SP, w3), BF), pltpu.VMEM((D, w3), F32), pltpu.SemaphoreType.DMA],
-    )
-    return out
+        more,
+    )
 
 
 def insert_bit(s, b, value):
@@ -675,7 +671,7 @@
 
     block = pl.BlockSpec((z, dr, w), lambda s, m: (0, 0, s))
     out = (jax.ShapeDtypeStruct((dr, width), BF), pl.BlockSpec((dr, w), lambda s, m: (0, s)))
-    sums, more = run("add_plane", 4, kernel, (width // w,), [(x, block) for x in arrays], [out] * z, (), more)
+    sums, more = run("add_plane", 0, kernel, (width // w,), [(x, block) for x in arrays], [out] * z, (), more)
     return [swap(x, k * 2 * lay.nt, lay.size) if k else x for k, x in enumerate(sums)], more
 
 
@@ -691,73 +687,77 @@
         self.lay = lay
         bits = list(range(lay.tbits))
         self.bits = bits[::-1] if reverse else bits
-        self.left = bits[::-1]
-        self.keep = own
-        self.got = swap(other, lay.core, lay.size)
-
-    def fold(self, run):
+        self.keep, self.got = [own], [swap(other, lay.core, lay.size)]
+        self.left = list(range(lay.nt))
+
+    def fold(self, run, more=()):
         bit = self.bits.pop(0)
-        low = len(self.left) - 1 - self.left.index(bit)
-        self.left.remove(bit)
-        n, z, dr, width = self.keep.shape
-        block = (1, z // 2, dr, width)
-        ins, outs = [], []
-        for value in (1, 0):
-            spec = pl.BlockSpec(block, lambda s, j, m, value=value: (insert_bit(s, low, value), j, 0, 0))
-            ins += [(self.keep, spec), (self.got, spec)]
-            shape = jax.ShapeDtypeStruct((n // 2, z, dr, width), BF)
-            outs.append((shape, pl.BlockSpec(block, lambda s, j, m: (s, j, 0, 0))))
+        n = len(self.left)
+        z, dr, width = self.keep[0].shape[-3:]
+        one = len(self.keep) == 1
+        block = pl.BlockSpec((n, 1, dr, width), lambda s, m: (0, s, 0, 0)) if one else None
+        piece = pl.BlockSpec((1, dr, width), lambda s, m: (s, 0, 0))
+        k = len(self.keep)
 
         def kernel(me_ref, *refs):
-            for i in range(2):
-                refs[4 + i][...] = refs[2 * i][...] + refs[2 * i + 1][...]
-
-        (send, self.keep), _ = run("add", 4, kernel, (n // 2, 2), ins, outs)
-        self.got = swap(send, 1 << bit, self.lay.size)
+            for i in range(n):
+                a, b = (refs[0][i], refs[1][i]) if one else (refs[i][...], refs[k + i][...])
+                refs[2 * k + i][...] = a + b
+
+        shape = jax.ShapeDtypeStruct((z, dr, width), BF)
+        sums, more = run(
+            "add", 0, kernel, (z,), [(x, block or piece) for x in (*self.keep, *self.got)], [(shape, piece)] * n, (), more
+        )
+        self.keep = [x for t, x in zip(self.left, sums) if not t >> bit & 1]
+        self.got = [swap(x, 1 << bit, self.lay.size) for t, x in zip(self.left, sums) if t >> bit & 1]
+        self.left = [t for t in self.left if not t >> bit & 1]
+        return more
 
     def along(self, run, more=()):
-        self.ends, more = along(self.lay, run, [self.keep[0], self.got[0]], more)
+        self.ends, more = along(self.lay, run, self.keep + self.got, more)
         return more
 
 
 class Direct:
     def __init__(self, lay):
         self.lay = lay
-        self.parts = []
+        self.parts, self.waiting = [], []
 
     def start(self, to, other, own):
-        self.waiting = (to, own[0], swap(other[0], self.lay.core, self.lay.size))
-
-    def spread(self, run):
-        to, own, got = self.waiting
+        self.waiting.append((to, own[0], swap(other[0], self.lay.core, self.lay.size)))
+
+    def spread(self, run, more=()):
+        to, own, got = self.waiting.pop(0)
         z, dr, width = own.shape
 
         def kernel(me_ref, a_ref, b_ref, o_ref):
             o_ref[...] = a_ref[...] + b_ref[...]
 
         block = pl.BlockSpec((1, dr, width), lambda s, m: (s, 0, 0))
-        (x,), _ = run("add_core", 2, kernel, (z,), [(own, block), (got, block)], [(jax.ShapeDtypeStruct(own.shape, BF), block)])
+        shape = jax.ShapeDtypeStruct(own.shape, BF)
+        (x,), more = run("add_core", 0, kernel, (z,), [(own, block), (got, block)], [(shape, block)], (), more)
         self.parts.append(swap(x, to, self.lay.size))
+        return more
 
     def along(self, run, more=()):
-        self.ends, more = along(self.lay, run, list(self.waiting[1:]) + self.parts, more)
+        self.ends, more = along(self.lay, run, [*self.waiting[0][1:], *self.parts], more)
         return more
 
 
 class Sum:
     def __init__(self, lay, x, combine=jnp.add):
         self.lay, self.x, self.combine = lay, x, combine
-        self.masks = [1 << b for b in range((lay.size - 1).bit_length())]
+        step = 2 * lay.nt
+        self.stages = [list(range(1, lay.nt)), [z * step for z in range(1, lay.nz)], [lay.core]]
         self.send()
 
     def send(self):
-        self.got = swap(self.x, self.masks.pop(0), self.lay.size)
+        self.got = [swap(self.x, mask, self.lay.size) for mask in self.stages.pop(0)]
 
     def land(self, passed=None):
-        if passed:
-            self.got = passed[0]
-        self.x = self.combine(self.x, self.got)
-        if self.masks:
+        for got in passed or self.got:
+            self.x = self.combine(self.x, got)
+        if self.stages:
             self.send()
         else:
             self.got = None
@@ -801,20 +801,16 @@
     count = image_count[0]
     run = Runner(jnp.stack([dp // 2, dp % 2, tensor, count]))
 
-    shrink_t = shrink_weight.T
     split = 3 * cw // 2 if cw % 256 == 0 else 2 * cw
     flat = joint_weight.reshape(dr, 3 * cw)
     joint = [Chain(lay, flat[:, :split], False), Chain(lay, flat[:, split:], True)]
+    for chain in joint:
+        chain.send()
     small = jnp.concatenate([joint_bias.reshape(-1), expand_bias.reshape(-1)])
     n_small = small.shape[0]
-    piece = jnp.concatenate([output_weight.T, jnp.pad(small[None], ((0, 15), (0, cw - n_small)))])
-    ((piece,),) = gate(run, [piece])
-    output = Shards(lay, piece)
-    halves = [
-        jnp.concatenate([w[:, g * half : (g + 1) * half] for w in (expand_weight, shrink_t)], axis=1)
-        for g in range(2)
-    ]
-    feeds = [Gather(lay, halves[0])]
+    output = jnp.concatenate([output_weight.T, jnp.pad(small[None], ((0, 15), (0, cw - n_small)))])
+    ((output,),) = gate(run, [output])
+    output = Shards(lay, output)
 
     biases = output.bufs[0][:, dr].astype(F32)
     nb = joint_bias.size
@@ -834,63 +830,93 @@
     normed = (unit * first_gain + first_shift).astype(BF)
     row = lambda v: v.reshape(1, D)
 
-    for chain in joint:
+    def land(chains):
+        for chain in chains:
+            chain.land()
+            chain.send_last() if len(chain.stages) == 1 else chain.send()
+
+    ((joint[0].got, joint[1].got),) = gate(run, [chain.got for chain in joint])
+    land(joint)
+    shrink_t = (shrink_weight + run.token[0, 0].astype(BF)).T
+    feeds = [Chain(lay, expand_weight[:, :half], False), Chain(lay, shrink_t[:, :half], True)]
+    rest = jnp.concatenate([expand_weight[:, half:], shrink_t[:, half:]], axis=1)
+    for chain in feeds:
         chain.send()
     while len(joint[0].stages) > 2:
-        for chain in joint:
-            chain.land()
-            chain.send()
-    (joint[0].got, joint[1].got), (feeds[0].held,) = gate(run, [chain.got for chain in joint], [feeds[0].held])
+        land(joint)
+        if len(feeds[0].stages) > 3:
+            land(feeds)
+    (joint[0].got, joint[1].got), (feeds[0].got, feeds[1].got) = gate(
+        run, [chain.got for chain in joint], [chain.got for chain in feeds]
+    )
+    land(joint)
+    while len(feeds[0].stages) > 2:
+        land(feeds)
+    (joint[0].got, joint[1].got), (feeds[0].got, feeds[1].got), (inputs, dresult, normed), (rest,) = gate(
+        run, [chain.got for chain in joint], [chain.got for chain in feeds], [inputs, dresult, normed], [rest]
+    )
     for chain in joint:
-        chain.land()
-        chain.send()
-    feeds[0].along()
-    (joint[0].got, joint[1].got), feeds[0].got[1:], (inputs, dresult, normed), (halves[1],) = gate(
-        run, [chain.got for chain in joint], feeds[0].got[1:], [inputs, dresult, normed], [halves[1]]
-    )
-    for chain in joint:
-        chain.land()
         chain.share()
-    feeds.append(Shards(lay, halves[1]))
-    feeds[0].spread()
+    rest = Shards(lay, rest)
+    land(feeds)
     packed, mixed, lse, tops = attend_all(lay, run, joint, normed, bias_rows)
-    (feeds[0].got[1:],) = gate(run, feeds[0].got[1:])
-    feeds[0].share()
+    (feeds[0].got, feeds[1].got), = gate(run, [chain.got for chain in feeds])
+    for chain in feeds:
+        chain.share()
+    shrinks = [(feeds[1], 0), (rest, half)]
     middle, second = out_project(
         lay, run, output, mixed, inputs, row(output_bias), row(second_gain), row(second_shift)
     )
 
-    (active0, expand_sum0, dsecond, *pieces), _ = feed(lay, run, feeds[0], second, dresult, expand_rows[0])
+    active0, expand_sum0, dsecond, *pieces = feed(
+        lay, run, (feeds[0], 0), shrinks[0], second, dresult, expand_rows[0]
+    )
     grads = [Butterfly(lay, True, *pieces)]
     active1, expand_sum1, dsecond, *pieces = feed(
-        lay, run, feeds[1], second, dresult, expand_rows[1], dsecond
-    )[0]
+        lay, run, (rest, 0), shrinks[1], second, dresult, expand_rows[1], dsecond
+    )
     grads.append(Butterfly(lay, False, *pieces))
-    grads[0].fold(run)
+    for sc in grads:
+        sc.fold(run)
     dmiddle, dmixed, sums_two, *out_pieces = feed_back(
         lay, run, output, dsecond, middle, dresult, mixed, row(second_gain)
     )
-    grads[1].fold(run)
 
     packed_sums, dnormed = [], []
     total = Direct(lay)
 
-    def back(to, last=None):
-        part, out, *more = attend_back(
-            lay, run, to, joint, packed, mixed, dmixed, lse, normed, out_pieces, last
+    def back(to, last=None, more=()):
+        (part, out, *rest), more = attend_back(
+            lay, run, to, joint, packed, mixed, dmixed, lse, normed, out_pieces, last, more
         )
         packed_sums.append(part)
-        total.start(to, *more[-2:])
-        return out, more[0]
+        total.start(to, *rest[-2:])
+        return out, rest[0], list(more)
+
+    def spread(more=()):
+        return list(total.spread(run, more))
 
     for n, to in enumerate(range(nt - 1, 0, -1)):
-        dnormed.append(back(to)[0])
-        if n < 2:
-            grads[n].fold(run)
-        elif n == 2 and not grads[0].bits:
-            grads[0].along(run)
-        total.spread(run)
-    token_rows, sums_one = back(0, (dnormed, inputs, dmiddle, row(first_gain)))
+        if n == 0:
+            out, _, more = back(to, None, [grads[0].got[0], grads[1].got[0]])
+            grads[0].got[0], grads[1].got[0] = more
+        else:
+            out = back(to)[0]
+        dnormed.append(out)
+        if grads[0].bits:
+            for sc in grads:
+                sc.fold(run)
+            if n:
+                spread()
+        elif not hasattr(grads[0], "ends"):
+            for sc in grads:
+                sc.along(run)
+            spread()
+        else:
+            at = len(total.parts) - 1
+            total.parts[at], *grads[0].ends[1:] = spread([total.parts[at], *grads[0].ends[1:]])
+    token_rows, sums_one, _ = back(0, (dnormed, inputs, dmiddle, row(first_gain)))
+    grads[1].ends[1:] = spread(grads[1].ends[1:])
 
     tops = jnp.max(tops, axis=-1).reshape(own, HEADS) / LOG2E
     peak = jnp.max(jnp.where(image_live[:, None], tops, NEG), axis=0)
@@ -902,14 +928,10 @@
     sums = jnp.concatenate([peak] + [v.reshape(-1, 128) for v in vectors])
     is_peak = lax.broadcasted_iota(jnp.int32, sums.shape, 0) < HEADS
     small = Sum(lay, sums, lambda a, b: jnp.where(is_peak, jnp.maximum(a, b), a + b))
-    while grads[1].bits:
-        for sc in grads:
-            sc.fold(run)
-    if nt != 4:
-        grads[0].along(run)
-    small.land(grads[1].along(run, [small.got]))
-    small.land(total.along(run, [small.got]))
-    result, passed = feed_out(lay, run, feeds, [active0, active1], middle, row(shrink_bias), [small.got])
+    result, passed = feed_out(lay, run, shrinks[0], active0, middle, None, small.got)
+    small.land(passed)
+    total.along(run)
+    result, passed = feed_out(lay, run, shrinks[1], active1, result, row(shrink_bias), small.got)
     small.land(passed)
     while small.got is not None:
         small.land()

time: 570 us -> 526 us (0.923)
  the two profiles are of different devices: /device:TPU:0 before, /device:TPU:14 now
where the time goes in v3:
time: 526 us; the launch traced here: 518 us
  Pallas kernels  308 us (59%)
  waiting for transfers between devices  56.3 us (11%)
  starting transfers between devices  53.2 us (10%)
  local copies, waits for them, and re-layouts  52.5 us (10%)
  other arithmetic  31.5 us (6%)
  between operations  16.1 us (3%)
    pallas_call x26, Pallas kernels, __call__(): pl.pallas_call(body, grid_spec=pltpu.PrefetchScalarGridSpec(num_scalar_pr...  308 us
    ppermute x55, waiting for transfers between devices, swap(): return lax.ppermute(x, AXES, [(i, i ^ mask) for i in range(size)])  56.3 us
    ppermute x55, starting transfers between devices, swap(): return lax.ppermute(x, AXES, [(i, i ^ mask) for i in range(size)])  53.1 us
    unnamed x148, local copies, waits for them, and re-layouts  24.7 us
    concatenate x12, other arithmetic, land(): self.held = jnp.concatenate([self.held, self.got])  11.5 us
  transfers between devices with their start and end apart: 57, of which 11 were waited for; matrix products, arithmetic and copies ran while one was open for 11% of the time, Pallas kernels for 57%

profile of v3, /device:TPU:14, one launch (start us, length us, event | category | flops | bytes accessed | tf_op | source)
XLA Modules:
  0.0 517.6 jit_solution(5816433532241776140)
XLA Ops:
  14.4 2.7 collective-permute-start
  17.6 1.6 fusion.9
  19.2 2.6 collective-permute-start.6
  21.8 2.2 reshape.205
  25.0 1.3 copy-done.2
  26.2 1.7 broadcast_select_fusion
  32.9 3.6 collective-permute-start.8
  40.9 1.5 collective-permute-start.7
  43.8 1.6 collective-permute-start.9
  46.2 1.9 collective-permute-done.2
  50.7 1.7 pad.12
  52.3 2.1 reshape.207
  54.5 1.7 pad.13
  56.2 2.8 collective-permute-done.5.refs_2_
  59.0 12.8 %collective-permute-done.3.refs_1_ = bf16[4,128,384]{2,1,0:T(8,128)(2,1)} collective-permute-done((bf16[4,128,384]{2,1,0:T(8,128)(2,1)}, bf16[4,128,384]{2,1,0:T(8,128)(2,1)}, u32[]{:S(2)}, u32[]{:S(2)}) %collective-permute-start.3) | collective-permute-done | bytes 393248 | tf_op jit(solution)/shard_map/ppermute | solution.py:89
  77.2 2.0 collective-permute-start.12
  79.3 2.4 add_convert_fusion.refs_7_
  82.4 6.0 %collective-permute-done.13.refs_4_ = bf16[4,128,512]{2,1,0:T(8,128)(2,1)S(1)} collective-permute-done((bf16[4,128,512]{2,1,0:T(8,128)(2,1)S(1)}, bf16[4,128,512]{2,1,0:T(8,128)(2,1)S(1)}, u32[]{:S(2)}, u32[]{:S(2)}) %collective-permute-start.13) | collective-permute-done | bytes 524320 | tf_op jit(solution)/shard_map/ppermute | solution.py:89
  88.4 5.6 %collective-permute-done.12.refs_3_ = bf16[4,128,512]{2,1,0:T(8,128)(2,1)S(1)} collective-permute-done((bf16[4,128,512]{2,1,0:T(8,128)(2,1)S(1)}, bf16[4,128,512]{2,1,0:T(8,128)(2,1)S(1)}, u32[]{:S(2)}, u32[]{:S(2)}) %collective-permute-start.12) | collective-permute-done | bytes 524320 | tf_op jit(solution)/shard_map/ppermute | solution.py:89
  96.8 2.1 pad_maximum_fusion.1.refs_4_.refs_0_
  104.5 36.3 %attend.1 = (bf16[1184,3072]{1,0:T(8,128)(2,1)}, bf16[1184,1024]{1,0:T(8,128)(2,1)}, f32[2,4,4,640]{3,2,1,0:T(4,128)}, f32[2,4,4,640]{3,2,1,0:T(4,128)}, f32[8,128]{1,0:T(8,128)}) custom-call(s32[4]{0:T(128)} %pad_add_fusion.me_ref, bf16[8,128,384]{2,1,0:T(8,128)(2,1)} %copy-done.41, ...), custom_call_target="tpu_custom_call", output_to_operand_aliasing={{4}: (11, {})} | custom-call | flops 39600001024 | bytes 36000000 | tf_op jit(solution)/shard_map/attend/pallas_call | solution.py:52
  144.6 9.3 %out_project.1 = (bf16[1184,1024]{1,0:T(8,128)(2,1)}, bf16[1184,1024]{1,0:T(8,128)(2,1)}, f32[8,128]{1,0:T(8,128)}) custom-call(s32[4]{0:T(128)} %pad_add_fusion.me_ref, bf16[32,144,256]{2,1,0:T(8,128)(2,1)} %bitcast.109, bf16[1184,1024]{1,0:T(8,128)(2,1)} %get-tuple-element.156.refs_1_.refs_4_.refs_9_, ...), custom_call_target="tpu_custom_call", output_to_operand_aliasing={{2}: (7, {})} | custom-call | flops 9900000256 | bytes 9000000 | tf_op jit(solution)/shard_map/out_project/pallas_call | solution.py:52
  155.3 39.7 %feed.2 = (bf16[1184,2048]{1,0:T(8,128)(2,1)}, f32[1,2048]{1,0:T(1,128)}, f32[1184,1024]{1,0:T(8,128)}, bf16[4,4,128,1024]{3,2,1,0:T(8,128)(2,1)}, bf16[4,4,128,1024]{3,2,1,0:T(8,128)(2,1)}, /*index=5*/f32[8,128]{1,0:T(8,128)}) custom-call(s32[4]{0:T(128)} %pad_add_fusion.me_ref, ...), custom_call_target="tpu_custom_call", output_to_operand_aliasing={{5}: (12, {})} | custom-call | flops 44000002048 | bytes 40000000 | tf_op jit(solution)/shard_map/feed/pallas_call | solution.py:52
  195.5 41.2 %feed.3 = (bf16[1184,2048]{1,0:T(8,128)(2,1)}, f32[1,2048]{1,0:T(1,128)}, bf16[1184,1024]{1,0:T(8,128)(2,1)}, bf16[4,4,128,1024]{3,2,1,0:T(8,128)(2,1)}, bf16[4,...) custom-call(s32[4]{0:T(128)} %pad_add_fusion.me_ref, ...), custom_call_target="tpu_custom_call", output_to_operand_aliasing={{5}: (7, {})} | custom-call | flops 44000002048 | bytes 40000000 | tf_op jit(solution)/shard_map/feed/pallas_call | solution.py:52
  237.3 6.5 %add.188 = (bf16[4,128,1024]{2,1,0:T(8,128)(2,1)}, bf16[4,128,1024]{2,1,0:T(8,128)(2,1)}, bf16[4,128,1024]{2,1,0:T(8,128)(2,1)}, bf16[4,128,1024]{2,1,0:T(8,128)(2,1)}, f32[8,128]{1,0:T(8,128)}) custom-call(s32[4]{0:T(128)} %pad_add_fusion.me_ref, bf16[4,4,128,1024]{3,2,1,0:T(8,128)(2,1)} %get-tuple-element.176.refs_0_, ...), custom_call_target="tpu_custom_call", output_to_operand_aliasing={{4}: (3, {})} | custom-call | tf_op jit(solution)/shard_map/add/pallas_call | solution.py:52
  243.9 1.3 collective-permute-start.26
  245.9 6.5 %add.189 = (bf16[4,128,1024]{2,1,0:T(8,128)(2,1)}, bf16[4,128,1024]{2,1,0:T(8,128)(2,1)}, bf16[4,128,1024]{2,1,0:T(8,128)(2,1)}, bf16[4,128,1024]{2,1,0:T(8,128)(2,1)}, f32[8,128]{1,0:T(8,128)}) custom-call(s32[4]{0:T(128)} %pad_add_fusion.me_ref, bf16[4,4,128,1024]{3,2,1,0:T(8,128)(2,1)} %get-tuple-element.174.refs_0_, ...), custom_call_target="tpu_custom_call", output_to_operand_aliasing={{4}: (3, {})} | custom-call | tf_op jit(solution)/shard_map/add/pallas_call | solution.py:52
  254.5 18.5 %feed_back.1 = (bf16[1184,1024]{1,0:T(8,128)(2,1)}, bf16[1184,1024]{1,0:T(8,128)(2,1)}, f32[4,1024]{1,0:T(4,128)}, bf16[4,4,128,256]{3,2,1,0:T(8,128)(2,1)}, bf1...) custom-call(s32[4]{0:T(128)} %pad_add_fusion.me_ref, ...), custom_call_target="tpu_custom_call", output_to_operand_aliasing={{5}: (7, {})} | custom-call | flops 20899999744 | bytes 19000000 | tf_op jit(solution)/shard_map/feed_back/pallas_call | solution.py:52
  273.7 5.0 collective-permute-done.27.refs_17_
  278.8 20.1 %attend_back.4 = (f32[2,1,1,768]{3,2,1,0:T(1,128)}, bf16[1184,1024]{1,0:T(8,128)(2,1)}, bf16[1,4,128,1024]{3,2,1,0:T(8,128)(2,1)}, bf16[1,4,128,1024]{3,2,1,0:T(...) custom-call(s32[4]{0:T(128)} %pad_add_fusion.me_ref, ...), custom_call_target="tpu_custom_call", output_to_operand_aliasing={{4}: (16, {}), {5}: (17, {}), {6}: (18, {})} | custom-call | flops 22000001024 | bytes 20000000 | tf_op jit(solution)/shard_map/attend_back/pallas_call | solution.py:52
  300.0 4.9 add.190
  306.8 4.8 add.191
  311.6 2.0 collective-permute-start.31
  313.6 20.5 %attend_back.5 = (f32[2,1,1,768]{3,2,1,0:T(1,128)}, bf16[1184,1024]{1,0:T(8,128)(2,1)}, bf16[1,4,128,1024]{3,2,1,0:T(8,128)(2,1)}, bf16[1,4,128,1024]{3,2,1,0:T(8,128)(2,1)}, f32[8,128]{1,0:T(8,128)}) custom-call(s32[4]{0:T(128)} %pad_add_fusion.me_ref, bf16[8,128,384]{2,1,0:T(8,128)(2,1)} %copy-done.41, ...), custom_call_target="tpu_custom_call", output_to_operand_aliasing={{4}: (16, {})} | custom-call | flops 22000001024 | bytes 20000000 | tf_op jit(solution)/shard_map/attend_back/pallas_call | solution.py:52
  336.5 4.2 add_plane.3
  340.7 4.3 add_plane.4
  345.9 4.2 add_core.3
  351.8 2.5 collective-permute-start.37
  354.7 20.0 %attend_back.6 = (f32[2,1,1,768]{3,2,1,0:T(1,128)}, bf16[1184,1024]{1,0:T(8,128)(2,1)}, bf16[1,4,128,1024]{3,2,1,0:T(8,128)(2,1)}, bf16[1,4,128,1024]{3,2,1,0:T(8,128)(2,1)}, f32[8,128]{1,0:T(8,128)}) custom-call(s32[4]{0:T(128)} %pad_add_fusion.me_ref, bf16[8,128,384]{2,1,0:T(8,128)(2,1)} %copy-done.41, ...), custom_call_target="tpu_custom_call", output_to_operand_aliasing={{4}: (16, {})} | custom-call | flops 22000001024 | bytes 20000000 | tf_op jit(solution)/shard_map/attend_back/pallas_call | solution.py:52
  376.4 1.5 collective-permute-start.39
  377.9 2.3 collective-permute-start.40
  381.8 4.2 add_core.4
  386.0 25.4 %attend_back.7 = (f32[2,1,1,768]{3,2,1,0:T(1,128)}, bf16[1184,1024]{1,0:T(8,128)(2,1)}, f32[2,1024]{1,0:T(2,128)}, bf16[1,4,128,1024]{3,2,1,0:T(8,128)(2,1)}, bf...) custom-call(s32[4]{0:T(128)} %pad_add_fusion.me_ref, ...), custom_call_target="tpu_custom_call", output_to_operand_aliasing={{5}: (22, {})} | custom-call | flops 22000001024 | bytes 20000000 | tf_op jit(solution)/shard_map/attend_back/pallas_call | solution.py:52
  413.5 2.1 collective-permute-start.42
  417.8 1.3 collective-permute-start.44
  420.1 4.2 add_core.5
  424.3 2.0 collective-permute-start.47
  426.3 1.3 convert_add_fusion
  428.3 12.2 %feed_out.2 = (f32[1184,1024]{1,0:T(8,128)}, f32[8,128]{1,0:T(8,128)}, f32[112,128]{1,0:T(8,128)}, f32[112,128]{1,0:T(8,128)}, f32[112,128]{1,0:T(8,128)}) custom-call(s32[4]{0:T(128)} %pad_add_fusion.me_ref, bf16[8,128,512]{2,1,0:T(8,128)(2,1)} %pad_maximum_fusion.1.refs_4_.refs_0_, ...), custom_call_target="tpu_custom_call", output_to_operand_aliasing={{1}: (7, {}), {2}: (8, {}), {3}: (9, {}), {4}: (10, {})} | custom-call | flops 13200000000 | bytes 12000000 | tf_op jit(solution)/shard_map/feed_out/pallas_call | solution.py:52
  441.5 2.2 collective-permute-start.48
  443.7 1.7 collective-permute-start.49
  445.4 3.4 collective-permute-done.47.refs_4_
  448.8 1.4 collective-permute-start.50
  451.0 2.6 collective-permute-done.46.refs_3_
  454.5 4.9 add_plane.5
  460.1 12.4 %feed_out.3 = (bf16[1184,1024]{1,0:T(8,128)(2,1)}, f32[8,128]{1,0:T(8,128)}, f32[112,128]{1,0:T(8,128)}, f32[112,128]{1,0:T(8,128)}, f32[112,128]{1,0:T(8,128)}) custom-call(s32[4]{0:T(128)} %pad_add_fusion.me_ref, bf16[32,128,1024]{2,1,0:T(8,128)(2,1)} %bitcast.113, ...), custom_call_target="tpu_custom_call", output_to_operand_aliasing={{1}: (5, {}), {2}: (6, {}), {3}: (7, {}), {4}: (8, {})} | custom-call | flops 13200000000 | bytes 12000000 | tf_op jit(solution)/shard_map/feed_out/pallas_call | solution.py:52
  475.5 1.9 slice.167
  477.4 1.9 reshape.223
  479.3 1.4 collective-permute-start.52
  480.7 2.4 collective-permute-start.53
  483.6 1.9 slice.166
  485.5 1.9 reshape.221
  492.5 8.8 %collective-permute-done.53 = bf16[128,1024]{1,0:T(8,128)(2,1)S(1)} collective-permute-done((bf16[128,1024]{1,0:T(8,128)(2,1)}, bf16[128,1024]{1,0:T(8,128)(2,1)S(1)}, u32[]{:S(2)}, u32[]{:S(2)}) %collective-permute-start.53) | collective-permute-done | bytes 262176 | tf_op jit(solution)/shard_map/ppermute | solution.py:89
  501.3 6.2 %collective-permute-done.54 = bf16[128,1024]{1,0:T(8,128)(2,1)} collective-permute-done((bf16[128,1024]{1,0:T(8,128)(2,1)}, bf16[128,1024]{1,0:T(8,128)(2,1)}, u32[]{:S(2)}, u32[]{:S(2)}) %collective-permute-start.54) | collective-permute-done | bytes 262176 | tf_op jit(solution)/shard_map/ppermute | solution.py:89
  (341 shorter events, 78.1 us)
Async XLA Ops:
  7.2 94.2 %all-gather.7.cloned.1.call-start = ((), (), s32[]{:S(2)}) async-start(), calls=%async_computation.1 | async-start | bytes 2433024 | tf_op jit(solution)/shard_map/all_gather | solution.py:131
  13.1 182.4 %all-gather.5.cloned.1.call-start = ((), (), s32[]{:S(2)}) async-start(), calls=%async_computation | async-start | bytes 8650752 | tf_op jit(solution)/shard_map/all_gather | solution.py:131
  14.4 14.6 %collective-permute-start = (bf16[1,128,384]{2,1,0:T(8,128)(2,1)S(1)}, bf16[1,128,384]{2,1,0:T(8,128)(2,1)S(1)}, u32[]{:S(2)}, u32[]{:S(2)}) collective-permute-start(bf16[1,128,384]{2,1,0:T(8,128)(2,1)S(1)} %bitcast.83), channel_id=1, source_target_pairs={{0,16},{1,17},{2,18},{3,19},{4,20},{5,21},{6,22},{7,23},{8,24},{9,... | collective-permute-start | bytes 294920 | tf_op jit(solution)/shard_map/ppermute | solution.py:89
  17.2 11.9 %collective-permute-start.1 = (bf16[1,128,384]{2,1,0:T(8,128)(2,1)S(1)}, bf16[1,128,384]{2,1,0:T(8,128)(2,1)S(1)}, u32[]{:S(2)}, u32[]{:S(2)}) collective-permute-start(bf16[1,128,384]{2,1,0:T(8,128)(2,1)S(1)} %bitcast.87), channel_id=1, source_target_pairs={{0,16},{1,17},{2,18},{3,19},{4,20},{5,21},{6,22},{7,23},{8,24},{9,... | collective-permute-start | bytes 294920 | tf_op jit(solution)/shard_map/ppermute | solution.py:89
  19.2 20.3 %collective-permute-start.6 = (bf16[1,128,512]{2,1,0:T(8,128)(2,1)S(1)}, bf16[1,128,512]{2,1,0:T(8,128)(2,1)S(1)}, u32[]{:S(2)}, u32[]{:S(2)}) collective-permute-start(bf16[1,128,512]{2,1,0:T(8,128)(2,1)S(1)} %get-tuple-element.321), channel_id=1, source_target_pairs={{0,16},{1,17},{2,18},{3,19},{4,20},{5,21},{6,22},{7,23},{8,24},{9,... | collective-permute-start | bytes 393224 | tf_op jit(solution)/shard_map/ppermute | solution.py:89
  32.9 9.5 %collective-permute-start.8 = (bf16[1,128,512]{2,1,0:T(8,128)(2,1)S(1)}, bf16[1,128,512]{2,1,0:T(8,128)(2,1)S(1)}, u32[]{:S(2)}, u32[]{:S(2)}) collective-permute-start(bf16[1,128,512]{2,1,0:T(8,128)(2,1)S(1)} %get-tuple-element.323), channel_id=1, source_target_pairs={{0,16},{1,17},{2,18},{3,19},{4,20},{5,21},{6,22},{7,23},{8,24},{9,... | collective-permute-start | bytes 393224 | tf_op jit(solution)/shard_map/ppermute | solution.py:89
  37.5 7.9 %collective-permute-start.4 = (bf16[2,128,384]{2,1,0:T(8,128)(2,1)S(1)}, bf16[2,128,384]{2,1,0:T(8,128)(2,1)S(1)}, u32[]{:S(2)}, u32[]{:S(2)}) collective-permute-start(bf16[2,128,384]{2,1,0:T(8,128)(2,1)S(1)} %pad_maximum_fusion.13), channel_id=1, source_target_pairs={{0,2},{1,3},{2,0},{3,1},{4,6},{5,7},{6,4},{7,5},{8,10},{9,11},{10,... | collective-permute-start | bytes 589832 | tf_op jit(solution)/shard_map/ppermute | solution.py:89
  38.9 9.1 %collective-permute-start.2 = (bf16[2,128,384]{2,1,0:T(8,128)(2,1)S(1)}, bf16[2,128,384]{2,1,0:T(8,128)(2,1)S(1)}, u32[]{:S(2)}, u32[]{:S(2)}) collective-permute-start(bf16[2,128,384]{2,1,0:T(8,128)(2,1)S(1)} %pad_maximum_fusion.12), channel_id=1, source_target_pairs={{0,1},{1,0},{2,3},{3,2},{4,5},{5,4},{6,7},{7,6},{8,9},{9,8},{10,11... | collective-permute-start | bytes 589832 | tf_op jit(solution)/shard_map/ppermute | solution.py:89
  40.9 15.3 %collective-permute-start.7 = (bf16[2,128,512]{2,1,0:T(8,128)(2,1)}, bf16[2,128,512]{2,1,0:T(8,128)(2,1)S(1)}, u32[]{:S(2)}, u32[]{:S(2)}) collective-permute-start(bf16[2,128,512]{2,1,0:T(8,128)(2,1)} %pad_maximum_fusion.9), channel_id=1, source_target_pairs={{0,1},{1,0},{2,3},{3,2},{4,5},{5,4},{6,7},{7,6},{8,9},{9,8},{10,11... | collective-permute-start | bytes 786440 | tf_op jit(solution)/shard_map/ppermute | solution.py:89
  43.8 12.4 %collective-permute-start.9 = (bf16[2,128,512]{2,1,0:T(8,128)(2,1)}, bf16[2,128,512]{2,1,0:T(8,128)(2,1)S(1)}, u32[]{:S(2)}, u32[]{:S(2)}) collective-permute-start(bf16[2,128,512]{2,1,0:T(8,128)(2,1)} %pad_maximum_fusion.10), channel_id=1, source_target_pairs={{0,2},{1,3},{2,0},{3,1},{4,6},{5,7},{6,4},{7,5},{8,10},{9,11},{10,... | collective-permute-start | bytes 786440 | tf_op jit(solution)/shard_map/ppermute | solution.py:89
  46.2 12.8 %collective-permute-start.5 = (bf16[4,128,384]{2,1,0:T(8,128)(2,1)}, bf16[4,128,384]{2,1,0:T(8,128)(2,1)}, u32[]{:S(2)}, u32[]{:S(2)}) collective-permute-start(bf16[4,128,384]{2,1,0:T(8,128)(2,1)} %pad_maximum_fusion.8), channel_id=1, source_target_pairs={{0,8},{1,9},{2,10},{3,11},{4,12},{5,13},{6,14},{7,15},{8,0},{9,1},... | collective-permute-start | bytes 1179656 | tf_op jit(solution)/shard_map/ppermute | solution.py:89
  49.5 22.3 %collective-permute-start.3 = (bf16[4,128,384]{2,1,0:T(8,128)(2,1)}, bf16[4,128,384]{2,1,0:T(8,128)(2,1)}, u32[]{:S(2)}, u32[]{:S(2)}) collective-permute-start(bf16[4,128,384]{2,1,0:T(8,128)(2,1)} %pad_maximum_fusion.7), channel_id=1, source_target_pairs={{0,8},{1,9},{2,10},{3,11},{4,12},{5,13},{6,14},{7,15},{8,0},{9,1},... | collective-permute-start | bytes 1179656 | tf_op jit(solution)/shard_map/ppermute | solution.py:89
  73.8 14.7 %collective-permute-start.13 = (bf16[4,128,512]{2,1,0:T(8,128)(2,1)S(1)}, bf16[4,128,512]{2,1,0:T(8,128)(2,1)S(1)}, u32[]{:S(2)}, u32[]{:S(2)}) collective-permute-start(bf16[4,128,512]{2,1,0:T(8,128)(2,1)S(1)} %pad_maximum_fusion.5), channel_id=1, source_target_pairs={{0,8},{1,9},{2,10},{3,11},{4,12},{5,13},{6,14},{7,15},{8,0},{9,1},... | collective-permute-start | bytes 1572872 | tf_op jit(solution)/shard_map/ppermute | solution.py:89
  75.5 18.5 %collective-permute-start.11 = (bf16[8,128,384]{2,1,0:T(8,128)(2,1)S(1)}, bf16[8,128,384]{2,1,0:T(8,128)(2,1)S(1)}, u32[]{:S(2)}, u32[]{:S(2)}) collective-permute-start(bf16[8,128,384]{2,1,0:T(8,128)(2,1)S(1)} %pad_maximum_fusion.3.refs_4_), channel_id=1, source_target_pairs={{0,1},{1,0},{2,3},{3,2},{4,5},{5,4},{6,7},{7,6},{8,9},{9,8},{10,11... | collective-permute-start | bytes 2359304 | tf_op jit(solution)/shard_map/ppermute | solution.py:89
  77.0 17.0 %collective-permute-start.10 = (bf16[8,128,384]{2,1,0:T(8,128)(2,1)S(1)}, bf16[8,128,384]{2,1,0:T(8,128)(2,1)S(1)}, u32[]{:S(2)}, u32[]{:S(2)}) collective-permute-start(bf16[8,128,384]{2,1,0:T(8,128)(2,1)S(1)} %pad_maximum_fusion.2.refs_0_), channel_id=1, source_target_pairs={{0,2},{1,3},{2,0},{3,1},{4,6},{5,7},{6,4},{7,5},{8,10},{9,11},{10,... | collective-permute-start | bytes 2359304 | tf_op jit(solution)/shard_map/ppermute | solution.py:89
  77.2 16.8 %collective-permute-start.12 = (bf16[4,128,512]{2,1,0:T(8,128)(2,1)S(1)}, bf16[4,128,512]{2,1,0:T(8,128)(2,1)S(1)}, u32[]{:S(2)}, u32[]{:S(2)}) collective-permute-start(bf16[4,128,512]{2,1,0:T(8,128)(2,1)S(1)} %pad_maximum_fusion.4), channel_id=1, source_target_pairs={{0,8},{1,9},{2,10},{3,11},{4,12},{5,13},{6,14},{7,15},{8,0},{9,1},... | collective-permute-start | bytes 1572872 | tf_op jit(solution)/shard_map/ppermute | solution.py:89
  96.3 7.2 %collective-permute-start.16 = (bf16[8,128,384]{2,1,0:T(8,128)(2,1)}, bf16[8,128,384]{2,1,0:T(8,128)(2,1)}, u32[]{:S(2)}, u32[]{:S(2)}) collective-permute-start(bf16[8,128,384]{2,1,0:T(8,128)(2,1)} %copy-done.40), channel_id=1, source_target_pairs={{0,4},{1,5},{2,6},{3,7},{4,0},{5,1},{6,2},{7,3},{8,12},{9,13},{10,... | collective-permute-start | bytes 2359304 | tf_op jit(solution)/shard_map/ppermute | solution.py:89
  96.3 7.2 %collective-permute-start.14 = (bf16[8,128,384]{2,1,0:T(8,128)(2,1)}, bf16[8,128,384]{2,1,0:T(8,128)(2,1)}, u32[]{:S(2)}, u32[]{:S(2)}) collective-permute-start(bf16[8,128,384]{2,1,0:T(8,128)(2,1)} %copy-done.41), channel_id=1, source_target_pairs={{0,4},{1,5},{2,6},{3,7},{4,0},{5,1},{6,2},{7,3},{8,12},{9,13},{10,... | collective-permute-start | bytes 2359304 | tf_op jit(solution)/shard_map/ppermute | solution.py:89
  98.9 42.0 %collective-permute-start.19 = (bf16[8,128,512]{2,1,0:T(8,128)(2,1)}, bf16[8,128,512]{2,1,0:T(8,128)(2,1)S(1)}, u32[]{:S(2)}, u32[]{:S(2)}) collective-permute-start(bf16[8,128,512]{2,1,0:T(8,128)(2,1)} %pad_maximum_fusion.1.refs_4_.refs_0_), channel_id=1, source_target_pairs={{0,1},{1,0},{2,3},{3,2},{4,5},{5,4},{6,7},{7,6},{8,9},{9,8},{10,11... | collective-permute-start | bytes 3145736 | tf_op jit(solution)/shard_map/ppermute | solution.py:89
  99.8 4.6 collective-permute-start.15
  99.8 4.7 collective-permute-start.17
  103.5 50.4 %collective-permute-start.22 = (bf16[8,128,512]{2,1,0:T(8,128)(2,1)}, bf16[8,128,512]{2,1,0:T(8,128)(2,1)}, u32[]{:S(2)}, u32[]{:S(2)}) collective-permute-start(bf16[8,128,512]{2,1,0:T(8,128)(2,1)} %pad_maximum_fusion.1.refs_4_.refs_0_), channel_id=1, source_target_pairs={{0,4},{1,5},{2,6},{3,7},{4,0},{5,1},{6,2},{7,3},{8,12},{9,13},{10,... | collective-permute-start | bytes 3145736 | tf_op jit(solution)/shard_map/ppermute | solution.py:89
  103.5 37.4 %collective-permute-start.18 = (bf16[8,128,512]{2,1,0:T(8,128)(2,1)}, bf16[8,128,512]{2,1,0:T(8,128)(2,1)S(1)}, u32[]{:S(2)}, u32[]{:S(2)}) collective-permute-start(bf16[8,128,512]{2,1,0:T(8,128)(2,1)} %pad_maximum_fusion.refs_0_), channel_id=1, source_target_pairs={{0,2},{1,3},{2,0},{3,1},{4,6},{5,7},{6,4},{7,5},{8,10},{9,11},{10,... | collective-permute-start | bytes 3145736 | tf_op jit(solution)/shard_map/ppermute | solution.py:89
  104.4 49.6 %collective-permute-start.20 = (bf16[8,128,512]{2,1,0:T(8,128)(2,1)}, bf16[8,128,512]{2,1,0:T(8,128)(2,1)}, u32[]{:S(2)}, u32[]{:S(2)}) collective-permute-start(bf16[8,128,512]{2,1,0:T(8,128)(2,1)} %pad_maximum_fusion.refs_0_), channel_id=1, source_target_pairs={{0,4},{1,5},{2,6},{3,7},{4,0},{5,1},{6,2},{7,3},{8,12},{9,13},{10,... | collective-permute-start | bytes 3145736 | tf_op jit(solution)/shard_map/ppermute | solution.py:89
  142.9 11.0 %collective-permute-start.21 = (bf16[8,128,512]{2,1,0:T(8,128)(2,1)}, bf16[8,128,512]{2,1,0:T(8,128)(2,1)S(1)}, u32[]{:S(2)}, u32[]{:S(2)}) collective-permute-start(bf16[8,128,512]{2,1,0:T(8,128)(2,1)} %get-tuple-element.164.refs_1_), channel_id=1, source_target_pairs={{0,4},{1,5},{2,6},{3,7},{4,0},{5,1},{6,2},{7,3},{8,12},{9,13},{10,... | collective-permute-start | bytes 3145736 | tf_op jit(solution)/shard_map/ppermute | solution.py:89
  143.3 10.6 %collective-permute-start.23 = (bf16[8,128,512]{2,1,0:T(8,128)(2,1)}, bf16[8,128,512]{2,1,0:T(8,128)(2,1)S(1)}, u32[]{:S(2)}, u32[]{:S(2)}) collective-permute-start(bf16[8,128,512]{2,1,0:T(8,128)(2,1)} %get-tuple-element.165.refs_5_.refs_1_), channel_id=1, source_target_pairs={{0,4},{1,5},{2,6},{3,7},{4,0},{5,1},{6,2},{7,3},{8,12},{9,13},{10,... | collective-permute-start | bytes 3145736 | tf_op jit(solution)/shard_map/ppermute | solution.py:89
  195.0 42.3 %collective-permute-start.25 = (bf16[4,4,128,1024]{3,2,1,0:T(8,128)(2,1)}, bf16[4,4,128,1024]{3,2,1,0:T(8,128)(2,1)}, u32[]{:S(2)}, u32[]{:S(2)}) collective-permute-start(bf16[4,4,128,1024]{3,2,1,0:T(8,128)(2,1)} %get-tuple-element.177), channel_id=1, source_target_pairs={{0,4},{1,5},{2,6},{3,7},{4,0},{5,1},{6,2},{7,3},{8,12},{9,13},{10,... | collective-permute-start | bytes 12582920 | tf_op jit(solution)/shard_map/ppermute | solution.py:89
  195.5 41.4 %copy-start.50 = (f32[2,4,4,640]{3,2,1,0:T(4,128)S(1)}, f32[2,4,4,640]{3,2,1,0:T(4,128)}, u32[]{:S(2)}) copy-start(f32[2,4,4,640]{3,2,1,0:T(4,128)} %get-tuple-element.228) | copy-start | bytes 245764
  195.5 41.5 %copy-start.62 = (pred[2]{0:T(512)(128)(4,1)S(1)}, pred[2]{0:T(512)(128)(4,1)}, u32[]{:S(2)}) copy-start(pred[2]{0:T(512)(128)(4,1)} %copy-done.61) | copy-start | bytes 10
  236.8 9.2 %collective-permute-start.24 = (bf16[4,4,128,1024]{3,2,1,0:T(8,128)(2,1)}, bf16[4,4,128,1024]{3,2,1,0:T(8,128)(2,1)}, u32[]{:S(2)}, u32[]{:S(2)}) collective-permute-start(bf16[4,4,128,1024]{3,2,1,0:T(8,128)(2,1)} %get-tuple-element.175), channel_id=1, source_target_pairs={{0,4},{1,5},{2,6},{3,7},{4,0},{5,1},{6,2},{7,3},{8,12},{9,13},{10,... | collective-permute-start | bytes 12582920 | tf_op jit(solution)/shard_map/ppermute | solution.py:89
  243.9 29.9 %collective-permute-start.26 = (bf16[4,128,1024]{2,1,0:T(8,128)(2,1)}, bf16[4,128,1024]{2,1,0:T(8,128)(2,1)S(1)}, u32[]{:S(2)}, u32[]{:S(2)}) collective-permute-start(bf16[4,128,1024]{2,1,0:T(8,128)(2,1)} %get-tuple-element.186), channel_id=1, source_target_pairs={{0,2},{1,3},{2,0},{3,1},{4,6},{5,7},{6,4},{7,5},{8,10},{9,11},{10,... | collective-permute-start | bytes 3145736 | tf_op jit(solution)/shard_map/ppermute | solution.py:89
  245.2 53.7 %collective-permute-start.30 = (bf16[4,128,1024]{2,1,0:T(8,128)(2,1)}, bf16[4,128,1024]{2,1,0:T(8,128)(2,1)S(1)}, u32[]{:S(2)}, u32[]{:S(2)}) collective-permute-start(bf16[4,128,1024]{2,1,0:T(8,128)(2,1)} %get-tuple-element.197), channel_id=1, source_target_pairs={{0,2},{1,3},{2,0},{3,1},{4,6},{5,7},{6,4},{7,5},{8,10},{9,11},{10,... | collective-permute-start | bytes 3145736 | tf_op jit(solution)/shard_map/ppermute | solution.py:89
  252.4 26.4 %collective-permute-start.27 = (bf16[4,128,1024]{2,1,0:T(8,128)(2,1)}, bf16[4,128,1024]{2,1,0:T(8,128)(2,1)}, u32[]{:S(2)}, u32[]{:S(2)}) collective-permute-start(bf16[4,128,1024]{2,1,0:T(8,128)(2,1)} %get-tuple-element.187), channel_id=1, source_target_pairs={{0,1},{1,0},{2,3},{3,2},{4,5},{5,4},{6,7},{7,6},{8,9},{9,8},{10,11... | collective-permute-start | bytes 3145736 | tf_op jit(solution)/shard_map/ppermute | solution.py:89
  253.5 52.4 %collective-permute-start.29 = (bf16[4,128,1024]{2,1,0:T(8,128)(2,1)}, bf16[4,128,1024]{2,1,0:T(8,128)(2,1)S(1)}, u32[]{:S(2)}, u32[]{:S(2)}) collective-permute-start(bf16[4,128,1024]{2,1,0:T(8,128)(2,1)} %get-tuple-element.193), channel_id=1, source_target_pairs={{0,1},{1,0},{2,3},{3,2},{4,5},{5,4},{6,7},{7,6},{8,9},{9,8},{10,11... | collective-permute-start | bytes 3145736 | tf_op jit(solution)/shard_map/ppermute | solution.py:89
  304.9 30.7 %collective-permute-start.32 = (bf16[4,128,1024]{2,1,0:T(8,128)(2,1)}, bf16[4,128,1024]{2,1,0:T(8,128)(2,1)S(1)}, u32[]{:S(2)}, u32[]{:S(2)}) collective-permute-start(bf16[4,128,1024]{2,1,0:T(8,128)(2,1)} %get-tuple-element.203), channel_id=1, source_target_pairs={{0,1},{1,0},{2,3},{3,2},{4,5},{5,4},{6,7},{7,6},{8,9},{9,8},{10,11... | collective-permute-start | bytes 3145736 | tf_op jit(solution)/shard_map/ppermute | solution.py:89
  311.6 29.1 %collective-permute-start.31 = (bf16[4,128,1024]{2,1,0:T(8,128)(2,1)}, bf16[4,128,1024]{2,1,0:T(8,128)(2,1)}, u32[]{:S(2)}, u32[]{:S(2)}) collective-permute-start(bf16[4,128,1024]{2,1,0:T(8,128)(2,1)} %get-tuple-element.201), channel_id=1, source_target_pairs={{0,2},{1,3},{2,0},{3,1},{4,6},{5,7},{6,4},{7,5},{8,10},{9,11},{10,... | collective-permute-start | bytes 3145736 | tf_op jit(solution)/shard_map/ppermute | solution.py:89
  313.6 31.3 %collective-permute-start.28 = (bf16[4,128,1024]{2,1,0:T(8,128)(2,1)}, bf16[4,128,1024]{2,1,0:T(8,128)(2,1)S(1)}, u32[]{:S(2)}, u32[]{:S(2)}) collective-permute-start(bf16[4,128,1024]{2,1,0:T(8,128)(2,1)} %bitcast.116), channel_id=1, source_target_pairs={{0,4},{1,5},{2,6},{3,7},{4,0},{5,1},{6,2},{7,3},{8,12},{9,13},{10,... | collective-permute-start | bytes 3145736 | tf_op jit(solution)/shard_map/ppermute | solution.py:89
  313.6 21.8 %copy-start.56 = (f32[2,1,1,768]{3,2,1,0:T(1,128)S(1)}, f32[2,1,1,768]{3,2,1,0:T(1,128)}, u32[]{:S(2)}) copy-start(f32[2,1,1,768]{3,2,1,0:T(1,128)} %get-tuple-element.236) | copy-start | bytes 18436
  334.2 41.3 %collective-permute-start.34 = (bf16[4,128,1024]{2,1,0:T(8,128)(2,1)}, bf16[4,128,1024]{2,1,0:T(8,128)(2,1)S(1)}, u32[]{:S(2)}, u32[]{:S(2)}) collective-permute-start(bf16[4,128,1024]{2,1,0:T(8,128)(2,1)} %bitcast.117), channel_id=1, source_target_pairs={{0,4},{1,5},{2,6},{3,7},{4,0},{5,1},{6,2},{7,3},{8,12},{9,13},{10,... | collective-permute-start | bytes 3145736 | tf_op jit(solution)/shard_map/ppermute | solution.py:89
  350.1 30.7 %collective-permute-start.35 = (bf16[4,128,1024]{2,1,0:T(8,128)(2,1)}, bf16[4,128,1024]{2,1,0:T(8,128)(2,1)S(1)}, u32[]{:S(2)}, u32[]{:S(2)}) collective-permute-start(bf16[4,128,1024]{2,1,0:T(8,128)(2,1)} %get-tuple-element.218), channel_id=1, source_target_pairs={{0,3},{1,2},{2,1},{3,0},{4,7},{5,6},{6,5},{7,4},{8,11},{9,10},{10,... | collective-permute-start | bytes 3145736 | tf_op jit(solution)/shard_map/ppermute | solution.py:89
  350.7 24.9 %collective-permute-start.36 = (bf16[128,1024]{1,0:T(8,128)(2,1)}, bf16[128,1024]{1,0:T(8,128)(2,1)S(1)}, u32[]{:S(2)}, u32[]{:S(2)}) collective-permute-start(bf16[128,1024]{1,0:T(8,128)(2,1)} %get-tuple-element.219), channel_id=1, source_target_pairs={{0,8},{1,9},{2,10},{3,11},{4,12},{5,13},{6,14},{7,15},{8,0},{9,1},... | collective-permute-start | bytes 786440 | tf_op jit(solution)/shard_map/ppermute | solution.py:89
  351.8 26.1 %collective-permute-start.37 = (bf16[128,1024]{1,0:T(8,128)(2,1)}, bf16[128,1024]{1,0:T(8,128)(2,1)}, u32[]{:S(2)}, u32[]{:S(2)}) collective-permute-start(bf16[128,1024]{1,0:T(8,128)(2,1)} %get-tuple-element.220), channel_id=1, source_target_pairs={{0,16},{1,17},{2,18},{3,19},{4,20},{5,21},{6,22},{7,23},{8,24},{9,... | collective-permute-start | bytes 786440 | tf_op jit(solution)/shard_map/ppermute | solution.py:89
  354.3 25.9 %collective-permute-start.38 = (bf16[128,1024]{1,0:T(8,128)(2,1)}, bf16[128,1024]{1,0:T(8,128)(2,1)}, u32[]{:S(2)}, u32[]{:S(2)}) collective-permute-start(bf16[128,1024]{1,0:T(8,128)(2,1)} %get-tuple-element.221), channel_id=1, source_target_pairs={{0,24},{1,25},{2,26},{3,27},{4,28},{5,29},{6,30},{7,31},{8,16},{9,... | collective-permute-start | bytes 786440 | tf_op jit(solution)/shard_map/ppermute | solution.py:89
  375.5 43.7 %collective-permute-start.33 = (bf16[4,128,1024]{2,1,0:T(8,128)(2,1)}, bf16[4,128,1024]{2,1,0:T(8,128)(2,1)S(1)}, u32[]{:S(2)}, u32[]{:S(2)}) collective-permute-start(bf16[4,128,1024]{2,1,0:T(8,128)(2,1)} %bitcast.115), channel_id=1, source_target_pairs={{0,4},{1,5},{2,6},{3,7},{4,0},{5,1},{6,2},{7,3},{8,12},{9,13},{10,... | collective-permute-start | bytes 3145736 | tf_op jit(solution)/shard_map/ppermute | solution.py:89
  376.4 41.3 %collective-permute-start.39 = (bf16[128,1024]{1,0:T(8,128)(2,1)}, bf16[128,1024]{1,0:T(8,128)(2,1)S(1)}, u32[]{:S(2)}, u32[]{:S(2)}) collective-permute-start(bf16[128,1024]{1,0:T(8,128)(2,1)} %get-tuple-element.224), channel_id=1, source_target_pairs={{0,8},{1,9},{2,10},{3,11},{4,12},{5,13},{6,14},{7,15},{8,0},{9,1},... | collective-permute-start | bytes 786440 | tf_op jit(solution)/shard_map/ppermute | solution.py:89
  377.9 39.9 %collective-permute-start.40 = (bf16[128,1024]{1,0:T(8,128)(2,1)}, bf16[128,1024]{1,0:T(8,128)(2,1)}, u32[]{:S(2)}, u32[]{:S(2)}) collective-permute-start(bf16[128,1024]{1,0:T(8,128)(2,1)} %get-tuple-element.225), channel_id=1, source_target_pairs={{0,16},{1,17},{2,18},{3,19},{4,20},{5,21},{6,22},{7,23},{8,24},{9,... | collective-permute-start | bytes 786440 | tf_op jit(solution)/shard_map/ppermute | solution.py:89
  380.2 38.9 %collective-permute-start.41 = (bf16[128,1024]{1,0:T(8,128)(2,1)}, bf16[128,1024]{1,0:T(8,128)(2,1)}, u32[]{:S(2)}, u32[]{:S(2)}) collective-permute-start(bf16[128,1024]{1,0:T(8,128)(2,1)} %get-tuple-element.226), channel_id=1, source_target_pairs={{0,24},{1,25},{2,26},{3,27},{4,28},{5,29},{6,30},{7,31},{8,16},{9,... | collective-permute-start | bytes 786440 | tf_op jit(solution)/shard_map/ppermute | solution.py:89
  386.0 29.6 %copy-start.31 = (bf16[128,1024]{1,0:T(8,128)(2,1)S(1)}, bf16[128,1024]{1,0:T(8,128)(2,1)}, u32[]{:S(2)}) copy-start(bf16[128,1024]{1,0:T(8,128)(2,1)} %get-tuple-element.258) | copy-start | bytes 786436
  386.0 29.6 %copy-start.48 = (bf16[128,1024]{1,0:T(8,128)(2,1)S(1)}, bf16[128,1024]{1,0:T(8,128)(2,1)}, u32[]{:S(2)}) copy-start(bf16[128,1024]{1,0:T(8,128)(2,1)} %get-tuple-element.257) | copy-start | bytes 786436
  413.5 14.2 %collective-permute-start.42 = (f32[112,128]{1,0:T(8,128)S(1)}, f32[112,128]{1,0:T(8,128)S(1)}, u32[]{:S(2)}, u32[]{:S(2)}) collective-permute-start(f32[112,128]{1,0:T(8,128)S(1)} %constant_dynamic-update-slice_fusion), channel_id=1, source_target_pairs={{0,1},{1,0},{2,3},{3,2},{4,5},{5,4},{6,7},{7,6},{8,9},{9,8},{10,11... | collective-permute-start | bytes 172040 | tf_op jit(solution)/shard_map/ppermute | solution.py:89
  417.6 10.3 %collective-permute-start.43 = (f32[112,128]{1,0:T(8,128)S(1)}, f32[112,128]{1,0:T(8,128)}, u32[]{:S(2)}, u32[]{:S(2)}) collective-permute-start(f32[112,128]{1,0:T(8,128)S(1)} %constant_dynamic-update-slice_fusion), channel_id=1, source_target_pairs={{0,2},{1,3},{2,0},{3,1},{4,6},{5,7},{6,4},{7,5},{8,10},{9,11},{10,... | collective-permute-start | bytes 172040 | tf_op jit(solution)/shard_map/ppermute | solution.py:89
  417.8 10.1 %collective-permute-start.44 = (f32[112,128]{1,0:T(8,128)S(1)}, f32[112,128]{1,0:T(8,128)}, u32[]{:S(2)}, u32[]{:S(2)}) collective-permute-start(f32[112,128]{1,0:T(8,128)S(1)} %constant_dynamic-update-slice_fusion), channel_id=1, source_target_pairs={{0,3},{1,2},{2,1},{3,0},{4,7},{5,6},{6,5},{7,4},{8,11},{9,10},{10,... | collective-permute-start | bytes 172040 | tf_op jit(solution)/shard_map/ppermute | solution.py:89
  424.3 24.5 %collective-permute-start.47 = (bf16[4,128,1024]{2,1,0:T(8,128)(2,1)}, bf16[4,128,1024]{2,1,0:T(8,128)(2,1)S(1)}, u32[]{:S(2)}, u32[]{:S(2)}) collective-permute-start(bf16[4,128,1024]{2,1,0:T(8,128)(2,1)} %get-tuple-element.242), channel_id=1, source_target_pairs={{0,1},{1,0},{2,3},{3,2},{4,5},{5,4},{6,7},{7,6},{8,9},{9,8},{10,11... | collective-permute-start | bytes 3145736 | tf_op jit(solution)/shard_map/ppermute | solution.py:89
  426.3 24.6 %collective-permute-start.45 = (bf16[4,128,1024]{2,1,0:T(8,128)(2,1)}, bf16[4,128,1024]{2,1,0:T(8,128)(2,1)S(1)}, u32[]{:S(2)}, u32[]{:S(2)}) collective-permute-start(bf16[4,128,1024]{2,1,0:T(8,128)(2,1)} %bitcast.114), channel_id=1, source_target_pairs={{0,4},{1,5},{2,6},{3,7},{4,0},{5,1},{6,2},{7,3},{8,12},{9,13},{10,... | collective-permute-start | bytes 3145736 | tf_op jit(solution)/shard_map/ppermute | solution.py:89
  427.7 25.8 %collective-permute-start.46 = (bf16[4,128,1024]{2,1,0:T(8,128)(2,1)}, bf16[4,128,1024]{2,1,0:T(8,128)(2,1)S(1)}, u32[]{:S(2)}, u32[]{:S(2)}) collective-permute-start(bf16[4,128,1024]{2,1,0:T(8,128)(2,1)} %get-tuple-element.241), channel_id=1, source_target_pairs={{0,2},{1,3},{2,0},{3,1},{4,6},{5,7},{6,4},{7,5},{8,10},{9,11},{10,... | collective-permute-start | bytes 3145736 | tf_op jit(solution)/shard_map/ppermute | solution.py:89
  441.5 18.0 %collective-permute-start.48 = (f32[112,128]{1,0:T(8,128)S(1)}, f32[112,128]{1,0:T(8,128)S(1)}, u32[]{:S(2)}, u32[]{:S(2)}) collective-permute-start(f32[112,128]{1,0:T(8,128)S(1)} %add_select_fusion.2), channel_id=1, source_target_pairs={{0,8},{1,9},{2,10},{3,11},{4,12},{5,13},{6,14},{7,15},{8,0},{9,1},... | collective-permute-start | bytes 172040 | tf_op jit(solution)/shard_map/ppermute | solution.py:89
  443.7 15.8 %collective-permute-start.49 = (f32[112,128]{1,0:T(8,128)S(1)}, f32[112,128]{1,0:T(8,128)S(1)}, u32[]{:S(2)}, u32[]{:S(2)}) collective-permute-start(f32[112,128]{1,0:T(8,128)S(1)} %add_select_fusion.2), channel_id=1, source_target_pairs={{0,16},{1,17},{2,18},{3,19},{4,20},{5,21},{6,22},{7,23},{8,24},{9,... | collective-permute-start | bytes 172040 | tf_op jit(solution)/shard_map/ppermute | solution.py:89
  448.8 10.7 %collective-permute-start.50 = (f32[112,128]{1,0:T(8,128)S(1)}, f32[112,128]{1,0:T(8,128)}, u32[]{:S(2)}, u32[]{:S(2)}) collective-permute-start(f32[112,128]{1,0:T(8,128)S(1)} %add_select_fusion.2), channel_id=1, source_target_pairs={{0,24},{1,25},{2,26},{3,27},{4,28},{5,29},{6,30},{7,31},{8,16},{9,... | collective-permute-start | bytes 172040 | tf_op jit(solution)/shard_map/ppermute | solution.py:89
  473.5 13.9 %collective-permute-start.51 = (f32[112,128]{1,0:T(8,128)S(1)}, f32[112,128]{1,0:T(8,128)S(1)}, u32[]{:S(2)}, u32[]{:S(2)}) collective-permute-start(f32[112,128]{1,0:T(8,128)S(1)} %add_select_fusion.1), channel_id=1, source_target_pairs={{0,4},{1,5},{2,6},{3,7},{4,0},{5,1},{6,2},{7,3},{8,12},{9,13},{10,... | collective-permute-start | bytes 172040 | tf_op jit(solution)/shard_map/ppermute | solution.py:89
  479.3 13.2 %collective-permute-start.52 = (bf16[128,1024]{1,0:T(8,128)(2,1)}, bf16[128,1024]{1,0:T(8,128)(2,1)S(1)}, u32[]{:S(2)}, u32[]{:S(2)}) collective-permute-start(bf16[128,1024]{1,0:T(8,128)(2,1)} %get-tuple-element.254), channel_id=1, source_target_pairs={{0,8},{1,9},{2,10},{3,11},{4,12},{5,13},{6,14},{7,15},{8,0},{9,1},... | collective-permute-start | bytes 786440 | tf_op jit(solution)/shard_map/ppermute | solution.py:89
  480.7 20.6 %collective-permute-start.53 = (bf16[128,1024]{1,0:T(8,128)(2,1)}, bf16[128,1024]{1,0:T(8,128)(2,1)S(1)}, u32[]{:S(2)}, u32[]{:S(2)}) collective-permute-start(bf16[128,1024]{1,0:T(8,128)(2,1)} %get-tuple-element.255), channel_id=1, source_target_pairs={{0,16},{1,17},{2,18},{3,19},{4,20},{5,21},{6,22},{7,23},{8,24},{9,... | collective-permute-start | bytes 786440 | tf_op jit(solution)/shard_map/ppermute | solution.py:89
  483.0 24.4 %collective-permute-start.54 = (bf16[128,1024]{1,0:T(8,128)(2,1)}, bf16[128,1024]{1,0:T(8,128)(2,1)}, u32[]{:S(2)}, u32[]{:S(2)}) collective-permute-start(bf16[128,1024]{1,0:T(8,128)(2,1)} %get-tuple-element.256), channel_id=1, source_target_pairs={{0,24},{1,25},{2,26},{3,27},{4,28},{5,29},{6,30},{7,31},{8,16},{9,... | collective-permute-start | bytes 786440 | tf_op jit(solution)/shard_map/ppermute | solution.py:89
  485.5 22.0 %copy-start.49 = (bf16[128,1024]{1,0:T(8,128)(2,1)S(1)}, bf16[128,1024]{1,0:T(8,128)(2,1)}, u32[]{:S(2)}) copy-start(bf16[128,1024]{1,0:T(8,128)(2,1)} %get-tuple-element.253) | copy-start | bytes 786436
  487.8 22.7 %copy-start.60 = (f32[4]{0:T(128)}, f32[4]{0:T(128)S(1)}, u32[]{:S(2)}) copy-start(f32[4]{0:T(128)S(1)} %fusion.6) | copy-start | bytes 52
  (60 other events, 318.9 us)
Sparse Core Ops, SparseCore 0:
  13.2 60.5 all-gather.6
  96.3 81.2 all-gather.4

commit v4 on v3

--- a/solution.py
+++ b/solution.py
@@ -141,7 +141,11 @@
 def start_pieces(lay, group, bufs, me_ref, spans, sem, keep=None):
     me = (me_ref[0], me_ref[1], me_ref[2])
     if isinstance(group, Shards):
-        pieces = [(0, dp * lay.nt + t, dp * lay.rows, t ^ me[2], t) for t in range(lay.nt) for dp in range(lay.ndp)]
+        pieces = []
+        for to in range(lay.nt):
+            t = to ^ me[2]
+            if keep is None or keep(to):
+                pieces += [(0, dp * lay.nt + t, dp * lay.rows, to, t) for dp in range(lay.ndp)]
     else:
         pieces = []
         for b, i, z, t, c in group.pieces:
@@ -316,6 +320,30 @@
         start_pieces(lay, chain, bufs[4 * h : 4 * h + 4], me_ref, spans, sem, keep)
 
 
+def prepare(run, tokens, cotangent, gain, shift):
+    own = tokens.shape[0] // SEQ
+
+    def kernel(me_ref, x_ref, c_ref, g_ref, s_ref, in_ref, n_ref, d_ref):
+        none = jnp.zeros((SP - SEQ, D), F32)
+        for i in range(own):
+            rows, to = slice(i * SEQ, (i + 1) * SEQ), slice(i * SP, (i + 1) * SP)
+            x = jnp.concatenate([x_ref[...].astype(F32)[rows], none])
+            in_ref[to, :] = x.astype(BF)
+            unit, _ = unit_of(x)
+            n_ref[to, :] = (unit * g_ref[...] + s_ref[...]).astype(BF)
+            c = jnp.concatenate([c_ref[...].astype(F32)[rows], none])
+            live = me_ref[2] * own + i < me_ref[3]
+            d_ref[to, :] = jnp.where(live, c, 0.0).astype(BF)
+
+    shape = (jax.ShapeDtypeStruct((own * SP, D), BF), whole((own * SP, D)))
+    out, _ = run(
+        "prepare", 20, kernel, (1,),
+        [(v, whole(v.shape)) for v in (tokens, cotangent, gain, shift)],
+        [shape] * 3,
+    )
+    return out
+
+
 def attend_all(lay, run, joint, normed, bias_rows):
     rows = normed.shape[0]
     own, cw = rows // SP, lay.cw
@@ -327,9 +355,12 @@
         x_ref, b_ref, p_ref, o_ref, lse_ref, top_ref, w, sem = refs[8:]
         o, i = pl.program_id(0), pl.program_id(1)
 
-        @pl.when((o == 0) & (i == 0))
-        def _():
-            start_joint(lay, joint, bufs, me_ref, lambda to: w.at[to], lambda to: sem.at[to])
+        for k in range(1, lay.nt):
+
+            @pl.when((o == k - 1) & (i == 0))
+            def _(k=k):
+                keep = lambda to: to == k or (k == 1 and to == 0)
+                start_joint(lay, joint, bufs, me_ref, lambda to: w.at[to], lambda to: sem.at[to], keep)
 
         @pl.when(i == 0)
         def _():
@@ -409,12 +440,23 @@
         a_ref, s_ref, sec_ref, other, mine, we, ws, d_s, acc, sem_e, sem_s, sem = refs
         o = pl.program_id(0)
 
+        def fetch(k):
+            keep = lambda to: to == k
+            spans = [(first_e, half, lambda to, t: (we.at[to], 0))]
+            start_pieces(lay, group_e, bufs_e, me_ref, spans, lambda to: sem_e.at[to], keep)
+            spans = [(first_s, half, lambda to, t: (ws.at[to], 0))]
+            start_pieces(lay, group_s, bufs_s, me_ref, spans, lambda to: sem_s.at[to], keep)
+
+        for k in range(1, lay.nt):
+
+            @pl.when(o == k - 1)
+            def _(k=k):
+                if k == 1:
+                    fetch(0)
+                fetch(k)
+
         @pl.when(o == 0)
         def _():
-            spans = [(first_e, half, lambda to, t: (we.at[to], 0))]
-            start_pieces(lay, group_e, bufs_e, me_ref, spans, lambda to: sem_e.at[to])
-            spans = [(first_s, half, lambda to, t: (ws.at[to], 0))]
-            start_pieces(lay, group_s, bufs_s, me_ref, spans, lambda to: sem_s.at[to])
             if more:
                 pltpu.make_async_copy(before, acc, sem).start()
                 pltpu.make_async_copy(before, acc, sem).wait()
@@ -428,10 +470,11 @@
             rs = slice(r * SP, (r + 1) * SP)
             hidden = jnp.dot(x_ref[rs, :], we[o], preferred_element_type=F32) + b_ref[...]
             dact = jnp.dot(g_ref[rs, :], ws[o], preferred_element_type=F32)
+            hidden = hidden.astype(BF)
             sigma = 0.5 + 0.5 * jnp.tanh(0.851 * hidden)
             active = hidden * sigma
-            a_ref[rs, :] = active.astype(BF)
-            dh = (dact * (sigma + 1.702 * active * (1.0 - sigma))).astype(BF)
+            a_ref[rs, :] = active
+            dh = dact.astype(BF) * (sigma + 1.702 * active * (1.0 - sigma))
             d_s[rs, :] = dh
             part = column_sum(dh.astype(F32))
             total = part if total is None else total + part
@@ -660,7 +703,7 @@
 def along(lay, run, arrays, more=()):
     z, dr, width = arrays[0].shape
     n = len(arrays)
-    w = 256 if width % 256 == 0 else 128
+    w = width // 2
 
     def kernel(me_ref, *refs):
         for k in range(z):
@@ -696,7 +739,8 @@
         z, dr, width = self.keep[0].shape[-3:]
         one = len(self.keep) == 1
         block = pl.BlockSpec((n, 1, dr, width), lambda s, m: (0, s, 0, 0)) if one else None
-        piece = pl.BlockSpec((1, dr, width), lambda s, m: (s, 0, 0))
+        deep = 1 if one else z // 2
+        piece = pl.BlockSpec((deep, dr, width), lambda s, m: (s, 0, 0))
         k = len(self.keep)
 
         def kernel(me_ref, *refs):
@@ -706,7 +750,7 @@
 
         shape = jax.ShapeDtypeStruct((z, dr, width), BF)
         sums, more = run(
-            "add", 0, kernel, (z,), [(x, block or piece) for x in (*self.keep, *self.got)], [(shape, piece)] * n, (), more
+            "add", 0, kernel, (z // deep,), [(x, block or piece) for x in (*self.keep, *self.got)], [(shape, piece)] * n, (), more
         )
         self.keep = [x for t, x in zip(self.left, sums) if not t >> bit & 1]
         self.got = [swap(x, 1 << bit, self.lay.size) for t, x in zip(self.left, sums) if t >> bit & 1]
@@ -733,39 +777,15 @@
         def kernel(me_ref, a_ref, b_ref, o_ref):
             o_ref[...] = a_ref[...] + b_ref[...]
 
-        block = pl.BlockSpec((1, dr, width), lambda s, m: (s, 0, 0))
+        block = pl.BlockSpec((z, dr, width), lambda s, m: (0, 0, 0))
         shape = jax.ShapeDtypeStruct(own.shape, BF)
-        (x,), more = run("add_core", 0, kernel, (z,), [(own, block), (got, block)], [(shape, block)], (), more)
+        (x,), more = run("add_core", 0, kernel, (1,), [(own, block), (got, block)], [(shape, block)], (), more)
         self.parts.append(swap(x, to, self.lay.size))
         return more
 
     def along(self, run, more=()):
         self.ends, more = along(self.lay, run, [*self.waiting[0][1:], *self.parts], more)
         return more
-
-
-class Sum:
-    def __init__(self, lay, x, combine=jnp.add):
-        self.lay, self.x, self.combine = lay, x, combine
-        step = 2 * lay.nt
-        self.stages = [list(range(1, lay.nt)), [z * step for z in range(1, lay.nz)], [lay.core]]
-        self.send()
-
-    def send(self):
-        self.got = [swap(self.x, mask, self.lay.size) for mask in self.stages.pop(0)]
-
-    def land(self, passed=None):
-        for got in passed or self.got:
-            self.x = self.combine(self.x, got)
-        if self.stages:
-            self.send()
-        else:
-            self.got = None
-
-
-def pad_rows(x):
-    own = x.shape[0] // SEQ
-    return jnp.pad(x.reshape(own, SEQ, D), ((0, 0), (0, SP - SEQ), (0, 0))).reshape(own * SP, D)
 
 
 def unpad_rows(x):
@@ -809,7 +829,7 @@
     small = jnp.concatenate([joint_bias.reshape(-1), expand_bias.reshape(-1)])
     n_small = small.shape[0]
     output = jnp.concatenate([output_weight.T, jnp.pad(small[None], ((0, 15), (0, cw - n_small)))])
-    ((output,),) = gate(run, [output])
+    (joint[0].got, joint[1].got), (output,) = gate(run, [chain.got for chain in joint], [output])
     output = Shards(lay, output)
 
     biases = output.bufs[0][:, dr].astype(F32)
@@ -823,11 +843,6 @@
 
     image_ids = tensor * own + jnp.arange(own, dtype=jnp.int32)
     image_live = image_ids < count
-    inputs = pad_rows(tokens)
-    live_rows = jnp.repeat(image_live, SEQ)[:, None]
-    dresult = pad_rows(jnp.where(live_rows, cotangent, jnp.zeros_like(cotangent)))
-    unit, _ = unit_of(inputs.astype(F32))
-    normed = (unit * first_gain + first_shift).astype(BF)
     row = lambda v: v.reshape(1, D)
 
     def land(chains):
@@ -835,7 +850,6 @@
             chain.land()
             chain.send_last() if len(chain.stages) == 1 else chain.send()
 
-    ((joint[0].got, joint[1].got),) = gate(run, [chain.got for chain in joint])
     land(joint)
     shrink_t = (shrink_weight + run.token[0, 0].astype(BF)).T
     feeds = [Chain(lay, expand_weight[:, :half], False), Chain(lay, shrink_t[:, :half], True)]
@@ -852,8 +866,9 @@
     land(joint)
     while len(feeds[0].stages) > 2:
         land(feeds)
-    (joint[0].got, joint[1].got), (feeds[0].got, feeds[1].got), (inputs, dresult, normed), (rest,) = gate(
-        run, [chain.got for chain in joint], [chain.got for chain in feeds], [inputs, dresult, normed], [rest]
+    inputs, normed, dresult = prepare(run, tokens, cotangent, row(first_gain), row(first_shift))
+    (joint[0].got, joint[1].got), (feeds[0].got, feeds[1].got), (rest,) = gate(
+        run, [chain.got for chain in joint], [chain.got for chain in feeds], [rest]
     )
     for chain in joint:
         chain.share()
@@ -926,20 +941,15 @@
     heads = heads[jnp.arange(nt) ^ tensor]
     vectors = [sums_two, expand_sum, sums_one, heads[:, 0], heads[:, 2]]
     sums = jnp.concatenate([peak] + [v.reshape(-1, 128) for v in vectors])
-    is_peak = lax.broadcasted_iota(jnp.int32, sums.shape, 0) < HEADS
-    small = Sum(lay, sums, lambda a, b: jnp.where(is_peak, jnp.maximum(a, b), a + b))
-    result, passed = feed_out(lay, run, shrinks[0], active0, middle, None, small.got)
-    small.land(passed)
+    sums = lax.all_gather(sums, AXES)
+    result, _ = feed_out(lay, run, shrinks[0], active0, middle)
     total.along(run)
-    result, passed = feed_out(lay, run, shrinks[1], active1, result, row(shrink_bias), small.got)
-    small.land(passed)
-    while small.got is not None:
-        small.land()
+    result, _ = feed_out(lay, run, shrinks[1], active1, result, row(shrink_bias))
 
     block_out = unpad_rows(result)
     tokens_grad = unpad_rows(token_rows)
-    sums = small.x
-    peak = sums[:HEADS, 0]
+    peak = jnp.max(sums[:, :HEADS, 0], axis=0)
+    sums = jnp.sum(sums, axis=0)
     at = [HEADS, HEADS + 4 * D // 128, HEADS + (4 * D + FF) // 128, HEADS + (6 * D + FF) // 128]
     sums_two = sums[at[0] : at[1]].reshape(4, D)
     expand_sum = sums[at[1] : at[2]].reshape(FF)

time: 526 us -> 498 us (0.947)
  the two profiles are of different devices: /device:TPU:14 before, /device:TPU:0 now
where the time goes in v4:
time: 498 us; the launch traced here: 489 us
  Pallas kernels  302 us (61%)
  waiting for transfers between devices  56.4 us (11%)
  starting transfers between devices  53.8 us (11%)
  local copies, waits for them, and re-layouts  35.7 us (7%)
  other arithmetic  25 us (5%)
  between operations  15.7 us (3%)
    pallas_call x26, Pallas kernels, __call__(): pl.pallas_call(body, grid_spec=pltpu.PrefetchScalarGridSpec(num_scalar_pr...  302 us
    ppermute x48, waiting for transfers between devices, swap(): return lax.ppermute(x, AXES, [(i, i ^ mask) for i in range(size)])  56.4 us
    ppermute x48, starting transfers between devices, swap(): return lax.ppermute(x, AXES, [(i, i ^ mask) for i in range(size)])  53.2 us
    unnamed x108, local copies, waits for them, and re-layouts  18.2 us
  transfers between devices with their start and end apart: 51, of which 11 were waited for; matrix products, arithmetic and copies ran while one was open for 8% of the time, Pallas kernels for 62%

profile of v4, /device:TPU:0, one launch (start us, length us, event | category | flops | bytes accessed | tf_op | source)
XLA Modules:
  0.0 488.7 jit_solution(8799584235236128889)
XLA Ops:
  7.2 1.1 copy.107
  8.5 4.1 collective-permute-start
  17.4 3.1 collective-permute-done.refs_1_
  20.5 1.3 collective-permute-done.1.refs_2_
  26.5 1.6 collective-permute-start.4
  29.1 1.6 collective-permute-start.2
  31.3 3.0 collective-permute-start.8
  34.3 3.0 collective-permute-start.5
  37.4 2.7 collective-permute-start.3
  40.1 1.6 collective-permute-start.7
  43.0 4.0 collective-permute-done.7.refs_3_
  46.9 1.6 collective-permute-done.9.refs_4_
  48.5 8.3 %collective-permute-done.3.refs_1_ = bf16[4,128,384]{2,1,0:T(8,128)(2,1)S(1)} collective-permute-done((bf16[4,128,384]{2,1,0:T(8,128)(2,1)S(1)}, bf16[4,128,384]{2,1,0:T(8,128)(2,1)S(1)}, u32[]{:S(2)}, u32[]{:S(2)}) %collective-permute-start.3) | collective-permute-done | bytes 393248 | tf_op jit(solution)/shard_map/ppermute | solution.py:89
  58.2 1.2 pad_maximum_fusion.3.refs_4_
  60.5 1.8 pad_maximum_fusion.5
  62.3 2.5 collective-permute-start.13
  64.9 1.6 collective-permute-start.10
  67.3 7.8 %prepare.1 = (bf16[1184,1024]{1,0:T(8,128)(2,1)}, bf16[1184,1024]{1,0:T(8,128)(2,1)}, bf16[1184,1024]{1,0:T(8,128)(2,1)}, f32[8,128]{1,0:T(8,128)}) custom-call(s32[4]{0:T(128)} %pad_add_fusion.me_ref, bf16[1154,1024]{1,0:T(8,128)(2,1)} %refs_0_.1, bf16[1154,1024]{1,0:T(8,128)(2,1)} %refs_1_.1, ...), custom_call_target="tpu_custom_call", output_to_operand_aliasing={{3}: (5, {})} | custom-call | flops 22000001024 | bytes 20000000 | tf_op jit(solution)/shard_map/prepare/pallas_call | solution.py:52
  75.2 8.8 %collective-permute-done.13.refs_4_ = bf16[4,128,512]{2,1,0:T(8,128)(2,1)S(1)} collective-permute-done((bf16[4,128,512]{2,1,0:T(8,128)(2,1)}, bf16[4,128,512]{2,1,0:T(8,128)(2,1)S(1)}, u32[]{:S(2)}, u32[]{:S(2)}) %collective-permute-start.13) | collective-permute-done | bytes 524320 | tf_op jit(solution)/shard_map/ppermute | solution.py:89
  84.0 7.9 %collective-permute-done.12.refs_3_ = bf16[4,128,512]{2,1,0:T(8,128)(2,1)S(1)} collective-permute-done((bf16[4,128,512]{2,1,0:T(8,128)(2,1)}, bf16[4,128,512]{2,1,0:T(8,128)(2,1)S(1)}, u32[]{:S(2)}, u32[]{:S(2)}) %collective-permute-start.12) | collective-permute-done | bytes 524320 | tf_op jit(solution)/shard_map/ppermute | solution.py:89
  94.6 2.2 pad_maximum_fusion.1.refs_4_.refs_0_
  96.8 1.5 collective-permute-start.19
  98.8 1.1 pad_maximum_fusion.refs_0_
  102.6 35.2 %attend.1 = (bf16[1184,3072]{1,0:T(8,128)(2,1)}, bf16[1184,1024]{1,0:T(8,128)(2,1)}, f32[2,4,4,640]{3,2,1,0:T(4,128)}, f32[2,4,4,640]{3,2,1,0:T(4,128)}, f32[8,128]{1,0:T(8,128)}) custom-call(s32[4]{0:T(128)} %pad_add_fusion.me_ref, bf16[8,128,384]{2,1,0:T(8,128)(2,1)} %copy-done.29, ...), custom_call_target="tpu_custom_call", output_to_operand_aliasing={{4}: (11, {})} | custom-call | flops 39600001024 | bytes 36000000 | tf_op jit(solution)/shard_map/attend/pallas_call | solution.py:52
  141.5 9.3 %out_project.1 = (bf16[1184,1024]{1,0:T(8,128)(2,1)}, bf16[1184,1024]{1,0:T(8,128)(2,1)}, f32[8,128]{1,0:T(8,128)}) custom-call(s32[4]{0:T(128)} %pad_add_fusion.me_ref, bf16[32,144,256]{2,1,0:T(8,128)(2,1)} %bitcast.103, bf16[1184,1024]{1,0:T(8,128)(2,1)} %get-tuple-element.150.refs_1_.refs_4_.refs_9_, ...), custom_call_target="tpu_custom_call", output_to_operand_aliasing={{2}: (7, {})} | custom-call | flops 9900000256 | bytes 9000000 | tf_op jit(solution)/shard_map/out_project/pallas_call | solution.py:52
  152.2 37.9 %feed.2 = (bf16[1184,2048]{1,0:T(8,128)(2,1)}, f32[1,2048]{1,0:T(1,128)}, f32[1184,1024]{1,0:T(8,128)}, bf16[4,4,128,1024]{3,2,1,0:T(8,128)(2,1)}, bf16[4,4,128,1024]{3,2,1,0:T(8,128)(2,1)}, /*index=5*/f32[8,128]{1,0:T(8,128)}) custom-call(s32[4]{0:T(128)} %pad_add_fusion.me_ref, ...), custom_call_target="tpu_custom_call", output_to_operand_aliasing={{5}: (12, {})} | custom-call | flops 44000002048 | bytes 40000000 | tf_op jit(solution)/shard_map/feed/pallas_call | solution.py:52
  190.3 39.2 %feed.3 = (bf16[1184,2048]{1,0:T(8,128)(2,1)}, f32[1,2048]{1,0:T(1,128)}, bf16[1184,1024]{1,0:T(8,128)(2,1)}, bf16[4,4,128,1024]{3,2,1,0:T(8,128)(2,1)}, bf16[4,...) custom-call(s32[4]{0:T(128)} %pad_add_fusion.me_ref, ...), custom_call_target="tpu_custom_call", output_to_operand_aliasing={{5}: (7, {})} | custom-call | flops 44000002048 | bytes 40000000 | tf_op jit(solution)/shard_map/feed/pallas_call | solution.py:52
  231.5 6.4 %add.128 = (bf16[4,128,1024]{2,1,0:T(8,128)(2,1)}, bf16[4,128,1024]{2,1,0:T(8,128)(2,1)}, bf16[4,128,1024]{2,1,0:T(8,128)(2,1)}, bf16[4,128,1024]{2,1,0:T(8,128)(2,1)}, f32[8,128]{1,0:T(8,128)}) custom-call(s32[4]{0:T(128)} %pad_add_fusion.me_ref, bf16[4,4,128,1024]{3,2,1,0:T(8,128)(2,1)} %get-tuple-element.170.refs_0_, ...), custom_call_target="tpu_custom_call", output_to_operand_aliasing={{4}: (3, {})} | custom-call | tf_op jit(solution)/shard_map/add/pallas_call | solution.py:52
  237.9 1.7 collective-permute-start.26
  240.7 6.4 %add.129 = (bf16[4,128,1024]{2,1,0:T(8,128)(2,1)}, bf16[4,128,1024]{2,1,0:T(8,128)(2,1)}, bf16[4,128,1024]{2,1,0:T(8,128)(2,1)}, bf16[4,128,1024]{2,1,0:T(8,128)(2,1)}, f32[8,128]{1,0:T(8,128)}) custom-call(s32[4]{0:T(128)} %pad_add_fusion.me_ref, bf16[4,4,128,1024]{3,2,1,0:T(8,128)(2,1)} %get-tuple-element.168.refs_0_, ...), custom_call_target="tpu_custom_call", output_to_operand_aliasing={{4}: (3, {})} | custom-call | tf_op jit(solution)/shard_map/add/pallas_call | solution.py:52
  247.2 1.4 collective-permute-start.27
  249.2 18.5 %feed_back.1 = (bf16[1184,1024]{1,0:T(8,128)(2,1)}, bf16[1184,1024]{1,0:T(8,128)(2,1)}, f32[4,1024]{1,0:T(4,128)}, bf16[4,4,128,256]{3,2,1,0:T(8,128)(2,1)}, bf1...) custom-call(s32[4]{0:T(128)} %pad_add_fusion.me_ref, ...), custom_call_target="tpu_custom_call", output_to_operand_aliasing={{5}: (7, {})} | custom-call | flops 20899999744 | bytes 19000000 | tf_op jit(solution)/shard_map/feed_back/pallas_call | solution.py:52
  268.5 5.0 %collective-permute-done.27.refs_17_ = bf16[4,128,1024]{2,1,0:T(8,128)(2,1)} collective-permute-done((bf16[4,128,1024]{2,1,0:T(8,128)(2,1)}, bf16[4,128,1024]{2,1,0:T(8,128)(2,1)}, u32[]{:S(2)}, u32[]{:S(2)}) %collective-permute-start.27) | collective-permute-done | bytes 1048608 | tf_op jit(solution)/shard_map/ppermute | solution.py:89
  273.5 20.1 %attend_back.4 = (f32[2,1,1,768]{3,2,1,0:T(1,128)}, bf16[1184,1024]{1,0:T(8,128)(2,1)}, bf16[1,4,128,1024]{3,2,1,0:T(8,128)(2,1)}, bf16[1,4,128,1024]{3,2,1,0:T(...) custom-call(s32[4]{0:T(128)} %pad_add_fusion.me_ref, ...), custom_call_target="tpu_custom_call", output_to_operand_aliasing={{4}: (16, {}), {5}: (17, {}), {6}: (18, {})} | custom-call | flops 22000001024 | bytes 20000000 | tf_op jit(solution)/shard_map/attend_back/pallas_call | solution.py:52
  294.7 3.9 add.130
  298.6 1.4 collective-permute-start.32
  301.0 3.9 add.131
  305.8 20.5 %attend_back.5 = (f32[2,1,1,768]{3,2,1,0:T(1,128)}, bf16[1184,1024]{1,0:T(8,128)(2,1)}, bf16[1,4,128,1024]{3,2,1,0:T(8,128)(2,1)}, bf16[1,4,128,1024]{3,2,1,0:T(8,128)(2,1)}, f32[8,128]{1,0:T(8,128)}) custom-call(s32[4]{0:T(128)} %pad_add_fusion.me_ref, bf16[8,128,384]{2,1,0:T(8,128)(2,1)} %copy-done.29, ...), custom_call_target="tpu_custom_call", output_to_operand_aliasing={{4}: (16, {})} | custom-call | flops 22000001024 | bytes 20000000 | tf_op jit(solution)/shard_map/attend_back/pallas_call | solution.py:52
  327.6 3.0 add_plane.3
  331.6 3.1 add_plane.4
  335.7 3.3 add_core.3
  339.0 1.2 collective-permute-start.35
  340.2 1.4 collective-permute-start.36
  341.6 4.8 collective-permute-start.37
  346.9 20.0 %attend_back.6 = (f32[2,1,1,768]{3,2,1,0:T(1,128)}, bf16[1184,1024]{1,0:T(8,128)(2,1)}, bf16[1,4,128,1024]{3,2,1,0:T(8,128)(2,1)}, bf16[1,4,128,1024]{3,2,1,0:T(8,128)(2,1)}, f32[8,128]{1,0:T(8,128)}) custom-call(s32[4]{0:T(128)} %pad_add_fusion.me_ref, bf16[8,128,384]{2,1,0:T(8,128)(2,1)} %copy-done.29, ...), custom_call_target="tpu_custom_call", output_to_operand_aliasing={{4}: (16, {})} | custom-call | flops 22000001024 | bytes 20000000 | tf_op jit(solution)/shard_map/attend_back/pallas_call | solution.py:52
  369.2 3.3 collective-permute-start.40
  374.0 3.3 add_core.4
  377.2 25.4 %attend_back.7 = (f32[2,1,1,768]{3,2,1,0:T(1,128)}, bf16[1184,1024]{1,0:T(8,128)(2,1)}, f32[2,1024]{1,0:T(2,128)}, bf16[1,4,128,1024]{3,2,1,0:T(8,128)(2,1)}, bf...) custom-call(s32[4]{0:T(128)} %pad_add_fusion.me_ref, ...), custom_call_target="tpu_custom_call", output_to_operand_aliasing={{5}: (22, {})} | custom-call | flops 22000001024 | bytes 20000000 | tf_op jit(solution)/shard_map/attend_back/pallas_call | solution.py:52
  405.5 1.2 convert_add_fusion.1
  407.7 3.3 add_core.5
  411.0 1.3 convert_add_fusion
  414.2 1.1 collective-permute-start.44
  416.1 1.9 slice.165
  418.0 1.9 reshape.176
  419.8 12.3 %feed_out.2 = (f32[1184,1024]{1,0:T(8,128)}, f32[8,128]{1,0:T(8,128)}) custom-call(s32[4]{0:T(128)} %pad_add_fusion.me_ref, bf16[8,128,512]{2,1,0:T(8,128)(2,1)} %pad_maximum_fusion.1.refs_4_.refs_0_, bf16[8,128,512]{2,1,0:T(8,128)(2,1)} %get-tuple-element.159.refs_5_.refs_1_, ...), custom_call_target="tpu_custom_call", output_to_operand_aliasing={{1}: (7, {})} | custom-call | flops 13200000000 | bytes 12000000 | tf_op jit(solution)/shard_map/feed_out/pallas_call | solution.py:52
  432.1 8.9 %collective-permute-done.44.refs_4_ = bf16[4,128,1024]{2,1,0:T(8,128)(2,1)S(1)} collective-permute-done((bf16[4,128,1024]{2,1,0:T(8,128)(2,1)}, bf16[4,128,1024]{2,1,0:T(8,128)(2,1)S(1)}, u32[]{:S(2)}, u32[]{:S(2)}) %collective-permute-start.44) | collective-permute-done | bytes 1048608 | tf_op jit(solution)/shard_map/ppermute | solution.py:89
  442.1 4.2 add_plane.5
  447.0 3.7 collective-permute-start.46
  450.7 12.3 %feed_out.3 = (bf16[1184,1024]{1,0:T(8,128)(2,1)}, f32[8,128]{1,0:T(8,128)}) custom-call(s32[4]{0:T(128)} %pad_add_fusion.me_ref, bf16[32,128,1024]{2,1,0:T(8,128)(2,1)} %bitcast.107, bf16[1184,2048]{1,0:T(8,128)(2,1)} %get-tuple-element.163.refs_1_, f32[1184,1024]{1,0:T(8,128)} %get-tuple-element.222.refs_2_, ...), custom_call_target="tpu_custom_call", output_to_operand_aliasing={{1}: (5, {})} | custom-call | flops 13200000000 | bytes 12000000 | tf_op jit(solution)/shard_map/feed_out/pallas_call | solution.py:52
  463.0 1.9 slice.164
  464.9 1.9 reshape.174
  466.8 6.4 %collective-permute-done.46 = bf16[128,1024]{1,0:T(8,128)(2,1)S(1)} collective-permute-done((bf16[128,1024]{1,0:T(8,128)(2,1)}, bf16[128,1024]{1,0:T(8,128)(2,1)S(1)}, u32[]{:S(2)}, u32[]{:S(2)}) %collective-permute-start.46) | collective-permute-done | bytes 262176 | tf_op jit(solution)/shard_map/ppermute | solution.py:89
  475.3 1.1 slice_reduce_fusion
  476.4 1.6 reduce_sum.49
  (278 shorter events, 55.1 us)
Async XLA Ops:
  7.2 17.0 %copy-start.32 = (bf16[1024,128]{1,0:T(8,128)(2,1)S(1)}, bf16[1024,128]{1,0:T(8,128)(2,1)}, u32[]{:S(2)}) copy-start(bf16[1024,128]{1,0:T(8,128)(2,1)} %param.27) | copy-start | bytes 786436
  7.2 92.7 %all-gather.9.cloned.1.call-start = ((), (), s32[]{:S(2)}) async-start(), calls=%async_computation.1 | async-start | bytes 2433024 | tf_op jit(solution)/shard_map/all_gather | solution.py:131
  8.5 11.9 %collective-permute-start = (bf16[1,128,384]{2,1,0:T(8,128)(2,1)S(1)}, bf16[1,128,384]{2,1,0:T(8,128)(2,1)S(1)}, u32[]{:S(2)}, u32[]{:S(2)}) collective-permute-start(bf16[1,128,384]{2,1,0:T(8,128)(2,1)S(1)} %bitcast.80), channel_id=1, source_target_pairs={{0,16},{1,17},{2,18},{3,19},{4,20},{5,21},{6,22},{7,23},{8,24},{9,... | collective-permute-start | bytes 294920 | tf_op jit(solution)/shard_map/ppermute | solution.py:89
  12.7 9.0 %collective-permute-start.1 = (bf16[1,128,384]{2,1,0:T(8,128)(2,1)S(1)}, bf16[1,128,384]{2,1,0:T(8,128)(2,1)S(1)}, u32[]{:S(2)}, u32[]{:S(2)}) collective-permute-start(bf16[1,128,384]{2,1,0:T(8,128)(2,1)S(1)} %bitcast.84), channel_id=1, source_target_pairs={{0,16},{1,17},{2,18},{3,19},{4,20},{5,21},{6,22},{7,23},{8,24},{9,... | collective-permute-start | bytes 294920 | tf_op jit(solution)/shard_map/ppermute | solution.py:89
  23.0 11.2 %copy-start.11 = (bf16[1,128,384]{2,1,0:T(8,128)(2,1)S(1)}, bf16[1,128,384]{2,1,0:T(8,128)(2,1)}, u32[]{:S(2)}) copy-start(bf16[1,128,384]{2,1,0:T(8,128)(2,1)} %get-tuple-element.137) | copy-start | bytes 294916
  23.1 14.3 %copy-start.9 = (bf16[1,128,384]{2,1,0:T(8,128)(2,1)S(1)}, bf16[1,128,384]{2,1,0:T(8,128)(2,1)}, u32[]{:S(2)}) copy-start(bf16[1,128,384]{2,1,0:T(8,128)(2,1)} %get-tuple-element.136) | copy-start | bytes 294916
  23.1 167.2 %all-gather.7.cloned.1.call-start = ((), (), s32[]{:S(2)}) async-start(), calls=%async_computation | async-start | bytes 8650752 | tf_op jit(solution)/shard_map/all_gather | solution.py:131
  24.1 15.9 %collective-permute-start.6 = (bf16[1,128,512]{2,1,0:T(8,128)(2,1)S(1)}, bf16[1,128,512]{2,1,0:T(8,128)(2,1)S(1)}, u32[]{:S(2)}, u32[]{:S(2)}) collective-permute-start(bf16[1,128,512]{2,1,0:T(8,128)(2,1)S(1)} %get-tuple-element.309), channel_id=1, source_target_pairs={{0,16},{1,17},{2,18},{3,19},{4,20},{5,21},{6,22},{7,23},{8,24},{9,... | collective-permute-start | bytes 393224 | tf_op jit(solution)/shard_map/ppermute | solution.py:89
  26.5 7.8 %collective-permute-start.4 = (bf16[2,128,384]{2,1,0:T(8,128)(2,1)S(1)}, bf16[2,128,384]{2,1,0:T(8,128)(2,1)S(1)}, u32[]{:S(2)}, u32[]{:S(2)}) collective-permute-start(bf16[2,128,384]{2,1,0:T(8,128)(2,1)S(1)} %pad_maximum_fusion.13), channel_id=1, source_target_pairs={{0,2},{1,3},{2,0},{3,1},{4,6},{5,7},{6,4},{7,5},{8,10},{9,11},{10,... | collective-permute-start | bytes 589832 | tf_op jit(solution)/shard_map/ppermute | solution.py:89
  29.1 8.3 %collective-permute-start.2 = (bf16[2,128,384]{2,1,0:T(8,128)(2,1)S(1)}, bf16[2,128,384]{2,1,0:T(8,128)(2,1)S(1)}, u32[]{:S(2)}, u32[]{:S(2)}) collective-permute-start(bf16[2,128,384]{2,1,0:T(8,128)(2,1)S(1)} %pad_maximum_fusion.12), channel_id=1, source_target_pairs={{0,1},{1,0},{2,3},{3,2},{4,5},{5,4},{6,7},{7,6},{8,9},{9,8},{10,11... | collective-permute-start | bytes 589832 | tf_op jit(solution)/shard_map/ppermute | solution.py:89
  31.3 10.3 %collective-permute-start.8 = (bf16[1,128,512]{2,1,0:T(8,128)(2,1)S(1)}, bf16[1,128,512]{2,1,0:T(8,128)(2,1)S(1)}, u32[]{:S(2)}, u32[]{:S(2)}) collective-permute-start(bf16[1,128,512]{2,1,0:T(8,128)(2,1)S(1)} %get-tuple-element.311), channel_id=1, source_target_pairs={{0,16},{1,17},{2,18},{3,19},{4,20},{5,21},{6,22},{7,23},{8,24},{9,... | collective-permute-start | bytes 393224 | tf_op jit(solution)/shard_map/ppermute | solution.py:89
  34.3 14.2 %collective-permute-start.5 = (bf16[4,128,384]{2,1,0:T(8,128)(2,1)S(1)}, bf16[4,128,384]{2,1,0:T(8,128)(2,1)S(1)}, u32[]{:S(2)}, u32[]{:S(2)}) collective-permute-start(bf16[4,128,384]{2,1,0:T(8,128)(2,1)S(1)} %pad_maximum_fusion.8), channel_id=1, source_target_pairs={{0,8},{1,9},{2,10},{3,11},{4,12},{5,13},{6,14},{7,15},{8,0},{9,1},... | collective-permute-start | bytes 1179656 | tf_op jit(solution)/shard_map/ppermute | solution.py:89
  37.4 11.2 %copy-start.30 = (bf16[2,128,384]{2,1,0:T(8,128)(2,1)}, bf16[2,128,384]{2,1,0:T(8,128)(2,1)S(1)}, u32[]{:S(2)}) copy-start(bf16[2,128,384]{2,1,0:T(8,128)(2,1)S(1)} %collective-permute-done.2) | copy-start | bytes 589828
  37.4 19.4 %collective-permute-start.3 = (bf16[4,128,384]{2,1,0:T(8,128)(2,1)S(1)}, bf16[4,128,384]{2,1,0:T(8,128)(2,1)S(1)}, u32[]{:S(2)}, u32[]{:S(2)}) collective-permute-start(bf16[4,128,384]{2,1,0:T(8,128)(2,1)S(1)} %pad_maximum_fusion.7), channel_id=1, source_target_pairs={{0,8},{1,9},{2,10},{3,11},{4,12},{5,13},{6,14},{7,15},{8,0},{9,1},... | collective-permute-start | bytes 1179656 | tf_op jit(solution)/shard_map/ppermute | solution.py:89
  40.1 6.8 %collective-permute-start.7 = (bf16[2,128,512]{2,1,0:T(8,128)(2,1)S(1)}, bf16[2,128,512]{2,1,0:T(8,128)(2,1)S(1)}, u32[]{:S(2)}, u32[]{:S(2)}) collective-permute-start(bf16[2,128,512]{2,1,0:T(8,128)(2,1)S(1)} %pad_maximum_fusion.9), channel_id=1, source_target_pairs={{0,1},{1,0},{2,3},{3,2},{4,5},{5,4},{6,7},{7,6},{8,9},{9,8},{10,11... | collective-permute-start | bytes 786440 | tf_op jit(solution)/shard_map/ppermute | solution.py:89
  41.7 6.8 %collective-permute-start.9 = (bf16[2,128,512]{2,1,0:T(8,128)(2,1)S(1)}, bf16[2,128,512]{2,1,0:T(8,128)(2,1)S(1)}, u32[]{:S(2)}, u32[]{:S(2)}) collective-permute-start(bf16[2,128,512]{2,1,0:T(8,128)(2,1)S(1)} %pad_maximum_fusion.10), channel_id=1, source_target_pairs={{0,2},{1,3},{2,0},{3,1},{4,6},{5,7},{6,4},{7,5},{8,10},{9,11},{10,... | collective-permute-start | bytes 786440 | tf_op jit(solution)/shard_map/ppermute | solution.py:89
  46.9 9.8 %copy-start.1 = (bf16[2,128,512]{2,1,0:T(8,128)(2,1)}, bf16[2,128,512]{2,1,0:T(8,128)(2,1)S(1)}, u32[]{:S(2)}) copy-start(bf16[2,128,512]{2,1,0:T(8,128)(2,1)S(1)} %collective-permute-done.7.refs_3_) | copy-start | bytes 786436
  59.4 34.6 %copy-start.28 = (bf16[8,128,384]{2,1,0:T(8,128)(2,1)}, bf16[8,128,384]{2,1,0:T(8,128)(2,1)S(1)}, u32[]{:S(2)}) copy-start(bf16[8,128,384]{2,1,0:T(8,128)(2,1)S(1)} %pad_maximum_fusion.3.refs_4_) | copy-start | bytes 2359300
  59.4 32.5 %collective-permute-start.11 = (bf16[8,128,384]{2,1,0:T(8,128)(2,1)S(1)}, bf16[8,128,384]{2,1,0:T(8,128)(2,1)}, u32[]{:S(2)}, u32[]{:S(2)}) collective-permute-start(bf16[8,128,384]{2,1,0:T(8,128)(2,1)S(1)} %pad_maximum_fusion.3.refs_4_), channel_id=1, source_target_pairs={{0,1},{1,0},{2,3},{3,2},{4,5},{5,4},{6,7},{7,6},{8,9},{9,8},{10,11... | collective-permute-start | bytes 2359304 | tf_op jit(solution)/shard_map/ppermute | solution.py:89
  62.3 21.7 %collective-permute-start.13 = (bf16[4,128,512]{2,1,0:T(8,128)(2,1)}, bf16[4,128,512]{2,1,0:T(8,128)(2,1)S(1)}, u32[]{:S(2)}, u32[]{:S(2)}) collective-permute-start(bf16[4,128,512]{2,1,0:T(8,128)(2,1)} %pad_maximum_fusion.5), channel_id=1, source_target_pairs={{0,8},{1,9},{2,10},{3,11},{4,12},{5,13},{6,14},{7,15},{8,0},{9,1},... | collective-permute-start | bytes 1572872 | tf_op jit(solution)/shard_map/ppermute | solution.py:89
  64.9 10.3 %copy-start.29 = (bf16[8,128,384]{2,1,0:T(8,128)(2,1)}, bf16[8,128,384]{2,1,0:T(8,128)(2,1)S(1)}, u32[]{:S(2)}) copy-start(bf16[8,128,384]{2,1,0:T(8,128)(2,1)S(1)} %pad_maximum_fusion.2.refs_0_) | copy-start | bytes 2359300
  64.9 27.0 %collective-permute-start.10 = (bf16[8,128,384]{2,1,0:T(8,128)(2,1)S(1)}, bf16[8,128,384]{2,1,0:T(8,128)(2,1)}, u32[]{:S(2)}, u32[]{:S(2)}) collective-permute-start(bf16[8,128,384]{2,1,0:T(8,128)(2,1)S(1)} %pad_maximum_fusion.2.refs_0_), channel_id=1, source_target_pairs={{0,2},{1,3},{2,0},{3,1},{4,6},{5,7},{6,4},{7,5},{8,10},{9,11},{10,... | collective-permute-start | bytes 2359304 | tf_op jit(solution)/shard_map/ppermute | solution.py:89
  67.3 24.6 %collective-permute-start.12 = (bf16[4,128,512]{2,1,0:T(8,128)(2,1)}, bf16[4,128,512]{2,1,0:T(8,128)(2,1)S(1)}, u32[]{:S(2)}, u32[]{:S(2)}) collective-permute-start(bf16[4,128,512]{2,1,0:T(8,128)(2,1)} %pad_maximum_fusion.4), channel_id=1, source_target_pairs={{0,8},{1,9},{2,10},{3,11},{4,12},{5,13},{6,14},{7,15},{8,0},{9,1},... | collective-permute-start | bytes 1572872 | tf_op jit(solution)/shard_map/ppermute | solution.py:89
  75.2 19.4 %copy-start.4 = (bf16[2,128,512]{2,1,0:T(8,128)(2,1)S(1)}, bf16[2,128,512]{2,1,0:T(8,128)(2,1)}, u32[]{:S(2)}) copy-start(bf16[2,128,512]{2,1,0:T(8,128)(2,1)} %get-tuple-element.143) | copy-start | bytes 786436
  93.4 381.9 %all-gather.11.cloned.1.call-start = ((), (), s32[]{:S(2)}) async-start(), calls=%async_computation.2 | async-start | bytes 1892352 | tf_op jit(solution)/shard_map/all_gather | solution.py:944
  94.1 7.9 %collective-permute-start.16 = (bf16[8,128,384]{2,1,0:T(8,128)(2,1)S(1)}, bf16[8,128,384]{2,1,0:T(8,128)(2,1)}, u32[]{:S(2)}, u32[]{:S(2)}) collective-permute-start(bf16[8,128,384]{2,1,0:T(8,128)(2,1)S(1)} %pad_maximum_fusion.3.refs_4_), channel_id=1, source_target_pairs={{0,4},{1,5},{2,6},{3,7},{4,0},{5,1},{6,2},{7,3},{8,12},{9,13},{10,... | collective-permute-start | bytes 2359304 | tf_op jit(solution)/shard_map/ppermute | solution.py:89
  94.1 7.9 %collective-permute-start.14 = (bf16[8,128,384]{2,1,0:T(8,128)(2,1)}, bf16[8,128,384]{2,1,0:T(8,128)(2,1)}, u32[]{:S(2)}, u32[]{:S(2)}) collective-permute-start(bf16[8,128,384]{2,1,0:T(8,128)(2,1)} %copy-done.29), channel_id=1, source_target_pairs={{0,4},{1,5},{2,6},{3,7},{4,0},{5,1},{6,2},{7,3},{8,12},{9,13},{10,... | collective-permute-start | bytes 2359304 | tf_op jit(solution)/shard_map/ppermute | solution.py:89
  96.8 41.1 %collective-permute-start.19 = (bf16[8,128,512]{2,1,0:T(8,128)(2,1)}, bf16[8,128,512]{2,1,0:T(8,128)(2,1)S(1)}, u32[]{:S(2)}, u32[]{:S(2)}) collective-permute-start(bf16[8,128,512]{2,1,0:T(8,128)(2,1)} %pad_maximum_fusion.1.refs_4_.refs_0_), channel_id=1, source_target_pairs={{0,1},{1,0},{2,3},{3,2},{4,5},{5,4},{6,7},{7,6},{8,9},{9,8},{10,11... | collective-permute-start | bytes 3145736 | tf_op jit(solution)/shard_map/ppermute | solution.py:89
  98.3 4.0 collective-permute-start.15
  98.3 4.3 collective-permute-start.17
  102.0 48.8 %collective-permute-start.22 = (bf16[8,128,512]{2,1,0:T(8,128)(2,1)}, bf16[8,128,512]{2,1,0:T(8,128)(2,1)}, u32[]{:S(2)}, u32[]{:S(2)}) collective-permute-start(bf16[8,128,512]{2,1,0:T(8,128)(2,1)} %pad_maximum_fusion.1.refs_4_.refs_0_), channel_id=1, source_target_pairs={{0,4},{1,5},{2,6},{3,7},{4,0},{5,1},{6,2},{7,3},{8,12},{9,13},{10,... | collective-permute-start | bytes 3145736 | tf_op jit(solution)/shard_map/ppermute | solution.py:89
  102.0 35.8 %collective-permute-start.18 = (bf16[8,128,512]{2,1,0:T(8,128)(2,1)}, bf16[8,128,512]{2,1,0:T(8,128)(2,1)S(1)}, u32[]{:S(2)}, u32[]{:S(2)}) collective-permute-start(bf16[8,128,512]{2,1,0:T(8,128)(2,1)} %pad_maximum_fusion.refs_0_), channel_id=1, source_target_pairs={{0,2},{1,3},{2,0},{3,1},{4,6},{5,7},{6,4},{7,5},{8,10},{9,11},{10,... | collective-permute-start | bytes 3145736 | tf_op jit(solution)/shard_map/ppermute | solution.py:89
  102.3 48.5 %collective-permute-start.20 = (bf16[8,128,512]{2,1,0:T(8,128)(2,1)}, bf16[8,128,512]{2,1,0:T(8,128)(2,1)}, u32[]{:S(2)}, u32[]{:S(2)}) collective-permute-start(bf16[8,128,512]{2,1,0:T(8,128)(2,1)} %pad_maximum_fusion.refs_0_), channel_id=1, source_target_pairs={{0,4},{1,5},{2,6},{3,7},{4,0},{5,1},{6,2},{7,3},{8,12},{9,13},{10,... | collective-permute-start | bytes 3145736 | tf_op jit(solution)/shard_map/ppermute | solution.py:89
  139.8 11.0 %collective-permute-start.21 = (bf16[8,128,512]{2,1,0:T(8,128)(2,1)}, bf16[8,128,512]{2,1,0:T(8,128)(2,1)S(1)}, u32[]{:S(2)}, u32[]{:S(2)}) collective-permute-start(bf16[8,128,512]{2,1,0:T(8,128)(2,1)} %get-tuple-element.158.refs_1_), channel_id=1, source_target_pairs={{0,4},{1,5},{2,6},{3,7},{4,0},{5,1},{6,2},{7,3},{8,12},{9,13},{10,... | collective-permute-start | bytes 3145736 | tf_op jit(solution)/shard_map/ppermute | solution.py:89
  140.1 10.8 %collective-permute-start.23 = (bf16[8,128,512]{2,1,0:T(8,128)(2,1)}, bf16[8,128,512]{2,1,0:T(8,128)(2,1)S(1)}, u32[]{:S(2)}, u32[]{:S(2)}) collective-permute-start(bf16[8,128,512]{2,1,0:T(8,128)(2,1)} %get-tuple-element.159.refs_5_.refs_1_), channel_id=1, source_target_pairs={{0,4},{1,5},{2,6},{3,7},{4,0},{5,1},{6,2},{7,3},{8,12},{9,13},{10,... | collective-permute-start | bytes 3145736 | tf_op jit(solution)/shard_map/ppermute | solution.py:89
  190.1 41.4 %collective-permute-start.25 = (bf16[4,4,128,1024]{3,2,1,0:T(8,128)(2,1)}, bf16[4,4,128,1024]{3,2,1,0:T(8,128)(2,1)}, u32[]{:S(2)}, u32[]{:S(2)}) collective-permute-start(bf16[4,4,128,1024]{3,2,1,0:T(8,128)(2,1)} %get-tuple-element.171), channel_id=1, source_target_pairs={{0,4},{1,5},{2,6},{3,7},{4,0},{5,1},{6,2},{7,3},{8,12},{9,13},{10,... | collective-permute-start | bytes 12582920 | tf_op jit(solution)/shard_map/ppermute | solution.py:89
  190.3 39.6 %copy-start.36 = (f32[2,4,4,640]{3,2,1,0:T(4,128)S(1)}, f32[2,4,4,640]{3,2,1,0:T(4,128)}, u32[]{:S(2)}) copy-start(f32[2,4,4,640]{3,2,1,0:T(4,128)} %get-tuple-element.232) | copy-start | bytes 245764
  190.3 40.5 %copy-start.39 = (f32[1,2048]{1,0:T(1,128)S(1)}, f32[1,2048]{1,0:T(1,128)}, u32[]{:S(2)}) copy-start(f32[1,2048]{1,0:T(1,128)} %get-tuple-element.234) | copy-start | bytes 24580
  229.5 11.2 %collective-permute-start.24 = (bf16[4,4,128,1024]{3,2,1,0:T(8,128)(2,1)}, bf16[4,4,128,1024]{3,2,1,0:T(8,128)(2,1)}, u32[]{:S(2)}, u32[]{:S(2)}) collective-permute-start(bf16[4,4,128,1024]{3,2,1,0:T(8,128)(2,1)} %get-tuple-element.169), channel_id=1, source_target_pairs={{0,4},{1,5},{2,6},{3,7},{4,0},{5,1},{6,2},{7,3},{8,12},{9,13},{10,... | collective-permute-start | bytes 12582920 | tf_op jit(solution)/shard_map/ppermute | solution.py:89
  237.9 30.6 %collective-permute-start.26 = (bf16[4,128,1024]{2,1,0:T(8,128)(2,1)}, bf16[4,128,1024]{2,1,0:T(8,128)(2,1)S(1)}, u32[]{:S(2)}, u32[]{:S(2)}) collective-permute-start(bf16[4,128,1024]{2,1,0:T(8,128)(2,1)} %get-tuple-element.180), channel_id=1, source_target_pairs={{0,2},{1,3},{2,0},{3,1},{4,6},{5,7},{6,4},{7,5},{8,10},{9,11},{10,... | collective-permute-start | bytes 3145736 | tf_op jit(solution)/shard_map/ppermute | solution.py:89
  239.6 54.1 %collective-permute-start.30 = (bf16[4,128,1024]{2,1,0:T(8,128)(2,1)}, bf16[4,128,1024]{2,1,0:T(8,128)(2,1)S(1)}, u32[]{:S(2)}, u32[]{:S(2)}) collective-permute-start(bf16[4,128,1024]{2,1,0:T(8,128)(2,1)} %get-tuple-element.191), channel_id=1, source_target_pairs={{0,2},{1,3},{2,0},{3,1},{4,6},{5,7},{6,4},{7,5},{8,10},{9,11},{10,... | collective-permute-start | bytes 3145736 | tf_op jit(solution)/shard_map/ppermute | solution.py:89
  247.2 26.4 %collective-permute-start.27 = (bf16[4,128,1024]{2,1,0:T(8,128)(2,1)}, bf16[4,128,1024]{2,1,0:T(8,128)(2,1)}, u32[]{:S(2)}, u32[]{:S(2)}) collective-permute-start(bf16[4,128,1024]{2,1,0:T(8,128)(2,1)} %get-tuple-element.181), channel_id=1, source_target_pairs={{0,1},{1,0},{2,3},{3,2},{4,5},{5,4},{6,7},{7,6},{8,9},{9,8},{10,11... | collective-permute-start | bytes 3145736 | tf_op jit(solution)/shard_map/ppermute | solution.py:89
  248.6 51.4 %collective-permute-start.29 = (bf16[4,128,1024]{2,1,0:T(8,128)(2,1)}, bf16[4,128,1024]{2,1,0:T(8,128)(2,1)S(1)}, u32[]{:S(2)}, u32[]{:S(2)}) collective-permute-start(bf16[4,128,1024]{2,1,0:T(8,128)(2,1)} %get-tuple-element.187), channel_id=1, source_target_pairs={{0,1},{1,0},{2,3},{3,2},{4,5},{5,4},{6,7},{7,6},{8,9},{9,8},{10,11... | collective-permute-start | bytes 3145736 | tf_op jit(solution)/shard_map/ppermute | solution.py:89
  298.6 29.0 %collective-permute-start.32 = (bf16[4,128,1024]{2,1,0:T(8,128)(2,1)}, bf16[4,128,1024]{2,1,0:T(8,128)(2,1)}, u32[]{:S(2)}, u32[]{:S(2)}) collective-permute-start(bf16[4,128,1024]{2,1,0:T(8,128)(2,1)} %get-tuple-element.197), channel_id=1, source_target_pairs={{0,1},{1,0},{2,3},{3,2},{4,5},{5,4},{6,7},{7,6},{8,9},{9,8},{10,11... | collective-permute-start | bytes 3145736 | tf_op jit(solution)/shard_map/ppermute | solution.py:89
  304.9 25.7 %collective-permute-start.31 = (bf16[4,128,1024]{2,1,0:T(8,128)(2,1)}, bf16[4,128,1024]{2,1,0:T(8,128)(2,1)S(1)}, u32[]{:S(2)}, u32[]{:S(2)}) collective-permute-start(bf16[4,128,1024]{2,1,0:T(8,128)(2,1)} %get-tuple-element.195), channel_id=1, source_target_pairs={{0,2},{1,3},{2,0},{3,1},{4,6},{5,7},{6,4},{7,5},{8,10},{9,11},{10,... | collective-permute-start | bytes 3145736 | tf_op jit(solution)/shard_map/ppermute | solution.py:89
  305.7 29.0 %collective-permute-start.28 = (bf16[4,128,1024]{2,1,0:T(8,128)(2,1)}, bf16[4,128,1024]{2,1,0:T(8,128)(2,1)S(1)}, u32[]{:S(2)}, u32[]{:S(2)}) collective-permute-start(bf16[4,128,1024]{2,1,0:T(8,128)(2,1)} %bitcast.23), channel_id=1, source_target_pairs={{0,4},{1,5},{2,6},{3,7},{4,0},{5,1},{6,2},{7,3},{8,12},{9,13},{10,... | collective-permute-start | bytes 3145736 | tf_op jit(solution)/shard_map/ppermute | solution.py:89
  305.8 21.8 %copy-start.40 = (f32[2,1,1,768]{3,2,1,0:T(1,128)S(1)}, f32[2,1,1,768]{3,2,1,0:T(1,128)}, u32[]{:S(2)}) copy-start(f32[2,1,1,768]{3,2,1,0:T(1,128)} %get-tuple-element.240) | copy-start | bytes 18436
  326.3 41.4 %collective-permute-start.34 = (bf16[4,128,1024]{2,1,0:T(8,128)(2,1)}, bf16[4,128,1024]{2,1,0:T(8,128)(2,1)S(1)}, u32[]{:S(2)}, u32[]{:S(2)}) collective-permute-start(bf16[4,128,1024]{2,1,0:T(8,128)(2,1)} %bitcast.109), channel_id=1, source_target_pairs={{0,4},{1,5},{2,6},{3,7},{4,0},{5,1},{6,2},{7,3},{8,12},{9,13},{10,... | collective-permute-start | bytes 3145736 | tf_op jit(solution)/shard_map/ppermute | solution.py:89
  339.0 34.0 %collective-permute-start.35 = (bf16[4,128,1024]{2,1,0:T(8,128)(2,1)}, bf16[4,128,1024]{2,1,0:T(8,128)(2,1)S(1)}, u32[]{:S(2)}, u32[]{:S(2)}) collective-permute-start(bf16[4,128,1024]{2,1,0:T(8,128)(2,1)} %get-tuple-element.212), channel_id=1, source_target_pairs={{0,3},{1,2},{2,1},{3,0},{4,7},{5,6},{6,5},{7,4},{8,11},{9,10},{10,... | collective-permute-start | bytes 3145736 | tf_op jit(solution)/shard_map/ppermute | solution.py:89
  340.2 27.5 %collective-permute-start.36 = (bf16[128,1024]{1,0:T(8,128)(2,1)}, bf16[128,1024]{1,0:T(8,128)(2,1)S(1)}, u32[]{:S(2)}, u32[]{:S(2)}) collective-permute-start(bf16[128,1024]{1,0:T(8,128)(2,1)} %get-tuple-element.213), channel_id=1, source_target_pairs={{0,8},{1,9},{2,10},{3,11},{4,12},{5,13},{6,14},{7,15},{8,0},{9,1},... | collective-permute-start | bytes 786440 | tf_op jit(solution)/shard_map/ppermute | solution.py:89
  341.6 27.6 %collective-permute-start.37 = (bf16[128,1024]{1,0:T(8,128)(2,1)}, bf16[128,1024]{1,0:T(8,128)(2,1)}, u32[]{:S(2)}, u32[]{:S(2)}) collective-permute-start(bf16[128,1024]{1,0:T(8,128)(2,1)} %get-tuple-element.214), channel_id=1, source_target_pairs={{0,16},{1,17},{2,18},{3,19},{4,20},{5,21},{6,22},{7,23},{8,24},{9,... | collective-permute-start | bytes 786440 | tf_op jit(solution)/shard_map/ppermute | solution.py:89
  346.4 26.1 %collective-permute-start.38 = (bf16[128,1024]{1,0:T(8,128)(2,1)}, bf16[128,1024]{1,0:T(8,128)(2,1)}, u32[]{:S(2)}, u32[]{:S(2)}) collective-permute-start(bf16[128,1024]{1,0:T(8,128)(2,1)} %get-tuple-element.215), channel_id=1, source_target_pairs={{0,24},{1,25},{2,26},{3,27},{4,28},{5,29},{6,30},{7,31},{8,16},{9,... | collective-permute-start | bytes 786440 | tf_op jit(solution)/shard_map/ppermute | solution.py:89
  367.7 39.0 %collective-permute-start.33 = (bf16[4,128,1024]{2,1,0:T(8,128)(2,1)}, bf16[4,128,1024]{2,1,0:T(8,128)(2,1)S(1)}, u32[]{:S(2)}, u32[]{:S(2)}) collective-permute-start(bf16[4,128,1024]{2,1,0:T(8,128)(2,1)} %bitcast.108), channel_id=1, source_target_pairs={{0,4},{1,5},{2,6},{3,7},{4,0},{5,1},{6,2},{7,3},{8,12},{9,13},{10,... | collective-permute-start | bytes 3145736 | tf_op jit(solution)/shard_map/ppermute | solution.py:89
  368.6 38.1 %collective-permute-start.39 = (bf16[128,1024]{1,0:T(8,128)(2,1)}, bf16[128,1024]{1,0:T(8,128)(2,1)S(1)}, u32[]{:S(2)}, u32[]{:S(2)}) collective-permute-start(bf16[128,1024]{1,0:T(8,128)(2,1)} %get-tuple-element.218), channel_id=1, source_target_pairs={{0,8},{1,9},{2,10},{3,11},{4,12},{5,13},{6,14},{7,15},{8,0},{9,1},... | collective-permute-start | bytes 786440 | tf_op jit(solution)/shard_map/ppermute | solution.py:89
  369.2 37.5 %collective-permute-start.40 = (bf16[128,1024]{1,0:T(8,128)(2,1)}, bf16[128,1024]{1,0:T(8,128)(2,1)}, u32[]{:S(2)}, u32[]{:S(2)}) collective-permute-start(bf16[128,1024]{1,0:T(8,128)(2,1)} %get-tuple-element.219), channel_id=1, source_target_pairs={{0,16},{1,17},{2,18},{3,19},{4,20},{5,21},{6,22},{7,23},{8,24},{9,... | collective-permute-start | bytes 786440 | tf_op jit(solution)/shard_map/ppermute | solution.py:89
  372.5 34.2 %collective-permute-start.41 = (bf16[128,1024]{1,0:T(8,128)(2,1)}, bf16[128,1024]{1,0:T(8,128)(2,1)}, u32[]{:S(2)}, u32[]{:S(2)}) collective-permute-start(bf16[128,1024]{1,0:T(8,128)(2,1)} %get-tuple-element.220), channel_id=1, source_target_pairs={{0,24},{1,25},{2,26},{3,27},{4,28},{5,29},{6,30},{7,31},{8,16},{9,... | collective-permute-start | bytes 786440 | tf_op jit(solution)/shard_map/ppermute | solution.py:89
  377.2 28.2 %copy-start.26 = (bf16[128,1024]{1,0:T(8,128)(2,1)S(1)}, bf16[128,1024]{1,0:T(8,128)(2,1)}, u32[]{:S(2)}) copy-start(bf16[128,1024]{1,0:T(8,128)(2,1)} %get-tuple-element.246) | copy-start | bytes 786436
  377.2 28.2 %copy-start.34 = (bf16[128,1024]{1,0:T(8,128)(2,1)S(1)}, bf16[128,1024]{1,0:T(8,128)(2,1)}, u32[]{:S(2)}) copy-start(bf16[128,1024]{1,0:T(8,128)(2,1)} %get-tuple-element.245) | copy-start | bytes 786436
  414.2 26.8 %collective-permute-start.44 = (bf16[4,128,1024]{2,1,0:T(8,128)(2,1)}, bf16[4,128,1024]{2,1,0:T(8,128)(2,1)S(1)}, u32[]{:S(2)}, u32[]{:S(2)}) collective-permute-start(bf16[4,128,1024]{2,1,0:T(8,128)(2,1)} %get-tuple-element.227), channel_id=1, source_target_pairs={{0,1},{1,0},{2,3},{3,2},{4,5},{5,4},{6,7},{7,6},{8,9},{9,8},{10,11... | collective-permute-start | bytes 3145736 | tf_op jit(solution)/shard_map/ppermute | solution.py:89
  415.4 25.7 %collective-permute-start.42 = (bf16[4,128,1024]{2,1,0:T(8,128)(2,1)}, bf16[4,128,1024]{2,1,0:T(8,128)(2,1)}, u32[]{:S(2)}, u32[]{:S(2)}) collective-permute-start(bf16[4,128,1024]{2,1,0:T(8,128)(2,1)} %bitcast.30), channel_id=1, source_target_pairs={{0,4},{1,5},{2,6},{3,7},{4,0},{5,1},{6,2},{7,3},{8,12},{9,13},{10,... | collective-permute-start | bytes 3145736 | tf_op jit(solution)/shard_map/ppermute | solution.py:89
  415.4 26.7 %collective-permute-start.43 = (bf16[4,128,1024]{2,1,0:T(8,128)(2,1)}, bf16[4,128,1024]{2,1,0:T(8,128)(2,1)}, u32[]{:S(2)}, u32[]{:S(2)}) collective-permute-start(bf16[4,128,1024]{2,1,0:T(8,128)(2,1)} %get-tuple-element.226), channel_id=1, source_target_pairs={{0,2},{1,3},{2,0},{3,1},{4,6},{5,7},{6,4},{7,5},{8,10},{9,11},{10,... | collective-permute-start | bytes 3145736 | tf_op jit(solution)/shard_map/ppermute | solution.py:89
  446.3 20.5 %collective-permute-start.45 = (bf16[128,1024]{1,0:T(8,128)(2,1)}, bf16[128,1024]{1,0:T(8,128)(2,1)S(1)}, u32[]{:S(2)}, u32[]{:S(2)}) collective-permute-start(bf16[128,1024]{1,0:T(8,128)(2,1)} %get-tuple-element.242), channel_id=1, source_target_pairs={{0,8},{1,9},{2,10},{3,11},{4,12},{5,13},{6,14},{7,15},{8,0},{9,1},... | collective-permute-start | bytes 786440 | tf_op jit(solution)/shard_map/ppermute | solution.py:89
  447.0 26.2 %collective-permute-start.46 = (bf16[128,1024]{1,0:T(8,128)(2,1)}, bf16[128,1024]{1,0:T(8,128)(2,1)S(1)}, u32[]{:S(2)}, u32[]{:S(2)}) collective-permute-start(bf16[128,1024]{1,0:T(8,128)(2,1)} %get-tuple-element.243), channel_id=1, source_target_pairs={{0,16},{1,17},{2,18},{3,19},{4,20},{5,21},{6,22},{7,23},{8,24},{9,... | collective-permute-start | bytes 786440 | tf_op jit(solution)/shard_map/ppermute | solution.py:89
  450.7 22.5 %collective-permute-start.47 = (bf16[128,1024]{1,0:T(8,128)(2,1)}, bf16[128,1024]{1,0:T(8,128)(2,1)S(1)}, u32[]{:S(2)}, u32[]{:S(2)}) collective-permute-start(bf16[128,1024]{1,0:T(8,128)(2,1)} %get-tuple-element.244), channel_id=1, source_target_pairs={{0,24},{1,25},{2,26},{3,27},{4,28},{5,29},{6,30},{7,31},{8,16},{9,... | collective-permute-start | bytes 786440 | tf_op jit(solution)/shard_map/ppermute | solution.py:89
  (34 other events, 124.9 us)
Sparse Core Ops, SparseCore 0:
  23.2 62.8 all-gather.8
  93.5 82.3 all-gather.6
  405.6 69.1 all-gather.10

commit v5 on v4

--- a/solution.py
+++ b/solution.py
@@ -19,7 +19,7 @@
 BF = jnp.bfloat16
 F32 = jnp.float32
 AXES = ("dp", "tensor")
-VMEM_LIMIT = 60 * 2**20
+VMEM_LIMIT = 64 * 2**20 - 2**18
 
 
 def dotf(a, b, ca, cb):
@@ -931,7 +931,6 @@
             at = len(total.parts) - 1
             total.parts[at], *grads[0].ends[1:] = spread([total.parts[at], *grads[0].ends[1:]])
     token_rows, sums_one, _ = back(0, (dnormed, inputs, dmiddle, row(first_gain)))
-    grads[1].ends[1:] = spread(grads[1].ends[1:])
 
     tops = jnp.max(tops, axis=-1).reshape(own, HEADS) / LOG2E
     peak = jnp.max(jnp.where(image_live[:, None], tops, NEG), axis=0)
@@ -941,10 +940,17 @@
     heads = heads[jnp.arange(nt) ^ tensor]
     vectors = [sums_two, expand_sum, sums_one, heads[:, 0], heads[:, 2]]
     sums = jnp.concatenate([peak] + [v.reshape(-1, 128) for v in vectors])
+    ((sums,),) = gate(run, [sums])
     sums = lax.all_gather(sums, AXES)
+    grads[1].ends[1:] = spread(grads[1].ends[1:])
     result, _ = feed_out(lay, run, shrinks[0], active0, middle)
     total.along(run)
-    result, _ = feed_out(lay, run, shrinks[1], active1, result, row(shrink_bias))
+    ends = [x for sc in grads for x in sc.ends]
+    result, (token_rows, *ends) = feed_out(
+        lay, run, shrinks[1], active1, result, row(shrink_bias), [token_rows, *ends]
+    )
+    for n, sc in enumerate(grads):
+        sc.ends = ends[n * lay.nz : (n + 1) * lay.nz]
 
     block_out = unpad_rows(result)
     tokens_grad = unpad_rows(token_rows)

time: 498 us -> 488 us (0.980)
  local copies, waits for them, and re-layouts: 35.7 us -> 25.9 us
    unnamed x108 -> x70, local copies, waits for them, and re-layouts: 18.2 us -> 8.92 us
    ppermute x48, waiting for transfers between devices: 56.4 us -> 50.5 us  [swap(): return lax.ppermute(x, AXES, [(i, i ^ mask) for i in range(size)])]
    concatenate x12, other arithmetic: 9.15 us -> 14.4 us  [land(): self.held = jnp.concatenate([self.held, self.got])]
    pallas_call x26 -> x27, Pallas kernels: 302 us -> 303 us  [__call__(): pl.pallas_call(body, grid_spec=pltpu.PrefetchScalarGridSpec(num_scalar_pr...]
  transfers between devices with their start and end apart: 51 -> 51, of which waited for: 11 -> 12; matrix products, arithmetic and copies ran while one was open for 8% -> 9% of each run, Pallas kernels for 62% -> 62%
where the time goes in v5:
time: 488 us; the launch traced here: 482 us
  Pallas kernels  303 us (62%)
  starting transfers between devices  54.9 us (11%)
  waiting for transfers between devices  53.1 us (11%)
  other arithmetic  29.3 us (6%)
  local copies, waits for them, and re-layouts  25.9 us (5%)
  between operations  15.6 us (3%)
    pallas_call x27, Pallas kernels, __call__(): pl.pallas_call(body, grid_spec=pltpu.PrefetchScalarGridSpec(num_scalar_pr...  303 us
    ppermute x48, starting transfers between devices, swap(): return lax.ppermute(x, AXES, [(i, i ^ mask) for i in range(size)])  54.2 us
    ppermute x48, waiting for transfers between devices, swap(): return lax.ppermute(x, AXES, [(i, i ^ mask) for i in range(size)])  50.5 us
    concatenate x12, other arithmetic, land(): self.held = jnp.concatenate([self.held, self.got])  14.4 us
  transfers between devices with their start and end apart: 51, of which 12 were waited for; matrix products, arithmetic and copies ran while one was open for 9% of the time, Pallas kernels for 62%

profile of v5, /device:TPU:0, one launch (start us, length us, event | category | flops | bytes accessed | tf_op | source)
XLA Modules:
  0.0 481.7 jit_solution(6087499945198769609)
XLA Ops:
  9.1 4.0 collective-permute-start
  17.9 3.1 collective-permute-done.refs_1_
  28.1 1.6 collective-permute-start.4
  30.7 1.6 collective-permute-start.2
  33.0 3.0 collective-permute-start.8
  36.0 3.4 collective-permute-start.5
  39.5 2.2 collective-permute-start.3
  41.7 1.5 collective-permute-start.7
  44.7 4.1 collective-permute-done.7.refs_3_
  48.8 1.3 collective-permute-done.9.refs_4_
  50.3 8.1 %collective-permute-done.3.refs_1_ = bf16[4,128,384]{2,1,0:T(8,128)(2,1)} collective-permute-done((bf16[4,128,384]{2,1,0:T(8,128)(2,1)S(1)}, bf16[4,128,384]{2,1,0:T(8,128)(2,1)}, u32[]{:S(2)}, u32[]{:S(2)}) %collective-permute-start.3) | collective-permute-done | bytes 393248 | tf_op jit(solution)/shard_map/ppermute | solution.py:89
  59.2 2.2 pad_maximum_fusion.3.refs_4_
  62.3 1.9 pad_maximum_fusion.5
  64.2 2.6 collective-permute-start.13
  66.8 2.0 pad_maximum_fusion.2.refs_0_
  68.8 2.0 collective-permute-start.10
  70.8 1.8 pad_maximum_fusion.4
  72.6 7.8 %prepare.1 = (bf16[1184,1024]{1,0:T(8,128)(2,1)}, bf16[1184,1024]{1,0:T(8,128)(2,1)}, bf16[1184,1024]{1,0:T(8,128)(2,1)}, f32[8,128]{1,0:T(8,128)}) custom-call(s32[4]{0:T(128)} %pad_add_fusion.me_ref, bf16[1154,1024]{1,0:T(8,128)(2,1)} %refs_0_.1, bf16[1154,1024]{1,0:T(8,128)(2,1)} %refs_1_.1, ...), custom_call_target="tpu_custom_call", output_to_operand_aliasing={{3}: (5, {})} | custom-call | flops 22000001024 | bytes 20000000 | tf_op jit(solution)/shard_map/prepare/pallas_call | solution.py:52
  80.4 5.8 %collective-permute-done.13.refs_4_ = bf16[4,128,512]{2,1,0:T(8,128)(2,1)} collective-permute-done((bf16[4,128,512]{2,1,0:T(8,128)(2,1)}, bf16[4,128,512]{2,1,0:T(8,128)(2,1)}, u32[]{:S(2)}, u32[]{:S(2)}) %collective-permute-start.13) | collective-permute-done | bytes 524320 | tf_op jit(solution)/shard_map/ppermute | solution.py:89
  86.3 7.3 %collective-permute-done.12.refs_3_ = bf16[4,128,512]{2,1,0:T(8,128)(2,1)} collective-permute-done((bf16[4,128,512]{2,1,0:T(8,128)(2,1)}, bf16[4,128,512]{2,1,0:T(8,128)(2,1)}, u32[]{:S(2)}, u32[]{:S(2)}) %collective-permute-start.12) | collective-permute-done | bytes 524320 | tf_op jit(solution)/shard_map/ppermute | solution.py:89
  95.4 2.3 pad_maximum_fusion.1.refs_4_.refs_0_
  97.7 1.6 collective-permute-start.19
  99.9 2.2 pad_maximum_fusion.refs_0_
  104.2 1.6 collective-permute-start.18
  105.9 35.2 %attend.1 = (bf16[1184,3072]{1,0:T(8,128)(2,1)}, bf16[1184,1024]{1,0:T(8,128)(2,1)}, f32[2,4,4,640]{3,2,1,0:T(4,128)}, f32[2,4,4,640]{3,2,1,0:T(4,128)}, f32[8,128]{1,0:T(8,128)}) custom-call(s32[4]{0:T(128)} %pad_add_fusion.me_ref, bf16[8,128,384]{2,1,0:T(8,128)(2,1)} %pad_maximum_fusion.2.refs_0_, ...), custom_call_target="tpu_custom_call", output_to_operand_aliasing={{4}: (11, {})} | custom-call | flops 39600001024 | bytes 36000000 | tf_op jit(solution)/shard_map/attend/pallas_call | solution.py:52
  143.5 9.3 %out_project.1 = (bf16[1184,1024]{1,0:T(8,128)(2,1)}, bf16[1184,1024]{1,0:T(8,128)(2,1)}, f32[8,128]{1,0:T(8,128)}) custom-call(s32[4]{0:T(128)} %pad_add_fusion.me_ref, bf16[32,144,256]{2,1,0:T(8,128)(2,1)} %bitcast.107, bf16[1184,1024]{1,0:T(8,128)(2,1)} %get-tuple-element.161.refs_1_.refs_4_.refs_9_, ...), custom_call_target="tpu_custom_call", output_to_operand_aliasing={{2}: (7, {})} | custom-call | flops 9900000256 | bytes 9000000 | tf_op jit(solution)/shard_map/out_project/pallas_call | solution.py:52
  152.9 37.9 %feed.2 = (bf16[1184,2048]{1,0:T(8,128)(2,1)}, f32[1,2048]{1,0:T(1,128)}, f32[1184,1024]{1,0:T(8,128)}, bf16[4,4,128,1024]{3,2,1,0:T(8,128)(2,1)}, bf16[4,4,128,1024]{3,2,1,0:T(8,128)(2,1)}, /*index=5*/f32[8,128]{1,0:T(8,128)}) custom-call(s32[4]{0:T(128)} %pad_add_fusion.me_ref, ...), custom_call_target="tpu_custom_call", output_to_operand_aliasing={{5}: (12, {})} | custom-call | flops 44000002048 | bytes 40000000 | tf_op jit(solution)/shard_map/feed/pallas_call | solution.py:52
  191.1 39.2 %feed.3 = (bf16[1184,2048]{1,0:T(8,128)(2,1)}, f32[1,2048]{1,0:T(1,128)}, bf16[1184,1024]{1,0:T(8,128)(2,1)}, bf16[4,4,128,1024]{3,2,1,0:T(8,128)(2,1)}, bf16[4,...) custom-call(s32[4]{0:T(128)} %pad_add_fusion.me_ref, ...), custom_call_target="tpu_custom_call", output_to_operand_aliasing={{5}: (7, {})} | custom-call | flops 44000002048 | bytes 40000000 | tf_op jit(solution)/shard_map/feed/pallas_call | solution.py:52
  230.9 6.6 %add.120 = (bf16[4,128,1024]{2,1,0:T(8,128)(2,1)}, bf16[4,128,1024]{2,1,0:T(8,128)(2,1)}, bf16[4,128,1024]{2,1,0:T(8,128)(2,1)}, bf16[4,128,1024]{2,1,0:T(8,128)(2,1)}, f32[8,128]{1,0:T(8,128)}) custom-call(s32[4]{0:T(128)} %pad_add_fusion.me_ref, bf16[4,4,128,1024]{3,2,1,0:T(8,128)(2,1)} %get-tuple-element.181.refs_0_, ...), custom_call_target="tpu_custom_call", output_to_operand_aliasing={{4}: (3, {})} | custom-call | tf_op jit(solution)/shard_map/add/pallas_call | solution.py:52
  238.1 1.5 collective-permute-start.30
  239.6 6.4 %add.121 = (bf16[4,128,1024]{2,1,0:T(8,128)(2,1)}, bf16[4,128,1024]{2,1,0:T(8,128)(2,1)}, bf16[4,128,1024]{2,1,0:T(8,128)(2,1)}, bf16[4,128,1024]{2,1,0:T(8,128)(2,1)}, f32[8,128]{1,0:T(8,128)}) custom-call(s32[4]{0:T(128)} %pad_add_fusion.me_ref, bf16[4,4,128,1024]{3,2,1,0:T(8,128)(2,1)} %get-tuple-element.179.refs_0_, ...), custom_call_target="tpu_custom_call", output_to_operand_aliasing={{4}: (3, {})} | custom-call | tf_op jit(solution)/shard_map/add/pallas_call | solution.py:52
  246.0 1.8 collective-permute-start.27
  248.1 18.6 %feed_back.1 = (bf16[1184,1024]{1,0:T(8,128)(2,1)}, bf16[1184,1024]{1,0:T(8,128)(2,1)}, f32[4,1024]{1,0:T(4,128)}, bf16[4,4,128,256]{3,2,1,0:T(8,128)(2,1)}, bf1...) custom-call(s32[4]{0:T(128)} %pad_add_fusion.me_ref, ...), custom_call_target="tpu_custom_call", output_to_operand_aliasing={{5}: (7, {})} | custom-call | flops 20899999744 | bytes 19000000 | tf_op jit(solution)/shard_map/feed_back/pallas_call | solution.py:52
  267.4 5.0 %collective-permute-done.27.refs_17_ = bf16[4,128,1024]{2,1,0:T(8,128)(2,1)} collective-permute-done((bf16[4,128,1024]{2,1,0:T(8,128)(2,1)}, bf16[4,128,1024]{2,1,0:T(8,128)(2,1)}, u32[]{:S(2)}, u32[]{:S(2)}) %collective-permute-start.27) | collective-permute-done | bytes 1048608 | tf_op jit(solution)/shard_map/ppermute | solution.py:89
  272.4 20.1 %attend_back.4 = (f32[2,1,1,768]{3,2,1,0:T(1,128)}, bf16[1184,1024]{1,0:T(8,128)(2,1)}, bf16[1,4,128,1024]{3,2,1,0:T(8,128)(2,1)}, bf16[1,4,128,1024]{3,2,1,0:T(...) custom-call(s32[4]{0:T(128)} %pad_add_fusion.me_ref, ...), custom_call_target="tpu_custom_call", output_to_operand_aliasing={{4}: (16, {}), {5}: (17, {}), {6}: (18, {})} | custom-call | flops 22000001024 | bytes 20000000 | tf_op jit(solution)/shard_map/attend_back/pallas_call | solution.py:52
  292.5 3.9 add.122
  296.5 1.8 collective-permute-start.32
  298.3 3.9 add.123
  302.5 20.5 %attend_back.5 = (f32[2,1,1,768]{3,2,1,0:T(1,128)}, bf16[1184,1024]{1,0:T(8,128)(2,1)}, bf16[1,4,128,1024]{3,2,1,0:T(8,128)(2,1)}, bf16[1,4,128,1024]{3,2,1,0:T(8,128)(2,1)}, f32[8,128]{1,0:T(8,128)}) custom-call(s32[4]{0:T(128)} %pad_add_fusion.me_ref, bf16[8,128,384]{2,1,0:T(8,128)(2,1)} %pad_maximum_fusion.2.refs_0_, ...), custom_call_target="tpu_custom_call", output_to_operand_aliasing={{4}: (16, {})} | custom-call | flops 22000001024 | bytes 20000000 | tf_op jit(solution)/shard_map/attend_back/pallas_call | solution.py:52
  324.4 3.0 add_plane.3
  327.4 3.1 add_plane.4
  330.6 3.3 add_core.3
  333.9 1.4 collective-permute-start.35
  335.2 1.7 collective-permute-start.36
  337.0 4.1 collective-permute-start.37
  341.1 20.0 %attend_back.6 = (f32[2,1,1,768]{3,2,1,0:T(1,128)}, bf16[1184,1024]{1,0:T(8,128)(2,1)}, bf16[1,4,128,1024]{3,2,1,0:T(8,128)(2,1)}, bf16[1,4,128,1024]{3,2,1,0:T(8,128)(2,1)}, f32[8,128]{1,0:T(8,128)}) custom-call(s32[4]{0:T(128)} %pad_add_fusion.me_ref, bf16[8,128,384]{2,1,0:T(8,128)(2,1)} %pad_maximum_fusion.2.refs_0_, ...), custom_call_target="tpu_custom_call", output_to_operand_aliasing={{4}: (16, {})} | custom-call | flops 22000001024 | bytes 20000000 | tf_op jit(solution)/shard_map/attend_back/pallas_call | solution.py:52
  362.6 3.8 collective-permute-start.40
  366.4 3.3 add_core.4
  369.7 25.3 %attend_back.7 = (f32[2,1,1,768]{3,2,1,0:T(1,128)}, bf16[1184,1024]{1,0:T(8,128)(2,1)}, f32[2,1024]{1,0:T(2,128)}, bf16[1,4,128,1024]{3,2,1,0:T(8,128)(2,1)}, bf...) custom-call(s32[4]{0:T(128)} %pad_add_fusion.me_ref, ...), custom_call_target="tpu_custom_call", output_to_operand_aliasing={{5}: (22, {})} | custom-call | flops 22000001024 | bytes 20000000 | tf_op jit(solution)/shard_map/attend_back/pallas_call | solution.py:52
  398.4 3.3 add_core.5
  401.7 2.0 collective-permute-start.44
  403.8 12.0 %feed_out.2 = (f32[1184,1024]{1,0:T(8,128)}, f32[8,128]{1,0:T(8,128)}) custom-call(s32[4]{0:T(128)} %pad_add_fusion.me_ref, bf16[8,128,512]{2,1,0:T(8,128)(2,1)} %pad_maximum_fusion.1.refs_4_.refs_0_, bf16[8,128,512]{2,1,0:T(8,128)(2,1)} %get-tuple-element.170.refs_5_.refs_1_, ...), custom_call_target="tpu_custom_call", output_to_operand_aliasing={{1}: (7, {})} | custom-call | flops 13200000000 | bytes 12000000 | tf_op jit(solution)/shard_map/feed_out/pallas_call | solution.py:52
  415.8 11.8 %collective-permute-done.44.refs_4_ = bf16[4,128,1024]{2,1,0:T(8,128)(2,1)} collective-permute-done((bf16[4,128,1024]{2,1,0:T(8,128)(2,1)}, bf16[4,128,1024]{2,1,0:T(8,128)(2,1)}, u32[]{:S(2)}, u32[]{:S(2)}) %collective-permute-start.44) | collective-permute-done | bytes 1048608 | tf_op jit(solution)/shard_map/ppermute | solution.py:89
  427.6 2.4 collective-permute-done.43.refs_3_
  430.0 4.5 add_plane.5
  435.2 3.8 collective-permute-start.46
  438.9 12.3 %feed_out.3 = (bf16[1184,1024]{1,0:T(8,128)(2,1)}, f32[8,128]{1,0:T(8,128)}, bf16[1184,1024]{1,0:T(8,128)(2,1)}, bf16[128,1024]{1,0:T(8,128)(2,1)}, bf16[128,102...) custom-call(s32[4]{0:T(128)} %pad_add_fusion.me_ref, ...), custom_call_target="tpu_custom_call", output_to_operand_aliasing={{1}: (5, {}), {2}: (6, {}), {3}: (7, {}), {4}: (8, {}), {5}... | custom-call | flops 13200000000 | bytes 12000000 | tf_op jit(solution)/shard_map/feed_out/pallas_call | solution.py:52
  451.2 1.8 convert_add_fusion
  454.2 1.9 slice.166
  456.1 1.9 reshape.177
  458.0 1.9 slice.167
  459.9 1.9 reshape.179
  465.8 2.6 all-gather.11.cloned.1.call-done
  468.3 1.6 reduce_sum.49
  (235 shorter events, 44.9 us)
Async XLA Ops:
  7.2 94.8 %all-gather.9.cloned.1.call-start = ((), (), s32[]{:S(2)}) async-start(), calls=%async_computation.1 | async-start | bytes 2433024 | tf_op jit(solution)/shard_map/all_gather | solution.py:131
  9.1 11.9 %collective-permute-start = (bf16[1,128,384]{2,1,0:T(8,128)(2,1)S(1)}, bf16[1,128,384]{2,1,0:T(8,128)(2,1)S(1)}, u32[]{:S(2)}, u32[]{:S(2)}) collective-permute-start(bf16[1,128,384]{2,1,0:T(8,128)(2,1)S(1)} %bitcast.82), channel_id=1, source_target_pairs={{0,16},{1,17},{2,18},{3,19},{4,20},{5,21},{6,22},{7,23},{8,24},{9,... | collective-permute-start | bytes 294920 | tf_op jit(solution)/shard_map/ppermute | solution.py:89
  13.3 7.7 %copy-start.4 = (bf16[128,384]{1,0:T(8,128)(2,1)}, bf16[128,384]{1,0:T(8,128)(2,1)S(1)}, u32[]{:S(2)}) copy-start(bf16[128,384]{1,0:T(8,128)(2,1)S(1)} %copy.139) | copy-start | bytes 294916
  13.3 9.0 %collective-permute-start.1 = (bf16[1,128,384]{2,1,0:T(8,128)(2,1)S(1)}, bf16[1,128,384]{2,1,0:T(8,128)(2,1)S(1)}, u32[]{:S(2)}, u32[]{:S(2)}) collective-permute-start(bf16[1,128,384]{2,1,0:T(8,128)(2,1)S(1)} %bitcast.86), channel_id=1, source_target_pairs={{0,16},{1,17},{2,18},{3,19},{4,20},{5,21},{6,22},{7,23},{8,24},{9,... | collective-permute-start | bytes 294920 | tf_op jit(solution)/shard_map/ppermute | solution.py:89
  23.6 12.4 %copy-start.5 = (bf16[128,384]{1,0:T(8,128)(2,1)S(1)}, bf16[128,384]{1,0:T(8,128)(2,1)}, u32[]{:S(2)}) copy-start(bf16[128,384]{1,0:T(8,128)(2,1)} %copy-done.4) | copy-start | bytes 294916
  23.6 12.4 %copy-start.10 = (bf16[1,128,384]{2,1,0:T(8,128)(2,1)S(1)}, bf16[1,128,384]{2,1,0:T(8,128)(2,1)}, u32[]{:S(2)}) copy-start(bf16[1,128,384]{2,1,0:T(8,128)(2,1)} %get-tuple-element.148) | copy-start | bytes 294916
  23.6 15.9 %copy-start.2 = (bf16[128,384]{1,0:T(8,128)(2,1)S(1)}, bf16[128,384]{1,0:T(8,128)(2,1)}, u32[]{:S(2)}) copy-start(bf16[128,384]{1,0:T(8,128)(2,1)} %copy-done.1) | copy-start | bytes 294916
  23.6 15.9 %copy-start.7 = (bf16[1,128,384]{2,1,0:T(8,128)(2,1)S(1)}, bf16[1,128,384]{2,1,0:T(8,128)(2,1)}, u32[]{:S(2)}) copy-start(bf16[1,128,384]{2,1,0:T(8,128)(2,1)} %get-tuple-element.147) | copy-start | bytes 294916
  23.6 167.5 %all-gather.7.cloned.1.call-start = ((), (), s32[]{:S(2)}) async-start(), calls=%async_computation | async-start | bytes 8650752 | tf_op jit(solution)/shard_map/all_gather | solution.py:131
  24.7 17.0 %collective-permute-start.6 = (bf16[1,128,512]{2,1,0:T(8,128)(2,1)S(1)}, bf16[1,128,512]{2,1,0:T(8,128)(2,1)S(1)}, u32[]{:S(2)}, u32[]{:S(2)}) collective-permute-start(bf16[1,128,512]{2,1,0:T(8,128)(2,1)S(1)} %get-tuple-element.331), channel_id=1, source_target_pairs={{0,16},{1,17},{2,18},{3,19},{4,20},{5,21},{6,22},{7,23},{8,24},{9,... | collective-permute-start | bytes 393224 | tf_op jit(solution)/shard_map/ppermute | solution.py:89
  28.1 7.9 %collective-permute-start.4 = (bf16[2,128,384]{2,1,0:T(8,128)(2,1)S(1)}, bf16[2,128,384]{2,1,0:T(8,128)(2,1)S(1)}, u32[]{:S(2)}, u32[]{:S(2)}) collective-permute-start(bf16[2,128,384]{2,1,0:T(8,128)(2,1)S(1)} %pad_maximum_fusion.13), channel_id=1, source_target_pairs={{0,2},{1,3},{2,0},{3,1},{4,6},{5,7},{6,4},{7,5},{8,10},{9,11},{10,... | collective-permute-start | bytes 589832 | tf_op jit(solution)/shard_map/ppermute | solution.py:89
  30.7 8.7 %collective-permute-start.2 = (bf16[2,128,384]{2,1,0:T(8,128)(2,1)S(1)}, bf16[2,128,384]{2,1,0:T(8,128)(2,1)S(1)}, u32[]{:S(2)}, u32[]{:S(2)}) collective-permute-start(bf16[2,128,384]{2,1,0:T(8,128)(2,1)S(1)} %pad_maximum_fusion.12), channel_id=1, source_target_pairs={{0,1},{1,0},{2,3},{3,2},{4,5},{5,4},{6,7},{7,6},{8,9},{9,8},{10,11... | collective-permute-start | bytes 589832 | tf_op jit(solution)/shard_map/ppermute | solution.py:89
  32.9 10.3 %copy-start = (bf16[1,128,512]{2,1,0:T(8,128)(2,1)}, bf16[1,128,512]{2,1,0:T(8,128)(2,1)S(1)}, u32[]{:S(2)}) copy-start(bf16[1,128,512]{2,1,0:T(8,128)(2,1)S(1)} %get-tuple-element.333) | copy-start | bytes 393220
  33.0 10.3 %collective-permute-start.8 = (bf16[1,128,512]{2,1,0:T(8,128)(2,1)S(1)}, bf16[1,128,512]{2,1,0:T(8,128)(2,1)S(1)}, u32[]{:S(2)}, u32[]{:S(2)}) collective-permute-start(bf16[1,128,512]{2,1,0:T(8,128)(2,1)S(1)} %get-tuple-element.333), channel_id=1, source_target_pairs={{0,16},{1,17},{2,18},{3,19},{4,20},{5,21},{6,22},{7,23},{8,24},{9,... | collective-permute-start | bytes 393224 | tf_op jit(solution)/shard_map/ppermute | solution.py:89
  35.9 8.0 %copy-start.17 = (bf16[2,128,384]{2,1,0:T(8,128)(2,1)}, bf16[2,128,384]{2,1,0:T(8,128)(2,1)S(1)}, u32[]{:S(2)}) copy-start(bf16[2,128,384]{2,1,0:T(8,128)(2,1)S(1)} %collective-permute-done.4) | copy-start | bytes 589828
  36.0 14.3 %collective-permute-start.5 = (bf16[4,128,384]{2,1,0:T(8,128)(2,1)S(1)}, bf16[4,128,384]{2,1,0:T(8,128)(2,1)}, u32[]{:S(2)}, u32[]{:S(2)}) collective-permute-start(bf16[4,128,384]{2,1,0:T(8,128)(2,1)S(1)} %pad_maximum_fusion.8), channel_id=1, source_target_pairs={{0,8},{1,9},{2,10},{3,11},{4,12},{5,13},{6,14},{7,15},{8,0},{9,1},... | collective-permute-start | bytes 1179656 | tf_op jit(solution)/shard_map/ppermute | solution.py:89
  39.5 18.9 %collective-permute-start.3 = (bf16[4,128,384]{2,1,0:T(8,128)(2,1)S(1)}, bf16[4,128,384]{2,1,0:T(8,128)(2,1)}, u32[]{:S(2)}, u32[]{:S(2)}) collective-permute-start(bf16[4,128,384]{2,1,0:T(8,128)(2,1)S(1)} %pad_maximum_fusion.7), channel_id=1, source_target_pairs={{0,8},{1,9},{2,10},{3,11},{4,12},{5,13},{6,14},{7,15},{8,0},{9,1},... | collective-permute-start | bytes 1179656 | tf_op jit(solution)/shard_map/ppermute | solution.py:89
  41.7 7.0 %collective-permute-start.7 = (bf16[2,128,512]{2,1,0:T(8,128)(2,1)S(1)}, bf16[2,128,512]{2,1,0:T(8,128)(2,1)}, u32[]{:S(2)}, u32[]{:S(2)}) collective-permute-start(bf16[2,128,512]{2,1,0:T(8,128)(2,1)S(1)} %pad_maximum_fusion.9), channel_id=1, source_target_pairs={{0,1},{1,0},{2,3},{3,2},{4,5},{5,4},{6,7},{7,6},{8,9},{9,8},{10,11... | collective-permute-start | bytes 786440 | tf_op jit(solution)/shard_map/ppermute | solution.py:89
  43.3 6.8 %collective-permute-start.9 = (bf16[2,128,512]{2,1,0:T(8,128)(2,1)S(1)}, bf16[2,128,512]{2,1,0:T(8,128)(2,1)}, u32[]{:S(2)}, u32[]{:S(2)}) collective-permute-start(bf16[2,128,512]{2,1,0:T(8,128)(2,1)S(1)} %pad_maximum_fusion.10), channel_id=1, source_target_pairs={{0,2},{1,3},{2,0},{3,1},{4,6},{5,7},{6,4},{7,5},{8,10},{9,11},{10,... | collective-permute-start | bytes 786440 | tf_op jit(solution)/shard_map/ppermute | solution.py:89
  59.1 11.6 %copy-start.12 = (bf16[1,128,512]{2,1,0:T(8,128)(2,1)S(1)}, bf16[1,128,512]{2,1,0:T(8,128)(2,1)}, u32[]{:S(2)}) copy-start(bf16[1,128,512]{2,1,0:T(8,128)(2,1)} %copy-done.11) | copy-start | bytes 393220
  61.3 32.2 %collective-permute-start.11 = (bf16[8,128,384]{2,1,0:T(8,128)(2,1)}, bf16[8,128,384]{2,1,0:T(8,128)(2,1)}, u32[]{:S(2)}, u32[]{:S(2)}) collective-permute-start(bf16[8,128,384]{2,1,0:T(8,128)(2,1)} %pad_maximum_fusion.3.refs_4_), channel_id=1, source_target_pairs={{0,1},{1,0},{2,3},{3,2},{4,5},{5,4},{6,7},{7,6},{8,9},{9,8},{10,11... | collective-permute-start | bytes 2359304 | tf_op jit(solution)/shard_map/ppermute | solution.py:89
  64.2 22.1 %collective-permute-start.13 = (bf16[4,128,512]{2,1,0:T(8,128)(2,1)}, bf16[4,128,512]{2,1,0:T(8,128)(2,1)}, u32[]{:S(2)}, u32[]{:S(2)}) collective-permute-start(bf16[4,128,512]{2,1,0:T(8,128)(2,1)} %pad_maximum_fusion.5), channel_id=1, source_target_pairs={{0,8},{1,9},{2,10},{3,11},{4,12},{5,13},{6,14},{7,15},{8,0},{9,1},... | collective-permute-start | bytes 1572872 | tf_op jit(solution)/shard_map/ppermute | solution.py:89
  68.8 24.8 %collective-permute-start.10 = (bf16[8,128,384]{2,1,0:T(8,128)(2,1)}, bf16[8,128,384]{2,1,0:T(8,128)(2,1)}, u32[]{:S(2)}, u32[]{:S(2)}) collective-permute-start(bf16[8,128,384]{2,1,0:T(8,128)(2,1)} %pad_maximum_fusion.2.refs_0_), channel_id=1, source_target_pairs={{0,2},{1,3},{2,0},{3,1},{4,6},{5,7},{6,4},{7,5},{8,10},{9,11},{10,... | collective-permute-start | bytes 2359304 | tf_op jit(solution)/shard_map/ppermute | solution.py:89
  72.6 21.0 %collective-permute-start.12 = (bf16[4,128,512]{2,1,0:T(8,128)(2,1)}, bf16[4,128,512]{2,1,0:T(8,128)(2,1)}, u32[]{:S(2)}, u32[]{:S(2)}) collective-permute-start(bf16[4,128,512]{2,1,0:T(8,128)(2,1)} %pad_maximum_fusion.4), channel_id=1, source_target_pairs={{0,8},{1,9},{2,10},{3,11},{4,12},{5,13},{6,14},{7,15},{8,0},{9,1},... | collective-permute-start | bytes 1572872 | tf_op jit(solution)/shard_map/ppermute | solution.py:89
  94.3 374.1 %all-gather.11.cloned.1.call-start = ((), (), s32[]{:S(2)}) async-start(), calls=%async_computation.2 | async-start | bytes 1892352 | tf_op jit(solution)/shard_map/all_gather | solution.py:944
  94.9 9.2 %collective-permute-start.16 = (bf16[8,128,384]{2,1,0:T(8,128)(2,1)}, bf16[8,128,384]{2,1,0:T(8,128)(2,1)}, u32[]{:S(2)}, u32[]{:S(2)}) collective-permute-start(bf16[8,128,384]{2,1,0:T(8,128)(2,1)} %pad_maximum_fusion.3.refs_4_), channel_id=1, source_target_pairs={{0,4},{1,5},{2,6},{3,7},{4,0},{5,1},{6,2},{7,3},{8,12},{9,13},{10,... | collective-permute-start | bytes 2359304 | tf_op jit(solution)/shard_map/ppermute | solution.py:89
  94.9 9.2 %collective-permute-start.14 = (bf16[8,128,384]{2,1,0:T(8,128)(2,1)}, bf16[8,128,384]{2,1,0:T(8,128)(2,1)}, u32[]{:S(2)}, u32[]{:S(2)}) collective-permute-start(bf16[8,128,384]{2,1,0:T(8,128)(2,1)} %pad_maximum_fusion.2.refs_0_), channel_id=1, source_target_pairs={{0,4},{1,5},{2,6},{3,7},{4,0},{5,1},{6,2},{7,3},{8,12},{9,13},{10,... | collective-permute-start | bytes 2359304 | tf_op jit(solution)/shard_map/ppermute | solution.py:89
  97.7 43.4 %collective-permute-start.19 = (bf16[8,128,512]{2,1,0:T(8,128)(2,1)}, bf16[8,128,512]{2,1,0:T(8,128)(2,1)}, u32[]{:S(2)}, u32[]{:S(2)}) collective-permute-start(bf16[8,128,512]{2,1,0:T(8,128)(2,1)} %pad_maximum_fusion.1.refs_4_.refs_0_), channel_id=1, source_target_pairs={{0,1},{1,0},{2,3},{3,2},{4,5},{5,4},{6,7},{7,6},{8,9},{9,8},{10,11... | collective-permute-start | bytes 3145736 | tf_op jit(solution)/shard_map/ppermute | solution.py:89
  99.3 6.4 %collective-permute-start.15 = (bf16[8,128,384]{2,1,0:T(8,128)(2,1)}, bf16[8,128,384]{2,1,0:T(8,128)(2,1)}, u32[]{:S(2)}, u32[]{:S(2)}) collective-permute-start(bf16[8,128,384]{2,1,0:T(8,128)(2,1)} %get-tuple-element.157.refs_1_), channel_id=1, source_target_pairs={{0,4},{1,5},{2,6},{3,7},{4,0},{5,1},{6,2},{7,3},{8,12},{9,13},{10,... | collective-permute-start | bytes 2359304 | tf_op jit(solution)/shard_map/ppermute | solution.py:89
  99.3 6.5 %collective-permute-start.17 = (bf16[8,128,384]{2,1,0:T(8,128)(2,1)}, bf16[8,128,384]{2,1,0:T(8,128)(2,1)}, u32[]{:S(2)}, u32[]{:S(2)}) collective-permute-start(bf16[8,128,384]{2,1,0:T(8,128)(2,1)} %get-tuple-element.158.refs_5_), channel_id=1, source_target_pairs={{0,4},{1,5},{2,6},{3,7},{4,0},{5,1},{6,2},{7,3},{8,12},{9,13},{10,... | collective-permute-start | bytes 2359304 | tf_op jit(solution)/shard_map/ppermute | solution.py:89
  104.1 48.7 %collective-permute-start.22 = (bf16[8,128,512]{2,1,0:T(8,128)(2,1)}, bf16[8,128,512]{2,1,0:T(8,128)(2,1)}, u32[]{:S(2)}, u32[]{:S(2)}) collective-permute-start(bf16[8,128,512]{2,1,0:T(8,128)(2,1)} %pad_maximum_fusion.1.refs_4_.refs_0_), channel_id=1, source_target_pairs={{0,4},{1,5},{2,6},{3,7},{4,0},{5,1},{6,2},{7,3},{8,12},{9,13},{10,... | collective-permute-start | bytes 3145736 | tf_op jit(solution)/shard_map/ppermute | solution.py:89
  104.2 37.0 %collective-permute-start.18 = (bf16[8,128,512]{2,1,0:T(8,128)(2,1)}, bf16[8,128,512]{2,1,0:T(8,128)(2,1)}, u32[]{:S(2)}, u32[]{:S(2)}) collective-permute-start(bf16[8,128,512]{2,1,0:T(8,128)(2,1)} %pad_maximum_fusion.refs_0_), channel_id=1, source_target_pairs={{0,2},{1,3},{2,0},{3,1},{4,6},{5,7},{6,4},{7,5},{8,10},{9,11},{10,... | collective-permute-start | bytes 3145736 | tf_op jit(solution)/shard_map/ppermute | solution.py:89
  105.7 47.1 %collective-permute-start.20 = (bf16[8,128,512]{2,1,0:T(8,128)(2,1)}, bf16[8,128,512]{2,1,0:T(8,128)(2,1)}, u32[]{:S(2)}, u32[]{:S(2)}) collective-permute-start(bf16[8,128,512]{2,1,0:T(8,128)(2,1)} %pad_maximum_fusion.refs_0_), channel_id=1, source_target_pairs={{0,4},{1,5},{2,6},{3,7},{4,0},{5,1},{6,2},{7,3},{8,12},{9,13},{10,... | collective-permute-start | bytes 3145736 | tf_op jit(solution)/shard_map/ppermute | solution.py:89
  141.8 11.0 %collective-permute-start.21 = (bf16[8,128,512]{2,1,0:T(8,128)(2,1)}, bf16[8,128,512]{2,1,0:T(8,128)(2,1)}, u32[]{:S(2)}, u32[]{:S(2)}) collective-permute-start(bf16[8,128,512]{2,1,0:T(8,128)(2,1)} %get-tuple-element.169.refs_1_), channel_id=1, source_target_pairs={{0,4},{1,5},{2,6},{3,7},{4,0},{5,1},{6,2},{7,3},{8,12},{9,13},{10,... | collective-permute-start | bytes 3145736 | tf_op jit(solution)/shard_map/ppermute | solution.py:89
  142.2 10.6 %collective-permute-start.23 = (bf16[8,128,512]{2,1,0:T(8,128)(2,1)}, bf16[8,128,512]{2,1,0:T(8,128)(2,1)}, u32[]{:S(2)}, u32[]{:S(2)}) collective-permute-start(bf16[8,128,512]{2,1,0:T(8,128)(2,1)} %get-tuple-element.170.refs_5_.refs_1_), channel_id=1, source_target_pairs={{0,4},{1,5},{2,6},{3,7},{4,0},{5,1},{6,2},{7,3},{8,12},{9,13},{10,... | collective-permute-start | bytes 3145736 | tf_op jit(solution)/shard_map/ppermute | solution.py:89
  190.7 40.2 %collective-permute-start.25 = (bf16[4,4,128,1024]{3,2,1,0:T(8,128)(2,1)}, bf16[4,4,128,1024]{3,2,1,0:T(8,128)(2,1)}, u32[]{:S(2)}, u32[]{:S(2)}) collective-permute-start(bf16[4,4,128,1024]{3,2,1,0:T(8,128)(2,1)} %get-tuple-element.182), channel_id=1, source_target_pairs={{0,4},{1,5},{2,6},{3,7},{4,0},{5,1},{6,2},{7,3},{8,12},{9,13},{10,... | collective-permute-start | bytes 12582920 | tf_op jit(solution)/shard_map/ppermute | solution.py:89
  191.1 39.4 %copy-start.20 = (f32[2,4,4,640]{3,2,1,0:T(4,128)S(1)}, f32[2,4,4,640]{3,2,1,0:T(4,128)}, u32[]{:S(2)}) copy-start(f32[2,4,4,640]{3,2,1,0:T(4,128)} %get-tuple-element.229) | copy-start | bytes 245764
  230.3 9.2 %collective-permute-start.24 = (bf16[4,4,128,1024]{3,2,1,0:T(8,128)(2,1)}, bf16[4,4,128,1024]{3,2,1,0:T(8,128)(2,1)}, u32[]{:S(2)}, u32[]{:S(2)}) collective-permute-start(bf16[4,4,128,1024]{3,2,1,0:T(8,128)(2,1)} %get-tuple-element.180), channel_id=1, source_target_pairs={{0,4},{1,5},{2,6},{3,7},{4,0},{5,1},{6,2},{7,3},{8,12},{9,13},{10,... | collective-permute-start | bytes 12582920 | tf_op jit(solution)/shard_map/ppermute | solution.py:89
  230.9 8.6 %copy-start.21 = (f32[1,2048]{1,0:T(1,128)S(1)}, f32[1,2048]{1,0:T(1,128)}, u32[]{:S(2)}) copy-start(f32[1,2048]{1,0:T(1,128)} %get-tuple-element.231) | copy-start | bytes 24580
  230.9 8.6 %copy-start.22 = (f32[1,2048]{1,0:T(1,128)S(1)}, f32[1,2048]{1,0:T(1,128)}, u32[]{:S(2)}) copy-start(f32[1,2048]{1,0:T(1,128)} %get-tuple-element.232) | copy-start | bytes 24580
  237.5 29.9 %collective-permute-start.26 = (bf16[4,128,1024]{2,1,0:T(8,128)(2,1)}, bf16[4,128,1024]{2,1,0:T(8,128)(2,1)}, u32[]{:S(2)}, u32[]{:S(2)}) collective-permute-start(bf16[4,128,1024]{2,1,0:T(8,128)(2,1)} %get-tuple-element.191), channel_id=1, source_target_pairs={{0,2},{1,3},{2,0},{3,1},{4,6},{5,7},{6,4},{7,5},{8,10},{9,11},{10,... | collective-permute-start | bytes 3145736 | tf_op jit(solution)/shard_map/ppermute | solution.py:89
  238.1 54.5 %collective-permute-start.30 = (bf16[4,128,1024]{2,1,0:T(8,128)(2,1)}, bf16[4,128,1024]{2,1,0:T(8,128)(2,1)}, u32[]{:S(2)}, u32[]{:S(2)}) collective-permute-start(bf16[4,128,1024]{2,1,0:T(8,128)(2,1)} %get-tuple-element.202), channel_id=1, source_target_pairs={{0,2},{1,3},{2,0},{3,1},{4,6},{5,7},{6,4},{7,5},{8,10},{9,11},{10,... | collective-permute-start | bytes 3145736 | tf_op jit(solution)/shard_map/ppermute | solution.py:89
  246.0 26.4 %collective-permute-start.27 = (bf16[4,128,1024]{2,1,0:T(8,128)(2,1)}, bf16[4,128,1024]{2,1,0:T(8,128)(2,1)}, u32[]{:S(2)}, u32[]{:S(2)}) collective-permute-start(bf16[4,128,1024]{2,1,0:T(8,128)(2,1)} %get-tuple-element.192), channel_id=1, source_target_pairs={{0,1},{1,0},{2,3},{3,2},{4,5},{5,4},{6,7},{7,6},{8,9},{9,8},{10,11... | collective-permute-start | bytes 3145736 | tf_op jit(solution)/shard_map/ppermute | solution.py:89
  247.8 50.4 %collective-permute-start.29 = (bf16[4,128,1024]{2,1,0:T(8,128)(2,1)}, bf16[4,128,1024]{2,1,0:T(8,128)(2,1)}, u32[]{:S(2)}, u32[]{:S(2)}) collective-permute-start(bf16[4,128,1024]{2,1,0:T(8,128)(2,1)} %get-tuple-element.198), channel_id=1, source_target_pairs={{0,1},{1,0},{2,3},{3,2},{4,5},{5,4},{6,7},{7,6},{8,9},{9,8},{10,11... | collective-permute-start | bytes 3145736 | tf_op jit(solution)/shard_map/ppermute | solution.py:89
  296.5 27.9 %collective-permute-start.32 = (bf16[4,128,1024]{2,1,0:T(8,128)(2,1)}, bf16[4,128,1024]{2,1,0:T(8,128)(2,1)}, u32[]{:S(2)}, u32[]{:S(2)}) collective-permute-start(bf16[4,128,1024]{2,1,0:T(8,128)(2,1)} %get-tuple-element.208), channel_id=1, source_target_pairs={{0,1},{1,0},{2,3},{3,2},{4,5},{5,4},{6,7},{7,6},{8,9},{9,8},{10,11... | collective-permute-start | bytes 3145736 | tf_op jit(solution)/shard_map/ppermute | solution.py:89
  302.2 25.3 %collective-permute-start.31 = (bf16[4,128,1024]{2,1,0:T(8,128)(2,1)}, bf16[4,128,1024]{2,1,0:T(8,128)(2,1)}, u32[]{:S(2)}, u32[]{:S(2)}) collective-permute-start(bf16[4,128,1024]{2,1,0:T(8,128)(2,1)} %get-tuple-element.206), channel_id=1, source_target_pairs={{0,2},{1,3},{2,0},{3,1},{4,6},{5,7},{6,4},{7,5},{8,10},{9,11},{10,... | collective-permute-start | bytes 3145736 | tf_op jit(solution)/shard_map/ppermute | solution.py:89
  302.5 28.1 %collective-permute-start.28 = (bf16[4,128,1024]{2,1,0:T(8,128)(2,1)}, bf16[4,128,1024]{2,1,0:T(8,128)(2,1)}, u32[]{:S(2)}, u32[]{:S(2)}) collective-permute-start(bf16[4,128,1024]{2,1,0:T(8,128)(2,1)} %bitcast.114), channel_id=1, source_target_pairs={{0,4},{1,5},{2,6},{3,7},{4,0},{5,1},{6,2},{7,3},{8,12},{9,13},{10,... | collective-permute-start | bytes 3145736 | tf_op jit(solution)/shard_map/ppermute | solution.py:89
  302.5 21.8 %copy-start.23 = (f32[2,1,1,768]{3,2,1,0:T(1,128)S(1)}, f32[2,1,1,768]{3,2,1,0:T(1,128)}, u32[]{:S(2)}) copy-start(f32[2,1,1,768]{3,2,1,0:T(1,128)} %get-tuple-element.237) | copy-start | bytes 18436
  323.0 38.8 %collective-permute-start.34 = (bf16[4,128,1024]{2,1,0:T(8,128)(2,1)}, bf16[4,128,1024]{2,1,0:T(8,128)(2,1)}, u32[]{:S(2)}, u32[]{:S(2)}) collective-permute-start(bf16[4,128,1024]{2,1,0:T(8,128)(2,1)} %bitcast.115), channel_id=1, source_target_pairs={{0,4},{1,5},{2,6},{3,7},{4,0},{5,1},{6,2},{7,3},{8,12},{9,13},{10,... | collective-permute-start | bytes 3145736 | tf_op jit(solution)/shard_map/ppermute | solution.py:89
  333.9 32.5 %collective-permute-start.35 = (bf16[4,128,1024]{2,1,0:T(8,128)(2,1)}, bf16[4,128,1024]{2,1,0:T(8,128)(2,1)}, u32[]{:S(2)}, u32[]{:S(2)}) collective-permute-start(bf16[4,128,1024]{2,1,0:T(8,128)(2,1)} %get-tuple-element.223), channel_id=1, source_target_pairs={{0,3},{1,2},{2,1},{3,0},{4,7},{5,6},{6,5},{7,4},{8,11},{9,10},{10,... | collective-permute-start | bytes 3145736 | tf_op jit(solution)/shard_map/ppermute | solution.py:89
  335.2 26.7 %collective-permute-start.36 = (bf16[128,1024]{1,0:T(8,128)(2,1)}, bf16[128,1024]{1,0:T(8,128)(2,1)}, u32[]{:S(2)}, u32[]{:S(2)}) collective-permute-start(bf16[128,1024]{1,0:T(8,128)(2,1)} %get-tuple-element.224), channel_id=1, source_target_pairs={{0,8},{1,9},{2,10},{3,11},{4,12},{5,13},{6,14},{7,15},{8,0},{9,1},... | collective-permute-start | bytes 786440 | tf_op jit(solution)/shard_map/ppermute | solution.py:89
  337.0 25.6 %collective-permute-start.37 = (bf16[128,1024]{1,0:T(8,128)(2,1)}, bf16[128,1024]{1,0:T(8,128)(2,1)}, u32[]{:S(2)}, u32[]{:S(2)}) collective-permute-start(bf16[128,1024]{1,0:T(8,128)(2,1)} %get-tuple-element.225), channel_id=1, source_target_pairs={{0,16},{1,17},{2,18},{3,19},{4,20},{5,21},{6,22},{7,23},{8,24},{9,... | collective-permute-start | bytes 786440 | tf_op jit(solution)/shard_map/ppermute | solution.py:89
  341.1 25.3 %collective-permute-start.38 = (bf16[128,1024]{1,0:T(8,128)(2,1)}, bf16[128,1024]{1,0:T(8,128)(2,1)}, u32[]{:S(2)}, u32[]{:S(2)}) collective-permute-start(bf16[128,1024]{1,0:T(8,128)(2,1)} %get-tuple-element.226), channel_id=1, source_target_pairs={{0,24},{1,25},{2,26},{3,27},{4,28},{5,29},{6,30},{7,31},{8,16},{9,... | collective-permute-start | bytes 786440 | tf_op jit(solution)/shard_map/ppermute | solution.py:89
  361.8 36.6 %collective-permute-start.33 = (bf16[4,128,1024]{2,1,0:T(8,128)(2,1)}, bf16[4,128,1024]{2,1,0:T(8,128)(2,1)}, u32[]{:S(2)}, u32[]{:S(2)}) collective-permute-start(bf16[4,128,1024]{2,1,0:T(8,128)(2,1)} %bitcast.112), channel_id=1, source_target_pairs={{0,4},{1,5},{2,6},{3,7},{4,0},{5,1},{6,2},{7,3},{8,12},{9,13},{10,... | collective-permute-start | bytes 3145736 | tf_op jit(solution)/shard_map/ppermute | solution.py:89
  361.9 36.4 %collective-permute-start.39 = (bf16[128,1024]{1,0:T(8,128)(2,1)}, bf16[128,1024]{1,0:T(8,128)(2,1)}, u32[]{:S(2)}, u32[]{:S(2)}) collective-permute-start(bf16[128,1024]{1,0:T(8,128)(2,1)} %get-tuple-element.239), channel_id=1, source_target_pairs={{0,8},{1,9},{2,10},{3,11},{4,12},{5,13},{6,14},{7,15},{8,0},{9,1},... | collective-permute-start | bytes 786440 | tf_op jit(solution)/shard_map/ppermute | solution.py:89
  362.6 35.8 %collective-permute-start.40 = (bf16[128,1024]{1,0:T(8,128)(2,1)}, bf16[128,1024]{1,0:T(8,128)(2,1)}, u32[]{:S(2)}, u32[]{:S(2)}) collective-permute-start(bf16[128,1024]{1,0:T(8,128)(2,1)} %get-tuple-element.240), channel_id=1, source_target_pairs={{0,16},{1,17},{2,18},{3,19},{4,20},{5,21},{6,22},{7,23},{8,24},{9,... | collective-permute-start | bytes 786440 | tf_op jit(solution)/shard_map/ppermute | solution.py:89
  366.4 32.0 %collective-permute-start.41 = (bf16[128,1024]{1,0:T(8,128)(2,1)}, bf16[128,1024]{1,0:T(8,128)(2,1)}, u32[]{:S(2)}, u32[]{:S(2)}) collective-permute-start(bf16[128,1024]{1,0:T(8,128)(2,1)} %get-tuple-element.241), channel_id=1, source_target_pairs={{0,24},{1,25},{2,26},{3,27},{4,28},{5,29},{6,30},{7,31},{8,16},{9,... | collective-permute-start | bytes 786440 | tf_op jit(solution)/shard_map/ppermute | solution.py:89
  401.7 25.9 %collective-permute-start.44 = (bf16[4,128,1024]{2,1,0:T(8,128)(2,1)}, bf16[4,128,1024]{2,1,0:T(8,128)(2,1)}, u32[]{:S(2)}, u32[]{:S(2)}) collective-permute-start(bf16[4,128,1024]{2,1,0:T(8,128)(2,1)} %get-tuple-element.248), channel_id=1, source_target_pairs={{0,1},{1,0},{2,3},{3,2},{4,5},{5,4},{6,7},{7,6},{8,9},{9,8},{10,11... | collective-permute-start | bytes 3145736 | tf_op jit(solution)/shard_map/ppermute | solution.py:89
  403.7 23.9 %collective-permute-start.42 = (bf16[4,128,1024]{2,1,0:T(8,128)(2,1)}, bf16[4,128,1024]{2,1,0:T(8,128)(2,1)}, u32[]{:S(2)}, u32[]{:S(2)}) collective-permute-start(bf16[4,128,1024]{2,1,0:T(8,128)(2,1)} %bitcast.113), channel_id=1, source_target_pairs={{0,4},{1,5},{2,6},{3,7},{4,0},{5,1},{6,2},{7,3},{8,12},{9,13},{10,... | collective-permute-start | bytes 3145736 | tf_op jit(solution)/shard_map/ppermute | solution.py:89
  403.7 26.3 %collective-permute-start.43 = (bf16[4,128,1024]{2,1,0:T(8,128)(2,1)}, bf16[4,128,1024]{2,1,0:T(8,128)(2,1)}, u32[]{:S(2)}, u32[]{:S(2)}) collective-permute-start(bf16[4,128,1024]{2,1,0:T(8,128)(2,1)} %get-tuple-element.247), channel_id=1, source_target_pairs={{0,2},{1,3},{2,0},{3,1},{4,6},{5,7},{6,4},{7,5},{8,10},{9,11},{10,... | collective-permute-start | bytes 3145736 | tf_op jit(solution)/shard_map/ppermute | solution.py:89
  434.5 28.1 %collective-permute-start.45 = (bf16[128,1024]{1,0:T(8,128)(2,1)}, bf16[128,1024]{1,0:T(8,128)(2,1)}, u32[]{:S(2)}, u32[]{:S(2)}) collective-permute-start(bf16[128,1024]{1,0:T(8,128)(2,1)} %get-tuple-element.264), channel_id=1, source_target_pairs={{0,8},{1,9},{2,10},{3,11},{4,12},{5,13},{6,14},{7,15},{8,0},{9,1},... | collective-permute-start | bytes 786440 | tf_op jit(solution)/shard_map/ppermute | solution.py:89
  435.2 27.4 %collective-permute-start.46 = (bf16[128,1024]{1,0:T(8,128)(2,1)}, bf16[128,1024]{1,0:T(8,128)(2,1)}, u32[]{:S(2)}, u32[]{:S(2)}) collective-permute-start(bf16[128,1024]{1,0:T(8,128)(2,1)} %get-tuple-element.265), channel_id=1, source_target_pairs={{0,16},{1,17},{2,18},{3,19},{4,20},{5,21},{6,22},{7,23},{8,24},{9,... | collective-permute-start | bytes 786440 | tf_op jit(solution)/shard_map/ppermute | solution.py:89
  438.9 23.6 %collective-permute-start.47 = (bf16[128,1024]{1,0:T(8,128)(2,1)}, bf16[128,1024]{1,0:T(8,128)(2,1)}, u32[]{:S(2)}, u32[]{:S(2)}) collective-permute-start(bf16[128,1024]{1,0:T(8,128)(2,1)} %get-tuple-element.266), channel_id=1, source_target_pairs={{0,24},{1,25},{2,26},{3,27},{4,28},{5,29},{6,30},{7,31},{8,16},{9,... | collective-permute-start | bytes 786440 | tf_op jit(solution)/shard_map/ppermute | solution.py:89
  463.9 10.2 %slice-start = ((bf16[128,3,256]{2,0,1:T(8,128)(2,1)}), bf16[128,2,256]{2,0,1:T(8,128)(2,1)S(1)}, s32[]{:S(2)}) async-start(bf16[128,3,256]{2,0,1:T(8,128)(2,1)} %param.19), calls=%async_computation.3 | async-start | bytes 262144 | tf_op jit(solution)/shard_map/slice | solution.py:978
  (15 other events, 60.2 us)
Sparse Core Ops, SparseCore 0:
  23.8 63.5 all-gather.8
  94.4 83.7 all-gather.6
  403.9 64.3 all-gather.10

commit v6 on v5

--- a/solution.py
+++ b/solution.py
@@ -208,10 +208,10 @@
         k = xt[cw + h * HEAD_DIM : cw + (h + 1) * HEAD_DIM]
         v = xt[2 * cw + h * HEAD_DIM : 2 * cw + (h + 1) * HEAD_DIM]
         hi, lo = split_query(q)
-        s = dotf(jnp.concatenate([k, k, aux], 0), jnp.concatenate([hi, lo, none], 0), 0, 0)
+        s = dotf(jnp.concatenate([k, k, aux], 0)[:, :SP], jnp.concatenate([hi, lo, none], 0), 0, 0)
         m = jnp.max(s, axis=0, keepdims=True)
         p = jnp.exp2(s - m).astype(BF)
-        o = dotf(jnp.concatenate([v, ones], 0), p, 1, 0)
+        o = dotf(jnp.concatenate([v, ones], 0)[:, :SP], p, 1, 0)
         total = o[HEAD_DIM : HEAD_DIM + 1]
         outs.append((o[:HEAD_DIM] / total).astype(BF))
         lse_ref[0, 0, h : h + 1, :] = m + jnp.log2(total)
@@ -236,14 +236,14 @@
         hi, lo = split_query(q)
         delta = jnp.sum(ot[at].astype(F32) * g.astype(F32), axis=0, keepdims=True)
         minus = split_rows(-lse_ref[0, 0, h : h + 1, :])
-        s = dotf(jnp.concatenate([k, k, aux], 0), jnp.concatenate([hi, lo, minus], 0), 0, 0)
+        s = dotf(jnp.concatenate([k, k, aux], 0)[:, :SP], jnp.concatenate([hi, lo, minus], 0), 0, 0)
         p = jnp.exp2(s)
-        d = dotf(jnp.concatenate([v, ones], 0), jnp.concatenate([g, split_rows(-delta)], 0), 0, 0)
+        d = dotf(jnp.concatenate([v, ones], 0)[:, :SP], jnp.concatenate([g, split_rows(-delta)], 0), 0, 0)
         ds = (p * d).astype(BF)
         dv.append(dotf(g, p.astype(BF), 1, 1).astype(BF))
-        dq.append((HEAD_DIM**-0.5 * dotf(k, ds, 1, 0)).astype(BF))
+        dq.append((HEAD_DIM**-0.5 * dotf(k[:, :SP], ds, 1, 0)).astype(BF))
         dk.append(dotf(q, ds, 1, 1).astype(BF))
-    out = jnp.concatenate(dq + dk + dv, 0).T[:SP]
+    out = jnp.concatenate([jnp.concatenate(dq, 0).T[:SP], jnp.concatenate(dk + dv, 0).T], 1)
     d_ref[...] = out
     sum_ref[0, 0, :, :] = jnp.sum(out.astype(F32), axis=0, keepdims=True)
 

time: 488 us -> 485 us (level)
  no operation moved by 1% of the time
where the time goes in v6:
time: 485 us; the launch traced here: 479 us
  Pallas kernels  301 us (62%)
  starting transfers between devices  54.6 us (11%)
  waiting for transfers between devices  53 us (11%)
  other arithmetic  29.4 us (6%)
  local copies, waits for them, and re-layouts  25.9 us (5%)
  between operations  15.6 us (3%)
    pallas_call x27, Pallas kernels, __call__(): pl.pallas_call(body, grid_spec=pltpu.PrefetchScalarGridSpec(num_scalar_pr...  301 us
    ppermute x48, starting transfers between devices, swap(): return lax.ppermute(x, AXES, [(i, i ^ mask) for i in range(size)])  53.9 us
    ppermute x48, waiting for transfers between devices, swap(): return lax.ppermute(x, AXES, [(i, i ^ mask) for i in range(size)])  50.3 us
    concatenate x12, other arithmetic, land(): self.held = jnp.concatenate([self.held, self.got])  14.4 us
  transfers between devices with their start and end apart: 51, of which 12 were waited for; matrix products, arithmetic and copies ran while one was open for 9% of the time, Pallas kernels for 62%

profile of v6, /device:TPU:0, one launch (start us, length us, event | category | flops | bytes accessed | tf_op | source)
XLA Modules:
  0.0 479.0 jit_solution(8430465699265525002)
XLA Ops:
  9.1 4.0 collective-permute-start
  17.9 3.1 collective-permute-done.refs_1_
  28.1 1.6 collective-permute-start.4
  30.7 1.6 collective-permute-start.2
  33.0 3.0 collective-permute-start.8
  36.0 3.4 collective-permute-start.5
  39.5 2.2 collective-permute-start.3
  41.7 1.5 collective-permute-start.7
  44.7 4.1 collective-permute-done.7.refs_3_
  48.8 1.3 collective-permute-done.9.refs_4_
  50.3 8.1 %collective-permute-done.3.refs_1_ = bf16[4,128,384]{2,1,0:T(8,128)(2,1)} collective-permute-done((bf16[4,128,384]{2,1,0:T(8,128)(2,1)S(1)}, bf16[4,128,384]{2,1,0:T(8,128)(2,1)}, u32[]{:S(2)}, u32[]{:S(2)}) %collective-permute-start.3) | collective-permute-done | bytes 393248 | tf_op jit(solution)/shard_map/ppermute | solution.py:89
  59.2 2.2 pad_maximum_fusion.3.refs_4_
  62.3 1.9 pad_maximum_fusion.5
  64.2 2.6 collective-permute-start.13
  66.8 2.0 pad_maximum_fusion.2.refs_0_
  68.8 2.0 collective-permute-start.10
  70.8 1.8 pad_maximum_fusion.4
  72.6 7.8 %prepare.1 = (bf16[1184,1024]{1,0:T(8,128)(2,1)}, bf16[1184,1024]{1,0:T(8,128)(2,1)}, bf16[1184,1024]{1,0:T(8,128)(2,1)}, f32[8,128]{1,0:T(8,128)}) custom-call(s32[4]{0:T(128)} %pad_add_fusion.me_ref, bf16[1154,1024]{1,0:T(8,128)(2,1)} %refs_0_.1, bf16[1154,1024]{1,0:T(8,128)(2,1)} %refs_1_.1, ...), custom_call_target="tpu_custom_call", output_to_operand_aliasing={{3}: (5, {})} | custom-call | flops 22000001024 | bytes 20000000 | tf_op jit(solution)/shard_map/prepare/pallas_call | solution.py:52
  80.4 5.8 %collective-permute-done.13.refs_4_ = bf16[4,128,512]{2,1,0:T(8,128)(2,1)} collective-permute-done((bf16[4,128,512]{2,1,0:T(8,128)(2,1)}, bf16[4,128,512]{2,1,0:T(8,128)(2,1)}, u32[]{:S(2)}, u32[]{:S(2)}) %collective-permute-start.13) | collective-permute-done | bytes 524320 | tf_op jit(solution)/shard_map/ppermute | solution.py:89
  86.3 7.3 %collective-permute-done.12.refs_3_ = bf16[4,128,512]{2,1,0:T(8,128)(2,1)} collective-permute-done((bf16[4,128,512]{2,1,0:T(8,128)(2,1)}, bf16[4,128,512]{2,1,0:T(8,128)(2,1)}, u32[]{:S(2)}, u32[]{:S(2)}) %collective-permute-start.12) | collective-permute-done | bytes 524320 | tf_op jit(solution)/shard_map/ppermute | solution.py:89
  95.4 2.3 pad_maximum_fusion.1.refs_4_.refs_0_
  97.7 1.6 collective-permute-start.19
  99.9 2.2 pad_maximum_fusion.refs_0_
  104.2 1.6 collective-permute-start.18
  105.9 34.3 %attend.1 = (bf16[1184,3072]{1,0:T(8,128)(2,1)}, bf16[1184,1024]{1,0:T(8,128)(2,1)}, f32[2,4,4,640]{3,2,1,0:T(4,128)}, f32[2,4,4,640]{3,2,1,0:T(4,128)}, f32[8,128]{1,0:T(8,128)}) custom-call(s32[4]{0:T(128)} %pad_add_fusion.me_ref, bf16[8,128,384]{2,1,0:T(8,128)(2,1)} %pad_maximum_fusion.2.refs_0_, ...), custom_call_target="tpu_custom_call", output_to_operand_aliasing={{4}: (11, {})} | custom-call | flops 39600001024 | bytes 36000000 | tf_op jit(solution)/shard_map/attend/pallas_call | solution.py:52
  142.6 9.3 %out_project.1 = (bf16[1184,1024]{1,0:T(8,128)(2,1)}, bf16[1184,1024]{1,0:T(8,128)(2,1)}, f32[8,128]{1,0:T(8,128)}) custom-call(s32[4]{0:T(128)} %pad_add_fusion.me_ref, bf16[32,144,256]{2,1,0:T(8,128)(2,1)} %bitcast.107, bf16[1184,1024]{1,0:T(8,128)(2,1)} %get-tuple-element.161.refs_1_.refs_4_.refs_9_, ...), custom_call_target="tpu_custom_call", output_to_operand_aliasing={{2}: (7, {})} | custom-call | flops 9900000256 | bytes 9000000 | tf_op jit(solution)/shard_map/out_project/pallas_call | solution.py:52
  152.0 37.9 %feed.2 = (bf16[1184,2048]{1,0:T(8,128)(2,1)}, f32[1,2048]{1,0:T(1,128)}, f32[1184,1024]{1,0:T(8,128)}, bf16[4,4,128,1024]{3,2,1,0:T(8,128)(2,1)}, bf16[4,4,128,1024]{3,2,1,0:T(8,128)(2,1)}, /*index=5*/f32[8,128]{1,0:T(8,128)}) custom-call(s32[4]{0:T(128)} %pad_add_fusion.me_ref, ...), custom_call_target="tpu_custom_call", output_to_operand_aliasing={{5}: (12, {})} | custom-call | flops 44000002048 | bytes 40000000 | tf_op jit(solution)/shard_map/feed/pallas_call | solution.py:52
  190.3 39.2 %feed.3 = (bf16[1184,2048]{1,0:T(8,128)(2,1)}, f32[1,2048]{1,0:T(1,128)}, bf16[1184,1024]{1,0:T(8,128)(2,1)}, bf16[4,4,128,1024]{3,2,1,0:T(8,128)(2,1)}, bf16[4,...) custom-call(s32[4]{0:T(128)} %pad_add_fusion.me_ref, ...), custom_call_target="tpu_custom_call", output_to_operand_aliasing={{5}: (7, {})} | custom-call | flops 44000002048 | bytes 40000000 | tf_op jit(solution)/shard_map/feed/pallas_call | solution.py:52
  230.1 6.6 %add.120 = (bf16[4,128,1024]{2,1,0:T(8,128)(2,1)}, bf16[4,128,1024]{2,1,0:T(8,128)(2,1)}, bf16[4,128,1024]{2,1,0:T(8,128)(2,1)}, bf16[4,128,1024]{2,1,0:T(8,128)(2,1)}, f32[8,128]{1,0:T(8,128)}) custom-call(s32[4]{0:T(128)} %pad_add_fusion.me_ref, bf16[4,4,128,1024]{3,2,1,0:T(8,128)(2,1)} %get-tuple-element.181.refs_0_, ...), custom_call_target="tpu_custom_call", output_to_operand_aliasing={{4}: (3, {})} | custom-call | tf_op jit(solution)/shard_map/add/pallas_call | solution.py:52
  237.2 1.5 collective-permute-start.30
  238.8 6.4 %add.121 = (bf16[4,128,1024]{2,1,0:T(8,128)(2,1)}, bf16[4,128,1024]{2,1,0:T(8,128)(2,1)}, bf16[4,128,1024]{2,1,0:T(8,128)(2,1)}, bf16[4,128,1024]{2,1,0:T(8,128)(2,1)}, f32[8,128]{1,0:T(8,128)}) custom-call(s32[4]{0:T(128)} %pad_add_fusion.me_ref, bf16[4,4,128,1024]{3,2,1,0:T(8,128)(2,1)} %get-tuple-element.179.refs_0_, ...), custom_call_target="tpu_custom_call", output_to_operand_aliasing={{4}: (3, {})} | custom-call | tf_op jit(solution)/shard_map/add/pallas_call | solution.py:52
  245.2 1.8 collective-permute-start.27
  247.2 18.6 %feed_back.1 = (bf16[1184,1024]{1,0:T(8,128)(2,1)}, bf16[1184,1024]{1,0:T(8,128)(2,1)}, f32[4,1024]{1,0:T(4,128)}, bf16[4,4,128,256]{3,2,1,0:T(8,128)(2,1)}, bf1...) custom-call(s32[4]{0:T(128)} %pad_add_fusion.me_ref, ...), custom_call_target="tpu_custom_call", output_to_operand_aliasing={{5}: (7, {})} | custom-call | flops 20899999744 | bytes 19000000 | tf_op jit(solution)/shard_map/feed_back/pallas_call | solution.py:52
  266.6 5.0 %collective-permute-done.27.refs_17_ = bf16[4,128,1024]{2,1,0:T(8,128)(2,1)} collective-permute-done((bf16[4,128,1024]{2,1,0:T(8,128)(2,1)}, bf16[4,128,1024]{2,1,0:T(8,128)(2,1)}, u32[]{:S(2)}, u32[]{:S(2)}) %collective-permute-start.27) | collective-permute-done | bytes 1048608 | tf_op jit(solution)/shard_map/ppermute | solution.py:89
  271.6 19.8 %attend_back.4 = (f32[2,1,1,768]{3,2,1,0:T(1,128)}, bf16[1184,1024]{1,0:T(8,128)(2,1)}, bf16[1,4,128,1024]{3,2,1,0:T(8,128)(2,1)}, bf16[1,4,128,1024]{3,2,1,0:T(...) custom-call(s32[4]{0:T(128)} %pad_add_fusion.me_ref, ...), custom_call_target="tpu_custom_call", output_to_operand_aliasing={{4}: (16, {}), {5}: (17, {}), {6}: (18, {})} | custom-call | flops 22000001024 | bytes 20000000 | tf_op jit(solution)/shard_map/attend_back/pallas_call | solution.py:52
  291.4 3.9 add.122
  295.4 1.8 collective-permute-start.32
  297.2 3.9 add.123
  301.4 20.2 %attend_back.5 = (f32[2,1,1,768]{3,2,1,0:T(1,128)}, bf16[1184,1024]{1,0:T(8,128)(2,1)}, bf16[1,4,128,1024]{3,2,1,0:T(8,128)(2,1)}, bf16[1,4,128,1024]{3,2,1,0:T(8,128)(2,1)}, f32[8,128]{1,0:T(8,128)}) custom-call(s32[4]{0:T(128)} %pad_add_fusion.me_ref, bf16[8,128,384]{2,1,0:T(8,128)(2,1)} %pad_maximum_fusion.2.refs_0_, ...), custom_call_target="tpu_custom_call", output_to_operand_aliasing={{4}: (16, {})} | custom-call | flops 22000001024 | bytes 20000000 | tf_op jit(solution)/shard_map/attend_back/pallas_call | solution.py:52
  322.9 3.0 add_plane.3
  326.0 3.1 add_plane.4
  329.1 3.3 add_core.3
  332.4 1.4 collective-permute-start.35
  333.8 1.7 collective-permute-start.36
  335.5 3.9 collective-permute-start.37
  339.4 19.7 %attend_back.6 = (f32[2,1,1,768]{3,2,1,0:T(1,128)}, bf16[1184,1024]{1,0:T(8,128)(2,1)}, bf16[1,4,128,1024]{3,2,1,0:T(8,128)(2,1)}, bf16[1,4,128,1024]{3,2,1,0:T(8,128)(2,1)}, f32[8,128]{1,0:T(8,128)}) custom-call(s32[4]{0:T(128)} %pad_add_fusion.me_ref, bf16[8,128,384]{2,1,0:T(8,128)(2,1)} %pad_maximum_fusion.2.refs_0_, ...), custom_call_target="tpu_custom_call", output_to_operand_aliasing={{4}: (16, {})} | custom-call | flops 22000001024 | bytes 20000000 | tf_op jit(solution)/shard_map/attend_back/pallas_call | solution.py:52
  360.6 3.8 collective-permute-start.40
  364.5 3.3 add_core.4
  367.7 24.7 %attend_back.7 = (f32[2,1,1,768]{3,2,1,0:T(1,128)}, bf16[1184,1024]{1,0:T(8,128)(2,1)}, f32[2,1024]{1,0:T(2,128)}, bf16[1,4,128,1024]{3,2,1,0:T(8,128)(2,1)}, bf...) custom-call(s32[4]{0:T(128)} %pad_add_fusion.me_ref, ...), custom_call_target="tpu_custom_call", output_to_operand_aliasing={{5}: (22, {})} | custom-call | flops 22000001024 | bytes 20000000 | tf_op jit(solution)/shard_map/attend_back/pallas_call | solution.py:52
  395.8 3.3 add_core.5
  399.1 1.8 collective-permute-start.44
  401.2 12.0 %feed_out.2 = (f32[1184,1024]{1,0:T(8,128)}, f32[8,128]{1,0:T(8,128)}) custom-call(s32[4]{0:T(128)} %pad_add_fusion.me_ref, bf16[8,128,512]{2,1,0:T(8,128)(2,1)} %pad_maximum_fusion.1.refs_4_.refs_0_, bf16[8,128,512]{2,1,0:T(8,128)(2,1)} %get-tuple-element.170.refs_5_.refs_1_, ...), custom_call_target="tpu_custom_call", output_to_operand_aliasing={{1}: (7, {})} | custom-call | flops 13200000000 | bytes 12000000 | tf_op jit(solution)/shard_map/feed_out/pallas_call | solution.py:52
  413.3 11.6 %collective-permute-done.44.refs_4_ = bf16[4,128,1024]{2,1,0:T(8,128)(2,1)} collective-permute-done((bf16[4,128,1024]{2,1,0:T(8,128)(2,1)}, bf16[4,128,1024]{2,1,0:T(8,128)(2,1)}, u32[]{:S(2)}, u32[]{:S(2)}) %collective-permute-start.44) | collective-permute-done | bytes 1048608 | tf_op jit(solution)/shard_map/ppermute | solution.py:89
  424.9 2.4 collective-permute-done.43.refs_3_
  427.3 4.2 add_plane.5
  432.1 3.8 collective-permute-start.46
  435.9 12.5 %feed_out.3 = (bf16[1184,1024]{1,0:T(8,128)(2,1)}, f32[8,128]{1,0:T(8,128)}, bf16[1184,1024]{1,0:T(8,128)(2,1)}, bf16[128,1024]{1,0:T(8,128)(2,1)}, bf16[128,102...) custom-call(s32[4]{0:T(128)} %pad_add_fusion.me_ref, ...), custom_call_target="tpu_custom_call", output_to_operand_aliasing={{1}: (5, {}), {2}: (6, {}), {3}: (7, {}), {4}: (8, {}), {5}... | custom-call | flops 13200000000 | bytes 12000000 | tf_op jit(solution)/shard_map/feed_out/pallas_call | solution.py:52
  448.4 1.8 convert_add_fusion
  451.4 1.9 slice.166
  453.3 1.9 reshape.177
  455.2 1.9 slice.167
  457.1 1.9 reshape.179
  463.0 2.7 all-gather.11.cloned.1.call-done
  465.7 1.6 reduce_sum.49
  (235 shorter events, 44.9 us)
Async XLA Ops:
  7.2 94.8 %all-gather.9.cloned.1.call-start = ((), (), s32[]{:S(2)}) async-start(), calls=%async_computation.1 | async-start | bytes 2433024 | tf_op jit(solution)/shard_map/all_gather | solution.py:131
  9.1 11.9 %collective-permute-start = (bf16[1,128,384]{2,1,0:T(8,128)(2,1)S(1)}, bf16[1,128,384]{2,1,0:T(8,128)(2,1)S(1)}, u32[]{:S(2)}, u32[]{:S(2)}) collective-permute-start(bf16[1,128,384]{2,1,0:T(8,128)(2,1)S(1)} %bitcast.82), channel_id=1, source_target_pairs={{0,16},{1,17},{2,18},{3,19},{4,20},{5,21},{6,22},{7,23},{8,24},{9,... | collective-permute-start | bytes 294920 | tf_op jit(solution)/shard_map/ppermute | solution.py:89
  13.3 7.7 %copy-start.4 = (bf16[128,384]{1,0:T(8,128)(2,1)}, bf16[128,384]{1,0:T(8,128)(2,1)S(1)}, u32[]{:S(2)}) copy-start(bf16[128,384]{1,0:T(8,128)(2,1)S(1)} %copy.139) | copy-start | bytes 294916
  13.3 9.0 %collective-permute-start.1 = (bf16[1,128,384]{2,1,0:T(8,128)(2,1)S(1)}, bf16[1,128,384]{2,1,0:T(8,128)(2,1)S(1)}, u32[]{:S(2)}, u32[]{:S(2)}) collective-permute-start(bf16[1,128,384]{2,1,0:T(8,128)(2,1)S(1)} %bitcast.86), channel_id=1, source_target_pairs={{0,16},{1,17},{2,18},{3,19},{4,20},{5,21},{6,22},{7,23},{8,24},{9,... | collective-permute-start | bytes 294920 | tf_op jit(solution)/shard_map/ppermute | solution.py:89
  23.6 12.4 %copy-start.5 = (bf16[128,384]{1,0:T(8,128)(2,1)S(1)}, bf16[128,384]{1,0:T(8,128)(2,1)}, u32[]{:S(2)}) copy-start(bf16[128,384]{1,0:T(8,128)(2,1)} %copy-done.4) | copy-start | bytes 294916
  23.6 12.4 %copy-start.10 = (bf16[1,128,384]{2,1,0:T(8,128)(2,1)S(1)}, bf16[1,128,384]{2,1,0:T(8,128)(2,1)}, u32[]{:S(2)}) copy-start(bf16[1,128,384]{2,1,0:T(8,128)(2,1)} %get-tuple-element.148) | copy-start | bytes 294916
  23.6 15.9 %copy-start.2 = (bf16[128,384]{1,0:T(8,128)(2,1)S(1)}, bf16[128,384]{1,0:T(8,128)(2,1)}, u32[]{:S(2)}) copy-start(bf16[128,384]{1,0:T(8,128)(2,1)} %copy-done.1) | copy-start | bytes 294916
  23.6 15.9 %copy-start.7 = (bf16[1,128,384]{2,1,0:T(8,128)(2,1)S(1)}, bf16[1,128,384]{2,1,0:T(8,128)(2,1)}, u32[]{:S(2)}) copy-start(bf16[1,128,384]{2,1,0:T(8,128)(2,1)} %get-tuple-element.147) | copy-start | bytes 294916
  23.6 166.6 %all-gather.7.cloned.1.call-start = ((), (), s32[]{:S(2)}) async-start(), calls=%async_computation | async-start | bytes 8650752 | tf_op jit(solution)/shard_map/all_gather | solution.py:131
  24.7 17.0 %collective-permute-start.6 = (bf16[1,128,512]{2,1,0:T(8,128)(2,1)S(1)}, bf16[1,128,512]{2,1,0:T(8,128)(2,1)S(1)}, u32[]{:S(2)}, u32[]{:S(2)}) collective-permute-start(bf16[1,128,512]{2,1,0:T(8,128)(2,1)S(1)} %get-tuple-element.331), channel_id=1, source_target_pairs={{0,16},{1,17},{2,18},{3,19},{4,20},{5,21},{6,22},{7,23},{8,24},{9,... | collective-permute-start | bytes 393224 | tf_op jit(solution)/shard_map/ppermute | solution.py:89
  28.1 7.9 %collective-permute-start.4 = (bf16[2,128,384]{2,1,0:T(8,128)(2,1)S(1)}, bf16[2,128,384]{2,1,0:T(8,128)(2,1)S(1)}, u32[]{:S(2)}, u32[]{:S(2)}) collective-permute-start(bf16[2,128,384]{2,1,0:T(8,128)(2,1)S(1)} %pad_maximum_fusion.13), channel_id=1, source_target_pairs={{0,2},{1,3},{2,0},{3,1},{4,6},{5,7},{6,4},{7,5},{8,10},{9,11},{10,... | collective-permute-start | bytes 589832 | tf_op jit(solution)/shard_map/ppermute | solution.py:89
  30.7 8.7 %collective-permute-start.2 = (bf16[2,128,384]{2,1,0:T(8,128)(2,1)S(1)}, bf16[2,128,384]{2,1,0:T(8,128)(2,1)S(1)}, u32[]{:S(2)}, u32[]{:S(2)}) collective-permute-start(bf16[2,128,384]{2,1,0:T(8,128)(2,1)S(1)} %pad_maximum_fusion.12), channel_id=1, source_target_pairs={{0,1},{1,0},{2,3},{3,2},{4,5},{5,4},{6,7},{7,6},{8,9},{9,8},{10,11... | collective-permute-start | bytes 589832 | tf_op jit(solution)/shard_map/ppermute | solution.py:89
  32.9 10.3 %copy-start = (bf16[1,128,512]{2,1,0:T(8,128)(2,1)}, bf16[1,128,512]{2,1,0:T(8,128)(2,1)S(1)}, u32[]{:S(2)}) copy-start(bf16[1,128,512]{2,1,0:T(8,128)(2,1)S(1)} %get-tuple-element.333) | copy-start | bytes 393220
  33.0 10.3 %collective-permute-start.8 = (bf16[1,128,512]{2,1,0:T(8,128)(2,1)S(1)}, bf16[1,128,512]{2,1,0:T(8,128)(2,1)S(1)}, u32[]{:S(2)}, u32[]{:S(2)}) collective-permute-start(bf16[1,128,512]{2,1,0:T(8,128)(2,1)S(1)} %get-tuple-element.333), channel_id=1, source_target_pairs={{0,16},{1,17},{2,18},{3,19},{4,20},{5,21},{6,22},{7,23},{8,24},{9,... | collective-permute-start | bytes 393224 | tf_op jit(solution)/shard_map/ppermute | solution.py:89
  35.9 8.0 %copy-start.17 = (bf16[2,128,384]{2,1,0:T(8,128)(2,1)}, bf16[2,128,384]{2,1,0:T(8,128)(2,1)S(1)}, u32[]{:S(2)}) copy-start(bf16[2,128,384]{2,1,0:T(8,128)(2,1)S(1)} %collective-permute-done.4) | copy-start | bytes 589828
  36.0 14.3 %collective-permute-start.5 = (bf16[4,128,384]{2,1,0:T(8,128)(2,1)S(1)}, bf16[4,128,384]{2,1,0:T(8,128)(2,1)}, u32[]{:S(2)}, u32[]{:S(2)}) collective-permute-start(bf16[4,128,384]{2,1,0:T(8,128)(2,1)S(1)} %pad_maximum_fusion.8), channel_id=1, source_target_pairs={{0,8},{1,9},{2,10},{3,11},{4,12},{5,13},{6,14},{7,15},{8,0},{9,1},... | collective-permute-start | bytes 1179656 | tf_op jit(solution)/shard_map/ppermute | solution.py:89
  39.5 18.9 %collective-permute-start.3 = (bf16[4,128,384]{2,1,0:T(8,128)(2,1)S(1)}, bf16[4,128,384]{2,1,0:T(8,128)(2,1)}, u32[]{:S(2)}, u32[]{:S(2)}) collective-permute-start(bf16[4,128,384]{2,1,0:T(8,128)(2,1)S(1)} %pad_maximum_fusion.7), channel_id=1, source_target_pairs={{0,8},{1,9},{2,10},{3,11},{4,12},{5,13},{6,14},{7,15},{8,0},{9,1},... | collective-permute-start | bytes 1179656 | tf_op jit(solution)/shard_map/ppermute | solution.py:89
  41.7 7.0 %collective-permute-start.7 = (bf16[2,128,512]{2,1,0:T(8,128)(2,1)S(1)}, bf16[2,128,512]{2,1,0:T(8,128)(2,1)}, u32[]{:S(2)}, u32[]{:S(2)}) collective-permute-start(bf16[2,128,512]{2,1,0:T(8,128)(2,1)S(1)} %pad_maximum_fusion.9), channel_id=1, source_target_pairs={{0,1},{1,0},{2,3},{3,2},{4,5},{5,4},{6,7},{7,6},{8,9},{9,8},{10,11... | collective-permute-start | bytes 786440 | tf_op jit(solution)/shard_map/ppermute | solution.py:89
  43.3 6.8 %collective-permute-start.9 = (bf16[2,128,512]{2,1,0:T(8,128)(2,1)S(1)}, bf16[2,128,512]{2,1,0:T(8,128)(2,1)}, u32[]{:S(2)}, u32[]{:S(2)}) collective-permute-start(bf16[2,128,512]{2,1,0:T(8,128)(2,1)S(1)} %pad_maximum_fusion.10), channel_id=1, source_target_pairs={{0,2},{1,3},{2,0},{3,1},{4,6},{5,7},{6,4},{7,5},{8,10},{9,11},{10,... | collective-permute-start | bytes 786440 | tf_op jit(solution)/shard_map/ppermute | solution.py:89
  59.1 11.6 %copy-start.12 = (bf16[1,128,512]{2,1,0:T(8,128)(2,1)S(1)}, bf16[1,128,512]{2,1,0:T(8,128)(2,1)}, u32[]{:S(2)}) copy-start(bf16[1,128,512]{2,1,0:T(8,128)(2,1)} %copy-done.11) | copy-start | bytes 393220
  61.3 32.2 %collective-permute-start.11 = (bf16[8,128,384]{2,1,0:T(8,128)(2,1)}, bf16[8,128,384]{2,1,0:T(8,128)(2,1)}, u32[]{:S(2)}, u32[]{:S(2)}) collective-permute-start(bf16[8,128,384]{2,1,0:T(8,128)(2,1)} %pad_maximum_fusion.3.refs_4_), channel_id=1, source_target_pairs={{0,1},{1,0},{2,3},{3,2},{4,5},{5,4},{6,7},{7,6},{8,9},{9,8},{10,11... | collective-permute-start | bytes 2359304 | tf_op jit(solution)/shard_map/ppermute | solution.py:89
  64.2 22.1 %collective-permute-start.13 = (bf16[4,128,512]{2,1,0:T(8,128)(2,1)}, bf16[4,128,512]{2,1,0:T(8,128)(2,1)}, u32[]{:S(2)}, u32[]{:S(2)}) collective-permute-start(bf16[4,128,512]{2,1,0:T(8,128)(2,1)} %pad_maximum_fusion.5), channel_id=1, source_target_pairs={{0,8},{1,9},{2,10},{3,11},{4,12},{5,13},{6,14},{7,15},{8,0},{9,1},... | collective-permute-start | bytes 1572872 | tf_op jit(solution)/shard_map/ppermute | solution.py:89
  68.8 24.8 %collective-permute-start.10 = (bf16[8,128,384]{2,1,0:T(8,128)(2,1)}, bf16[8,128,384]{2,1,0:T(8,128)(2,1)}, u32[]{:S(2)}, u32[]{:S(2)}) collective-permute-start(bf16[8,128,384]{2,1,0:T(8,128)(2,1)} %pad_maximum_fusion.2.refs_0_), channel_id=1, source_target_pairs={{0,2},{1,3},{2,0},{3,1},{4,6},{5,7},{6,4},{7,5},{8,10},{9,11},{10,... | collective-permute-start | bytes 2359304 | tf_op jit(solution)/shard_map/ppermute | solution.py:89
  72.6 21.0 %collective-permute-start.12 = (bf16[4,128,512]{2,1,0:T(8,128)(2,1)}, bf16[4,128,512]{2,1,0:T(8,128)(2,1)}, u32[]{:S(2)}, u32[]{:S(2)}) collective-permute-start(bf16[4,128,512]{2,1,0:T(8,128)(2,1)} %pad_maximum_fusion.4), channel_id=1, source_target_pairs={{0,8},{1,9},{2,10},{3,11},{4,12},{5,13},{6,14},{7,15},{8,0},{9,1},... | collective-permute-start | bytes 1572872 | tf_op jit(solution)/shard_map/ppermute | solution.py:89
  94.3 371.4 %all-gather.11.cloned.1.call-start = ((), (), s32[]{:S(2)}) async-start(), calls=%async_computation.2 | async-start | bytes 1892352 | tf_op jit(solution)/shard_map/all_gather | solution.py:944
  94.9 9.2 %collective-permute-start.16 = (bf16[8,128,384]{2,1,0:T(8,128)(2,1)}, bf16[8,128,384]{2,1,0:T(8,128)(2,1)}, u32[]{:S(2)}, u32[]{:S(2)}) collective-permute-start(bf16[8,128,384]{2,1,0:T(8,128)(2,1)} %pad_maximum_fusion.3.refs_4_), channel_id=1, source_target_pairs={{0,4},{1,5},{2,6},{3,7},{4,0},{5,1},{6,2},{7,3},{8,12},{9,13},{10,... | collective-permute-start | bytes 2359304 | tf_op jit(solution)/shard_map/ppermute | solution.py:89
  94.9 9.2 %collective-permute-start.14 = (bf16[8,128,384]{2,1,0:T(8,128)(2,1)}, bf16[8,128,384]{2,1,0:T(8,128)(2,1)}, u32[]{:S(2)}, u32[]{:S(2)}) collective-permute-start(bf16[8,128,384]{2,1,0:T(8,128)(2,1)} %pad_maximum_fusion.2.refs_0_), channel_id=1, source_target_pairs={{0,4},{1,5},{2,6},{3,7},{4,0},{5,1},{6,2},{7,3},{8,12},{9,13},{10,... | collective-permute-start | bytes 2359304 | tf_op jit(solution)/shard_map/ppermute | solution.py:89
  97.7 42.6 %collective-permute-start.19 = (bf16[8,128,512]{2,1,0:T(8,128)(2,1)}, bf16[8,128,512]{2,1,0:T(8,128)(2,1)}, u32[]{:S(2)}, u32[]{:S(2)}) collective-permute-start(bf16[8,128,512]{2,1,0:T(8,128)(2,1)} %pad_maximum_fusion.1.refs_4_.refs_0_), channel_id=1, source_target_pairs={{0,1},{1,0},{2,3},{3,2},{4,5},{5,4},{6,7},{7,6},{8,9},{9,8},{10,11... | collective-permute-start | bytes 3145736 | tf_op jit(solution)/shard_map/ppermute | solution.py:89
  99.3 6.4 %collective-permute-start.15 = (bf16[8,128,384]{2,1,0:T(8,128)(2,1)}, bf16[8,128,384]{2,1,0:T(8,128)(2,1)}, u32[]{:S(2)}, u32[]{:S(2)}) collective-permute-start(bf16[8,128,384]{2,1,0:T(8,128)(2,1)} %get-tuple-element.157.refs_1_), channel_id=1, source_target_pairs={{0,4},{1,5},{2,6},{3,7},{4,0},{5,1},{6,2},{7,3},{8,12},{9,13},{10,... | collective-permute-start | bytes 2359304 | tf_op jit(solution)/shard_map/ppermute | solution.py:89
  99.3 6.5 %collective-permute-start.17 = (bf16[8,128,384]{2,1,0:T(8,128)(2,1)}, bf16[8,128,384]{2,1,0:T(8,128)(2,1)}, u32[]{:S(2)}, u32[]{:S(2)}) collective-permute-start(bf16[8,128,384]{2,1,0:T(8,128)(2,1)} %get-tuple-element.158.refs_5_), channel_id=1, source_target_pairs={{0,4},{1,5},{2,6},{3,7},{4,0},{5,1},{6,2},{7,3},{8,12},{9,13},{10,... | collective-permute-start | bytes 2359304 | tf_op jit(solution)/shard_map/ppermute | solution.py:89
  104.1 47.8 %collective-permute-start.22 = (bf16[8,128,512]{2,1,0:T(8,128)(2,1)}, bf16[8,128,512]{2,1,0:T(8,128)(2,1)}, u32[]{:S(2)}, u32[]{:S(2)}) collective-permute-start(bf16[8,128,512]{2,1,0:T(8,128)(2,1)} %pad_maximum_fusion.1.refs_4_.refs_0_), channel_id=1, source_target_pairs={{0,4},{1,5},{2,6},{3,7},{4,0},{5,1},{6,2},{7,3},{8,12},{9,13},{10,... | collective-permute-start | bytes 3145736 | tf_op jit(solution)/shard_map/ppermute | solution.py:89
  104.2 36.1 %collective-permute-start.18 = (bf16[8,128,512]{2,1,0:T(8,128)(2,1)}, bf16[8,128,512]{2,1,0:T(8,128)(2,1)}, u32[]{:S(2)}, u32[]{:S(2)}) collective-permute-start(bf16[8,128,512]{2,1,0:T(8,128)(2,1)} %pad_maximum_fusion.refs_0_), channel_id=1, source_target_pairs={{0,2},{1,3},{2,0},{3,1},{4,6},{5,7},{6,4},{7,5},{8,10},{9,11},{10,... | collective-permute-start | bytes 3145736 | tf_op jit(solution)/shard_map/ppermute | solution.py:89
  105.7 46.3 %collective-permute-start.20 = (bf16[8,128,512]{2,1,0:T(8,128)(2,1)}, bf16[8,128,512]{2,1,0:T(8,128)(2,1)}, u32[]{:S(2)}, u32[]{:S(2)}) collective-permute-start(bf16[8,128,512]{2,1,0:T(8,128)(2,1)} %pad_maximum_fusion.refs_0_), channel_id=1, source_target_pairs={{0,4},{1,5},{2,6},{3,7},{4,0},{5,1},{6,2},{7,3},{8,12},{9,13},{10,... | collective-permute-start | bytes 3145736 | tf_op jit(solution)/shard_map/ppermute | solution.py:89
  141.0 11.0 %collective-permute-start.21 = (bf16[8,128,512]{2,1,0:T(8,128)(2,1)}, bf16[8,128,512]{2,1,0:T(8,128)(2,1)}, u32[]{:S(2)}, u32[]{:S(2)}) collective-permute-start(bf16[8,128,512]{2,1,0:T(8,128)(2,1)} %get-tuple-element.169.refs_1_), channel_id=1, source_target_pairs={{0,4},{1,5},{2,6},{3,7},{4,0},{5,1},{6,2},{7,3},{8,12},{9,13},{10,... | collective-permute-start | bytes 3145736 | tf_op jit(solution)/shard_map/ppermute | solution.py:89
  141.4 10.6 %collective-permute-start.23 = (bf16[8,128,512]{2,1,0:T(8,128)(2,1)}, bf16[8,128,512]{2,1,0:T(8,128)(2,1)}, u32[]{:S(2)}, u32[]{:S(2)}) collective-permute-start(bf16[8,128,512]{2,1,0:T(8,128)(2,1)} %get-tuple-element.170.refs_5_.refs_1_), channel_id=1, source_target_pairs={{0,4},{1,5},{2,6},{3,7},{4,0},{5,1},{6,2},{7,3},{8,12},{9,13},{10,... | collective-permute-start | bytes 3145736 | tf_op jit(solution)/shard_map/ppermute | solution.py:89
  189.9 40.2 %collective-permute-start.25 = (bf16[4,4,128,1024]{3,2,1,0:T(8,128)(2,1)}, bf16[4,4,128,1024]{3,2,1,0:T(8,128)(2,1)}, u32[]{:S(2)}, u32[]{:S(2)}) collective-permute-start(bf16[4,4,128,1024]{3,2,1,0:T(8,128)(2,1)} %get-tuple-element.182), channel_id=1, source_target_pairs={{0,4},{1,5},{2,6},{3,7},{4,0},{5,1},{6,2},{7,3},{8,12},{9,13},{10,... | collective-permute-start | bytes 12582920 | tf_op jit(solution)/shard_map/ppermute | solution.py:89
  190.3 39.5 %copy-start.20 = (f32[2,4,4,640]{3,2,1,0:T(4,128)S(1)}, f32[2,4,4,640]{3,2,1,0:T(4,128)}, u32[]{:S(2)}) copy-start(f32[2,4,4,640]{3,2,1,0:T(4,128)} %get-tuple-element.229) | copy-start | bytes 245764
  229.5 9.3 %collective-permute-start.24 = (bf16[4,4,128,1024]{3,2,1,0:T(8,128)(2,1)}, bf16[4,4,128,1024]{3,2,1,0:T(8,128)(2,1)}, u32[]{:S(2)}, u32[]{:S(2)}) collective-permute-start(bf16[4,4,128,1024]{3,2,1,0:T(8,128)(2,1)} %get-tuple-element.180), channel_id=1, source_target_pairs={{0,4},{1,5},{2,6},{3,7},{4,0},{5,1},{6,2},{7,3},{8,12},{9,13},{10,... | collective-permute-start | bytes 12582920 | tf_op jit(solution)/shard_map/ppermute | solution.py:89
  230.1 8.6 %copy-start.21 = (f32[1,2048]{1,0:T(1,128)S(1)}, f32[1,2048]{1,0:T(1,128)}, u32[]{:S(2)}) copy-start(f32[1,2048]{1,0:T(1,128)} %get-tuple-element.231) | copy-start | bytes 24580
  230.1 8.6 %copy-start.22 = (f32[1,2048]{1,0:T(1,128)S(1)}, f32[1,2048]{1,0:T(1,128)}, u32[]{:S(2)}) copy-start(f32[1,2048]{1,0:T(1,128)} %get-tuple-element.232) | copy-start | bytes 24580
  236.7 29.9 %collective-permute-start.26 = (bf16[4,128,1024]{2,1,0:T(8,128)(2,1)}, bf16[4,128,1024]{2,1,0:T(8,128)(2,1)}, u32[]{:S(2)}, u32[]{:S(2)}) collective-permute-start(bf16[4,128,1024]{2,1,0:T(8,128)(2,1)} %get-tuple-element.191), channel_id=1, source_target_pairs={{0,2},{1,3},{2,0},{3,1},{4,6},{5,7},{6,4},{7,5},{8,10},{9,11},{10,... | collective-permute-start | bytes 3145736 | tf_op jit(solution)/shard_map/ppermute | solution.py:89
  237.2 54.2 %collective-permute-start.30 = (bf16[4,128,1024]{2,1,0:T(8,128)(2,1)}, bf16[4,128,1024]{2,1,0:T(8,128)(2,1)}, u32[]{:S(2)}, u32[]{:S(2)}) collective-permute-start(bf16[4,128,1024]{2,1,0:T(8,128)(2,1)} %get-tuple-element.202), channel_id=1, source_target_pairs={{0,2},{1,3},{2,0},{3,1},{4,6},{5,7},{6,4},{7,5},{8,10},{9,11},{10,... | collective-permute-start | bytes 3145736 | tf_op jit(solution)/shard_map/ppermute | solution.py:89
  245.2 26.4 %collective-permute-start.27 = (bf16[4,128,1024]{2,1,0:T(8,128)(2,1)}, bf16[4,128,1024]{2,1,0:T(8,128)(2,1)}, u32[]{:S(2)}, u32[]{:S(2)}) collective-permute-start(bf16[4,128,1024]{2,1,0:T(8,128)(2,1)} %get-tuple-element.192), channel_id=1, source_target_pairs={{0,1},{1,0},{2,3},{3,2},{4,5},{5,4},{6,7},{7,6},{8,9},{9,8},{10,11... | collective-permute-start | bytes 3145736 | tf_op jit(solution)/shard_map/ppermute | solution.py:89
  247.0 50.2 %collective-permute-start.29 = (bf16[4,128,1024]{2,1,0:T(8,128)(2,1)}, bf16[4,128,1024]{2,1,0:T(8,128)(2,1)}, u32[]{:S(2)}, u32[]{:S(2)}) collective-permute-start(bf16[4,128,1024]{2,1,0:T(8,128)(2,1)} %get-tuple-element.198), channel_id=1, source_target_pairs={{0,1},{1,0},{2,3},{3,2},{4,5},{5,4},{6,7},{7,6},{8,9},{9,8},{10,11... | collective-permute-start | bytes 3145736 | tf_op jit(solution)/shard_map/ppermute | solution.py:89
  295.4 27.6 %collective-permute-start.32 = (bf16[4,128,1024]{2,1,0:T(8,128)(2,1)}, bf16[4,128,1024]{2,1,0:T(8,128)(2,1)}, u32[]{:S(2)}, u32[]{:S(2)}) collective-permute-start(bf16[4,128,1024]{2,1,0:T(8,128)(2,1)} %get-tuple-element.208), channel_id=1, source_target_pairs={{0,1},{1,0},{2,3},{3,2},{4,5},{5,4},{6,7},{7,6},{8,9},{9,8},{10,11... | collective-permute-start | bytes 3145736 | tf_op jit(solution)/shard_map/ppermute | solution.py:89
  301.1 24.9 %collective-permute-start.31 = (bf16[4,128,1024]{2,1,0:T(8,128)(2,1)}, bf16[4,128,1024]{2,1,0:T(8,128)(2,1)}, u32[]{:S(2)}, u32[]{:S(2)}) collective-permute-start(bf16[4,128,1024]{2,1,0:T(8,128)(2,1)} %get-tuple-element.206), channel_id=1, source_target_pairs={{0,2},{1,3},{2,0},{3,1},{4,6},{5,7},{6,4},{7,5},{8,10},{9,11},{10,... | collective-permute-start | bytes 3145736 | tf_op jit(solution)/shard_map/ppermute | solution.py:89
  301.4 27.8 %collective-permute-start.28 = (bf16[4,128,1024]{2,1,0:T(8,128)(2,1)}, bf16[4,128,1024]{2,1,0:T(8,128)(2,1)}, u32[]{:S(2)}, u32[]{:S(2)}) collective-permute-start(bf16[4,128,1024]{2,1,0:T(8,128)(2,1)} %bitcast.114), channel_id=1, source_target_pairs={{0,4},{1,5},{2,6},{3,7},{4,0},{5,1},{6,2},{7,3},{8,12},{9,13},{10,... | collective-permute-start | bytes 3145736 | tf_op jit(solution)/shard_map/ppermute | solution.py:89
  301.4 21.5 %copy-start.23 = (f32[2,1,1,768]{3,2,1,0:T(1,128)S(1)}, f32[2,1,1,768]{3,2,1,0:T(1,128)}, u32[]{:S(2)}) copy-start(f32[2,1,1,768]{3,2,1,0:T(1,128)} %get-tuple-element.237) | copy-start | bytes 18436
  321.6 38.3 %collective-permute-start.34 = (bf16[4,128,1024]{2,1,0:T(8,128)(2,1)}, bf16[4,128,1024]{2,1,0:T(8,128)(2,1)}, u32[]{:S(2)}, u32[]{:S(2)}) collective-permute-start(bf16[4,128,1024]{2,1,0:T(8,128)(2,1)} %bitcast.115), channel_id=1, source_target_pairs={{0,4},{1,5},{2,6},{3,7},{4,0},{5,1},{6,2},{7,3},{8,12},{9,13},{10,... | collective-permute-start | bytes 3145736 | tf_op jit(solution)/shard_map/ppermute | solution.py:89
  332.4 32.0 %collective-permute-start.35 = (bf16[4,128,1024]{2,1,0:T(8,128)(2,1)}, bf16[4,128,1024]{2,1,0:T(8,128)(2,1)}, u32[]{:S(2)}, u32[]{:S(2)}) collective-permute-start(bf16[4,128,1024]{2,1,0:T(8,128)(2,1)} %get-tuple-element.223), channel_id=1, source_target_pairs={{0,3},{1,2},{2,1},{3,0},{4,7},{5,6},{6,5},{7,4},{8,11},{9,10},{10,... | collective-permute-start | bytes 3145736 | tf_op jit(solution)/shard_map/ppermute | solution.py:89
  333.8 26.1 %collective-permute-start.36 = (bf16[128,1024]{1,0:T(8,128)(2,1)}, bf16[128,1024]{1,0:T(8,128)(2,1)}, u32[]{:S(2)}, u32[]{:S(2)}) collective-permute-start(bf16[128,1024]{1,0:T(8,128)(2,1)} %get-tuple-element.224), channel_id=1, source_target_pairs={{0,8},{1,9},{2,10},{3,11},{4,12},{5,13},{6,14},{7,15},{8,0},{9,1},... | collective-permute-start | bytes 786440 | tf_op jit(solution)/shard_map/ppermute | solution.py:89
  335.5 25.1 %collective-permute-start.37 = (bf16[128,1024]{1,0:T(8,128)(2,1)}, bf16[128,1024]{1,0:T(8,128)(2,1)}, u32[]{:S(2)}, u32[]{:S(2)}) collective-permute-start(bf16[128,1024]{1,0:T(8,128)(2,1)} %get-tuple-element.225), channel_id=1, source_target_pairs={{0,16},{1,17},{2,18},{3,19},{4,20},{5,21},{6,22},{7,23},{8,24},{9,... | collective-permute-start | bytes 786440 | tf_op jit(solution)/shard_map/ppermute | solution.py:89
  339.4 25.0 %collective-permute-start.38 = (bf16[128,1024]{1,0:T(8,128)(2,1)}, bf16[128,1024]{1,0:T(8,128)(2,1)}, u32[]{:S(2)}, u32[]{:S(2)}) collective-permute-start(bf16[128,1024]{1,0:T(8,128)(2,1)} %get-tuple-element.226), channel_id=1, source_target_pairs={{0,24},{1,25},{2,26},{3,27},{4,28},{5,29},{6,30},{7,31},{8,16},{9,... | collective-permute-start | bytes 786440 | tf_op jit(solution)/shard_map/ppermute | solution.py:89
  359.9 35.9 %collective-permute-start.33 = (bf16[4,128,1024]{2,1,0:T(8,128)(2,1)}, bf16[4,128,1024]{2,1,0:T(8,128)(2,1)}, u32[]{:S(2)}, u32[]{:S(2)}) collective-permute-start(bf16[4,128,1024]{2,1,0:T(8,128)(2,1)} %bitcast.112), channel_id=1, source_target_pairs={{0,4},{1,5},{2,6},{3,7},{4,0},{5,1},{6,2},{7,3},{8,12},{9,13},{10,... | collective-permute-start | bytes 3145736 | tf_op jit(solution)/shard_map/ppermute | solution.py:89
  360.0 35.8 %collective-permute-start.39 = (bf16[128,1024]{1,0:T(8,128)(2,1)}, bf16[128,1024]{1,0:T(8,128)(2,1)}, u32[]{:S(2)}, u32[]{:S(2)}) collective-permute-start(bf16[128,1024]{1,0:T(8,128)(2,1)} %get-tuple-element.239), channel_id=1, source_target_pairs={{0,8},{1,9},{2,10},{3,11},{4,12},{5,13},{6,14},{7,15},{8,0},{9,1},... | collective-permute-start | bytes 786440 | tf_op jit(solution)/shard_map/ppermute | solution.py:89
  360.6 35.2 %collective-permute-start.40 = (bf16[128,1024]{1,0:T(8,128)(2,1)}, bf16[128,1024]{1,0:T(8,128)(2,1)}, u32[]{:S(2)}, u32[]{:S(2)}) collective-permute-start(bf16[128,1024]{1,0:T(8,128)(2,1)} %get-tuple-element.240), channel_id=1, source_target_pairs={{0,16},{1,17},{2,18},{3,19},{4,20},{5,21},{6,22},{7,23},{8,24},{9,... | collective-permute-start | bytes 786440 | tf_op jit(solution)/shard_map/ppermute | solution.py:89
  364.4 31.4 %collective-permute-start.41 = (bf16[128,1024]{1,0:T(8,128)(2,1)}, bf16[128,1024]{1,0:T(8,128)(2,1)}, u32[]{:S(2)}, u32[]{:S(2)}) collective-permute-start(bf16[128,1024]{1,0:T(8,128)(2,1)} %get-tuple-element.241), channel_id=1, source_target_pairs={{0,24},{1,25},{2,26},{3,27},{4,28},{5,29},{6,30},{7,31},{8,16},{9,... | collective-permute-start | bytes 786440 | tf_op jit(solution)/shard_map/ppermute | solution.py:89
  399.1 25.7 %collective-permute-start.44 = (bf16[4,128,1024]{2,1,0:T(8,128)(2,1)}, bf16[4,128,1024]{2,1,0:T(8,128)(2,1)}, u32[]{:S(2)}, u32[]{:S(2)}) collective-permute-start(bf16[4,128,1024]{2,1,0:T(8,128)(2,1)} %get-tuple-element.248), channel_id=1, source_target_pairs={{0,1},{1,0},{2,3},{3,2},{4,5},{5,4},{6,7},{7,6},{8,9},{9,8},{10,11... | collective-permute-start | bytes 3145736 | tf_op jit(solution)/shard_map/ppermute | solution.py:89
  401.0 23.9 %collective-permute-start.42 = (bf16[4,128,1024]{2,1,0:T(8,128)(2,1)}, bf16[4,128,1024]{2,1,0:T(8,128)(2,1)}, u32[]{:S(2)}, u32[]{:S(2)}) collective-permute-start(bf16[4,128,1024]{2,1,0:T(8,128)(2,1)} %bitcast.113), channel_id=1, source_target_pairs={{0,4},{1,5},{2,6},{3,7},{4,0},{5,1},{6,2},{7,3},{8,12},{9,13},{10,... | collective-permute-start | bytes 3145736 | tf_op jit(solution)/shard_map/ppermute | solution.py:89
  401.0 26.3 %collective-permute-start.43 = (bf16[4,128,1024]{2,1,0:T(8,128)(2,1)}, bf16[4,128,1024]{2,1,0:T(8,128)(2,1)}, u32[]{:S(2)}, u32[]{:S(2)}) collective-permute-start(bf16[4,128,1024]{2,1,0:T(8,128)(2,1)} %get-tuple-element.247), channel_id=1, source_target_pairs={{0,2},{1,3},{2,0},{3,1},{4,6},{5,7},{6,4},{7,5},{8,10},{9,11},{10,... | collective-permute-start | bytes 3145736 | tf_op jit(solution)/shard_map/ppermute | solution.py:89
  431.5 28.3 %collective-permute-start.45 = (bf16[128,1024]{1,0:T(8,128)(2,1)}, bf16[128,1024]{1,0:T(8,128)(2,1)}, u32[]{:S(2)}, u32[]{:S(2)}) collective-permute-start(bf16[128,1024]{1,0:T(8,128)(2,1)} %get-tuple-element.264), channel_id=1, source_target_pairs={{0,8},{1,9},{2,10},{3,11},{4,12},{5,13},{6,14},{7,15},{8,0},{9,1},... | collective-permute-start | bytes 786440 | tf_op jit(solution)/shard_map/ppermute | solution.py:89
  432.1 27.7 %collective-permute-start.46 = (bf16[128,1024]{1,0:T(8,128)(2,1)}, bf16[128,1024]{1,0:T(8,128)(2,1)}, u32[]{:S(2)}, u32[]{:S(2)}) collective-permute-start(bf16[128,1024]{1,0:T(8,128)(2,1)} %get-tuple-element.265), channel_id=1, source_target_pairs={{0,16},{1,17},{2,18},{3,19},{4,20},{5,21},{6,22},{7,23},{8,24},{9,... | collective-permute-start | bytes 786440 | tf_op jit(solution)/shard_map/ppermute | solution.py:89
  435.9 23.9 %collective-permute-start.47 = (bf16[128,1024]{1,0:T(8,128)(2,1)}, bf16[128,1024]{1,0:T(8,128)(2,1)}, u32[]{:S(2)}, u32[]{:S(2)}) collective-permute-start(bf16[128,1024]{1,0:T(8,128)(2,1)} %get-tuple-element.266), channel_id=1, source_target_pairs={{0,24},{1,25},{2,26},{3,27},{4,28},{5,29},{6,30},{7,31},{8,16},{9,... | collective-permute-start | bytes 786440 | tf_op jit(solution)/shard_map/ppermute | solution.py:89
  461.1 10.3 %slice-start = ((bf16[128,3,256]{2,0,1:T(8,128)(2,1)}), bf16[128,2,256]{2,0,1:T(8,128)(2,1)S(1)}, s32[]{:S(2)}) async-start(bf16[128,3,256]{2,0,1:T(8,128)(2,1)} %param.19), calls=%async_computation.3 | async-start | bytes 262144 | tf_op jit(solution)/shard_map/slice | solution.py:978
  (15 other events, 60.4 us)
Sparse Core Ops, SparseCore 0:
  23.8 63.5 all-gather.8
  94.4 83.7 all-gather.6
  401.4 64.2 all-gather.10
